TPU v7x, 32 devices: a whole 2x2x4 slice. The times are simulated.
32 devices in a mesh: groups: 2 (over y), blk: 4 (over z), clus: 4 (over x, core).
Axes of the slice: x: 2, y: 2, z: 4, core: 2. Of those that a mesh axis runs over, the one named last changes fastest.
Arguments:
- embeddings: bfloat16 [8192, 1024], P(('groups', 'blk', 'clus')), parts along dimension 0
- cluster: int32 [8192], P(('groups', 'blk', 'clus')), parts along dimension 0, may hold values from 0 to 3, as said below
- row_ids: int32 [8192], P(('groups', 'blk', 'clus')), parts along dimension 0, may hold values from 0 to 4095, each once
Outputs:
- best_sim: float32 [8192], P(('groups', 'blk', 'clus')), parts along dimension 0
There are 2 independent parts, one for each index of `groups`. A program takes and returns all parts, laid end to end along the dimension named above; each array names one. Nothing has to cross between parts.
Inputs may be any that keep to these rules, and one draw needn't show every extreme that they name: In each device's aligned block of 256 rows no cluster appears more than 64 times, and some cluster appears exactly 64 times. `row_ids`: each index appears once.
All inputs are finite; a program needn't handle non-finite values.
Results may differ from a plain program's by a relative error of at most 0.00055.
Values may be sent and summed in bfloat16 or wider, within the bound.
No kernel may reach another device: no remote copies, remote signals or barrier semaphores. Data moves between devices by JAX's collectives and lax.ppermute only.
A program may use at most 64 MiB of HBM per device.

v0:
```python
import jax
import jax.numpy as jnp
from jax import lax
from jax.sharding import PartitionSpec as P

CAP = 64


sentinel_id = 1 << 30


def passed_along(value, axis, by):
    size = lax.axis_size(axis)
    return lax.ppermute(value, axis, [(i, (i + by) % size) for i in range(size)])


def local(embeddings, cluster, row_ids):
    owners = lax.axis_size("clus")
    loop_size = lax.axis_size("blk")
    feature_width = embeddings.shape[1]
    slot_count = owners * CAP
    values = embeddings.astype(jnp.float32)
    unit_rows = (
        values
        * lax.rsqrt(jnp.mean(values * values, axis=1, keepdims=True) + 1e-06)
        * feature_width ** (-0.5)
    ).astype(jnp.bfloat16)
    onehot = (cluster[:, None] == jnp.arange(owners, dtype=jnp.int32)[None, :]).astype(jnp.int32)
    before = jnp.cumsum(onehot, axis=0) - onehot
    position = jnp.sum(before * onehot, axis=1)
    target = cluster * CAP + position
    send_unit = jnp.zeros((slot_count, feature_width), jnp.bfloat16).at[target].set(unit_rows)
    send_ids = jnp.full((slot_count,), sentinel_id, jnp.int32).at[target].set(row_ids)
    got_unit, got_ids = (
        lax.all_to_all(
            send_unit.reshape(owners, CAP, feature_width),
            "clus",
            split_axis=0,
            concat_axis=0,
            tiled=True,
        ),
        lax.all_to_all(
            send_ids.reshape(owners, CAP), "clus", split_axis=0, concat_axis=0, tiled=True
        ),
    )
    keys_unit = got_unit.reshape(slot_count, feature_width)
    keys_ids = got_ids.reshape(slot_count)

    def scores_with(other_unit):
        return lax.dot_general(
            keys_unit, other_unit, (((1,), (1,)), ((), ())), preferred_element_type=jnp.float32
        )

    def absorb(best_now, other_unit, other_ids):
        scores = scores_with(other_unit)
        allowed = other_ids[None, :] < keys_ids[:, None]
        return jnp.maximum(best_now, jnp.max(jnp.where(allowed, scores, -1.0), axis=1))

    start_best = jnp.full((slot_count,), -1.0, jnp.float32)

    def advance(step_index, state_now):
        best_now, moving_unit, moving_ids = state_now
        moving_unit, moving_ids = passed_along((moving_unit, moving_ids), "blk", 1)
        return (absorb(best_now, moving_unit, moving_ids), moving_unit, moving_ids)

    best_sim, _, _ = lax.fori_loop(
        0, loop_size - 1, advance, (absorb(start_best, keys_unit, keys_ids), keys_unit, keys_ids)
    )
    returned = lax.all_to_all(
        best_sim.reshape(owners, CAP), "clus", split_axis=0, concat_axis=0, tiled=True
    )
    return returned.reshape(slot_count)[target]


def solution(mesh):
    return jax.shard_map(
        local,
        mesh=mesh,
        in_specs=(
            P(("groups", "blk", "clus"), None),
            P(("groups", "blk", "clus")),
            P(("groups", "blk", "clus")),
        ),
        out_specs=P(("groups", "blk", "clus")),
        check_vma=False,
    )
```

profile of v0, /device:TPU:0, one launch (start us, length us, event | category | flops | bytes accessed | tf_op | source)
XLA Modules:
  0.0 83.9 jit_solution(9714983383557874834)
XLA Ops:
  0.0 0.0 copy-start
  0.0 0.7 compare_convert_fusion
  0.7 1.2 %reduce-window.6 = s32[4,2,128]{2,1,0:T(2,128)S(1)} reduce-window(s32[4,2,128]{2,1,0:T(2,128)S(1)} %compare_convert_fusion, s32[]{:T(128)} %copy.25), window={size=1x1x128 pad=0_0x0_0x127_0}, to_apply=%region_0.0 | reduce-window | flops 130048 | bytes 8196 | tf_op jit(solution)/shard_map/reduce-window
  2.0 0.1 slice.10
  2.0 0.1 copy.8
  2.2 0.1 copy.9
  2.3 0.1 add_bitcast_fusion
  2.3 0.7 fusion.11
  3.0 0.7 compare_select_fusion
  3.7 1.6 %scatter_custom_fusion = s32[256]{0:T(256)S(1)} fusion(s32[256]{0:T(256)S(1)} %compare_select_fusion, s32[256]{0:T(256)} %param.7, s32[]{:T(128)} %constant.7.clone.1), kind=kCustom, calls=%fused_computation.26 | custom fusion | bytes 1536 | tf_op jit(solution)/shard_map/scatter | solution.py:33
  5.3 0.7 all_to_all.17
  6.0 4.2 %all-to-all-start = ((s32[4,1,64]{2,1,0:T(1,128)}), s32[4,1,64]{2,1,0:T(1,128)S(1)}, u32[]{:S(2)}, u32[]{:S(2)}) async-start(s32[4,1,64]{2,1,0:T(1,128)} %all_to_all.17), calls=%async_computation | async-start | bytes 4096 | tf_op jit(solution)/shard_map/all_to_all | solution.py:42
  10.2 1.2 %fusion.1 = f32[256]{0:T(256)S(1)} fusion(bf16[256,1024]{1,0:T(8,128)(2,1)} %param.5), kind=kLoop, calls=%fused_computation.8 | loop fusion | flops 786176 | bytes 525312 | tf_op jit(solution)/shard_map/reduce_sum | solution.py:25
  11.4 0.0 copy-done
  11.4 2.5 %scatter_custom_fusion.1 = bf16[256,1024]{1,0:T(8,128)(2,1)} fusion(s32[256]{0:T(256)S(1)} %compare_select_fusion, bf16[256,1024]{1,0:T(8,128)(2,1)S(1)} %copy-done, f32[]{:T(128)} %constant.13.clone.1, f32[256]{0:T(256)S(1)} %add_rsqrt_fusion, bf16[]{:T(256)} %constant.9.clone.1), kind=kCustom, calls=%fused_computation.11 | custom fusion | flops 1048576 | bytes 1049606 | tf_op jit(solution)/shard_map/scatter | solution.py:32
  14.0 0.0 all-to-all-done
  14.0 0.0 copy-start.1
  14.0 3.5 %all-to-all-start.1 = ((bf16[4,64,1024]{2,1,0:T(8,128)(2,1)}), bf16[4,64,1024]{2,1,0:T(8,128)(2,1)S(1)}, u32[]{:S(2)}, u32[]{:S(2)}) async-start(bf16[4,64,1024]{2,1,0:T(8,128)(2,1)} %bitcast.3), calls=%async_computation.1 | async-start | bytes 1048576 | tf_op jit(solution)/shard_map/all_to_all | solution.py:35
  17.4 0.5 broadcast.51
  17.9 0.6 reduce.6
  18.5 0.1 lt.39
  18.6 0.0 copy-done.1
  18.6 0.1 lt.50
  18.7 7.6 %all-to-all-done.1 = bf16[4,64,1024]{2,1,0:T(8,128)(2,1)S(1)} async-done(((bf16[4,64,1024]{2,1,0:T(8,128)(2,1)}), bf16[4,64,1024]{2,1,0:T(8,128)(2,1)S(1)}, u32[]{:S(2)}, u32[]{:S(2)}) %all-to-all-start.1) | async-done | bytes 524320 | tf_op jit(solution)/shard_map/all_to_all | solution.py:35
  26.3 0.4 fusion
  26.7 45.8 %while.15 = (s32[]{:T(128)}, f32[256]{0:T(256)S(1)}, bf16[256,1024]{1,0:T(8,128)(2,1)S(1)}, s32[256]{0:T(256)S(1)}, s32[4,64]{1,0:T(4,128)}, /*index=5*/bf16[256,1024]{1,0:T(8,128)(2,1)S(1)}, s32[256]{0:T(256)S(1)}, s32[]{:T(128)}) while((s32[]{:T(128)}, f32[256]{0:T(256)S(1)}, bf16[256,1024]{1,0:T(8,128)(2,1)S(1)}, ...), condition=%wide.wide.region_9.10_spmd, body=%wide.wide.region_7.9_spmd.sunk | while | flops 134414336 | bytes 4206757 | solution.py:66
  26.7 2.1 %collective-permute-start.1 = (bf16[256,1024]{1,0:T(8,128)(2,1)S(1)}, bf16[256,1024]{1,0:T(8,128)(2,1)S(1)}, u32[]{:S(2)}, u32[]{:S(2)}) collective-permute-start(bf16[256,1024]{1,0:T(8,128)(2,1)S(1)} %get-tuple-element.127), channel_id=1, source_target_pairs={{0,4},{4,8},{8,12},{12,0},{1,5},{5,9},{9,13},{13,1},{2,6},{6,10},{... | collective-permute-start | bytes 1572872 | tf_op jit(solution)/shard_map/while/body/eval_jaxpr/ppermute | solution.py:14
  28.8 1.6 %collective-permute-start = (s32[256]{0:T(256)S(1)}, s32[256]{0:T(256)S(1)}, u32[]{:S(2)}, u32[]{:S(2)}) collective-permute-start(s32[256]{0:T(256)S(1)} %get-tuple-element.128), channel_id=1, source_target_pairs={{0,4},{4,8},{8,12},{12,0},{1,5},{5,9},{9,13},{13,1},{2,6},{6,10},{... | collective-permute-start | bytes 3080 | tf_op jit(solution)/shard_map/while/body/eval_jaxpr/ppermute | solution.py:14
  30.4 12.2 %collective-permute-done = s32[256]{0:T(256)S(1)} collective-permute-done((s32[256]{0:T(256)S(1)}, s32[256]{0:T(256)S(1)}, u32[]{:S(2)}, u32[]{:S(2)}) %collective-permute-start) | collective-permute-done | bytes 1056 | tf_op jit(solution)/shard_map/while/body/eval_jaxpr/ppermute | solution.py:14
  42.6 0.0 collective-permute-done.1
  42.6 0.4 select_reduce_fusion.3
  43.0 0.1 collective-permute-start.1
  43.1 1.3 %collective-permute-start = (s32[256]{0:T(256)S(1)}, s32[256]{0:T(256)S(1)}, u32[]{:S(2)}, u32[]{:S(2)}) collective-permute-start(s32[256]{0:T(256)S(1)} %get-tuple-element.128), channel_id=1, source_target_pairs={{0,4},{4,8},{8,12},{12,0},{1,5},{5,9},{9,13},{13,1},{2,6},{6,10},{... | collective-permute-start | bytes 3080 | tf_op jit(solution)/shard_map/while/body/eval_jaxpr/ppermute | solution.py:14
  44.4 13.4 %collective-permute-done = s32[256]{0:T(256)S(1)} collective-permute-done((s32[256]{0:T(256)S(1)}, s32[256]{0:T(256)S(1)}, u32[]{:S(2)}, u32[]{:S(2)}) %collective-permute-start) | collective-permute-done | bytes 1056 | tf_op jit(solution)/shard_map/while/body/eval_jaxpr/ppermute | solution.py:14
  57.8 0.0 collective-permute-done.1
  57.8 0.4 select_reduce_fusion.3
  58.2 0.1 collective-permute-start.1
  58.3 0.1 collective-permute-start
  58.4 13.7 %collective-permute-done = s32[256]{0:T(256)S(1)} collective-permute-done((s32[256]{0:T(256)S(1)}, s32[256]{0:T(256)S(1)}, u32[]{:S(2)}, u32[]{:S(2)}) %collective-permute-start) | collective-permute-done | bytes 1056 | tf_op jit(solution)/shard_map/while/body/eval_jaxpr/ppermute | solution.py:14
  72.0 0.0 collective-permute-done.1
  72.0 0.4 select_reduce_fusion.3
  72.5 0.7 all_to_all.21
  73.1 3.2 %all-to-all-start.2 = ((f32[4,1,64]{2,1,0:T(1,128)}), f32[4,1,64]{2,1,0:T(1,128)S(1)}, u32[]{:S(2)}, u32[]{:S(2)}) async-start(f32[4,1,64]{2,1,0:T(1,128)} %all_to_all.21), calls=%async_computation.2 | async-start | bytes 4096 | tf_op jit(solution)/shard_map/all_to_all | solution.py:69
  76.4 3.7 %all-to-all-done.2 = f32[4,1,64]{2,1,0:T(1,128)S(1)} async-done(((f32[4,1,64]{2,1,0:T(1,128)}), f32[4,1,64]{2,1,0:T(1,128)S(1)}, u32[]{:S(2)}, u32[]{:S(2)}) %all-to-all-start.2) | async-done | bytes 1056 | tf_op jit(solution)/shard_map/all_to_all | solution.py:69
  80.1 0.5 broadcast.52
  80.6 0.7 reduce.7
  81.3 0.1 reshape.53
  81.4 2.5 %gather_fusion = f32[256]{0:T(256)} fusion(f32[256]{0:T(256)S(1)} %reshape.53, s32[1024]{0:T(1024)S(1)} %pad_clamp_fusion), kind=kCustom, calls=%fused_computation | custom fusion | bytes 3072 | tf_op jit(solution)/shard_map/gather | solution.py:72
  (15 shorter events, 0.2 us)
Async XLA Ops:
  0.0 11.4 %copy-start = (bf16[256,1024]{1,0:T(8,128)(2,1)S(1)}, bf16[256,1024]{1,0:T(8,128)(2,1)}, u32[]{:S(2)}) copy-start(bf16[256,1024]{1,0:T(8,128)(2,1)} %param.5) | copy-start | bytes 1572868
  6.0 8.0 %all-to-all-start = ((s32[4,1,64]{2,1,0:T(1,128)}), s32[4,1,64]{2,1,0:T(1,128)S(1)}, u32[]{:S(2)}, u32[]{:S(2)}) async-start(s32[4,1,64]{2,1,0:T(1,128)} %all_to_all.17), calls=%async_computation | async-start | bytes 4096 | tf_op jit(solution)/shard_map/all_to_all | solution.py:42
  14.0 4.7 %copy-start.1 = (s32[4,1,64]{2,1,0:T(1,128)}, s32[4,1,64]{2,1,0:T(1,128)S(1)}, u32[]{:S(2)}) copy-start(s32[4,1,64]{2,1,0:T(1,128)S(1)} %all-to-all-done) | copy-start | bytes 3076
  14.0 12.3 %all-to-all-start.1 = ((bf16[4,64,1024]{2,1,0:T(8,128)(2,1)}), bf16[4,64,1024]{2,1,0:T(8,128)(2,1)S(1)}, u32[]{:S(2)}, u32[]{:S(2)}) async-start(bf16[4,64,1024]{2,1,0:T(8,128)(2,1)} %bitcast.3), calls=%async_computation.1 | async-start | bytes 1048576 | tf_op jit(solution)/shard_map/all_to_all | solution.py:35
  26.7 15.9 %collective-permute-start.1 = (bf16[256,1024]{1,0:T(8,128)(2,1)S(1)}, bf16[256,1024]{1,0:T(8,128)(2,1)S(1)}, u32[]{:S(2)}, u32[]{:S(2)}) collective-permute-start(bf16[256,1024]{1,0:T(8,128)(2,1)S(1)} %get-tuple-element.127), channel_id=1, source_target_pairs={{0,4},{4,8},{8,12},{12,0},{1,5},{5,9},{9,13},{13,1},{2,6},{6,10},{... | collective-permute-start | bytes 1572872 | tf_op jit(solution)/shard_map/while/body/eval_jaxpr/ppermute | solution.py:14
  28.8 13.8 %collective-permute-start = (s32[256]{0:T(256)S(1)}, s32[256]{0:T(256)S(1)}, u32[]{:S(2)}, u32[]{:S(2)}) collective-permute-start(s32[256]{0:T(256)S(1)} %get-tuple-element.128), channel_id=1, source_target_pairs={{0,4},{4,8},{8,12},{12,0},{1,5},{5,9},{9,13},{13,1},{2,6},{6,10},{... | collective-permute-start | bytes 3080 | tf_op jit(solution)/shard_map/while/body/eval_jaxpr/ppermute | solution.py:14
  43.0 14.8 %collective-permute-start.1 = (bf16[256,1024]{1,0:T(8,128)(2,1)S(1)}, bf16[256,1024]{1,0:T(8,128)(2,1)S(1)}, u32[]{:S(2)}, u32[]{:S(2)}) collective-permute-start(bf16[256,1024]{1,0:T(8,128)(2,1)S(1)} %get-tuple-element.127), channel_id=1, source_target_pairs={{0,4},{4,8},{8,12},{12,0},{1,5},{5,9},{9,13},{13,1},{2,6},{6,10},{... | collective-permute-start | bytes 1572872 | tf_op jit(solution)/shard_map/while/body/eval_jaxpr/ppermute | solution.py:14
  43.1 14.7 %collective-permute-start = (s32[256]{0:T(256)S(1)}, s32[256]{0:T(256)S(1)}, u32[]{:S(2)}, u32[]{:S(2)}) collective-permute-start(s32[256]{0:T(256)S(1)} %get-tuple-element.128), channel_id=1, source_target_pairs={{0,4},{4,8},{8,12},{12,0},{1,5},{5,9},{9,13},{13,1},{2,6},{6,10},{... | collective-permute-start | bytes 3080 | tf_op jit(solution)/shard_map/while/body/eval_jaxpr/ppermute | solution.py:14
  58.2 13.8 %collective-permute-start.1 = (bf16[256,1024]{1,0:T(8,128)(2,1)S(1)}, bf16[256,1024]{1,0:T(8,128)(2,1)S(1)}, u32[]{:S(2)}, u32[]{:S(2)}) collective-permute-start(bf16[256,1024]{1,0:T(8,128)(2,1)S(1)} %get-tuple-element.127), channel_id=1, source_target_pairs={{0,4},{4,8},{8,12},{12,0},{1,5},{5,9},{9,13},{13,1},{2,6},{6,10},{... | collective-permute-start | bytes 1572872 | tf_op jit(solution)/shard_map/while/body/eval_jaxpr/ppermute | solution.py:14
  58.3 13.7 %collective-permute-start = (s32[256]{0:T(256)S(1)}, s32[256]{0:T(256)S(1)}, u32[]{:S(2)}, u32[]{:S(2)}) collective-permute-start(s32[256]{0:T(256)S(1)} %get-tuple-element.128), channel_id=1, source_target_pairs={{0,4},{4,8},{8,12},{12,0},{1,5},{5,9},{9,13},{13,1},{2,6},{6,10},{... | collective-permute-start | bytes 3080 | tf_op jit(solution)/shard_map/while/body/eval_jaxpr/ppermute | solution.py:14
  73.1 7.0 %all-to-all-start.2 = ((f32[4,1,64]{2,1,0:T(1,128)}), f32[4,1,64]{2,1,0:T(1,128)S(1)}, u32[]{:S(2)}, u32[]{:S(2)}) async-start(f32[4,1,64]{2,1,0:T(1,128)} %all_to_all.21), calls=%async_computation.2 | async-start | bytes 4096 | tf_op jit(solution)/shard_map/all_to_all | solution.py:69
where the time goes:
time: 84.3 us; the launch traced here: 83.9 us
  waiting for transfers between devices  50.6 us (60%)
  starting transfers between devices  16.1 us (19%)
  other arithmetic  8.51 us (10%)
  local copies, waits for them, and re-layouts  7.1 us (8%)
  matrix products  1.42 us (2%)
    ppermute x6, waiting for transfers between devices, passed_along(): lax.ppermute(value, axis, [(i, (i + by) % size) for i in range(size)])  39.3 us
    all_to_all x1, waiting for transfers between devices, local(): lax.all_to_all(send_unit.reshape(owners, CAP, feature_width), 'clus', spl...  7.55 us
    ppermute x6, starting transfers between devices, passed_along(): lax.ppermute(value, axis, [(i, (i + by) % size) for i in range(size)])  5.15 us
    all_to_all x1, starting transfers between devices, local(): lax.all_to_all(send_ids.reshape(owners, CAP), 'clus', split_axis=0, conca...  4.21 us
    all_to_all x1, waiting for transfers between devices, local(): lax.all_to_all(best_sim.reshape(owners, CAP), 'clus', split_axis=0, conca...  3.7 us
    all_to_all x1, starting transfers between devices, local(): lax.all_to_all(send_unit.reshape(owners, CAP, feature_width), 'clus', spl...  3.47 us
    all_to_all x1, starting transfers between devices, local(): lax.all_to_all(best_sim.reshape(owners, CAP), 'clus', split_axis=0, conca...  3.24 us
    scatter x1, other arithmetic, local(): jnp.zeros((slot_count, feature_width), jnp.bfloat16).at[target]  2.55 us
  transfers between devices with their start and end apart: 9, of which 5 were waited for; matrix products, arithmetic and copies ran while one was open for 6% of the time, Pallas kernels for 0%

commit v1 on v0

v1 whole, which is shorter than its diff:
```python
import functools

import jax
import jax.numpy as jnp
from jax import lax
from jax.experimental import pallas as pl
from jax.experimental.pallas import tpu as pltpu
from jax.sharding import PartitionSpec as P

CAP = 64
EPS = 1e-06
sentinel_id = 1 << 30
VMEM = pl.BlockSpec(memory_space=pltpu.VMEM)


def passed_along(value, axis, by):
    size = lax.axis_size(axis)
    return lax.ppermute(value, axis, [(i, (i + by) % size) for i in range(size)])


def ring(embeddings, cluster, row_ids):
    owners = lax.axis_size("clus")
    loop_size = lax.axis_size("blk")
    feature_width = embeddings.shape[1]
    slot_count = owners * CAP
    values = embeddings.astype(jnp.float32)
    unit_rows = (
        values
        * lax.rsqrt(jnp.mean(values * values, axis=1, keepdims=True) + EPS)
        * feature_width ** (-0.5)
    ).astype(jnp.bfloat16)
    onehot = (cluster[:, None] == jnp.arange(owners, dtype=jnp.int32)[None, :]).astype(jnp.int32)
    before = jnp.cumsum(onehot, axis=0) - onehot
    position = jnp.sum(before * onehot, axis=1)
    target = cluster * CAP + position
    send_unit = jnp.zeros((slot_count, feature_width), jnp.bfloat16).at[target].set(unit_rows)
    send_ids = jnp.full((slot_count,), sentinel_id, jnp.int32).at[target].set(row_ids)
    exchange = functools.partial(
        lax.all_to_all, axis_name="clus", split_axis=0, concat_axis=0, tiled=True
    )
    keys_unit = exchange(send_unit.reshape(owners, CAP, feature_width)).reshape(
        slot_count, feature_width
    )
    keys_ids = exchange(send_ids.reshape(owners, CAP)).reshape(slot_count)

    def absorb(best_now, other_unit, other_ids):
        scores = lax.dot_general(
            keys_unit, other_unit, (((1,), (1,)), ((), ())), preferred_element_type=jnp.float32
        )
        allowed = other_ids[None, :] < keys_ids[:, None]
        return jnp.maximum(best_now, jnp.max(jnp.where(allowed, scores, -1.0), axis=1))

    start_best = jnp.full((slot_count,), -1.0, jnp.float32)

    def advance(step_index, state_now):
        best_now, moving_unit, moving_ids = state_now
        moving_unit, moving_ids = passed_along((moving_unit, moving_ids), "blk", 1)
        return (absorb(best_now, moving_unit, moving_ids), moving_unit, moving_ids)

    best_sim, _, _ = lax.fori_loop(
        0, loop_size - 1, advance, (absorb(start_best, keys_unit, keys_ids), keys_unit, keys_ids)
    )
    returned = exchange(best_sim.reshape(owners, CAP)).reshape(slot_count)
    return returned[target]


def meeting_blk(c, blocks):
    return (blocks - 1) // 2 + (c % 2 if blocks > 1 else 0)


def meeting_here(owners, blocks):
    u = lax.axis_index("clus")
    b = lax.axis_index("blk")
    middle = (blocks - 1) // 2 + (lax.rem(u, 2) if blocks > 1 else 0)
    return u, b, b == middle


def sort_kernel(owners, emb_ref, cluster_ref, ids_ref, *outs):
    slot_refs, sorted_ids_ref, target_ref = outs[:owners], outs[owners], outs[owners + 1]
    rows, width = emb_ref.shape
    slots = owners * CAP
    u = lax.axis_index("clus")
    slot = lax.rem(cluster_ref[...] - u + owners, owners)
    onehot = lax.broadcasted_iota(jnp.int32, (8, rows), 0) == slot
    earlier = (
        lax.broadcasted_iota(jnp.int32, (rows, rows), 0)
        < lax.broadcasted_iota(jnp.int32, (rows, rows), 1)
    ).astype(jnp.bfloat16)
    before = jnp.dot(
        onehot.astype(jnp.bfloat16), earlier, preferred_element_type=jnp.float32
    )
    position = jnp.sum(jnp.where(onehot, before, 0.0), axis=0, keepdims=True)
    target = slot * CAP + position.astype(jnp.int32)
    target_ref[...] = target
    place = (lax.broadcasted_iota(jnp.int32, (slots, rows), 0) == target).astype(jnp.bfloat16)
    values = jnp.dot(place, emb_ref[...], preferred_element_type=jnp.float32)
    mean = jnp.mean(values * values, axis=1, keepdims=True)
    unit = (values * lax.rsqrt(mean + EPS) * width ** (-0.5)).astype(jnp.bfloat16)
    for j in range(owners):
        slot_refs[j][...] = unit[j * CAP : (j + 1) * CAP]
    ids = ids_ref[...]
    row = lax.broadcasted_iota(jnp.int32, (8, rows), 0)
    parts = jnp.where(row == 0, ids >> 8, jnp.where(row == 1, ids & 255, 1))
    moved = lax.dot_general(
        parts.astype(jnp.float32).astype(jnp.bfloat16),
        place,
        (((1,), (1,)), ((), ())),
        preferred_element_type=jnp.float32,
    ).astype(jnp.int32)
    sorted_ids = moved[0:1] * 256 + moved[1:2]
    sorted_ids_ref[...] = jnp.where(moved[2:3] > 0, sorted_ids, sentinel_id)


def order_kernel(owners, blocks, all_ids_ref, row_ref, column_ref):
    u, b, _ = meeting_here(owners, blocks)
    pieces = []
    for j in range(owners):
        for k in range(blocks):
            source = lax.rem(b - k + blocks, blocks) * owners + lax.rem(u - j + owners, owners)
            pieces.append(all_ids_ref[pl.ds(source, 1), :][:, j * CAP : (j + 1) * CAP])
    ids = jnp.concatenate(pieces, axis=1)
    row_ref[...] = ids
    for q in range(ids.shape[1] // 128):
        piece = ids[:, q * 128 : (q + 1) * 128]
        column_ref[q * 128 : (q + 1) * 128, :] = jnp.broadcast_to(piece, (128, 128)).T


def meet_kernel(owners, blocks, *refs):
    count = owners * blocks
    block_refs, row_ref, column_ref, best_ref = refs[:count], refs[count], refs[count + 1], refs[-1]
    _, _, here = meeting_here(owners, blocks)
    tile = 256
    per = tile // CAP
    tiles = count // per

    @pl.when(jnp.logical_not(here))
    def _():
        best_ref[...] = jnp.full(best_ref.shape, -1.0, jnp.float32)

    @pl.when(here)
    def _():
        def rows_of(t):
            return jnp.concatenate([r[...] for r in block_refs[t * per : (t + 1) * per]], axis=0)

        for query in range(tiles):
            query_rows = rows_of(query)
            query_ids = row_ref[:, query * tile : (query + 1) * tile]
            best = jnp.full((1, tile), -1.0, jnp.float32)
            for key in range(tiles):
                scores = lax.dot_general(
                    rows_of(key),
                    query_rows,
                    (((1,), (1,)), ((), ())),
                    preferred_element_type=jnp.float32,
                )
                key_ids = column_ref[key * tile : (key + 1) * tile, :]
                key_ids = jnp.concatenate([key_ids] * (tile // 128), axis=1)
                allowed = key_ids < query_ids
                best = jnp.maximum(
                    best, jnp.max(jnp.where(allowed, scores, -1.0), axis=0, keepdims=True)
                )
            for part in range(tile // 128):
                at = query * (tile // 128) + part
                best_ref[at : at + 1, :] = best[:, part * 128 : (part + 1) * 128]


def home_kernel(owners, blocks, *refs):
    count = owners * blocks
    got_refs, target_ref, out_ref = refs[:count], refs[count], refs[-1]
    u = lax.axis_index("clus")
    b = lax.axis_index("blk")
    slots = owners * CAP
    rows = target_ref.shape[1]
    pieces = []
    for j in range(owners):
        c = lax.rem(u + j, owners)
        middle = (blocks - 1) // 2 + (lax.rem(c, 2) if blocks > 1 else 0)
        want = lax.rem(middle - b + blocks, blocks)
        piece = None
        for k in range(blocks):
            q = j * blocks + k
            lane = q * CAP % 128
            value = got_refs[q][q * CAP // 128 : q * CAP // 128 + 1, lane : lane + CAP]
            piece = value if piece is None else jnp.where(want == k, value, piece)
        pieces.append(piece)
    best = jnp.concatenate(pieces, axis=1)
    high = best.astype(jnp.bfloat16).astype(jnp.float32)
    rest = best - high
    middle_part = rest.astype(jnp.bfloat16).astype(jnp.float32)
    low = rest - middle_part
    row = lax.broadcasted_iota(jnp.int32, (8, slots), 0)
    parts = jnp.where(row == 0, high, jnp.where(row == 1, middle_part, jnp.where(row == 2, low, 0.0)))
    place = lax.broadcasted_iota(jnp.int32, (slots, rows), 0) == target_ref[...]
    moved = jnp.dot(
        parts.astype(jnp.bfloat16), place.astype(jnp.bfloat16), preferred_element_type=jnp.float32
    )
    out_ref[...] = moved[0:1] + moved[1:2] + moved[2:3]


def meet(embeddings, cluster, row_ids):
    owners = lax.axis_size("clus")
    blocks = lax.axis_size("blk")
    rows, width = embeddings.shape
    slots = owners * CAP
    count = owners * blocks
    everyone = ("blk", "clus")

    def pairs(j, k):
        found = []
        for c in range(owners):
            middle = meeting_blk(c, blocks)
            source = ((middle - k) % blocks) * owners + (c - j) % owners
            found.append((source, middle * owners + c))
        return found

    *slot_rows, sorted_ids, target = pl.pallas_call(
        functools.partial(sort_kernel, owners),
        out_shape=[jax.ShapeDtypeStruct((CAP, width), jnp.bfloat16)] * owners
        + [
            jax.ShapeDtypeStruct((1, slots), jnp.int32),
            jax.ShapeDtypeStruct((1, rows), jnp.int32),
        ],
        in_specs=[VMEM] * 3,
        out_specs=[VMEM] * (owners + 2),
        name="sort_rows",
    )(embeddings, cluster.reshape(1, rows), row_ids.reshape(1, rows))
    all_ids = lax.all_gather(sorted_ids, everyone, axis=0, tiled=True)
    arrived = []
    for j in range(owners):
        for k in range(blocks):
            if j == 0 and k == 0:
                arrived.append(slot_rows[0])
            else:
                arrived.append(lax.ppermute(slot_rows[j], everyone, pairs(j, k)))
    ids_row, ids_column = pl.pallas_call(
        functools.partial(order_kernel, owners, blocks),
        out_shape=[
            jax.ShapeDtypeStruct((1, count * CAP), jnp.int32),
            jax.ShapeDtypeStruct((count * CAP, 128), jnp.int32),
        ],
        in_specs=[VMEM],
        out_specs=[VMEM] * 2,
        name="order_ids",
    )(all_ids)
    best = pl.pallas_call(
        functools.partial(meet_kernel, owners, blocks),
        out_shape=jax.ShapeDtypeStruct((count * CAP // 128, 128), jnp.float32),
        in_specs=[VMEM] * (count + 2),
        out_specs=VMEM,
        name="meet_scores",
    )(*arrived, ids_row, ids_column)
    returned = []
    for j in range(owners):
        for k in range(blocks):
            if j == 0 and k == 0:
                returned.append(best)
            else:
                returned.append(
                    lax.ppermute(best, everyone, [(t, s) for s, t in pairs(j, k)])
                )
    out = pl.pallas_call(
        functools.partial(home_kernel, owners, blocks),
        out_shape=jax.ShapeDtypeStruct((1, rows), jnp.float32),
        in_specs=[VMEM] * (count + 1),
        out_specs=VMEM,
        name="home_scores",
    )(*returned, target)
    return out.reshape(rows)


def solution(mesh):
    one_device_takes_a_cluster = mesh.shape["blk"] * mesh.shape["clus"] <= 16
    return jax.shard_map(
        meet if one_device_takes_a_cluster else ring,
        mesh=mesh,
        in_specs=(
            P(("groups", "blk", "clus"), None),
            P(("groups", "blk", "clus")),
            P(("groups", "blk", "clus")),
        ),
        out_specs=P(("groups", "blk", "clus")),
        check_vma=False,
    )
```

time: 84.3 us -> 88.8 us (1.053)
  waiting for transfers between devices: 50.6 us -> 17.7 us
  starting transfers between devices: 16.1 us -> 41.1 us
  blocking collectives: 0 us -> 17.6 us
  other arithmetic: 8.51 us -> 0 us
  Pallas kernels: 0 us -> 8.25 us
  local copies, waits for them, and re-layouts: 7.1 us -> 2.52 us
  matrix products: 1.42 us -> 0 us
    ppermute x6 -> x30, starting transfers between devices: 5.15 us -> 41.1 us  [the longest x15 28.7 us: meet(): arrived.append(lax.ppermute(slot_rows[j], everyone, pairs(j, k)))]
    ppermute x6 -> x30, waiting for transfers between devices: 39.3 us -> 17.7 us  [the longest x15 16.7 us: meet(): lax.ppermute(best, everyone, [(t, s) for s, t in pairs(j, k)])]
    all_gather x0 -> x1, blocking collectives: none -> 17.6 us  [meet(): all_ids = lax.all_gather(sorted_ids, everyone, axis=0, tiled=True)]
    all_to_all x3 -> x0, waiting for transfers between devices: 11.3 us -> none  [the longest x1 7.55 us: local(): lax.all_to_all(send_unit.reshape(owners, CAP, feature_width), 'clus', spl...]
    all_to_all x3 -> x0, starting transfers between devices: 10.9 us -> none  [the longest x1 4.21 us: local(): lax.all_to_all(send_ids.reshape(owners, CAP), 'clus', split_axis=0, conca...]
    pallas_call x0 -> x4, Pallas kernels: none -> 8.25 us  [the longest x1 2.38 us: meet(): pl.pallas_call(functools.partial(meet_kernel, owners, blocks), out_shape=...]
    scatter x1 -> x0, other arithmetic: 2.55 us -> none  [local(): jnp.zeros((slot_count, feature_width), jnp.bfloat16).at[target]]
    gather x1 -> x0, local copies, waits for them, and re-layouts: 2.5 us -> none  [local(): return returned.reshape(slot_count)[target]]
  transfers between devices with their start and end apart: 9 -> 30, of which waited for: 5 -> 5; matrix products, arithmetic and copies ran while one was open for 6% -> 1% of each run, Pallas kernels for 0% -> 2%
where the time goes in v1:
time: 88.8 us; the launch traced here: 87.9 us
  starting transfers between devices  41.1 us (46%)
  waiting for transfers between devices  17.7 us (20%)
  blocking collectives  17.6 us (20%)
  Pallas kernels  8.25 us (9%)
  local copies, waits for them, and re-layouts  2.52 us (3%)
    ppermute x15, starting transfers between devices, meet(): arrived.append(lax.ppermute(slot_rows[j], everyone, pairs(j, k)))  28.7 us
    all_gather x1, blocking collectives, meet(): all_ids = lax.all_gather(sorted_ids, everyone, axis=0, tiled=True)  17.6 us
    ppermute x15, waiting for transfers between devices, meet(): lax.ppermute(best, everyone, [(t, s) for s, t in pairs(j, k)])  16.7 us
    ppermute x15, starting transfers between devices, meet(): lax.ppermute(best, everyone, [(t, s) for s, t in pairs(j, k)])  12.4 us
    unnamed x63, local copies, waits for them, and re-layouts  2.52 us
    pallas_call x1, Pallas kernels, meet(): pl.pallas_call(functools.partial(meet_kernel, owners, blocks), out_shape=...  2.38 us
    pallas_call x1, Pallas kernels, meet(): pl.pallas_call(functools.partial(sort_kernel, owners), out_shape=[jax.Sha...  2.35 us
    pallas_call x1, Pallas kernels, meet(): pl.pallas_call(functools.partial(order_kernel, owners, blocks), out_shape...  1.8 us
  transfers between devices with their start and end apart: 30, of which 5 were waited for; matrix products, arithmetic and copies ran while one was open for 1% of the time, Pallas kernels for 2%

profile of v1, /device:TPU:0, one launch (start us, length us, event | category | flops | bytes accessed | tf_op | source)
XLA Modules:
  0.0 87.9 jit_solution(14765894909099963879)
XLA Ops:
  0.0 2.3 %sort_rows.1 = (bf16[64,1024]{1,0:T(8,128)(2,1)}, bf16[64,1024]{1,0:T(8,128)(2,1)}, bf16[64,1024]{1,0:T(8,128)(2,1)}, bf16[64,1024]{1,0:T(8,128)(2,1)}, s32[1,256]{1,0:T(1,128)}, /*index=5*/s32[1,256]{1,0:T(1,128)}) custom-call(bf16[256,1024]{1,0:T(8,128)(2,1)} %emb_ref.1, s32[1,256]{1,0:T(1,128)} %bitcast.8, s32[1,256]{1,0:T(1,128)} %bitcast.9), custom_call_target="tpu_custom_call" | custom-call | tf_op jit(solution)/shard_map/sort_rows/pallas_call | solution.py:216
  2.3 0.7 collective-permute-start.2
  3.0 0.7 collective-permute-start.1
  3.7 6.2 %collective-permute-start = (bf16[64,1024]{1,0:T(8,128)(2,1)}, bf16[64,1024]{1,0:T(8,128)(2,1)S(1)}, u32[]{:S(2)}, u32[]{:S(2)}) collective-permute-start(bf16[64,1024]{1,0:T(8,128)(2,1)} %get-tuple-element.13.refs_0_), channel_id=1, source_target_pairs={{0,4},{5,9},{2,6},{7,11},{16,20},{21,25},{18,22},{23,27}} | collective-permute-start | bytes 393224 | tf_op jit(solution)/shard_map/ppermute | solution.py:234
  9.9 0.7 collective-permute-start.6
  10.6 4.6 %collective-permute-start.5 = (bf16[64,1024]{1,0:T(8,128)(2,1)}, bf16[64,1024]{1,0:T(8,128)(2,1)S(1)}, u32[]{:S(2)}, u32[]{:S(2)}) collective-permute-start(bf16[64,1024]{1,0:T(8,128)(2,1)} %get-tuple-element.14), channel_id=1, source_target_pairs={{15,4},{0,9},{13,6},{2,11},{31,20},{16,25},{29,22},{18,27}} | collective-permute-start | bytes 393224 | tf_op jit(solution)/shard_map/ppermute | solution.py:234
  15.2 0.7 collective-permute-start.4
  15.9 0.0 collective-permute-done.1.refs_2_
  15.9 0.7 collective-permute-start.3
  16.6 0.0 collective-permute-done.refs_1_
  16.6 0.7 collective-permute-start.10
  17.3 0.7 collective-permute-start.9
  18.0 0.9 %collective-permute-done.5.refs_6_ = bf16[64,1024]{1,0:T(8,128)(2,1)S(1)} collective-permute-done((bf16[64,1024]{1,0:T(8,128)(2,1)}, bf16[64,1024]{1,0:T(8,128)(2,1)S(1)}, u32[]{:S(2)}, u32[]{:S(2)}) %collective-permute-start.5) | collective-permute-done | bytes 131104 | tf_op jit(solution)/shard_map/ppermute | solution.py:234
  18.9 4.1 %collective-permute-start.8 = (bf16[64,1024]{1,0:T(8,128)(2,1)}, bf16[64,1024]{1,0:T(8,128)(2,1)S(1)}, u32[]{:S(2)}, u32[]{:S(2)}) collective-permute-start(bf16[64,1024]{1,0:T(8,128)(2,1)} %get-tuple-element.15), channel_id=1, source_target_pairs={{2,4},{7,9},{0,6},{5,11},{18,20},{23,25},{16,22},{21,27}} | collective-permute-start | bytes 393224 | tf_op jit(solution)/shard_map/ppermute | solution.py:234
  23.0 0.7 collective-permute-start.7
  23.7 0.0 collective-permute-done.3.refs_4_
  23.7 0.7 collective-permute-start.14
  24.4 6.4 %collective-permute-start.13 = (bf16[64,1024]{1,0:T(8,128)(2,1)}, bf16[64,1024]{1,0:T(8,128)(2,1)S(1)}, u32[]{:S(2)}, u32[]{:S(2)}) collective-permute-start(bf16[64,1024]{1,0:T(8,128)(2,1)} %get-tuple-element.16), channel_id=1, source_target_pairs={{13,4},{2,9},{15,6},{0,11},{29,20},{18,25},{31,22},{16,27}} | collective-permute-start | bytes 393224 | tf_op jit(solution)/shard_map/ppermute | solution.py:234
  30.8 0.0 collective-permute-done.9.refs_10_
  30.8 0.7 collective-permute-start.12
  31.5 0.7 collective-permute-start.11
  32.2 0.0 copy-start.30
  32.2 0.7 copy-done.30
  32.9 17.6 %all-gather = s32[16,1,256]{2,1,0:T(1,128)S(1)} all-gather(s32[1,1,256]{2,1,0:T(1,128)S(1)} %bitcast.10), channel_id=1, replica_groups=mesh['groups'=2,'blk'=4,'clus'=4] {'blk','clus'}, dimensions={0}, use_global_device_ids=true | all-gather | bytes 17408 | tf_op jit(solution)/shard_map/all_gather | solution.py:227
  50.5 0.6 copy.6
  51.1 1.8 %order_ids.1 = (s32[1,1024]{1,0:T(1,128)}, s32[1024,128]{1,0:T(8,128)}) custom-call(s32[16,256]{1,0:T(8,128)} %bitcast.7), custom_call_target="tpu_custom_call" | custom-call | tf_op jit(solution)/shard_map/order_ids/pallas_call | solution.py:235
  52.9 0.0 collective-permute-done.14.refs_15_
  52.9 0.0 collective-permute-done.13.refs_14_
  53.0 0.0 collective-permute-done.11.refs_12_
  53.1 0.5 copy-done.10
  53.6 0.1 copy-done.11
  53.6 0.0 copy-done.12
  53.7 0.0 copy-done.13
  53.7 0.1 copy-done.14
  53.8 2.4 %meet_scores.1.refs_0_ = f32[8,128]{1,0:T(8,128)} custom-call(bf16[64,1024]{1,0:T(8,128)(2,1)} %get-tuple-element.13.refs_0_, bf16[64,1024]{1,0:T(8,128)(2,1)} %copy-done.2, bf16[64,1024]{1,0:T(8,128)(2,1)} %copy-done.1, bf16[64,1024]{1,0:T(8,128)(2,1)} %copy-done, bf16[64,1024]{1,0:T(8,128)(2,1)} %copy-done.6, bf16[64,1024]{1,0:T(8,128)(2,1)} %copy-done.5, ...), custom_call_target="tpu_custom_call" | custom-call | tf_op jit(solution)/shard_map/meet_scores/pallas_call | solution.py:245
  56.2 0.6 collective-permute-start.29
  56.8 1.3 %collective-permute-start.28 = (f32[8,128]{1,0:T(8,128)}, f32[8,128]{1,0:T(8,128)S(1)}, u32[]{:S(2)}, u32[]{:S(2)}) collective-permute-start(f32[8,128]{1,0:T(8,128)} %meet_scores.1.refs_0_), channel_id=1, source_target_pairs={{4,13},{9,2},{6,15},{11,0},{20,29},{25,18},{22,31},{27,16}} | collective-permute-start | bytes 12296 | tf_op jit(solution)/shard_map/ppermute | solution.py:259
  58.1 0.7 collective-permute-start.27
  58.8 0.7 collective-permute-start.26
  59.5 0.7 collective-permute-start.25
  60.1 0.0 collective-permute-done.29.refs_15_
  60.1 0.7 collective-permute-start.24
  60.8 2.9 %collective-permute-done.28.refs_14_ = f32[8,128]{1,0:T(8,128)S(1)} collective-permute-done((f32[8,128]{1,0:T(8,128)}, f32[8,128]{1,0:T(8,128)S(1)}, u32[]{:S(2)}, u32[]{:S(2)}) %collective-permute-start.28) | collective-permute-done | bytes 4128 | tf_op jit(solution)/shard_map/ppermute | solution.py:259
  63.7 1.3 %collective-permute-start.23 = (f32[8,128]{1,0:T(8,128)}, f32[8,128]{1,0:T(8,128)S(1)}, u32[]{:S(2)}, u32[]{:S(2)}) collective-permute-start(f32[8,128]{1,0:T(8,128)} %meet_scores.1.refs_0_), channel_id=1, source_target_pairs={{4,2},{9,7},{6,0},{11,5},{20,18},{25,23},{22,16},{27,21}} | collective-permute-start | bytes 12296 | tf_op jit(solution)/shard_map/ppermute | solution.py:259
  65.0 0.0 collective-permute-done.27.refs_13_
  65.1 0.7 collective-permute-start.22
  65.7 0.0 collective-permute-done.26.refs_12_
  65.7 0.7 collective-permute-start.21
  66.4 0.0 collective-permute-done.25.refs_11_
  66.4 1.3 %collective-permute-start.20 = (f32[8,128]{1,0:T(8,128)}, f32[8,128]{1,0:T(8,128)S(1)}, u32[]{:S(2)}, u32[]{:S(2)}) collective-permute-start(f32[8,128]{1,0:T(8,128)} %meet_scores.1.refs_0_), channel_id=1, source_target_pairs={{4,15},{9,0},{6,13},{11,2},{20,31},{25,16},{22,29},{27,18}} | collective-permute-start | bytes 12296 | tf_op jit(solution)/shard_map/ppermute | solution.py:259
  67.7 0.0 collective-permute-done.24.refs_10_
  67.8 0.7 collective-permute-start.19
  68.4 1.9 %collective-permute-done.23.refs_9_ = f32[8,128]{1,0:T(8,128)S(1)} collective-permute-done((f32[8,128]{1,0:T(8,128)}, f32[8,128]{1,0:T(8,128)S(1)}, u32[]{:S(2)}, u32[]{:S(2)}) %collective-permute-start.23) | collective-permute-done | bytes 4128 | tf_op jit(solution)/shard_map/ppermute | solution.py:259
  70.3 0.7 collective-permute-start.18
  71.0 0.0 collective-permute-done.22.refs_8_
  71.0 0.7 collective-permute-start.17
  71.7 0.0 collective-permute-done.21.refs_7_
  71.7 0.7 collective-permute-start.16
  72.4 5.2 %collective-permute-done.20.refs_6_ = f32[8,128]{1,0:T(8,128)S(1)} collective-permute-done((f32[8,128]{1,0:T(8,128)}, f32[8,128]{1,0:T(8,128)S(1)}, u32[]{:S(2)}, u32[]{:S(2)}) %collective-permute-start.20) | collective-permute-done | bytes 4128 | tf_op jit(solution)/shard_map/ppermute | solution.py:259
  77.6 1.3 %collective-permute-start.15 = (f32[8,128]{1,0:T(8,128)}, f32[8,128]{1,0:T(8,128)S(1)}, u32[]{:S(2)}, u32[]{:S(2)}) collective-permute-start(f32[8,128]{1,0:T(8,128)} %meet_scores.1.refs_0_), channel_id=1, source_target_pairs={{4,0},{9,5},{6,2},{11,7},{20,16},{25,21},{22,18},{27,23}} | collective-permute-start | bytes 12296 | tf_op jit(solution)/shard_map/ppermute | solution.py:259
  78.9 0.0 collective-permute-done.19.refs_5_
  78.9 6.7 %collective-permute-done.15.refs_1_ = f32[8,128]{1,0:T(8,128)S(1)} collective-permute-done((f32[8,128]{1,0:T(8,128)}, f32[8,128]{1,0:T(8,128)S(1)}, u32[]{:S(2)}, u32[]{:S(2)}) %collective-permute-start.15) | collective-permute-done | bytes 4128 | tf_op jit(solution)/shard_map/ppermute | solution.py:259
  85.7 0.5 copy-done.29
  86.2 1.7 %home_scores.1 = f32[1,256]{1,0:T(1,128)} custom-call(f32[8,128]{1,0:T(8,128)} %meet_scores.1.refs_0_, f32[8,128]{1,0:T(8,128)} %copy-done.29, f32[8,128]{1,0:T(8,128)} %copy-done.28, f32[8,128]{1,0:T(8,128)} %copy-done.27, f32[8,128]{1,0:T(8,128)} %copy-done.26, f32[8,128]{1,0:T(8,128)} %copy-done.25, f32[8,128]{1,0:T(8,128)} %copy-done.24, ...), custom_call_target="tpu_custom_call" | custom-call | tf_op jit(solution)/shard_map/home_scores/pallas_call | solution.py:261
  (64 shorter events, 0.1 us)
Async XLA Ops:
  2.3 12.9 %collective-permute-start.2 = (bf16[64,1024]{1,0:T(8,128)(2,1)}, bf16[64,1024]{1,0:T(8,128)(2,1)S(1)}, u32[]{:S(2)}, u32[]{:S(2)}) collective-permute-start(bf16[64,1024]{1,0:T(8,128)(2,1)} %get-tuple-element.13.refs_0_), channel_id=1, source_target_pairs={{8,4},{13,9},{10,6},{15,11},{24,20},{29,25},{26,22},{31,27}} | collective-permute-start | bytes 393224 | tf_op jit(solution)/shard_map/ppermute | solution.py:234
  3.0 12.9 %collective-permute-start.1 = (bf16[64,1024]{1,0:T(8,128)(2,1)}, bf16[64,1024]{1,0:T(8,128)(2,1)S(1)}, u32[]{:S(2)}, u32[]{:S(2)}) collective-permute-start(bf16[64,1024]{1,0:T(8,128)(2,1)} %get-tuple-element.13.refs_0_), channel_id=1, source_target_pairs={{12,4},{1,9},{14,6},{3,11},{28,20},{17,25},{30,22},{19,27}} | collective-permute-start | bytes 393224 | tf_op jit(solution)/shard_map/ppermute | solution.py:234
  3.7 12.9 %collective-permute-start = (bf16[64,1024]{1,0:T(8,128)(2,1)}, bf16[64,1024]{1,0:T(8,128)(2,1)S(1)}, u32[]{:S(2)}, u32[]{:S(2)}) collective-permute-start(bf16[64,1024]{1,0:T(8,128)(2,1)} %get-tuple-element.13.refs_0_), channel_id=1, source_target_pairs={{0,4},{5,9},{2,6},{7,11},{16,20},{21,25},{18,22},{23,27}} | collective-permute-start | bytes 393224 | tf_op jit(solution)/shard_map/ppermute | solution.py:234
  9.9 7.4 %collective-permute-start.6 = (bf16[64,1024]{1,0:T(8,128)(2,1)}, bf16[64,1024]{1,0:T(8,128)(2,1)S(1)}, u32[]{:S(2)}, u32[]{:S(2)}) collective-permute-start(bf16[64,1024]{1,0:T(8,128)(2,1)} %get-tuple-element.14), channel_id=1, source_target_pairs={{11,4},{12,9},{9,6},{14,11},{27,20},{28,25},{25,22},{30,27}} | collective-permute-start | bytes 393224 | tf_op jit(solution)/shard_map/ppermute | solution.py:234
  10.6 8.3 %collective-permute-start.5 = (bf16[64,1024]{1,0:T(8,128)(2,1)}, bf16[64,1024]{1,0:T(8,128)(2,1)S(1)}, u32[]{:S(2)}, u32[]{:S(2)}) collective-permute-start(bf16[64,1024]{1,0:T(8,128)(2,1)} %get-tuple-element.14), channel_id=1, source_target_pairs={{15,4},{0,9},{13,6},{2,11},{31,20},{16,25},{29,22},{18,27}} | collective-permute-start | bytes 393224 | tf_op jit(solution)/shard_map/ppermute | solution.py:234
  15.2 37.8 %copy-start = (bf16[64,1024]{1,0:T(8,128)(2,1)}, bf16[64,1024]{1,0:T(8,128)(2,1)S(1)}, u32[]{:S(2)}) copy-start(bf16[64,1024]{1,0:T(8,128)(2,1)S(1)} %collective-permute-done.2.refs_3_) | copy-start | bytes 393220
  15.2 7.7 %collective-permute-start.4 = (bf16[64,1024]{1,0:T(8,128)(2,1)}, bf16[64,1024]{1,0:T(8,128)(2,1)S(1)}, u32[]{:S(2)}, u32[]{:S(2)}) collective-permute-start(bf16[64,1024]{1,0:T(8,128)(2,1)} %get-tuple-element.14), channel_id=1, source_target_pairs={{3,4},{4,9},{1,6},{6,11},{19,20},{20,25},{17,22},{22,27}} | collective-permute-start | bytes 393224 | tf_op jit(solution)/shard_map/ppermute | solution.py:234
  15.9 37.1 %copy-start.1 = (bf16[64,1024]{1,0:T(8,128)(2,1)}, bf16[64,1024]{1,0:T(8,128)(2,1)S(1)}, u32[]{:S(2)}) copy-start(bf16[64,1024]{1,0:T(8,128)(2,1)S(1)} %collective-permute-done.1.refs_2_) | copy-start | bytes 393220
  15.9 7.7 %collective-permute-start.3 = (bf16[64,1024]{1,0:T(8,128)(2,1)}, bf16[64,1024]{1,0:T(8,128)(2,1)S(1)}, u32[]{:S(2)}, u32[]{:S(2)}) collective-permute-start(bf16[64,1024]{1,0:T(8,128)(2,1)} %get-tuple-element.14), channel_id=1, source_target_pairs={{7,4},{8,9},{5,6},{10,11},{23,20},{24,25},{21,22},{26,27}} | collective-permute-start | bytes 393224 | tf_op jit(solution)/shard_map/ppermute | solution.py:234
  16.6 36.4 %copy-start.2 = (bf16[64,1024]{1,0:T(8,128)(2,1)}, bf16[64,1024]{1,0:T(8,128)(2,1)S(1)}, u32[]{:S(2)}) copy-start(bf16[64,1024]{1,0:T(8,128)(2,1)S(1)} %collective-permute-done.refs_1_) | copy-start | bytes 393220
  16.6 7.7 %collective-permute-start.10 = (bf16[64,1024]{1,0:T(8,128)(2,1)}, bf16[64,1024]{1,0:T(8,128)(2,1)S(1)}, u32[]{:S(2)}, u32[]{:S(2)}) collective-permute-start(bf16[64,1024]{1,0:T(8,128)(2,1)} %get-tuple-element.15), channel_id=1, source_target_pairs={{10,4},{15,9},{8,6},{13,11},{26,20},{31,25},{24,22},{29,27}} | collective-permute-start | bytes 393224 | tf_op jit(solution)/shard_map/ppermute | solution.py:234
  17.3 35.7 %copy-start.3 = (bf16[64,1024]{1,0:T(8,128)(2,1)}, bf16[64,1024]{1,0:T(8,128)(2,1)S(1)}, u32[]{:S(2)}) copy-start(bf16[64,1024]{1,0:T(8,128)(2,1)S(1)} %collective-permute-done.6.refs_7_) | copy-start | bytes 393220
  17.3 13.5 %collective-permute-start.9 = (bf16[64,1024]{1,0:T(8,128)(2,1)}, bf16[64,1024]{1,0:T(8,128)(2,1)S(1)}, u32[]{:S(2)}, u32[]{:S(2)}) collective-permute-start(bf16[64,1024]{1,0:T(8,128)(2,1)} %get-tuple-element.15), channel_id=1, source_target_pairs={{14,4},{3,9},{12,6},{1,11},{30,20},{19,25},{28,22},{17,27}} | collective-permute-start | bytes 393224 | tf_op jit(solution)/shard_map/ppermute | solution.py:234
  18.9 34.2 %copy-start.4 = (bf16[64,1024]{1,0:T(8,128)(2,1)}, bf16[64,1024]{1,0:T(8,128)(2,1)S(1)}, u32[]{:S(2)}) copy-start(bf16[64,1024]{1,0:T(8,128)(2,1)S(1)} %collective-permute-done.5.refs_6_) | copy-start | bytes 393220
  18.9 12.6 %collective-permute-start.8 = (bf16[64,1024]{1,0:T(8,128)(2,1)}, bf16[64,1024]{1,0:T(8,128)(2,1)S(1)}, u32[]{:S(2)}, u32[]{:S(2)}) collective-permute-start(bf16[64,1024]{1,0:T(8,128)(2,1)} %get-tuple-element.15), channel_id=1, source_target_pairs={{2,4},{7,9},{0,6},{5,11},{18,20},{23,25},{16,22},{21,27}} | collective-permute-start | bytes 393224 | tf_op jit(solution)/shard_map/ppermute | solution.py:234
  23.0 30.1 %copy-start.5 = (bf16[64,1024]{1,0:T(8,128)(2,1)}, bf16[64,1024]{1,0:T(8,128)(2,1)S(1)}, u32[]{:S(2)}) copy-start(bf16[64,1024]{1,0:T(8,128)(2,1)S(1)} %collective-permute-done.4.refs_5_) | copy-start | bytes 393220
  23.0 30.0 %collective-permute-start.7 = (bf16[64,1024]{1,0:T(8,128)(2,1)}, bf16[64,1024]{1,0:T(8,128)(2,1)S(1)}, u32[]{:S(2)}, u32[]{:S(2)}) collective-permute-start(bf16[64,1024]{1,0:T(8,128)(2,1)} %get-tuple-element.15), channel_id=1, source_target_pairs={{6,4},{11,9},{4,6},{9,11},{22,20},{27,25},{20,22},{25,27}} | collective-permute-start | bytes 393224 | tf_op jit(solution)/shard_map/ppermute | solution.py:234
  23.7 29.4 %copy-start.6 = (bf16[64,1024]{1,0:T(8,128)(2,1)}, bf16[64,1024]{1,0:T(8,128)(2,1)S(1)}, u32[]{:S(2)}) copy-start(bf16[64,1024]{1,0:T(8,128)(2,1)S(1)} %collective-permute-done.3.refs_4_) | copy-start | bytes 393220
  23.7 29.3 %collective-permute-start.14 = (bf16[64,1024]{1,0:T(8,128)(2,1)}, bf16[64,1024]{1,0:T(8,128)(2,1)S(1)}, u32[]{:S(2)}, u32[]{:S(2)}) collective-permute-start(bf16[64,1024]{1,0:T(8,128)(2,1)} %get-tuple-element.16), channel_id=1, source_target_pairs={{9,4},{14,9},{11,6},{12,11},{25,20},{30,25},{27,22},{28,27}} | collective-permute-start | bytes 393224 | tf_op jit(solution)/shard_map/ppermute | solution.py:234
  24.4 28.7 %copy-start.7 = (bf16[64,1024]{1,0:T(8,128)(2,1)}, bf16[64,1024]{1,0:T(8,128)(2,1)S(1)}, u32[]{:S(2)}) copy-start(bf16[64,1024]{1,0:T(8,128)(2,1)S(1)} %collective-permute-done.10.refs_11_) | copy-start | bytes 393220
  24.4 28.6 %collective-permute-start.13 = (bf16[64,1024]{1,0:T(8,128)(2,1)}, bf16[64,1024]{1,0:T(8,128)(2,1)S(1)}, u32[]{:S(2)}, u32[]{:S(2)}) collective-permute-start(bf16[64,1024]{1,0:T(8,128)(2,1)} %get-tuple-element.16), channel_id=1, source_target_pairs={{13,4},{2,9},{15,6},{0,11},{29,20},{18,25},{31,22},{16,27}} | collective-permute-start | bytes 393224 | tf_op jit(solution)/shard_map/ppermute | solution.py:234
  30.8 22.3 %copy-start.8 = (bf16[64,1024]{1,0:T(8,128)(2,1)}, bf16[64,1024]{1,0:T(8,128)(2,1)S(1)}, u32[]{:S(2)}) copy-start(bf16[64,1024]{1,0:T(8,128)(2,1)S(1)} %collective-permute-done.9.refs_10_) | copy-start | bytes 393220
  30.8 22.1 %collective-permute-start.12 = (bf16[64,1024]{1,0:T(8,128)(2,1)}, bf16[64,1024]{1,0:T(8,128)(2,1)S(1)}, u32[]{:S(2)}, u32[]{:S(2)}) collective-permute-start(bf16[64,1024]{1,0:T(8,128)(2,1)} %get-tuple-element.16), channel_id=1, source_target_pairs={{1,4},{6,9},{3,6},{4,11},{17,20},{22,25},{19,22},{20,27}} | collective-permute-start | bytes 393224 | tf_op jit(solution)/shard_map/ppermute | solution.py:234
  31.5 21.6 %copy-start.9 = (bf16[64,1024]{1,0:T(8,128)(2,1)}, bf16[64,1024]{1,0:T(8,128)(2,1)S(1)}, u32[]{:S(2)}) copy-start(bf16[64,1024]{1,0:T(8,128)(2,1)S(1)} %collective-permute-done.8.refs_9_) | copy-start | bytes 393220
  31.5 21.4 %collective-permute-start.11 = (bf16[64,1024]{1,0:T(8,128)(2,1)}, bf16[64,1024]{1,0:T(8,128)(2,1)S(1)}, u32[]{:S(2)}, u32[]{:S(2)}) collective-permute-start(bf16[64,1024]{1,0:T(8,128)(2,1)} %get-tuple-element.16), channel_id=1, source_target_pairs={{5,4},{10,9},{7,6},{8,11},{21,20},{26,25},{23,22},{24,27}} | collective-permute-start | bytes 393224 | tf_op jit(solution)/shard_map/ppermute | solution.py:234
  32.2 0.7 copy-start.30
  52.9 0.7 copy-start.10
  52.9 0.7 copy-start.11
  53.0 0.7 copy-start.12
  53.0 0.7 copy-start.13
  53.0 0.8 copy-start.14
  56.2 4.0 %collective-permute-start.29 = (f32[8,128]{1,0:T(8,128)}, f32[8,128]{1,0:T(8,128)S(1)}, u32[]{:S(2)}, u32[]{:S(2)}) collective-permute-start(f32[8,128]{1,0:T(8,128)} %meet_scores.1.refs_0_), channel_id=1, source_target_pairs={{4,9},{9,14},{6,11},{11,12},{20,25},{25,30},{22,27},{27,28}} | collective-permute-start | bytes 12296 | tf_op jit(solution)/shard_map/ppermute | solution.py:259
  56.8 6.9 %collective-permute-start.28 = (f32[8,128]{1,0:T(8,128)}, f32[8,128]{1,0:T(8,128)S(1)}, u32[]{:S(2)}, u32[]{:S(2)}) collective-permute-start(f32[8,128]{1,0:T(8,128)} %meet_scores.1.refs_0_), channel_id=1, source_target_pairs={{4,13},{9,2},{6,15},{11,0},{20,29},{25,18},{22,31},{27,16}} | collective-permute-start | bytes 12296 | tf_op jit(solution)/shard_map/ppermute | solution.py:259
  58.1 6.9 %collective-permute-start.27 = (f32[8,128]{1,0:T(8,128)}, f32[8,128]{1,0:T(8,128)S(1)}, u32[]{:S(2)}, u32[]{:S(2)}) collective-permute-start(f32[8,128]{1,0:T(8,128)} %meet_scores.1.refs_0_), channel_id=1, source_target_pairs={{4,1},{9,6},{6,3},{11,4},{20,17},{25,22},{22,19},{27,20}} | collective-permute-start | bytes 12296 | tf_op jit(solution)/shard_map/ppermute | solution.py:259
  58.8 6.9 %collective-permute-start.26 = (f32[8,128]{1,0:T(8,128)}, f32[8,128]{1,0:T(8,128)S(1)}, u32[]{:S(2)}, u32[]{:S(2)}) collective-permute-start(f32[8,128]{1,0:T(8,128)} %meet_scores.1.refs_0_), channel_id=1, source_target_pairs={{4,5},{9,10},{6,7},{11,8},{20,21},{25,26},{22,23},{27,24}} | collective-permute-start | bytes 12296 | tf_op jit(solution)/shard_map/ppermute | solution.py:259
  59.5 7.0 %collective-permute-start.25 = (f32[8,128]{1,0:T(8,128)}, f32[8,128]{1,0:T(8,128)S(1)}, u32[]{:S(2)}, u32[]{:S(2)}) collective-permute-start(f32[8,128]{1,0:T(8,128)} %meet_scores.1.refs_0_), channel_id=1, source_target_pairs={{4,10},{9,15},{6,8},{11,13},{20,26},{25,31},{22,24},{27,29}} | collective-permute-start | bytes 12296 | tf_op jit(solution)/shard_map/ppermute | solution.py:259
  60.1 25.5 %copy-start.15 = (f32[8,128]{1,0:T(8,128)}, f32[8,128]{1,0:T(8,128)S(1)}, u32[]{:S(2)}) copy-start(f32[8,128]{1,0:T(8,128)S(1)} %collective-permute-done.29.refs_15_) | copy-start | bytes 12292
  60.1 7.6 %collective-permute-start.24 = (f32[8,128]{1,0:T(8,128)}, f32[8,128]{1,0:T(8,128)S(1)}, u32[]{:S(2)}, u32[]{:S(2)}) collective-permute-start(f32[8,128]{1,0:T(8,128)} %meet_scores.1.refs_0_), channel_id=1, source_target_pairs={{4,14},{9,3},{6,12},{11,1},{20,30},{25,19},{22,28},{27,17}} | collective-permute-start | bytes 12296 | tf_op jit(solution)/shard_map/ppermute | solution.py:259
  63.7 21.9 %copy-start.16 = (f32[8,128]{1,0:T(8,128)}, f32[8,128]{1,0:T(8,128)S(1)}, u32[]{:S(2)}) copy-start(f32[8,128]{1,0:T(8,128)S(1)} %collective-permute-done.28.refs_14_) | copy-start | bytes 12292
  63.7 6.6 %collective-permute-start.23 = (f32[8,128]{1,0:T(8,128)}, f32[8,128]{1,0:T(8,128)S(1)}, u32[]{:S(2)}, u32[]{:S(2)}) collective-permute-start(f32[8,128]{1,0:T(8,128)} %meet_scores.1.refs_0_), channel_id=1, source_target_pairs={{4,2},{9,7},{6,0},{11,5},{20,18},{25,23},{22,16},{27,21}} | collective-permute-start | bytes 12296 | tf_op jit(solution)/shard_map/ppermute | solution.py:259
  65.0 20.6 %copy-start.17 = (f32[8,128]{1,0:T(8,128)}, f32[8,128]{1,0:T(8,128)S(1)}, u32[]{:S(2)}) copy-start(f32[8,128]{1,0:T(8,128)S(1)} %collective-permute-done.27.refs_13_) | copy-start | bytes 12292
  65.1 6.0 %collective-permute-start.22 = (f32[8,128]{1,0:T(8,128)}, f32[8,128]{1,0:T(8,128)S(1)}, u32[]{:S(2)}, u32[]{:S(2)}) collective-permute-start(f32[8,128]{1,0:T(8,128)} %meet_scores.1.refs_0_), channel_id=1, source_target_pairs={{4,6},{9,11},{6,4},{11,9},{20,22},{25,27},{22,20},{27,25}} | collective-permute-start | bytes 12296 | tf_op jit(solution)/shard_map/ppermute | solution.py:259
  65.7 19.9 %copy-start.18 = (f32[8,128]{1,0:T(8,128)}, f32[8,128]{1,0:T(8,128)S(1)}, u32[]{:S(2)}) copy-start(f32[8,128]{1,0:T(8,128)S(1)} %collective-permute-done.26.refs_12_) | copy-start | bytes 12292
  65.7 6.0 %collective-permute-start.21 = (f32[8,128]{1,0:T(8,128)}, f32[8,128]{1,0:T(8,128)S(1)}, u32[]{:S(2)}, u32[]{:S(2)}) collective-permute-start(f32[8,128]{1,0:T(8,128)} %meet_scores.1.refs_0_), channel_id=1, source_target_pairs={{4,11},{9,12},{6,9},{11,14},{20,27},{25,28},{22,25},{27,30}} | collective-permute-start | bytes 12296 | tf_op jit(solution)/shard_map/ppermute | solution.py:259
  66.4 19.2 %copy-start.19 = (f32[8,128]{1,0:T(8,128)}, f32[8,128]{1,0:T(8,128)S(1)}, u32[]{:S(2)}) copy-start(f32[8,128]{1,0:T(8,128)S(1)} %collective-permute-done.25.refs_11_) | copy-start | bytes 12292
  66.4 11.1 %collective-permute-start.20 = (f32[8,128]{1,0:T(8,128)}, f32[8,128]{1,0:T(8,128)S(1)}, u32[]{:S(2)}, u32[]{:S(2)}) collective-permute-start(f32[8,128]{1,0:T(8,128)} %meet_scores.1.refs_0_), channel_id=1, source_target_pairs={{4,15},{9,0},{6,13},{11,2},{20,31},{25,16},{22,29},{27,18}} | collective-permute-start | bytes 12296 | tf_op jit(solution)/shard_map/ppermute | solution.py:259
  67.7 17.9 %copy-start.20 = (f32[8,128]{1,0:T(8,128)}, f32[8,128]{1,0:T(8,128)S(1)}, u32[]{:S(2)}) copy-start(f32[8,128]{1,0:T(8,128)S(1)} %collective-permute-done.24.refs_10_) | copy-start | bytes 12292
  67.8 11.1 %collective-permute-start.19 = (f32[8,128]{1,0:T(8,128)}, f32[8,128]{1,0:T(8,128)S(1)}, u32[]{:S(2)}, u32[]{:S(2)}) collective-permute-start(f32[8,128]{1,0:T(8,128)} %meet_scores.1.refs_0_), channel_id=1, source_target_pairs={{4,3},{9,4},{6,1},{11,6},{20,19},{25,20},{22,17},{27,22}} | collective-permute-start | bytes 12296 | tf_op jit(solution)/shard_map/ppermute | solution.py:259
  70.3 15.3 %copy-start.21 = (f32[8,128]{1,0:T(8,128)}, f32[8,128]{1,0:T(8,128)S(1)}, u32[]{:S(2)}) copy-start(f32[8,128]{1,0:T(8,128)S(1)} %collective-permute-done.23.refs_9_) | copy-start | bytes 12292
  70.3 8.5 %collective-permute-start.18 = (f32[8,128]{1,0:T(8,128)}, f32[8,128]{1,0:T(8,128)S(1)}, u32[]{:S(2)}, u32[]{:S(2)}) collective-permute-start(f32[8,128]{1,0:T(8,128)} %meet_scores.1.refs_0_), channel_id=1, source_target_pairs={{4,7},{9,8},{6,5},{11,10},{20,23},{25,24},{22,21},{27,26}} | collective-permute-start | bytes 12296 | tf_op jit(solution)/shard_map/ppermute | solution.py:259
  71.0 14.7 %copy-start.22 = (f32[8,128]{1,0:T(8,128)}, f32[8,128]{1,0:T(8,128)S(1)}, u32[]{:S(2)}) copy-start(f32[8,128]{1,0:T(8,128)S(1)} %collective-permute-done.22.refs_8_) | copy-start | bytes 12292
  71.0 7.9 %collective-permute-start.17 = (f32[8,128]{1,0:T(8,128)}, f32[8,128]{1,0:T(8,128)S(1)}, u32[]{:S(2)}, u32[]{:S(2)}) collective-permute-start(f32[8,128]{1,0:T(8,128)} %meet_scores.1.refs_0_), channel_id=1, source_target_pairs={{4,8},{9,13},{6,10},{11,15},{20,24},{25,29},{22,26},{27,31}} | collective-permute-start | bytes 12296 | tf_op jit(solution)/shard_map/ppermute | solution.py:259
  71.7 14.0 %copy-start.23 = (f32[8,128]{1,0:T(8,128)}, f32[8,128]{1,0:T(8,128)S(1)}, u32[]{:S(2)}) copy-start(f32[8,128]{1,0:T(8,128)S(1)} %collective-permute-done.21.refs_7_) | copy-start | bytes 12292
  71.7 7.2 %collective-permute-start.16 = (f32[8,128]{1,0:T(8,128)}, f32[8,128]{1,0:T(8,128)S(1)}, u32[]{:S(2)}, u32[]{:S(2)}) collective-permute-start(f32[8,128]{1,0:T(8,128)} %meet_scores.1.refs_0_), channel_id=1, source_target_pairs={{4,12},{9,1},{6,14},{11,3},{20,28},{25,17},{22,30},{27,19}} | collective-permute-start | bytes 12296 | tf_op jit(solution)/shard_map/ppermute | solution.py:259
  77.6 8.1 %copy-start.24 = (f32[8,128]{1,0:T(8,128)}, f32[8,128]{1,0:T(8,128)S(1)}, u32[]{:S(2)}) copy-start(f32[8,128]{1,0:T(8,128)S(1)} %collective-permute-done.20.refs_6_) | copy-start | bytes 12292
  77.6 8.0 %collective-permute-start.15 = (f32[8,128]{1,0:T(8,128)}, f32[8,128]{1,0:T(8,128)S(1)}, u32[]{:S(2)}, u32[]{:S(2)}) collective-permute-start(f32[8,128]{1,0:T(8,128)} %meet_scores.1.refs_0_), channel_id=1, source_target_pairs={{4,0},{9,5},{6,2},{11,7},{20,16},{25,21},{22,18},{27,23}} | collective-permute-start | bytes 12296 | tf_op jit(solution)/shard_map/ppermute | solution.py:259
  78.9 6.8 %copy-start.25 = (f32[8,128]{1,0:T(8,128)}, f32[8,128]{1,0:T(8,128)S(1)}, u32[]{:S(2)}) copy-start(f32[8,128]{1,0:T(8,128)S(1)} %collective-permute-done.19.refs_5_) | copy-start | bytes 12292
  78.9 6.8 %copy-start.26 = (f32[8,128]{1,0:T(8,128)}, f32[8,128]{1,0:T(8,128)S(1)}, u32[]{:S(2)}) copy-start(f32[8,128]{1,0:T(8,128)S(1)} %collective-permute-done.18.refs_4_) | copy-start | bytes 12292
  78.9 6.8 %copy-start.27 = (f32[8,128]{1,0:T(8,128)}, f32[8,128]{1,0:T(8,128)S(1)}, u32[]{:S(2)}) copy-start(f32[8,128]{1,0:T(8,128)S(1)} %collective-permute-done.17.refs_3_) | copy-start | bytes 12292
  78.9 6.8 %copy-start.28 = (f32[8,128]{1,0:T(8,128)}, f32[8,128]{1,0:T(8,128)S(1)}, u32[]{:S(2)}) copy-start(f32[8,128]{1,0:T(8,128)S(1)} %collective-permute-done.16.refs_2_) | copy-start | bytes 12292
  85.6 0.6 copy-start.29

commit v2 on v0

v2 whole, which is shorter than its diff:
```python
import functools

import jax
import jax.numpy as jnp
from jax import lax
from jax.experimental import pallas as pl
from jax.experimental.pallas import tpu as pltpu
from jax.sharding import PartitionSpec as P

CAP = 64
EPS = 1e-06
sentinel_id = 1 << 30
VMEM = pl.BlockSpec(memory_space=pltpu.VMEM)


def passed_along(value, axis, by):
    size = lax.axis_size(axis)
    return lax.ppermute(value, axis, [(i, (i + by) % size) for i in range(size)])


def ring(embeddings, cluster, row_ids):
    owners = lax.axis_size("clus")
    loop_size = lax.axis_size("blk")
    feature_width = embeddings.shape[1]
    slot_count = owners * CAP
    values = embeddings.astype(jnp.float32)
    unit_rows = (
        values
        * lax.rsqrt(jnp.mean(values * values, axis=1, keepdims=True) + EPS)
        * feature_width ** (-0.5)
    ).astype(jnp.bfloat16)
    onehot = (cluster[:, None] == jnp.arange(owners, dtype=jnp.int32)[None, :]).astype(jnp.int32)
    before = jnp.cumsum(onehot, axis=0) - onehot
    position = jnp.sum(before * onehot, axis=1)
    target = cluster * CAP + position
    send_unit = jnp.zeros((slot_count, feature_width), jnp.bfloat16).at[target].set(unit_rows)
    send_ids = jnp.full((slot_count,), sentinel_id, jnp.int32).at[target].set(row_ids)
    exchange = functools.partial(
        lax.all_to_all, axis_name="clus", split_axis=0, concat_axis=0, tiled=True
    )
    keys_unit = exchange(send_unit.reshape(owners, CAP, feature_width)).reshape(
        slot_count, feature_width
    )
    keys_ids = exchange(send_ids.reshape(owners, CAP)).reshape(slot_count)

    def absorb(best_now, other_unit, other_ids):
        scores = lax.dot_general(
            keys_unit, other_unit, (((1,), (1,)), ((), ())), preferred_element_type=jnp.float32
        )
        allowed = other_ids[None, :] < keys_ids[:, None]
        return jnp.maximum(best_now, jnp.max(jnp.where(allowed, scores, -1.0), axis=1))

    start_best = jnp.full((slot_count,), -1.0, jnp.float32)

    def advance(step_index, state_now):
        best_now, moving_unit, moving_ids = state_now
        moving_unit, moving_ids = passed_along((moving_unit, moving_ids), "blk", 1)
        return (absorb(best_now, moving_unit, moving_ids), moving_unit, moving_ids)

    best_sim, _, _ = lax.fori_loop(
        0, loop_size - 1, advance, (absorb(start_best, keys_unit, keys_ids), keys_unit, keys_ids)
    )
    returned = exchange(best_sim.reshape(owners, CAP)).reshape(slot_count)
    return returned[target]


SLABS_ROWS = 2 * CAP


def middle_of(core):
    return 1 + core


def sources():
    return [(0, 3), (1, 3), (0, 0), (0, 2), (1, 0), (1, 2), (1, 1)]


def blk_of(far_blk, core):
    return far_blk if core == 0 else 3 - far_blk


def here():
    u = lax.axis_index("clus")
    b = lax.axis_index("blk")
    return u, b


def put_slabs(ref, start, rows):
    for t in range(rows.shape[1] // 128):
        ref[pl.ds(start + t * SLABS_ROWS, rows.shape[0]), :] = rows[:, t * 128 : (t + 1) * 128]


def get_slabs(ref, start, count, slabs):
    return jnp.concatenate(
        [ref[t * SLABS_ROWS + start : t * SLABS_ROWS + start + count, :] for t in range(slabs)], axis=1
    )


def sort_kernel(emb_ref, cluster_ref, ids_ref, keep_ref, give_ref, target_ref):
    rows, width = emb_ref.shape
    slots = 4 * CAP
    u, _ = here()
    cluster = cluster_ref[...]
    slot = cluster ^ u
    onehot = lax.broadcasted_iota(jnp.int32, (8, rows), 0) == slot
    earlier = (
        lax.broadcasted_iota(jnp.int32, (rows, rows), 0)
        < lax.broadcasted_iota(jnp.int32, (rows, rows), 1)
    ).astype(jnp.bfloat16)
    before = jnp.dot(onehot.astype(jnp.bfloat16), earlier, preferred_element_type=jnp.float32)
    position = jnp.sum(jnp.where(onehot, before, 0.0), axis=0, keepdims=True).astype(jnp.int32)
    target_ref[...] = cluster * CAP + position
    order = (slot & 1) * 2 + (slot >> 1)
    place = (
        lax.broadcasted_iota(jnp.int32, (slots, rows), 0) == order * CAP + position
    ).astype(jnp.bfloat16)
    values = jnp.dot(place, emb_ref[...], preferred_element_type=jnp.float32)
    mean = jnp.mean(values * values, axis=1, keepdims=True)
    unit = (values * lax.rsqrt(mean + EPS) * width ** (-0.5)).astype(jnp.bfloat16)
    put_slabs(keep_ref, 0, unit[: 2 * CAP])
    put_slabs(give_ref, 0, unit[2 * CAP :])
    ids = ids_ref[...]
    row = lax.broadcasted_iota(jnp.int32, (16, rows), 0)
    parts = jnp.where(row == 0, ids >> 8, jnp.where(row == 1, ids & 255, 1))
    moved = lax.dot_general(
        parts.astype(jnp.float32).astype(jnp.bfloat16),
        place,
        (((1,), (1,)), ((), ())),
        preferred_element_type=jnp.float32,
    )
    row = lax.broadcasted_iota(jnp.int32, (16, slots), 0)
    moved = jnp.where((moved[2:3] == 0.0) & (row == 0), 256.0, moved).astype(jnp.bfloat16)
    tail = width // 128 * SLABS_ROWS
    keep_ref[tail : tail + 16, :] = moved[:, : 2 * CAP]
    give_ref[tail : tail + 16, :] = moved[:, 2 * CAP :]


def join_kernel(keep_ref, got_ref, near_ref, far_ref):
    u, _ = here()
    core = lax.rem(u, 2)
    tail = keep_ref.shape[0] - 16
    own_at = pl.multiple_of(core * CAP, CAP)
    other_at = pl.multiple_of((1 - core) * CAP, CAP)
    for out_ref, start in ((near_ref, 0), (far_ref, CAP)):
        for t in range(tail // SLABS_ROWS):
            base = t * SLABS_ROWS
            out_ref[pl.ds(base + own_at, CAP), :] = keep_ref[base + start : base + start + CAP, :]
            out_ref[pl.ds(base + other_at, CAP), :] = got_ref[base + start : base + start + CAP, :]
        own = keep_ref[tail:, :].astype(jnp.float32)[:, start : start + CAP]
        other = got_ref[tail:, :].astype(jnp.float32)[:, start : start + CAP]
        first = jnp.where(core == 0, own, other)
        second = jnp.where(core == 0, other, own)
        out_ref[tail:, :] = jnp.concatenate([first, second], axis=1).astype(jnp.bfloat16)


def meet_kernel(*refs):
    count = 8
    block_refs, best_ref = refs[:count], refs[-1]
    u, b = here()
    core = lax.rem(u, 2)
    tail = block_refs[0].shape[0] - 16
    slabs = tail // SLABS_ROWS
    tile = 256
    per = tile // SLABS_ROWS
    tiles = count // per

    @pl.when(b == middle_of(core))
    def _():
        def rows_of(t):
            return jnp.concatenate(
                [get_slabs(r, 0, SLABS_ROWS, slabs) for r in block_refs[t * per : (t + 1) * per]],
                axis=0,
            )

        ids_of = []
        for r in block_refs:
            parts = r[tail:, :].astype(jnp.float32)
            ids_of.append(parts[0:1] * 256.0 + parts[1:2])
        down = [jnp.broadcast_to(i, (SLABS_ROWS, 128)).T for i in ids_of]
        for query in range(tiles):
            query_rows = rows_of(query)
            query_ids = jnp.concatenate(ids_of[query * per : (query + 1) * per], axis=1)
            best = jnp.full((1, tile), -1.0, jnp.float32)
            for key in range(tiles):
                scores = lax.dot_general(
                    rows_of(key),
                    query_rows,
                    (((1,), (1,)), ((), ())),
                    preferred_element_type=jnp.float32,
                )
                key_ids = jnp.concatenate(down[key * per : (key + 1) * per], axis=0)
                key_ids = jnp.concatenate([key_ids] * (tile // 128), axis=1)
                best = jnp.maximum(
                    best,
                    jnp.max(jnp.where(key_ids < query_ids, scores, -1.0), axis=0, keepdims=True),
                )
            for part in range(per):
                q = query * per + part
                other, far_blk = (0, 0) if q == 0 else sources()[q - 1]
                if q == 0:
                    at_blk = b
                else:
                    at_blk = jnp.where(core == 0, far_blk, 3 - far_blk)
                chip = (u >> 1) ^ other
                row = best[:, part * 128 : (part + 1) * 128]
                for c in range(2):
                    best_ref[at_blk * 4 + chip * 2 + c] = row


def home_kernel(got_ref, target_ref, out_ref):
    u, _ = here()
    core = lax.rem(u, 2)
    slots = 4 * CAP
    rows = target_ref.shape[1]
    pieces = []
    for c in range(4):
        row = got_ref[middle_of(c % 2) * 4 + c]
        pieces.append(jnp.where(core == 0, row[:, :CAP], row[:, CAP:]))
    best = jnp.concatenate(pieces, axis=1)
    high = best.astype(jnp.bfloat16).astype(jnp.float32)
    rest = best - high
    middle_part = rest.astype(jnp.bfloat16).astype(jnp.float32)
    low = rest - middle_part
    row = lax.broadcasted_iota(jnp.int32, (8, slots), 0)
    parts = jnp.where(row == 0, high, jnp.where(row == 1, middle_part, jnp.where(row == 2, low, 0.0)))
    place = lax.broadcasted_iota(jnp.int32, (slots, rows), 0) == target_ref[...]
    moved = jnp.dot(
        parts.astype(jnp.bfloat16), place.astype(jnp.bfloat16), preferred_element_type=jnp.float32
    )
    out_ref[...] = moved[0:1] + moved[1:2] + moved[2:3]


def meet(embeddings, cluster, row_ids):
    rows, width = embeddings.shape
    everyone = ("blk", "clus")
    payload = jax.ShapeDtypeStruct((width // 128 * SLABS_ROWS + 16, 128), jnp.bfloat16)

    def pairs(other, far_blk):
        found = []
        for c in range(4):
            source = blk_of(far_blk, c % 2) * 4 + (c ^ (2 * other))
            found.append((source, middle_of(c % 2) * 4 + c))
        return found

    keep, give, target = pl.pallas_call(
        sort_kernel,
        out_shape=[payload, payload, jax.ShapeDtypeStruct((1, rows), jnp.int32)],
        in_specs=[VMEM] * 3,
        out_specs=[VMEM] * 3,
        name="sort_rows",
    )(embeddings, cluster.reshape(1, rows), row_ids.reshape(1, rows))
    got = lax.ppermute(give, "clus", [(c, c ^ 1) for c in range(4)])
    near, far = pl.pallas_call(
        join_kernel,
        out_shape=[payload] * 2,
        in_specs=[VMEM] * 2,
        out_specs=[VMEM] * 2,
        name="join_cores",
    )(keep, got)
    arrived = [near]
    for other, far_blk in sources():
        arrived.append(lax.ppermute(far if other else near, everyone, pairs(other, far_blk)))
    best = pl.pallas_call(
        meet_kernel,
        out_shape=jax.ShapeDtypeStruct((16, 1, 128), jnp.float32),
        in_specs=[VMEM] * 8,
        out_specs=VMEM,
        name="meet_scores",
    )(*arrived)
    returned = lax.all_to_all(best, everyone, split_axis=0, concat_axis=0, tiled=True)
    out = pl.pallas_call(
        home_kernel,
        out_shape=jax.ShapeDtypeStruct((1, rows), jnp.float32),
        in_specs=[VMEM] * 2,
        out_specs=VMEM,
        name="home_scores",
    )(returned, target)
    return out.reshape(rows)


def solution(mesh):
    takes_a_cluster = mesh.shape["blk"] == 4 and mesh.shape["clus"] == 4
    return jax.shard_map(
        meet if takes_a_cluster else ring,
        mesh=mesh,
        in_specs=(
            P(("groups", "blk", "clus"), None),
            P(("groups", "blk", "clus")),
            P(("groups", "blk", "clus")),
        ),
        out_specs=P(("groups", "blk", "clus")),
        check_vma=False,
    )
```

time: 84.3 us -> 47.9 us (0.57)
  waiting for transfers between devices: 50.6 us -> 6.68 us
  blocking collectives: 0 us -> 15.3 us
  other arithmetic: 8.51 us -> 0 us
  Pallas kernels: 0 us -> 7.94 us
  local copies, waits for them, and re-layouts: 7.1 us -> 2.06 us
  matrix products: 1.42 us -> 0 us
    ppermute x6 -> x8, waiting for transfers between devices: 39.3 us -> 6.68 us  [the longest x7 5.3 us: meet(): lax.ppermute(far if other else near, everyone, pairs(other, far_blk))]
    all_to_all x0 -> x1, blocking collectives: none -> 15.3 us  [meet(): lax.all_to_all(best, everyone, split_axis=0, concat_axis=0, tiled=True)]
    all_to_all x3 -> x0, waiting for transfers between devices: 11.3 us -> none  [the longest x1 7.55 us: local(): lax.all_to_all(send_unit.reshape(owners, CAP, feature_width), 'clus', spl...]
    all_to_all x3 -> x0, starting transfers between devices: 10.9 us -> none  [the longest x1 4.21 us: local(): lax.all_to_all(send_ids.reshape(owners, CAP), 'clus', split_axis=0, conca...]
    ppermute x6 -> x8, starting transfers between devices: 5.15 us -> 15.4 us  [the longest x7 14.9 us: meet(): lax.ppermute(far if other else near, everyone, pairs(other, far_blk))]
    pallas_call x0 -> x4, Pallas kernels: none -> 7.94 us  [the longest x1 2.41 us: meet(): pl.pallas_call(sort_kernel, out_shape=[payload, payload, jax.ShapeDtypeSt...]
    scatter x1 -> x0, other arithmetic: 2.55 us -> none  [local(): jnp.zeros((slot_count, feature_width), jnp.bfloat16).at[target]]
    gather x1 -> x0, local copies, waits for them, and re-layouts: 2.5 us -> none  [local(): return returned.reshape(slot_count)[target]]
  transfers between devices with their start and end apart: 9 -> 8, of which waited for: 5 -> 2; matrix products, arithmetic and copies ran while one was open for 6% -> 0% of each run, Pallas kernels for 0% -> 0%
where the time goes in v2:
time: 47.9 us; the launch traced here: 47.5 us
  starting transfers between devices  15.4 us (32%)
  blocking collectives  15.3 us (32%)
  Pallas kernels  7.94 us (17%)
  waiting for transfers between devices  6.68 us (14%)
  local copies, waits for them, and re-layouts  2.06 us (4%)
    all_to_all x1, blocking collectives, meet(): lax.all_to_all(best, everyone, split_axis=0, concat_axis=0, tiled=True)  15.3 us
    ppermute x7, starting transfers between devices, meet(): lax.ppermute(far if other else near, everyone, pairs(other, far_blk))  14.9 us
    ppermute x7, waiting for transfers between devices, meet(): lax.ppermute(far if other else near, everyone, pairs(other, far_blk))  5.3 us
    pallas_call x1, Pallas kernels, meet(): pl.pallas_call(sort_kernel, out_shape=[payload, payload, jax.ShapeDtypeSt...  2.41 us
    pallas_call x1, Pallas kernels, meet(): pl.pallas_call(meet_kernel, out_shape=jax.ShapeDtypeStruct((16, 1, 128),...  2.09 us
    unnamed x16, local copies, waits for them, and re-layouts  2.06 us
    pallas_call x1, Pallas kernels, meet(): pl.pallas_call(join_kernel, out_shape=[payload] * 2, in_specs=[VMEM] * 2,...  1.91 us
    pallas_call x1, Pallas kernels, meet(): pl.pallas_call(home_kernel, out_shape=jax.ShapeDtypeStruct((1, rows), jnp...  1.53 us
  transfers between devices with their start and end apart: 8, of which 2 were waited for; matrix products, arithmetic and copies ran while one was open for 0% of the time, Pallas kernels for 0%

profile of v2, /device:TPU:0, one launch (start us, length us, event | category | flops | bytes accessed | tf_op | source)
XLA Modules:
  0.0 47.5 jit_solution(5096682913978320569)
XLA Ops:
  0.0 2.4 %sort_rows.1 = (bf16[1040,128]{1,0:T(8,128)(2,1)}, bf16[1040,128]{1,0:T(8,128)(2,1)}, s32[1,256]{1,0:T(1,128)}) custom-call(bf16[256,1024]{1,0:T(8,128)(2,1)} %emb_ref.1, s32[1,256]{1,0:T(1,128)} %bitcast.3, s32[1,256]{1,0:T(1,128)} %bitcast.4), custom_call_target="tpu_custom_call" | custom-call | tf_op jit(solution)/shard_map/sort_rows/pallas_call | solution.py:245
  2.4 0.5 collective-permute-start
  2.9 1.4 %collective-permute-done.got_ref = bf16[1040,128]{1,0:T(8,128)(2,1)S(1)} collective-permute-done((bf16[1040,128]{1,0:T(8,128)(2,1)}, bf16[1040,128]{1,0:T(8,128)(2,1)S(1)}, u32[]{:S(2)}, u32[]{:S(2)}) %collective-permute-start) | collective-permute-done | bytes 266272 | tf_op jit(solution)/shard_map/ppermute | solution.py:252
  4.2 0.0 copy-start
  4.2 0.7 %copy-done = bf16[1040,128]{1,0:T(8,128)(2,1)} copy-done((bf16[1040,128]{1,0:T(8,128)(2,1)}, bf16[1040,128]{1,0:T(8,128)(2,1)S(1)}, u32[]{:S(2)}) %copy-start) | copy-done | bytes 266264
  4.9 1.9 %join_cores.1 = (bf16[1040,128]{1,0:T(8,128)(2,1)}, bf16[1040,128]{1,0:T(8,128)(2,1)}) custom-call(bf16[1040,128]{1,0:T(8,128)(2,1)} %get-tuple-element.10.keep_ref, bf16[1040,128]{1,0:T(8,128)(2,1)} %copy-done), custom_call_target="tpu_custom_call" | custom-call | tf_op jit(solution)/shard_map/join_cores/pallas_call | solution.py:253
  6.8 0.7 %collective-permute-start.4 = (bf16[1040,128]{1,0:T(8,128)(2,1)}, bf16[1040,128]{1,0:T(8,128)(2,1)S(1)}, u32[]{:S(2)}, u32[]{:S(2)}) collective-permute-start(bf16[1040,128]{1,0:T(8,128)(2,1)} %get-tuple-element.12.refs_0_), channel_id=1, source_target_pairs={{8,4},{5,9},{10,6},{7,11},{24,20},{21,25},{26,22},{23,27}} | collective-permute-start | bytes 798728 | tf_op jit(solution)/shard_map/ppermute | solution.py:262
  7.5 5.5 %collective-permute-start.3 = (bf16[1040,128]{1,0:T(8,128)(2,1)}, bf16[1040,128]{1,0:T(8,128)(2,1)S(1)}, u32[]{:S(2)}, u32[]{:S(2)}) collective-permute-start(bf16[1040,128]{1,0:T(8,128)(2,1)} %get-tuple-element.12.refs_0_), channel_id=1, source_target_pairs={{0,4},{13,9},{2,6},{15,11},{16,20},{29,25},{18,22},{31,27}} | collective-permute-start | bytes 798728 | tf_op jit(solution)/shard_map/ppermute | solution.py:262
  13.0 0.7 %collective-permute-start.1 = (bf16[1040,128]{1,0:T(8,128)(2,1)}, bf16[1040,128]{1,0:T(8,128)(2,1)S(1)}, u32[]{:S(2)}, u32[]{:S(2)}) collective-permute-start(bf16[1040,128]{1,0:T(8,128)(2,1)} %get-tuple-element.12.refs_0_), channel_id=1, source_target_pairs={{12,4},{1,9},{14,6},{3,11},{28,20},{17,25},{30,22},{19,27}} | collective-permute-start | bytes 798728 | tf_op jit(solution)/shard_map/ppermute | solution.py:262
  13.7 0.7 %collective-permute-start.7 = (bf16[1040,128]{1,0:T(8,128)(2,1)}, bf16[1040,128]{1,0:T(8,128)(2,1)S(1)}, u32[]{:S(2)}, u32[]{:S(2)}) collective-permute-start(bf16[1040,128]{1,0:T(8,128)(2,1)} %get-tuple-element.13), channel_id=1, source_target_pairs={{6,4},{11,9},{4,6},{9,11},{22,20},{27,25},{20,22},{25,27}} | collective-permute-start | bytes 798728 | tf_op jit(solution)/shard_map/ppermute | solution.py:262
  14.4 0.7 %collective-permute-start.6 = (bf16[1040,128]{1,0:T(8,128)(2,1)}, bf16[1040,128]{1,0:T(8,128)(2,1)S(1)}, u32[]{:S(2)}, u32[]{:S(2)}) collective-permute-start(bf16[1040,128]{1,0:T(8,128)(2,1)} %get-tuple-element.13), channel_id=1, source_target_pairs={{10,4},{7,9},{8,6},{5,11},{26,20},{23,25},{24,22},{21,27}} | collective-permute-start | bytes 798728 | tf_op jit(solution)/shard_map/ppermute | solution.py:262
  15.1 0.0 collective-permute-done.4.refs_4_
  15.1 0.0 copy-start.1
  15.1 6.1 %collective-permute-start.5 = (bf16[1040,128]{1,0:T(8,128)(2,1)}, bf16[1040,128]{1,0:T(8,128)(2,1)S(1)}, u32[]{:S(2)}, u32[]{:S(2)}) collective-permute-start(bf16[1040,128]{1,0:T(8,128)(2,1)} %get-tuple-element.13), channel_id=1, source_target_pairs={{2,4},{15,9},{0,6},{13,11},{18,20},{31,25},{16,22},{29,27}} | collective-permute-start | bytes 798728 | tf_op jit(solution)/shard_map/ppermute | solution.py:262
  21.1 0.0 collective-permute-done.3.refs_3_
  21.2 0.0 copy-start.2
  21.2 0.7 %collective-permute-start.2 = (bf16[1040,128]{1,0:T(8,128)(2,1)}, bf16[1040,128]{1,0:T(8,128)(2,1)S(1)}, u32[]{:S(2)}, u32[]{:S(2)}) collective-permute-start(bf16[1040,128]{1,0:T(8,128)(2,1)} %get-tuple-element.13), channel_id=1, source_target_pairs={{14,4},{3,9},{12,6},{1,11},{30,20},{19,25},{28,22},{17,27}} | collective-permute-start | bytes 798728 | tf_op jit(solution)/shard_map/ppermute | solution.py:262
  21.8 0.0 collective-permute-done.1.refs_1_
  21.9 0.0 copy-start.3
  21.9 0.0 collective-permute-done.7.refs_7_
  21.9 0.0 copy-start.4
  21.9 0.0 collective-permute-done.6.refs_6_
  21.9 0.0 copy-start.5
  21.9 5.3 %collective-permute-done.5.refs_5_ = bf16[1040,128]{1,0:T(8,128)(2,1)S(1)} collective-permute-done((bf16[1040,128]{1,0:T(8,128)(2,1)}, bf16[1040,128]{1,0:T(8,128)(2,1)S(1)}, u32[]{:S(2)}, u32[]{:S(2)}) %collective-permute-start.5) | collective-permute-done | bytes 266272 | tf_op jit(solution)/shard_map/ppermute | solution.py:262
  27.2 0.0 copy-start.6
  27.2 0.0 collective-permute-done.2.refs_2_
  27.2 0.0 copy-done.1
  27.2 0.0 copy-done.2
  27.2 0.0 copy-done.3
  27.2 0.0 copy-done.4
  27.2 0.0 copy-done.5
  27.2 0.6 %copy-done.6 = bf16[1040,128]{1,0:T(8,128)(2,1)} copy-done((bf16[1040,128]{1,0:T(8,128)(2,1)}, bf16[1040,128]{1,0:T(8,128)(2,1)S(1)}, u32[]{:S(2)}) %copy-start.6) | copy-done | bytes 266264
  27.9 0.0 copy-start.7
  27.9 0.7 %copy-done.7 = bf16[1040,128]{1,0:T(8,128)(2,1)} copy-done((bf16[1040,128]{1,0:T(8,128)(2,1)}, bf16[1040,128]{1,0:T(8,128)(2,1)S(1)}, u32[]{:S(2)}) %copy-start.7) | copy-done | bytes 266264
  28.6 2.1 %meet_scores.1 = f32[16,1,128]{2,1,0:T(1,128)} custom-call(bf16[1040,128]{1,0:T(8,128)(2,1)} %get-tuple-element.12.refs_0_, bf16[1040,128]{1,0:T(8,128)(2,1)} %copy-done.3, bf16[1040,128]{1,0:T(8,128)(2,1)} %copy-done.7, bf16[1040,128]{1,0:T(8,128)(2,1)} %copy-done.2, bf16[1040,128]{1,0:T(8,128)(2,1)} %copy-done.1, bf16[1040,128]{1,0:T(8,128)(2,1)} %copy-done.6, ...), custom_call_target="tpu_custom_call" | custom-call | tf_op jit(solution)/shard_map/meet_scores/pallas_call | solution.py:263
  30.7 15.3 %all_to_all.5.got_ref = f32[16,1,128]{2,1,0:T(1,128)} all-to-all(f32[16,1,128]{2,1,0:T(1,128)} %meet_scores.1), channel_id=1, replica_groups=mesh['groups'=2,'blk'=4,'clus'=4] {'blk','clus'}, dimensions={0} | all-to-all | bytes 16384 | tf_op jit(solution)/shard_map/all_to_all | solution.py:270
  46.0 1.5 %home_scores.1 = f32[1,256]{1,0:T(1,128)} custom-call(f32[16,1,128]{2,1,0:T(1,128)} %all_to_all.5.got_ref, s32[1,256]{1,0:T(1,128)} %get-tuple-element.14.target_ref), custom_call_target="tpu_custom_call" | custom-call | tf_op jit(solution)/shard_map/home_scores/pallas_call | solution.py:271
Async XLA Ops:
  2.4 1.8 %collective-permute-start = (bf16[1040,128]{1,0:T(8,128)(2,1)}, bf16[1040,128]{1,0:T(8,128)(2,1)S(1)}, u32[]{:S(2)}, u32[]{:S(2)}) collective-permute-start(bf16[1040,128]{1,0:T(8,128)(2,1)} %get-tuple-element.11), channel_id=1, source_target_pairs={{0,1},{1,0},{2,3},{3,2},{4,5},{5,4},{6,7},{7,6},{8,9},{9,8},{10,11... | collective-permute-start | bytes 798728 | tf_op jit(solution)/shard_map/ppermute | solution.py:252
  4.2 0.7 %copy-start = (bf16[1040,128]{1,0:T(8,128)(2,1)}, bf16[1040,128]{1,0:T(8,128)(2,1)S(1)}, u32[]{:S(2)}) copy-start(bf16[1040,128]{1,0:T(8,128)(2,1)S(1)} %collective-permute-done.got_ref) | copy-start | bytes 798724
  6.8 8.2 %collective-permute-start.4 = (bf16[1040,128]{1,0:T(8,128)(2,1)}, bf16[1040,128]{1,0:T(8,128)(2,1)S(1)}, u32[]{:S(2)}, u32[]{:S(2)}) collective-permute-start(bf16[1040,128]{1,0:T(8,128)(2,1)} %get-tuple-element.12.refs_0_), channel_id=1, source_target_pairs={{8,4},{5,9},{10,6},{7,11},{24,20},{21,25},{26,22},{23,27}} | collective-permute-start | bytes 798728 | tf_op jit(solution)/shard_map/ppermute | solution.py:262
  7.5 13.6 %collective-permute-start.3 = (bf16[1040,128]{1,0:T(8,128)(2,1)}, bf16[1040,128]{1,0:T(8,128)(2,1)S(1)}, u32[]{:S(2)}, u32[]{:S(2)}) collective-permute-start(bf16[1040,128]{1,0:T(8,128)(2,1)} %get-tuple-element.12.refs_0_), channel_id=1, source_target_pairs={{0,4},{13,9},{2,6},{15,11},{16,20},{29,25},{18,22},{31,27}} | collective-permute-start | bytes 798728 | tf_op jit(solution)/shard_map/ppermute | solution.py:262
  13.0 8.8 %collective-permute-start.1 = (bf16[1040,128]{1,0:T(8,128)(2,1)}, bf16[1040,128]{1,0:T(8,128)(2,1)S(1)}, u32[]{:S(2)}, u32[]{:S(2)}) collective-permute-start(bf16[1040,128]{1,0:T(8,128)(2,1)} %get-tuple-element.12.refs_0_), channel_id=1, source_target_pairs={{12,4},{1,9},{14,6},{3,11},{28,20},{17,25},{30,22},{19,27}} | collective-permute-start | bytes 798728 | tf_op jit(solution)/shard_map/ppermute | solution.py:262
  13.7 8.2 %collective-permute-start.7 = (bf16[1040,128]{1,0:T(8,128)(2,1)}, bf16[1040,128]{1,0:T(8,128)(2,1)S(1)}, u32[]{:S(2)}, u32[]{:S(2)}) collective-permute-start(bf16[1040,128]{1,0:T(8,128)(2,1)} %get-tuple-element.13), channel_id=1, source_target_pairs={{6,4},{11,9},{4,6},{9,11},{22,20},{27,25},{20,22},{25,27}} | collective-permute-start | bytes 798728 | tf_op jit(solution)/shard_map/ppermute | solution.py:262
  14.4 7.5 %collective-permute-start.6 = (bf16[1040,128]{1,0:T(8,128)(2,1)}, bf16[1040,128]{1,0:T(8,128)(2,1)S(1)}, u32[]{:S(2)}, u32[]{:S(2)}) collective-permute-start(bf16[1040,128]{1,0:T(8,128)(2,1)} %get-tuple-element.13), channel_id=1, source_target_pairs={{10,4},{7,9},{8,6},{5,11},{26,20},{23,25},{24,22},{21,27}} | collective-permute-start | bytes 798728 | tf_op jit(solution)/shard_map/ppermute | solution.py:262
  15.1 12.1 %copy-start.1 = (bf16[1040,128]{1,0:T(8,128)(2,1)}, bf16[1040,128]{1,0:T(8,128)(2,1)S(1)}, u32[]{:S(2)}) copy-start(bf16[1040,128]{1,0:T(8,128)(2,1)S(1)} %collective-permute-done.4.refs_4_) | copy-start | bytes 798724
  15.1 12.1 %collective-permute-start.5 = (bf16[1040,128]{1,0:T(8,128)(2,1)}, bf16[1040,128]{1,0:T(8,128)(2,1)S(1)}, u32[]{:S(2)}, u32[]{:S(2)}) collective-permute-start(bf16[1040,128]{1,0:T(8,128)(2,1)} %get-tuple-element.13), channel_id=1, source_target_pairs={{2,4},{15,9},{0,6},{13,11},{18,20},{31,25},{16,22},{29,27}} | collective-permute-start | bytes 798728 | tf_op jit(solution)/shard_map/ppermute | solution.py:262
  21.2 6.1 %copy-start.2 = (bf16[1040,128]{1,0:T(8,128)(2,1)}, bf16[1040,128]{1,0:T(8,128)(2,1)S(1)}, u32[]{:S(2)}) copy-start(bf16[1040,128]{1,0:T(8,128)(2,1)S(1)} %collective-permute-done.3.refs_3_) | copy-start | bytes 798724
  21.2 6.0 %collective-permute-start.2 = (bf16[1040,128]{1,0:T(8,128)(2,1)}, bf16[1040,128]{1,0:T(8,128)(2,1)S(1)}, u32[]{:S(2)}, u32[]{:S(2)}) collective-permute-start(bf16[1040,128]{1,0:T(8,128)(2,1)} %get-tuple-element.13), channel_id=1, source_target_pairs={{14,4},{3,9},{12,6},{1,11},{30,20},{19,25},{28,22},{17,27}} | collective-permute-start | bytes 798728 | tf_op jit(solution)/shard_map/ppermute | solution.py:262
  21.9 5.4 %copy-start.3 = (bf16[1040,128]{1,0:T(8,128)(2,1)}, bf16[1040,128]{1,0:T(8,128)(2,1)S(1)}, u32[]{:S(2)}) copy-start(bf16[1040,128]{1,0:T(8,128)(2,1)S(1)} %collective-permute-done.1.refs_1_) | copy-start | bytes 798724
  21.9 5.3 %copy-start.4 = (bf16[1040,128]{1,0:T(8,128)(2,1)}, bf16[1040,128]{1,0:T(8,128)(2,1)S(1)}, u32[]{:S(2)}) copy-start(bf16[1040,128]{1,0:T(8,128)(2,1)S(1)} %collective-permute-done.7.refs_7_) | copy-start | bytes 798724
  21.9 5.3 %copy-start.5 = (bf16[1040,128]{1,0:T(8,128)(2,1)}, bf16[1040,128]{1,0:T(8,128)(2,1)S(1)}, u32[]{:S(2)}) copy-start(bf16[1040,128]{1,0:T(8,128)(2,1)S(1)} %collective-permute-done.6.refs_6_) | copy-start | bytes 798724
  27.2 0.7 %copy-start.6 = (bf16[1040,128]{1,0:T(8,128)(2,1)}, bf16[1040,128]{1,0:T(8,128)(2,1)S(1)}, u32[]{:S(2)}) copy-start(bf16[1040,128]{1,0:T(8,128)(2,1)S(1)} %collective-permute-done.5.refs_5_) | copy-start | bytes 798724
  27.9 0.7 %copy-start.7 = (bf16[1040,128]{1,0:T(8,128)(2,1)}, bf16[1040,128]{1,0:T(8,128)(2,1)S(1)}, u32[]{:S(2)}) copy-start(bf16[1040,128]{1,0:T(8,128)(2,1)S(1)} %collective-permute-done.2.refs_2_) | copy-start | bytes 798724

commit v3 on v2

--- a/solution.py
+++ b/solution.py
@@ -65,14 +65,14 @@
 
 
 SLABS_ROWS = 2 * CAP
+SMALL = pltpu.CompilerParams(vmem_limit_bytes=8 << 20)
 
 
 def middle_of(core):
     return 1 + core
 
 
-def sources():
-    return [(0, 3), (1, 3), (0, 0), (0, 2), (1, 0), (1, 2), (1, 1)]
+FAR_BLKS = (2, 0, 3)
 
 
 def blk_of(far_blk, core):
@@ -141,7 +141,7 @@
     tail = keep_ref.shape[0] - 16
     own_at = pl.multiple_of(core * CAP, CAP)
     other_at = pl.multiple_of((1 - core) * CAP, CAP)
-    for out_ref, start in ((near_ref, 0), (far_ref, CAP)):
+    for out_ref, start in ((far_ref, CAP), (near_ref, 0)):
         for t in range(tail // SLABS_ROWS):
             base = t * SLABS_ROWS
             out_ref[pl.ds(base + own_at, CAP), :] = keep_ref[base + start : base + start + CAP, :]
@@ -196,11 +196,9 @@
                 )
             for part in range(per):
                 q = query * per + part
-                other, far_blk = (0, 0) if q == 0 else sources()[q - 1]
-                if q == 0:
-                    at_blk = b
-                else:
-                    at_blk = jnp.where(core == 0, far_blk, 3 - far_blk)
+                other, place = divmod(q, 4)
+                far_blk = FAR_BLKS[place - 1]
+                at_blk = jnp.where(core == 0, far_blk, 3 - far_blk) if place else b
                 chip = (u >> 1) ^ other
                 row = best[:, part * 128 : (part + 1) * 128]
                 for c in range(2):
@@ -235,18 +233,16 @@
     everyone = ("blk", "clus")
     payload = jax.ShapeDtypeStruct((width // 128 * SLABS_ROWS + 16, 128), jnp.bfloat16)
 
-    def pairs(other, far_blk):
-        found = []
-        for c in range(4):
-            source = blk_of(far_blk, c % 2) * 4 + (c ^ (2 * other))
-            found.append((source, middle_of(c % 2) * 4 + c))
-        return found
+    def to_meeting(value, far_blk):
+        pairs = [(blk_of(far_blk, c % 2) * 4 + c, middle_of(c % 2) * 4 + c) for c in range(4)]
+        return lax.ppermute(value, everyone, pairs)
 
     keep, give, target = pl.pallas_call(
         sort_kernel,
         out_shape=[payload, payload, jax.ShapeDtypeStruct((1, rows), jnp.int32)],
         in_specs=[VMEM] * 3,
         out_specs=[VMEM] * 3,
+        compiler_params=SMALL,
         name="sort_rows",
     )(embeddings, cluster.reshape(1, rows), row_ids.reshape(1, rows))
     got = lax.ppermute(give, "clus", [(c, c ^ 1) for c in range(4)])
@@ -255,16 +251,20 @@
         out_shape=[payload] * 2,
         in_specs=[VMEM] * 2,
         out_specs=[VMEM] * 2,
+        compiler_params=SMALL,
         name="join_cores",
     )(keep, got)
-    arrived = [near]
-    for other, far_blk in sources():
-        arrived.append(lax.ppermute(far if other else near, everyone, pairs(other, far_blk)))
+    crossed = lax.ppermute(far, "clus", [(c, c ^ 2) for c in range(4)])
+    arrived = []
+    for value in (near, crossed):
+        arrived.append(value)
+        arrived += [to_meeting(value, far_blk) for far_blk in FAR_BLKS]
     best = pl.pallas_call(
         meet_kernel,
         out_shape=jax.ShapeDtypeStruct((16, 1, 128), jnp.float32),
         in_specs=[VMEM] * 8,
         out_specs=VMEM,
+        compiler_params=SMALL,
         name="meet_scores",
     )(*arrived)
     returned = lax.all_to_all(best, everyone, split_axis=0, concat_axis=0, tiled=True)
@@ -273,6 +273,7 @@
         out_shape=jax.ShapeDtypeStruct((1, rows), jnp.float32),
         in_specs=[VMEM] * 2,
         out_specs=VMEM,
+        compiler_params=SMALL,
         name="home_scores",
     )(returned, target)
     return out.reshape(rows)

time: 47.9 us -> 41.1 us (0.86)
  Pallas kernels: 7.94 us -> 1.48 us
  blocking collectives: 15.3 us -> 16.4 us
  starting transfers between devices: 15.4 us -> 14.6 us
    pallas_call x1, Pallas kernels: 2.09 us -> 0.01 us  [meet(): pl.pallas_call(meet_kernel, out_shape=jax.ShapeDtypeStruct((16, 1, 128),...]
    pallas_call x1, Pallas kernels: 2.41 us -> 0.56 us  [meet(): pl.pallas_call(sort_kernel, out_shape=[payload, payload, jax.ShapeDtypeSt...]
    pallas_call x1, Pallas kernels: 1.91 us -> 0.09 us  [meet(): pl.pallas_call(join_kernel, out_shape=[payload] * 2, in_specs=[VMEM] * 2,...]
    all_to_all x1, blocking collectives: 15.3 us -> 16.4 us  [meet(): lax.all_to_all(best, everyone, split_axis=0, concat_axis=0, tiled=True)]
    ppermute x7, starting transfers between devices: 14.9 us -> 14.1 us  [the longest x6 11.2 us: to_meeting(): return lax.ppermute(value, everyone, pairs)]
    pallas_call x1, Pallas kernels: 1.53 us -> 0.83 us  [meet(): pl.pallas_call(home_kernel, out_shape=jax.ShapeDtypeStruct((1, rows), jnp...]
    unnamed x16 -> x6, local copies, waits for them, and re-layouts: 2.06 us -> 1.73 us
  transfers between devices with their start and end apart: 8 -> 8, of which waited for: 2 -> 3; matrix products, arithmetic and copies ran while one was open for 0% -> 0% of each run, Pallas kernels for 0% -> 0%
where the time goes in v3:
time: 41.1 us; the launch traced here: 40.8 us
  blocking collectives  16.4 us (40%)
  starting transfers between devices  14.6 us (36%)
  waiting for transfers between devices  6.47 us (16%)
  local copies, waits for them, and re-layouts  1.73 us (4%)
  Pallas kernels  1.48 us (4%)
    all_to_all x1, blocking collectives, meet(): lax.all_to_all(best, everyone, split_axis=0, concat_axis=0, tiled=True)  16.4 us
    ppermute x6, starting transfers between devices, to_meeting(): return lax.ppermute(value, everyone, pairs)  11.2 us
    ppermute x6, waiting for transfers between devices, to_meeting(): return lax.ppermute(value, everyone, pairs)  4.09 us
    ppermute x1, starting transfers between devices, meet(): crossed = lax.ppermute(far, 'clus', [(c, c ^ 2) for c in range(4)])  2.9 us
    unnamed x6, local copies, waits for them, and re-layouts  1.73 us
    ppermute x1, waiting for transfers between devices, meet(): crossed = lax.ppermute(far, 'clus', [(c, c ^ 2) for c in range(4)])  1.22 us
    ppermute x1, waiting for transfers between devices, meet(): got = lax.ppermute(give, 'clus', [(c, c ^ 1) for c in range(4)])  1.17 us
    pallas_call x1, Pallas kernels, meet(): pl.pallas_call(home_kernel, out_shape=jax.ShapeDtypeStruct((1, rows), jnp...  0.83 us
  transfers between devices with their start and end apart: 8, of which 3 were waited for; matrix products, arithmetic and copies ran while one was open for 0% of the time, Pallas kernels for 0%

profile of v3, /device:TPU:0, one launch (start us, length us, event | category | flops | bytes accessed | tf_op | source)
XLA Modules:
  0.0 40.8 jit_solution(9492544761469652576)
XLA Ops:
  0.0 0.0 copy-start.2
  0.0 0.0 copy-start.1
  0.0 0.7 %copy-done.2 = s32[256]{0:T(256)S(1)} copy-done((s32[256]{0:T(256)S(1)}, s32[256]{0:T(256)}, u32[]{:S(2)}) %copy-start.2) | copy-done | bytes 1048
  0.7 0.0 copy-done.1
  0.7 0.0 copy-start
  0.7 1.0 %copy-done = bf16[256,1024]{1,0:T(8,128)(2,1)S(1)} copy-done((bf16[256,1024]{1,0:T(8,128)(2,1)S(1)}, bf16[256,1024]{1,0:T(8,128)(2,1)}, u32[]{:S(2)}) %copy-start) | copy-done | bytes 524312
  1.7 0.6 %sort_rows.1 = (bf16[1040,128]{1,0:T(8,128)(2,1)S(1)}, bf16[1040,128]{1,0:T(8,128)(2,1)S(1)}, s32[1,256]{1,0:T(1,128)S(1)}) custom-call(bf16[256,1024]{1,0:T(8,128)(2,1)S(1)} %copy-done, s32[1,256]{1,0:T(1,128)S(1)} %bitcast.3, s32[1,256]{1,0:T(1,128)S(1)} %bitcast.4), custom_call_target="tpu_custom_call" | custom-call | tf_op jit(solution)/shard_map/sort_rows/pallas_call | solution.py:240
  2.3 0.5 %collective-permute-start = (bf16[1040,128]{1,0:T(8,128)(2,1)S(1)}, bf16[1040,128]{1,0:T(8,128)(2,1)S(1)}, u32[]{:S(2)}, u32[]{:S(2)}) collective-permute-start(bf16[1040,128]{1,0:T(8,128)(2,1)S(1)} %get-tuple-element.11), channel_id=1, source_target_pairs={{0,1},{1,0},{2,3},{3,2},{4,5},{5,4},{6,7},{7,6},{8,9},{9,8},{10,11... | collective-permute-start | bytes 798728 | tf_op jit(solution)/shard_map/ppermute | solution.py:248
  2.8 1.2 %collective-permute-done.got_ref = bf16[1040,128]{1,0:T(8,128)(2,1)S(1)} collective-permute-done((bf16[1040,128]{1,0:T(8,128)(2,1)S(1)}, bf16[1040,128]{1,0:T(8,128)(2,1)S(1)}, u32[]{:S(2)}, u32[]{:S(2)}) %collective-permute-start) | collective-permute-done | bytes 266272 | tf_op jit(solution)/shard_map/ppermute | solution.py:248
  4.0 0.1 join_cores.1
  4.1 2.9 %collective-permute-start.4 = (bf16[1040,128]{1,0:T(8,128)(2,1)S(1)}, bf16[1040,128]{1,0:T(8,128)(2,1)S(1)}, u32[]{:S(2)}, u32[]{:S(2)}) collective-permute-start(bf16[1040,128]{1,0:T(8,128)(2,1)S(1)} %get-tuple-element.13), channel_id=1, source_target_pairs={{0,2},{1,3},{2,0},{3,1},{4,6},{5,7},{6,4},{7,5},{8,10},{9,11},{10,... | collective-permute-start | bytes 798728 | tf_op jit(solution)/shard_map/ppermute | solution.py:257
  7.0 0.7 %collective-permute-start.3 = (bf16[1040,128]{1,0:T(8,128)(2,1)S(1)}, bf16[1040,128]{1,0:T(8,128)(2,1)S(1)}, u32[]{:S(2)}, u32[]{:S(2)}) collective-permute-start(bf16[1040,128]{1,0:T(8,128)(2,1)S(1)} %get-tuple-element.12.refs_0_), channel_id=1, source_target_pairs={{12,4},{1,9},{14,6},{3,11},{28,20},{17,25},{30,22},{19,27}} | collective-permute-start | bytes 798728 | tf_op jit(solution)/shard_map/ppermute | solution.py:238
  7.7 4.1 %collective-permute-start.2 = (bf16[1040,128]{1,0:T(8,128)(2,1)S(1)}, bf16[1040,128]{1,0:T(8,128)(2,1)S(1)}, u32[]{:S(2)}, u32[]{:S(2)}) collective-permute-start(bf16[1040,128]{1,0:T(8,128)(2,1)S(1)} %get-tuple-element.12.refs_0_), channel_id=1, source_target_pairs={{0,4},{13,9},{2,6},{15,11},{16,20},{29,25},{18,22},{31,27}} | collective-permute-start | bytes 798728 | tf_op jit(solution)/shard_map/ppermute | solution.py:238
  11.8 0.7 %collective-permute-start.1 = (bf16[1040,128]{1,0:T(8,128)(2,1)S(1)}, bf16[1040,128]{1,0:T(8,128)(2,1)S(1)}, u32[]{:S(2)}, u32[]{:S(2)}) collective-permute-start(bf16[1040,128]{1,0:T(8,128)(2,1)S(1)} %get-tuple-element.12.refs_0_), channel_id=1, source_target_pairs={{8,4},{5,9},{10,6},{7,11},{24,20},{21,25},{26,22},{23,27}} | collective-permute-start | bytes 798728 | tf_op jit(solution)/shard_map/ppermute | solution.py:238
  12.5 1.2 %collective-permute-done.4.refs_4_ = bf16[1040,128]{1,0:T(8,128)(2,1)S(1)} collective-permute-done((bf16[1040,128]{1,0:T(8,128)(2,1)S(1)}, bf16[1040,128]{1,0:T(8,128)(2,1)S(1)}, u32[]{:S(2)}, u32[]{:S(2)}) %collective-permute-start.4) | collective-permute-done | bytes 266272 | tf_op jit(solution)/shard_map/ppermute | solution.py:257
  13.7 0.7 %collective-permute-start.7 = (bf16[1040,128]{1,0:T(8,128)(2,1)S(1)}, bf16[1040,128]{1,0:T(8,128)(2,1)S(1)}, u32[]{:S(2)}, u32[]{:S(2)}) collective-permute-start(bf16[1040,128]{1,0:T(8,128)(2,1)S(1)} %collective-permute-done.4.refs_4_), channel_id=1, source_target_pairs={{12,4},{1,9},{14,6},{3,11},{28,20},{17,25},{30,22},{19,27}} | collective-permute-start | bytes 798728 | tf_op jit(solution)/shard_map/ppermute | solution.py:238
  14.4 4.4 %collective-permute-start.6 = (bf16[1040,128]{1,0:T(8,128)(2,1)S(1)}, bf16[1040,128]{1,0:T(8,128)(2,1)S(1)}, u32[]{:S(2)}, u32[]{:S(2)}) collective-permute-start(bf16[1040,128]{1,0:T(8,128)(2,1)S(1)} %collective-permute-done.4.refs_4_), channel_id=1, source_target_pairs={{0,4},{13,9},{2,6},{15,11},{16,20},{29,25},{18,22},{31,27}} | collective-permute-start | bytes 798728 | tf_op jit(solution)/shard_map/ppermute | solution.py:238
  18.7 0.0 collective-permute-done.3.refs_3_
  18.7 0.7 %collective-permute-start.5 = (bf16[1040,128]{1,0:T(8,128)(2,1)S(1)}, bf16[1040,128]{1,0:T(8,128)(2,1)S(1)}, u32[]{:S(2)}, u32[]{:S(2)}) collective-permute-start(bf16[1040,128]{1,0:T(8,128)(2,1)S(1)} %collective-permute-done.4.refs_4_), channel_id=1, source_target_pairs={{8,4},{5,9},{10,6},{7,11},{24,20},{21,25},{26,22},{23,27}} | collective-permute-start | bytes 798728 | tf_op jit(solution)/shard_map/ppermute | solution.py:238
  19.4 0.0 collective-permute-done.2.refs_2_
  19.4 0.0 collective-permute-done.1.refs_1_
  19.4 0.0 collective-permute-done.7.refs_7_
  19.5 4.1 %collective-permute-done.6.refs_6_ = bf16[1040,128]{1,0:T(8,128)(2,1)S(1)} collective-permute-done((bf16[1040,128]{1,0:T(8,128)(2,1)S(1)}, bf16[1040,128]{1,0:T(8,128)(2,1)S(1)}, u32[]{:S(2)}, u32[]{:S(2)}) %collective-permute-start.6) | collective-permute-done | bytes 266272 | tf_op jit(solution)/shard_map/ppermute | solution.py:238
  23.5 0.0 collective-permute-done.5.refs_5_
  23.5 16.4 %all_to_all.5.got_ref = f32[16,1,128]{2,1,0:T(1,128)S(1)} all-to-all(f32[16,1,128]{2,1,0:T(1,128)S(1)} %meet_scores.1), channel_id=1, replica_groups=mesh['groups'=2,'blk'=4,'clus'=4] {'blk','clus'}, dimensions={0} | all-to-all | bytes 16384 | tf_op jit(solution)/shard_map/all_to_all | solution.py:270
  40.0 0.8 %home_scores.1 = f32[1,256]{1,0:T(1,128)} custom-call(f32[16,1,128]{2,1,0:T(1,128)S(1)} %all_to_all.5.got_ref, s32[1,256]{1,0:T(1,128)S(1)} %get-tuple-element.14.target_ref), custom_call_target="tpu_custom_call" | custom-call | tf_op jit(solution)/shard_map/home_scores/pallas_call | solution.py:271
  (1 shorter events, 0.0 us)
Async XLA Ops:
  0.0 0.7 %copy-start.2 = (s32[256]{0:T(256)S(1)}, s32[256]{0:T(256)}, u32[]{:S(2)}) copy-start(s32[256]{0:T(256)} %param.5) | copy-start | bytes 3076
  0.0 0.7 %copy-start.1 = (s32[256]{0:T(256)S(1)}, s32[256]{0:T(256)}, u32[]{:S(2)}) copy-start(s32[256]{0:T(256)} %param.4) | copy-start | bytes 3076
  0.7 1.0 %copy-start = (bf16[256,1024]{1,0:T(8,128)(2,1)S(1)}, bf16[256,1024]{1,0:T(8,128)(2,1)}, u32[]{:S(2)}) copy-start(bf16[256,1024]{1,0:T(8,128)(2,1)} %emb_ref.1) | copy-start | bytes 1572868
  2.3 1.7 %collective-permute-start = (bf16[1040,128]{1,0:T(8,128)(2,1)S(1)}, bf16[1040,128]{1,0:T(8,128)(2,1)S(1)}, u32[]{:S(2)}, u32[]{:S(2)}) collective-permute-start(bf16[1040,128]{1,0:T(8,128)(2,1)S(1)} %get-tuple-element.11), channel_id=1, source_target_pairs={{0,1},{1,0},{2,3},{3,2},{4,5},{5,4},{6,7},{7,6},{8,9},{9,8},{10,11... | collective-permute-start | bytes 798728 | tf_op jit(solution)/shard_map/ppermute | solution.py:248
  4.1 9.6 %collective-permute-start.4 = (bf16[1040,128]{1,0:T(8,128)(2,1)S(1)}, bf16[1040,128]{1,0:T(8,128)(2,1)S(1)}, u32[]{:S(2)}, u32[]{:S(2)}) collective-permute-start(bf16[1040,128]{1,0:T(8,128)(2,1)S(1)} %get-tuple-element.13), channel_id=1, source_target_pairs={{0,2},{1,3},{2,0},{3,1},{4,6},{5,7},{6,4},{7,5},{8,10},{9,11},{10,... | collective-permute-start | bytes 798728 | tf_op jit(solution)/shard_map/ppermute | solution.py:257
  7.0 11.7 %collective-permute-start.3 = (bf16[1040,128]{1,0:T(8,128)(2,1)S(1)}, bf16[1040,128]{1,0:T(8,128)(2,1)S(1)}, u32[]{:S(2)}, u32[]{:S(2)}) collective-permute-start(bf16[1040,128]{1,0:T(8,128)(2,1)S(1)} %get-tuple-element.12.refs_0_), channel_id=1, source_target_pairs={{12,4},{1,9},{14,6},{3,11},{28,20},{17,25},{30,22},{19,27}} | collective-permute-start | bytes 798728 | tf_op jit(solution)/shard_map/ppermute | solution.py:238
  7.7 11.8 %collective-permute-start.2 = (bf16[1040,128]{1,0:T(8,128)(2,1)S(1)}, bf16[1040,128]{1,0:T(8,128)(2,1)S(1)}, u32[]{:S(2)}, u32[]{:S(2)}) collective-permute-start(bf16[1040,128]{1,0:T(8,128)(2,1)S(1)} %get-tuple-element.12.refs_0_), channel_id=1, source_target_pairs={{0,4},{13,9},{2,6},{15,11},{16,20},{29,25},{18,22},{31,27}} | collective-permute-start | bytes 798728 | tf_op jit(solution)/shard_map/ppermute | solution.py:238
  11.8 7.7 %collective-permute-start.1 = (bf16[1040,128]{1,0:T(8,128)(2,1)S(1)}, bf16[1040,128]{1,0:T(8,128)(2,1)S(1)}, u32[]{:S(2)}, u32[]{:S(2)}) collective-permute-start(bf16[1040,128]{1,0:T(8,128)(2,1)S(1)} %get-tuple-element.12.refs_0_), channel_id=1, source_target_pairs={{8,4},{5,9},{10,6},{7,11},{24,20},{21,25},{26,22},{23,27}} | collective-permute-start | bytes 798728 | tf_op jit(solution)/shard_map/ppermute | solution.py:238
  13.7 5.8 %collective-permute-start.7 = (bf16[1040,128]{1,0:T(8,128)(2,1)S(1)}, bf16[1040,128]{1,0:T(8,128)(2,1)S(1)}, u32[]{:S(2)}, u32[]{:S(2)}) collective-permute-start(bf16[1040,128]{1,0:T(8,128)(2,1)S(1)} %collective-permute-done.4.refs_4_), channel_id=1, source_target_pairs={{12,4},{1,9},{14,6},{3,11},{28,20},{17,25},{30,22},{19,27}} | collective-permute-start | bytes 798728 | tf_op jit(solution)/shard_map/ppermute | solution.py:238
  14.4 9.2 %collective-permute-start.6 = (bf16[1040,128]{1,0:T(8,128)(2,1)S(1)}, bf16[1040,128]{1,0:T(8,128)(2,1)S(1)}, u32[]{:S(2)}, u32[]{:S(2)}) collective-permute-start(bf16[1040,128]{1,0:T(8,128)(2,1)S(1)} %collective-permute-done.4.refs_4_), channel_id=1, source_target_pairs={{0,4},{13,9},{2,6},{15,11},{16,20},{29,25},{18,22},{31,27}} | collective-permute-start | bytes 798728 | tf_op jit(solution)/shard_map/ppermute | solution.py:238
  18.7 4.8 %collective-permute-start.5 = (bf16[1040,128]{1,0:T(8,128)(2,1)S(1)}, bf16[1040,128]{1,0:T(8,128)(2,1)S(1)}, u32[]{:S(2)}, u32[]{:S(2)}) collective-permute-start(bf16[1040,128]{1,0:T(8,128)(2,1)S(1)} %collective-permute-done.4.refs_4_), channel_id=1, source_target_pairs={{8,4},{5,9},{10,6},{7,11},{24,20},{21,25},{26,22},{23,27}} | collective-permute-start | bytes 798728 | tf_op jit(solution)/shard_map/ppermute | solution.py:238

commit v4 on v3

--- a/solution.py
+++ b/solution.py
@@ -72,7 +72,12 @@
     return 1 + core
 
 
-FAR_BLKS = (2, 0, 3)
+NEAR = (0, (((1, 0), (0, 0)), ((2, 1), (3, 1))))
+ACROSS = (2, (((1, 0), (1, 1)), ((2, 1), (2, 0))))
+FAR = (3, (((1, 0), (0, 1)), ((2, 1), (3, 0))))
+BLOCKS = (
+    (0, None), (0, FAR), (0, ACROSS), (0, NEAR), (1, None), (1, FAR), (1, ACROSS), (1, NEAR),
+)
 
 
 def blk_of(far_blk, core):
@@ -153,56 +158,61 @@
         out_ref[tail:, :] = jnp.concatenate([first, second], axis=1).astype(jnp.bfloat16)
 
 
-def meet_kernel(*refs):
-    count = 8
-    block_refs, best_ref = refs[:count], refs[-1]
+def take_in(refs, best, first, last):
+    tail = refs[0].shape[0] - 16
+    slabs = tail // SLABS_ROWS
+    ids_of = []
+    for r in refs[:last]:
+        parts = r[tail:, :].astype(jnp.float32)
+        ids_of.append(parts[0:1] * 256.0 + parts[1:2])
+    best = list(best)
+    for new in range(first, last):
+        rows = get_slabs(refs[new], 0, SLABS_ROWS, slabs)
+        down = jnp.broadcast_to(ids_of[new], (SLABS_ROWS, 128)).T
+        own = jnp.full((SLABS_ROWS, 128), -1.0, jnp.float32)
+        for start in range(0, new + 1, 2):
+            group = range(start, min(start + 2, new + 1))
+            others = jnp.concatenate(
+                [get_slabs(refs[q], 0, SLABS_ROWS, slabs) for q in group], axis=0
+            )
+            scores = lax.dot_general(
+                rows, others, (((1,), (1,)), ((), ())), preferred_element_type=jnp.float32
+            )
+            for n, q in enumerate(group):
+                part = scores[:, n * 128 : (n + 1) * 128]
+                own = jnp.maximum(own, jnp.where(ids_of[q] < down, part, -1.0))
+                if q != new:
+                    theirs = jnp.where(down < ids_of[q], part, -1.0)
+                    best[q] = jnp.maximum(best[q], jnp.max(theirs, axis=0, keepdims=True))
+        best.append(jnp.max(own.T, axis=0, keepdims=True))
+    return best
+
+
+def meet_kernel(first, last, *refs):
+    block_refs, best_ref = refs[:last], refs[-1]
+    u, b = here()
+
+    @pl.when(b == middle_of(lax.rem(u, 2)))
+    def _():
+        known = [refs[last][q : q + 1, :] for q in range(first)]
+        for q, row in enumerate(take_in(block_refs, known, first, last)):
+            best_ref[q : q + 1, :] = row
+
+
+def last_meet_kernel(first, last, *refs):
+    block_refs, best_ref = refs[:last], refs[-1]
     u, b = here()
     core = lax.rem(u, 2)
-    tail = block_refs[0].shape[0] - 16
-    slabs = tail // SLABS_ROWS
-    tile = 256
-    per = tile // SLABS_ROWS
-    tiles = count // per
 
     @pl.when(b == middle_of(core))
     def _():
-        def rows_of(t):
-            return jnp.concatenate(
-                [get_slabs(r, 0, SLABS_ROWS, slabs) for r in block_refs[t * per : (t + 1) * per]],
-                axis=0,
-            )
-
-        ids_of = []
-        for r in block_refs:
-            parts = r[tail:, :].astype(jnp.float32)
-            ids_of.append(parts[0:1] * 256.0 + parts[1:2])
-        down = [jnp.broadcast_to(i, (SLABS_ROWS, 128)).T for i in ids_of]
-        for query in range(tiles):
-            query_rows = rows_of(query)
-            query_ids = jnp.concatenate(ids_of[query * per : (query + 1) * per], axis=1)
-            best = jnp.full((1, tile), -1.0, jnp.float32)
-            for key in range(tiles):
-                scores = lax.dot_general(
-                    rows_of(key),
-                    query_rows,
-                    (((1,), (1,)), ((), ())),
-                    preferred_element_type=jnp.float32,
-                )
-                key_ids = jnp.concatenate(down[key * per : (key + 1) * per], axis=0)
-                key_ids = jnp.concatenate([key_ids] * (tile // 128), axis=1)
-                best = jnp.maximum(
-                    best,
-                    jnp.max(jnp.where(key_ids < query_ids, scores, -1.0), axis=0, keepdims=True),
-                )
-            for part in range(per):
-                q = query * per + part
-                other, place = divmod(q, 4)
-                far_blk = FAR_BLKS[place - 1]
-                at_blk = jnp.where(core == 0, far_blk, 3 - far_blk) if place else b
-                chip = (u >> 1) ^ other
-                row = best[:, part * 128 : (part + 1) * 128]
-                for c in range(2):
-                    best_ref[at_blk * 4 + chip * 2 + c] = row
+        known = [refs[last][q : q + 1, :] for q in range(first)]
+        for q, row in enumerate(take_in(block_refs, known, first, last)):
+            other, place = BLOCKS[q]
+            at_blk = b if place is None else jnp.where(core == 0, place[0], 3 - place[0])
+            chip = (u >> 1) ^ other
+            for c in range(2):
+                best_ref[at_blk * 4 + chip * 2 + c] = row
 
 
 def home_kernel(got_ref, target_ref, out_ref):
@@ -233,8 +243,17 @@
     everyone = ("blk", "clus")
     payload = jax.ShapeDtypeStruct((width // 128 * SLABS_ROWS + 16, 128), jnp.bfloat16)
 
-    def to_meeting(value, far_blk):
-        pairs = [(blk_of(far_blk, c % 2) * 4 + c, middle_of(c % 2) * 4 + c) for c in range(4)]
+    def to_meeting(value, place):
+        far_blk, others = place
+        moves = [((blk_of(far_blk, core), core), (middle_of(core), core)) for core in range(2)]
+        moves += others
+        sent = {source for source, _ in moves}
+        moves += [((b, core),) * 2 for b in range(4) for core in range(2) if (b, core) not in sent]
+        pairs = [
+            (sb * 4 + chip * 2 + sc, tb * 4 + chip * 2 + tc)
+            for (sb, sc), (tb, tc) in moves
+            for chip in range(2)
+        ]
         return lax.ppermute(value, everyone, pairs)
 
     keep, give, target = pl.pallas_call(
@@ -255,18 +274,24 @@
         name="join_cores",
     )(keep, got)
     crossed = lax.ppermute(far, "clus", [(c, c ^ 2) for c in range(4)])
-    arrived = []
-    for value in (near, crossed):
-        arrived.append(value)
-        arrived += [to_meeting(value, far_blk) for far_blk in FAR_BLKS]
-    best = pl.pallas_call(
-        meet_kernel,
-        out_shape=jax.ShapeDtypeStruct((16, 1, 128), jnp.float32),
-        in_specs=[VMEM] * 8,
-        out_specs=VMEM,
-        compiler_params=SMALL,
-        name="meet_scores",
-    )(*arrived)
+    arrived = [crossed if other else near for other, _ in BLOCKS]
+    for q in (3, 2, 1, 7, 6, 5):
+        arrived[q] = to_meeting(arrived[q], BLOCKS[q][1])
+
+    def meeting(kernel, first, last, known, shape):
+        return pl.pallas_call(
+            functools.partial(kernel, first, last),
+            out_shape=jax.ShapeDtypeStruct(shape, jnp.float32),
+            in_specs=[VMEM] * (last + len(known)),
+            out_specs=VMEM,
+            compiler_params=SMALL,
+            name=f"meet_{first}_{last}",
+        )(*arrived[:last], *known)
+
+    best = meeting(meet_kernel, 0, 5, [], (8, 128))
+    best = meeting(meet_kernel, 5, 6, [best], (8, 128))
+    best = meeting(meet_kernel, 6, 7, [best], (8, 128))
+    best = meeting(last_meet_kernel, 7, 8, [best], (16, 1, 128))
     returned = lax.all_to_all(best, everyone, split_axis=0, concat_axis=0, tiled=True)
     out = pl.pallas_call(
         home_kernel,

time: 41.1 us -> 39.7 us (0.966)
  blocking collectives: 16.4 us -> 10.5 us
  starting transfers between devices: 14.6 us -> 17.9 us
  waiting for transfers between devices: 6.47 us -> 7.52 us
    all_to_all x1, blocking collectives: 16.4 us -> 10.5 us  [meet(): lax.all_to_all(best, everyone, split_axis=0, concat_axis=0, tiled=True)]
    ppermute x6, starting transfers between devices: 11.2 us -> 14.5 us  [to_meeting(): return lax.ppermute(value, everyone, pairs)]
    ppermute x1, waiting for transfers between devices: 1.22 us -> 1.84 us  [meet(): crossed = lax.ppermute(far, 'clus', [(c, c ^ 2) for c in range(4)])]
    ppermute x6, waiting for transfers between devices: 4.09 us -> 4.51 us  [to_meeting(): return lax.ppermute(value, everyone, pairs)]
  transfers between devices with their start and end apart: 8 -> 8, of which waited for: 3 -> 4; matrix products, arithmetic and copies ran while one was open for 0% -> 0% of each run, Pallas kernels for 0% -> 0%
where the time goes in v4:
time: 39.7 us; the launch traced here: 39.3 us
  starting transfers between devices  17.9 us (45%)
  blocking collectives  10.5 us (26%)
  waiting for transfers between devices  7.52 us (19%)
  local copies, waits for them, and re-layouts  1.73 us (4%)
  Pallas kernels  1.54 us (4%)
    ppermute x6, starting transfers between devices, to_meeting(): return lax.ppermute(value, everyone, pairs)  14.5 us
    all_to_all x1, blocking collectives, meet(): lax.all_to_all(best, everyone, split_axis=0, concat_axis=0, tiled=True)  10.5 us
    ppermute x6, waiting for transfers between devices, to_meeting(): return lax.ppermute(value, everyone, pairs)  4.51 us
    ppermute x1, starting transfers between devices, meet(): crossed = lax.ppermute(far, 'clus', [(c, c ^ 2) for c in range(4)])  2.9 us
    ppermute x1, waiting for transfers between devices, meet(): crossed = lax.ppermute(far, 'clus', [(c, c ^ 2) for c in range(4)])  1.84 us
    unnamed x6, local copies, waits for them, and re-layouts  1.73 us
    ppermute x1, waiting for transfers between devices, meet(): got = lax.ppermute(give, 'clus', [(c, c ^ 1) for c in range(4)])  1.17 us
    pallas_call x1, Pallas kernels, meet(): pl.pallas_call(home_kernel, out_shape=jax.ShapeDtypeStruct((1, rows), jnp...  0.83 us
  transfers between devices with their start and end apart: 8, of which 4 were waited for; matrix products, arithmetic and copies ran while one was open for 0% of the time, Pallas kernels for 0%

profile of v4, /device:TPU:0, one launch (start us, length us, event | category | flops | bytes accessed | tf_op | source)
XLA Modules:
  0.0 39.3 jit_solution(3548017628964255055)
XLA Ops:
  0.0 0.0 copy-start.2
  0.0 0.0 copy-start.1
  0.0 0.7 %copy-done.2 = s32[256]{0:T(256)S(1)} copy-done((s32[256]{0:T(256)S(1)}, s32[256]{0:T(256)}, u32[]{:S(2)}) %copy-start.2) | copy-done | bytes 1048
  0.7 0.0 copy-done.1
  0.7 0.0 copy-start
  0.7 1.0 %copy-done = bf16[256,1024]{1,0:T(8,128)(2,1)S(1)} copy-done((bf16[256,1024]{1,0:T(8,128)(2,1)S(1)}, bf16[256,1024]{1,0:T(8,128)(2,1)}, u32[]{:S(2)}) %copy-start) | copy-done | bytes 524312
  1.7 0.6 %sort_rows.1 = (bf16[1040,128]{1,0:T(8,128)(2,1)S(1)}, bf16[1040,128]{1,0:T(8,128)(2,1)S(1)}, s32[1,256]{1,0:T(1,128)S(1)}) custom-call(bf16[256,1024]{1,0:T(8,128)(2,1)S(1)} %copy-done, s32[1,256]{1,0:T(1,128)S(1)} %bitcast.3, s32[1,256]{1,0:T(1,128)S(1)} %bitcast.4), custom_call_target="tpu_custom_call" | custom-call | tf_op jit(solution)/shard_map/sort_rows/pallas_call | solution.py:259
  2.3 0.5 %collective-permute-start = (bf16[1040,128]{1,0:T(8,128)(2,1)S(1)}, bf16[1040,128]{1,0:T(8,128)(2,1)S(1)}, u32[]{:S(2)}, u32[]{:S(2)}) collective-permute-start(bf16[1040,128]{1,0:T(8,128)(2,1)S(1)} %get-tuple-element.11), channel_id=1, source_target_pairs={{0,1},{1,0},{2,3},{3,2},{4,5},{5,4},{6,7},{7,6},{8,9},{9,8},{10,11... | collective-permute-start | bytes 798728 | tf_op jit(solution)/shard_map/ppermute | solution.py:267
  2.8 1.2 %collective-permute-done.got_ref = bf16[1040,128]{1,0:T(8,128)(2,1)S(1)} collective-permute-done((bf16[1040,128]{1,0:T(8,128)(2,1)S(1)}, bf16[1040,128]{1,0:T(8,128)(2,1)S(1)}, u32[]{:S(2)}, u32[]{:S(2)}) %collective-permute-start) | collective-permute-done | bytes 266272 | tf_op jit(solution)/shard_map/ppermute | solution.py:267
  4.0 0.1 join_cores.1
  4.1 2.9 %collective-permute-start.4 = (bf16[1040,128]{1,0:T(8,128)(2,1)S(1)}, bf16[1040,128]{1,0:T(8,128)(2,1)S(1)}, u32[]{:S(2)}, u32[]{:S(2)}) collective-permute-start(bf16[1040,128]{1,0:T(8,128)(2,1)S(1)} %get-tuple-element.13), channel_id=1, source_target_pairs={{0,2},{1,3},{2,0},{3,1},{4,6},{5,7},{6,4},{7,5},{8,10},{9,11},{10,... | collective-permute-start | bytes 798728 | tf_op jit(solution)/shard_map/ppermute | solution.py:276
  7.0 3.5 %collective-permute-start.3 = (bf16[1040,128]{1,0:T(8,128)(2,1)S(1)}, bf16[1040,128]{1,0:T(8,128)(2,1)S(1)}, u32[]{:S(2)}, u32[]{:S(2)}) collective-permute-start(bf16[1040,128]{1,0:T(8,128)(2,1)S(1)} %get-tuple-element.12.refs_0_), channel_id=1, source_target_pairs={{0,4},{2,6},{13,9},{15,11},{4,0},{6,2},{9,13},{11,15},{1,1},{3,3},... | collective-permute-start | bytes 798728 | tf_op jit(solution)/shard_map/ppermute | solution.py:257
  10.5 0.7 %collective-permute-start.2 = (bf16[1040,128]{1,0:T(8,128)(2,1)S(1)}, bf16[1040,128]{1,0:T(8,128)(2,1)S(1)}, u32[]{:S(2)}, u32[]{:S(2)}) collective-permute-start(bf16[1040,128]{1,0:T(8,128)(2,1)S(1)} %get-tuple-element.12.refs_0_), channel_id=1, source_target_pairs={{8,4},{10,6},{5,9},{7,11},{4,5},{6,7},{9,8},{11,10},{0,0},{2,2},{1... | collective-permute-start | bytes 798728 | tf_op jit(solution)/shard_map/ppermute | solution.py:257
  11.2 0.7 %collective-permute-start.1 = (bf16[1040,128]{1,0:T(8,128)(2,1)S(1)}, bf16[1040,128]{1,0:T(8,128)(2,1)S(1)}, u32[]{:S(2)}, u32[]{:S(2)}) collective-permute-start(bf16[1040,128]{1,0:T(8,128)(2,1)S(1)} %get-tuple-element.12.refs_0_), channel_id=1, source_target_pairs={{12,4},{14,6},{1,9},{3,11},{4,1},{6,3},{9,12},{11,14},{0,0},{2,2},... | collective-permute-start | bytes 798728 | tf_op jit(solution)/shard_map/ppermute | solution.py:257
  11.8 1.8 %collective-permute-done.4.refs_4_ = bf16[1040,128]{1,0:T(8,128)(2,1)S(1)} collective-permute-done((bf16[1040,128]{1,0:T(8,128)(2,1)S(1)}, bf16[1040,128]{1,0:T(8,128)(2,1)S(1)}, u32[]{:S(2)}, u32[]{:S(2)}) %collective-permute-start.4) | collective-permute-done | bytes 266272 | tf_op jit(solution)/shard_map/ppermute | solution.py:276
  13.7 0.7 %collective-permute-start.5 = (bf16[1040,128]{1,0:T(8,128)(2,1)S(1)}, bf16[1040,128]{1,0:T(8,128)(2,1)S(1)}, u32[]{:S(2)}, u32[]{:S(2)}) collective-permute-start(bf16[1040,128]{1,0:T(8,128)(2,1)S(1)} %collective-permute-done.4.refs_4_), channel_id=1, source_target_pairs={{12,4},{14,6},{1,9},{3,11},{4,1},{6,3},{9,12},{11,14},{0,0},{2,2},... | collective-permute-start | bytes 798728 | tf_op jit(solution)/shard_map/ppermute | solution.py:257
  14.4 0.7 %collective-permute-start.6 = (bf16[1040,128]{1,0:T(8,128)(2,1)S(1)}, bf16[1040,128]{1,0:T(8,128)(2,1)S(1)}, u32[]{:S(2)}, u32[]{:S(2)}) collective-permute-start(bf16[1040,128]{1,0:T(8,128)(2,1)S(1)} %collective-permute-done.4.refs_4_), channel_id=1, source_target_pairs={{8,4},{10,6},{5,9},{7,11},{4,5},{6,7},{9,8},{11,10},{0,0},{2,2},{1... | collective-permute-start | bytes 798728 | tf_op jit(solution)/shard_map/ppermute | solution.py:257
  15.0 0.2 collective-permute-done.3.refs_3_
  15.3 8.3 %collective-permute-start.7 = (bf16[1040,128]{1,0:T(8,128)(2,1)S(1)}, bf16[1040,128]{1,0:T(8,128)(2,1)S(1)}, u32[]{:S(2)}, u32[]{:S(2)}) collective-permute-start(bf16[1040,128]{1,0:T(8,128)(2,1)S(1)} %collective-permute-done.4.refs_4_), channel_id=1, source_target_pairs={{0,4},{2,6},{13,9},{15,11},{4,0},{6,2},{9,13},{11,15},{1,1},{3,3},... | collective-permute-start | bytes 798728 | tf_op jit(solution)/shard_map/ppermute | solution.py:257
  23.6 0.0 collective-permute-done.2.refs_2_
  23.6 0.0 collective-permute-done.1.refs_1_
  23.7 0.0 collective-permute-done.5.refs_5_
  23.7 0.0 collective-permute-done.6.refs_6_
  23.7 4.3 %collective-permute-done.7.refs_7_ = bf16[1040,128]{1,0:T(8,128)(2,1)S(1)} collective-permute-done((bf16[1040,128]{1,0:T(8,128)(2,1)S(1)}, bf16[1040,128]{1,0:T(8,128)(2,1)S(1)}, u32[]{:S(2)}, u32[]{:S(2)}) %collective-permute-start.7) | collective-permute-done | bytes 266272 | tf_op jit(solution)/shard_map/ppermute | solution.py:257
  28.0 10.5 %all_to_all.5.got_ref = f32[16,1,128]{2,1,0:T(1,128)S(1)} all-to-all(f32[16,1,128]{2,1,0:T(1,128)S(1)} %meet_7_8.1), channel_id=1, replica_groups=mesh['groups'=2,'blk'=4,'clus'=4] {'blk','clus'}, dimensions={0} | all-to-all | bytes 16384 | tf_op jit(solution)/shard_map/all_to_all | solution.py:295
  38.5 0.8 %home_scores.1 = f32[1,256]{1,0:T(1,128)} custom-call(f32[16,1,128]{2,1,0:T(1,128)S(1)} %all_to_all.5.got_ref, s32[1,256]{1,0:T(1,128)S(1)} %get-tuple-element.14.target_ref), custom_call_target="tpu_custom_call" | custom-call | tf_op jit(solution)/shard_map/home_scores/pallas_call | solution.py:296
  (4 shorter events, 0.1 us)
Async XLA Ops:
  0.0 0.7 %copy-start.2 = (s32[256]{0:T(256)S(1)}, s32[256]{0:T(256)}, u32[]{:S(2)}) copy-start(s32[256]{0:T(256)} %param.5) | copy-start | bytes 3076
  0.0 0.7 %copy-start.1 = (s32[256]{0:T(256)S(1)}, s32[256]{0:T(256)}, u32[]{:S(2)}) copy-start(s32[256]{0:T(256)} %param.4) | copy-start | bytes 3076
  0.7 1.0 %copy-start = (bf16[256,1024]{1,0:T(8,128)(2,1)S(1)}, bf16[256,1024]{1,0:T(8,128)(2,1)}, u32[]{:S(2)}) copy-start(bf16[256,1024]{1,0:T(8,128)(2,1)} %emb_ref.1) | copy-start | bytes 1572868
  2.3 1.7 %collective-permute-start = (bf16[1040,128]{1,0:T(8,128)(2,1)S(1)}, bf16[1040,128]{1,0:T(8,128)(2,1)S(1)}, u32[]{:S(2)}, u32[]{:S(2)}) collective-permute-start(bf16[1040,128]{1,0:T(8,128)(2,1)S(1)} %get-tuple-element.11), channel_id=1, source_target_pairs={{0,1},{1,0},{2,3},{3,2},{4,5},{5,4},{6,7},{7,6},{8,9},{9,8},{10,11... | collective-permute-start | bytes 798728 | tf_op jit(solution)/shard_map/ppermute | solution.py:267
  4.1 9.6 %collective-permute-start.4 = (bf16[1040,128]{1,0:T(8,128)(2,1)S(1)}, bf16[1040,128]{1,0:T(8,128)(2,1)S(1)}, u32[]{:S(2)}, u32[]{:S(2)}) collective-permute-start(bf16[1040,128]{1,0:T(8,128)(2,1)S(1)} %get-tuple-element.13), channel_id=1, source_target_pairs={{0,2},{1,3},{2,0},{3,1},{4,6},{5,7},{6,4},{7,5},{8,10},{9,11},{10,... | collective-permute-start | bytes 798728 | tf_op jit(solution)/shard_map/ppermute | solution.py:276
  7.0 8.3 %collective-permute-start.3 = (bf16[1040,128]{1,0:T(8,128)(2,1)S(1)}, bf16[1040,128]{1,0:T(8,128)(2,1)S(1)}, u32[]{:S(2)}, u32[]{:S(2)}) collective-permute-start(bf16[1040,128]{1,0:T(8,128)(2,1)S(1)} %get-tuple-element.12.refs_0_), channel_id=1, source_target_pairs={{0,4},{2,6},{13,9},{15,11},{4,0},{6,2},{9,13},{11,15},{1,1},{3,3},... | collective-permute-start | bytes 798728 | tf_op jit(solution)/shard_map/ppermute | solution.py:257
  10.5 13.1 %collective-permute-start.2 = (bf16[1040,128]{1,0:T(8,128)(2,1)S(1)}, bf16[1040,128]{1,0:T(8,128)(2,1)S(1)}, u32[]{:S(2)}, u32[]{:S(2)}) collective-permute-start(bf16[1040,128]{1,0:T(8,128)(2,1)S(1)} %get-tuple-element.12.refs_0_), channel_id=1, source_target_pairs={{8,4},{10,6},{5,9},{7,11},{4,5},{6,7},{9,8},{11,10},{0,0},{2,2},{1... | collective-permute-start | bytes 798728 | tf_op jit(solution)/shard_map/ppermute | solution.py:257
  11.2 12.5 %collective-permute-start.1 = (bf16[1040,128]{1,0:T(8,128)(2,1)S(1)}, bf16[1040,128]{1,0:T(8,128)(2,1)S(1)}, u32[]{:S(2)}, u32[]{:S(2)}) collective-permute-start(bf16[1040,128]{1,0:T(8,128)(2,1)S(1)} %get-tuple-element.12.refs_0_), channel_id=1, source_target_pairs={{12,4},{14,6},{1,9},{3,11},{4,1},{6,3},{9,12},{11,14},{0,0},{2,2},... | collective-permute-start | bytes 798728 | tf_op jit(solution)/shard_map/ppermute | solution.py:257
  13.7 10.0 %collective-permute-start.5 = (bf16[1040,128]{1,0:T(8,128)(2,1)S(1)}, bf16[1040,128]{1,0:T(8,128)(2,1)S(1)}, u32[]{:S(2)}, u32[]{:S(2)}) collective-permute-start(bf16[1040,128]{1,0:T(8,128)(2,1)S(1)} %collective-permute-done.4.refs_4_), channel_id=1, source_target_pairs={{12,4},{14,6},{1,9},{3,11},{4,1},{6,3},{9,12},{11,14},{0,0},{2,2},... | collective-permute-start | bytes 798728 | tf_op jit(solution)/shard_map/ppermute | solution.py:257
  14.4 9.3 %collective-permute-start.6 = (bf16[1040,128]{1,0:T(8,128)(2,1)S(1)}, bf16[1040,128]{1,0:T(8,128)(2,1)S(1)}, u32[]{:S(2)}, u32[]{:S(2)}) collective-permute-start(bf16[1040,128]{1,0:T(8,128)(2,1)S(1)} %collective-permute-done.4.refs_4_), channel_id=1, source_target_pairs={{8,4},{10,6},{5,9},{7,11},{4,5},{6,7},{9,8},{11,10},{0,0},{2,2},{1... | collective-permute-start | bytes 798728 | tf_op jit(solution)/shard_map/ppermute | solution.py:257
  15.3 12.7 %collective-permute-start.7 = (bf16[1040,128]{1,0:T(8,128)(2,1)S(1)}, bf16[1040,128]{1,0:T(8,128)(2,1)S(1)}, u32[]{:S(2)}, u32[]{:S(2)}) collective-permute-start(bf16[1040,128]{1,0:T(8,128)(2,1)S(1)} %collective-permute-done.4.refs_4_), channel_id=1, source_target_pairs={{0,4},{2,6},{13,9},{15,11},{4,0},{6,2},{9,13},{11,15},{1,1},{3,3},... | collective-permute-start | bytes 798728 | tf_op jit(solution)/shard_map/ppermute | solution.py:257

commit v5 on v4

--- a/solution.py
+++ b/solution.py
@@ -72,11 +72,9 @@
     return 1 + core
 
 
-NEAR = (0, (((1, 0), (0, 0)), ((2, 1), (3, 1))))
-ACROSS = (2, (((1, 0), (1, 1)), ((2, 1), (2, 0))))
-FAR = (3, (((1, 0), (0, 1)), ((2, 1), (3, 0))))
+NEAR, ACROSS, FAR = 0, 2, 3
 BLOCKS = (
-    (0, None), (0, FAR), (0, ACROSS), (0, NEAR), (1, None), (1, FAR), (1, ACROSS), (1, NEAR),
+    (0, None), (1, None), (0, FAR), (0, ACROSS), (1, FAR), (0, NEAR), (1, ACROSS), (1, NEAR),
 )
 
 
@@ -209,7 +207,7 @@
         known = [refs[last][q : q + 1, :] for q in range(first)]
         for q, row in enumerate(take_in(block_refs, known, first, last)):
             other, place = BLOCKS[q]
-            at_blk = b if place is None else jnp.where(core == 0, place[0], 3 - place[0])
+            at_blk = b if place is None else jnp.where(core == 0, place, 3 - place)
             chip = (u >> 1) ^ other
             for c in range(2):
                 best_ref[at_blk * 4 + chip * 2 + c] = row
@@ -243,16 +241,9 @@
     everyone = ("blk", "clus")
     payload = jax.ShapeDtypeStruct((width // 128 * SLABS_ROWS + 16, 128), jnp.bfloat16)
 
-    def to_meeting(value, place):
-        far_blk, others = place
-        moves = [((blk_of(far_blk, core), core), (middle_of(core), core)) for core in range(2)]
-        moves += others
-        sent = {source for source, _ in moves}
-        moves += [((b, core),) * 2 for b in range(4) for core in range(2) if (b, core) not in sent]
+    def to_meeting(value, place, cross=0):
         pairs = [
-            (sb * 4 + chip * 2 + sc, tb * 4 + chip * 2 + tc)
-            for (sb, sc), (tb, tc) in moves
-            for chip in range(2)
+            (blk_of(place, c % 2) * 4 + (c ^ 2 * cross), middle_of(c % 2) * 4 + c) for c in range(4)
         ]
         return lax.ppermute(value, everyone, pairs)
 
@@ -274,9 +265,13 @@
         name="join_cores",
     )(keep, got)
     crossed = lax.ppermute(far, "clus", [(c, c ^ 2) for c in range(4)])
-    arrived = [crossed if other else near for other, _ in BLOCKS]
-    for q in (3, 2, 1, 7, 6, 5):
-        arrived[q] = to_meeting(arrived[q], BLOCKS[q][1])
+    arrived = []
+    for other, place in BLOCKS:
+        if other and place == FAR:
+            arrived.append(to_meeting(far, place, cross=1))
+        else:
+            value = crossed if other else near
+            arrived.append(value if place is None else to_meeting(value, place))
 
     def meeting(kernel, first, last, known, shape):
         return pl.pallas_call(
@@ -288,8 +283,7 @@
             name=f"meet_{first}_{last}",
         )(*arrived[:last], *known)
 
-    best = meeting(meet_kernel, 0, 5, [], (8, 128))
-    best = meeting(meet_kernel, 5, 6, [best], (8, 128))
+    best = meeting(meet_kernel, 0, 6, [], (8, 128))
     best = meeting(meet_kernel, 6, 7, [best], (8, 128))
     best = meeting(last_meet_kernel, 7, 8, [best], (16, 1, 128))
     returned = lax.all_to_all(best, everyone, split_axis=0, concat_axis=0, tiled=True)

time: 39.7 us -> 39.1 us (0.985)
  waiting for transfers between devices: 7.52 us -> 5.52 us
  starting transfers between devices: 17.9 us -> 18.7 us
  blocking collectives: 10.5 us -> 11.2 us
    ppermute x1, waiting for transfers between devices: 1.84 us -> 0.53 us  [meet(): crossed = lax.ppermute(far, 'clus', [(c, c ^ 2) for c in range(4)])]
    ppermute x6, starting transfers between devices: 14.5 us -> 15.3 us  [to_meeting(): return lax.ppermute(value, everyone, pairs)]
    ppermute x6, waiting for transfers between devices: 4.51 us -> 3.82 us  [to_meeting(): return lax.ppermute(value, everyone, pairs)]
    all_to_all x1, blocking collectives: 10.5 us -> 11.2 us  [meet(): lax.all_to_all(best, everyone, split_axis=0, concat_axis=0, tiled=True)]
  transfers between devices with their start and end apart: 8 -> 8, of which waited for: 4 -> 3; matrix products, arithmetic and copies ran while one was open for 0% -> 0% of each run, Pallas kernels for 0% -> 0%
where the time goes in v5:
time: 39.1 us; the launch traced here: 38.8 us
  starting transfers between devices  18.7 us (48%)
  blocking collectives  11.2 us (29%)
  waiting for transfers between devices  5.52 us (14%)
  local copies, waits for them, and re-layouts  1.73 us (4%)
  Pallas kernels  1.52 us (4%)
    ppermute x6, starting transfers between devices, to_meeting(): return lax.ppermute(value, everyone, pairs)  15.3 us
    all_to_all x1, blocking collectives, meet(): lax.all_to_all(best, everyone, split_axis=0, concat_axis=0, tiled=True)  11.2 us
    ppermute x6, waiting for transfers between devices, to_meeting(): return lax.ppermute(value, everyone, pairs)  3.82 us
    ppermute x1, starting transfers between devices, meet(): crossed = lax.ppermute(far, 'clus', [(c, c ^ 2) for c in range(4)])  2.9 us
    unnamed x6, local copies, waits for them, and re-layouts  1.73 us
    ppermute x1, waiting for transfers between devices, meet(): got = lax.ppermute(give, 'clus', [(c, c ^ 1) for c in range(4)])  1.17 us
    pallas_call x1, Pallas kernels, meet(): pl.pallas_call(home_kernel, out_shape=jax.ShapeDtypeStruct((1, rows), jnp...  0.83 us
  transfers between devices with their start and end apart: 8, of which 3 were waited for; matrix products, arithmetic and copies ran while one was open for 0% of the time, Pallas kernels for 0%

profile of v5, /device:TPU:0, one launch (start us, length us, event | category | flops | bytes accessed | tf_op | source)
XLA Modules:
  0.0 38.8 jit_solution(6088550701159474457)
XLA Ops:
  0.0 0.0 copy-start.2
  0.0 0.0 copy-start.1
  0.0 0.7 %copy-done.2 = s32[256]{0:T(256)S(1)} copy-done((s32[256]{0:T(256)S(1)}, s32[256]{0:T(256)}, u32[]{:S(2)}) %copy-start.2) | copy-done | bytes 1048
  0.7 0.0 copy-done.1
  0.7 0.0 copy-start
  0.7 1.0 %copy-done = bf16[256,1024]{1,0:T(8,128)(2,1)S(1)} copy-done((bf16[256,1024]{1,0:T(8,128)(2,1)S(1)}, bf16[256,1024]{1,0:T(8,128)(2,1)}, u32[]{:S(2)}) %copy-start) | copy-done | bytes 524312
  1.7 0.6 %sort_rows.1 = (bf16[1040,128]{1,0:T(8,128)(2,1)S(1)}, bf16[1040,128]{1,0:T(8,128)(2,1)S(1)}, s32[1,256]{1,0:T(1,128)S(1)}) custom-call(bf16[256,1024]{1,0:T(8,128)(2,1)S(1)} %copy-done, s32[1,256]{1,0:T(1,128)S(1)} %bitcast.3, s32[1,256]{1,0:T(1,128)S(1)} %bitcast.4), custom_call_target="tpu_custom_call" | custom-call | tf_op jit(solution)/shard_map/sort_rows/pallas_call | solution.py:250
  2.3 0.5 %collective-permute-start = (bf16[1040,128]{1,0:T(8,128)(2,1)S(1)}, bf16[1040,128]{1,0:T(8,128)(2,1)S(1)}, u32[]{:S(2)}, u32[]{:S(2)}) collective-permute-start(bf16[1040,128]{1,0:T(8,128)(2,1)S(1)} %get-tuple-element.11), channel_id=1, source_target_pairs={{0,1},{1,0},{2,3},{3,2},{4,5},{5,4},{6,7},{7,6},{8,9},{9,8},{10,11... | collective-permute-start | bytes 798728 | tf_op jit(solution)/shard_map/ppermute | solution.py:258
  2.8 1.2 %collective-permute-done.got_ref = bf16[1040,128]{1,0:T(8,128)(2,1)S(1)} collective-permute-done((bf16[1040,128]{1,0:T(8,128)(2,1)S(1)}, bf16[1040,128]{1,0:T(8,128)(2,1)S(1)}, u32[]{:S(2)}, u32[]{:S(2)}) %collective-permute-start) | collective-permute-done | bytes 266272 | tf_op jit(solution)/shard_map/ppermute | solution.py:258
  4.0 0.1 join_cores.1
  4.1 2.9 %collective-permute-start.1 = (bf16[1040,128]{1,0:T(8,128)(2,1)S(1)}, bf16[1040,128]{1,0:T(8,128)(2,1)S(1)}, u32[]{:S(2)}, u32[]{:S(2)}) collective-permute-start(bf16[1040,128]{1,0:T(8,128)(2,1)S(1)} %get-tuple-element.13), channel_id=1, source_target_pairs={{0,2},{1,3},{2,0},{3,1},{4,6},{5,7},{6,4},{7,5},{8,10},{9,11},{10,... | collective-permute-start | bytes 798728 | tf_op jit(solution)/shard_map/ppermute | solution.py:267
  7.0 0.7 %collective-permute-start.4 = (bf16[1040,128]{1,0:T(8,128)(2,1)S(1)}, bf16[1040,128]{1,0:T(8,128)(2,1)S(1)}, u32[]{:S(2)}, u32[]{:S(2)}) collective-permute-start(bf16[1040,128]{1,0:T(8,128)(2,1)S(1)} %get-tuple-element.13), channel_id=1, source_target_pairs={{14,4},{3,9},{12,6},{1,11},{30,20},{19,25},{28,22},{17,27}} | collective-permute-start | bytes 798728 | tf_op jit(solution)/shard_map/ppermute | solution.py:248
  7.7 4.1 %collective-permute-start.5 = (bf16[1040,128]{1,0:T(8,128)(2,1)S(1)}, bf16[1040,128]{1,0:T(8,128)(2,1)S(1)}, u32[]{:S(2)}, u32[]{:S(2)}) collective-permute-start(bf16[1040,128]{1,0:T(8,128)(2,1)S(1)} %get-tuple-element.12.refs_0_), channel_id=1, source_target_pairs={{0,4},{13,9},{2,6},{15,11},{16,20},{29,25},{18,22},{31,27}} | collective-permute-start | bytes 798728 | tf_op jit(solution)/shard_map/ppermute | solution.py:248
  11.8 0.7 %collective-permute-start.3 = (bf16[1040,128]{1,0:T(8,128)(2,1)S(1)}, bf16[1040,128]{1,0:T(8,128)(2,1)S(1)}, u32[]{:S(2)}, u32[]{:S(2)}) collective-permute-start(bf16[1040,128]{1,0:T(8,128)(2,1)S(1)} %get-tuple-element.12.refs_0_), channel_id=1, source_target_pairs={{8,4},{5,9},{10,6},{7,11},{24,20},{21,25},{26,22},{23,27}} | collective-permute-start | bytes 798728 | tf_op jit(solution)/shard_map/ppermute | solution.py:248
  12.5 0.7 %collective-permute-start.2 = (bf16[1040,128]{1,0:T(8,128)(2,1)S(1)}, bf16[1040,128]{1,0:T(8,128)(2,1)S(1)}, u32[]{:S(2)}, u32[]{:S(2)}) collective-permute-start(bf16[1040,128]{1,0:T(8,128)(2,1)S(1)} %get-tuple-element.12.refs_0_), channel_id=1, source_target_pairs={{12,4},{1,9},{14,6},{3,11},{28,20},{17,25},{30,22},{19,27}} | collective-permute-start | bytes 798728 | tf_op jit(solution)/shard_map/ppermute | solution.py:248
  13.2 0.5 %collective-permute-done.1.refs_1_ = bf16[1040,128]{1,0:T(8,128)(2,1)S(1)} collective-permute-done((bf16[1040,128]{1,0:T(8,128)(2,1)S(1)}, bf16[1040,128]{1,0:T(8,128)(2,1)S(1)}, u32[]{:S(2)}, u32[]{:S(2)}) %collective-permute-start.1) | collective-permute-done | bytes 266272 | tf_op jit(solution)/shard_map/ppermute | solution.py:267
  13.7 0.7 %collective-permute-start.6 = (bf16[1040,128]{1,0:T(8,128)(2,1)S(1)}, bf16[1040,128]{1,0:T(8,128)(2,1)S(1)}, u32[]{:S(2)}, u32[]{:S(2)}) collective-permute-start(bf16[1040,128]{1,0:T(8,128)(2,1)S(1)} %collective-permute-done.1.refs_1_), channel_id=1, source_target_pairs={{8,4},{5,9},{10,6},{7,11},{24,20},{21,25},{26,22},{23,27}} | collective-permute-start | bytes 798728 | tf_op jit(solution)/shard_map/ppermute | solution.py:248
  14.4 0.0 collective-permute-done.4.refs_4_
  14.4 8.5 %collective-permute-start.7 = (bf16[1040,128]{1,0:T(8,128)(2,1)S(1)}, bf16[1040,128]{1,0:T(8,128)(2,1)S(1)}, u32[]{:S(2)}, u32[]{:S(2)}) collective-permute-start(bf16[1040,128]{1,0:T(8,128)(2,1)S(1)} %collective-permute-done.1.refs_1_), channel_id=1, source_target_pairs={{0,4},{13,9},{2,6},{15,11},{16,20},{29,25},{18,22},{31,27}} | collective-permute-start | bytes 798728 | tf_op jit(solution)/shard_map/ppermute | solution.py:248
  22.9 0.0 collective-permute-done.5.refs_5_
  22.9 0.0 collective-permute-done.3.refs_3_
  22.9 0.0 collective-permute-done.2.refs_2_
  23.0 0.0 collective-permute-done.6.refs_6_
  23.0 3.8 %collective-permute-done.7.refs_7_ = bf16[1040,128]{1,0:T(8,128)(2,1)S(1)} collective-permute-done((bf16[1040,128]{1,0:T(8,128)(2,1)S(1)}, bf16[1040,128]{1,0:T(8,128)(2,1)S(1)}, u32[]{:S(2)}, u32[]{:S(2)}) %collective-permute-start.7) | collective-permute-done | bytes 266272 | tf_op jit(solution)/shard_map/ppermute | solution.py:248
  26.8 11.2 %all_to_all.5.got_ref = f32[16,1,128]{2,1,0:T(1,128)S(1)} all-to-all(f32[16,1,128]{2,1,0:T(1,128)S(1)} %meet_7_8.1), channel_id=1, replica_groups=mesh['groups'=2,'blk'=4,'clus'=4] {'blk','clus'}, dimensions={0} | all-to-all | bytes 16384 | tf_op jit(solution)/shard_map/all_to_all | solution.py:289
  38.0 0.8 %home_scores.1 = f32[1,256]{1,0:T(1,128)} custom-call(f32[16,1,128]{2,1,0:T(1,128)S(1)} %all_to_all.5.got_ref, s32[1,256]{1,0:T(1,128)S(1)} %get-tuple-element.14.target_ref), custom_call_target="tpu_custom_call" | custom-call | tf_op jit(solution)/shard_map/home_scores/pallas_call | solution.py:290
  (3 shorter events, 0.0 us)
Async XLA Ops:
  0.0 0.7 %copy-start.2 = (s32[256]{0:T(256)S(1)}, s32[256]{0:T(256)}, u32[]{:S(2)}) copy-start(s32[256]{0:T(256)} %param.5) | copy-start | bytes 3076
  0.0 0.7 %copy-start.1 = (s32[256]{0:T(256)S(1)}, s32[256]{0:T(256)}, u32[]{:S(2)}) copy-start(s32[256]{0:T(256)} %param.4) | copy-start | bytes 3076
  0.7 1.0 %copy-start = (bf16[256,1024]{1,0:T(8,128)(2,1)S(1)}, bf16[256,1024]{1,0:T(8,128)(2,1)}, u32[]{:S(2)}) copy-start(bf16[256,1024]{1,0:T(8,128)(2,1)} %emb_ref.1) | copy-start | bytes 1572868
  2.3 1.7 %collective-permute-start = (bf16[1040,128]{1,0:T(8,128)(2,1)S(1)}, bf16[1040,128]{1,0:T(8,128)(2,1)S(1)}, u32[]{:S(2)}, u32[]{:S(2)}) collective-permute-start(bf16[1040,128]{1,0:T(8,128)(2,1)S(1)} %get-tuple-element.11), channel_id=1, source_target_pairs={{0,1},{1,0},{2,3},{3,2},{4,5},{5,4},{6,7},{7,6},{8,9},{9,8},{10,11... | collective-permute-start | bytes 798728 | tf_op jit(solution)/shard_map/ppermute | solution.py:258
  4.1 9.6 %collective-permute-start.1 = (bf16[1040,128]{1,0:T(8,128)(2,1)S(1)}, bf16[1040,128]{1,0:T(8,128)(2,1)S(1)}, u32[]{:S(2)}, u32[]{:S(2)}) collective-permute-start(bf16[1040,128]{1,0:T(8,128)(2,1)S(1)} %get-tuple-element.13), channel_id=1, source_target_pairs={{0,2},{1,3},{2,0},{3,1},{4,6},{5,7},{6,4},{7,5},{8,10},{9,11},{10,... | collective-permute-start | bytes 798728 | tf_op jit(solution)/shard_map/ppermute | solution.py:267
  7.0 7.4 %collective-permute-start.4 = (bf16[1040,128]{1,0:T(8,128)(2,1)S(1)}, bf16[1040,128]{1,0:T(8,128)(2,1)S(1)}, u32[]{:S(2)}, u32[]{:S(2)}) collective-permute-start(bf16[1040,128]{1,0:T(8,128)(2,1)S(1)} %get-tuple-element.13), channel_id=1, source_target_pairs={{14,4},{3,9},{12,6},{1,11},{30,20},{19,25},{28,22},{17,27}} | collective-permute-start | bytes 798728 | tf_op jit(solution)/shard_map/ppermute | solution.py:248
  7.7 15.2 %collective-permute-start.5 = (bf16[1040,128]{1,0:T(8,128)(2,1)S(1)}, bf16[1040,128]{1,0:T(8,128)(2,1)S(1)}, u32[]{:S(2)}, u32[]{:S(2)}) collective-permute-start(bf16[1040,128]{1,0:T(8,128)(2,1)S(1)} %get-tuple-element.12.refs_0_), channel_id=1, source_target_pairs={{0,4},{13,9},{2,6},{15,11},{16,20},{29,25},{18,22},{31,27}} | collective-permute-start | bytes 798728 | tf_op jit(solution)/shard_map/ppermute | solution.py:248
  11.8 11.1 %collective-permute-start.3 = (bf16[1040,128]{1,0:T(8,128)(2,1)S(1)}, bf16[1040,128]{1,0:T(8,128)(2,1)S(1)}, u32[]{:S(2)}, u32[]{:S(2)}) collective-permute-start(bf16[1040,128]{1,0:T(8,128)(2,1)S(1)} %get-tuple-element.12.refs_0_), channel_id=1, source_target_pairs={{8,4},{5,9},{10,6},{7,11},{24,20},{21,25},{26,22},{23,27}} | collective-permute-start | bytes 798728 | tf_op jit(solution)/shard_map/ppermute | solution.py:248
  12.5 10.5 %collective-permute-start.2 = (bf16[1040,128]{1,0:T(8,128)(2,1)S(1)}, bf16[1040,128]{1,0:T(8,128)(2,1)S(1)}, u32[]{:S(2)}, u32[]{:S(2)}) collective-permute-start(bf16[1040,128]{1,0:T(8,128)(2,1)S(1)} %get-tuple-element.12.refs_0_), channel_id=1, source_target_pairs={{12,4},{1,9},{14,6},{3,11},{28,20},{17,25},{30,22},{19,27}} | collective-permute-start | bytes 798728 | tf_op jit(solution)/shard_map/ppermute | solution.py:248
  13.7 9.3 %collective-permute-start.6 = (bf16[1040,128]{1,0:T(8,128)(2,1)S(1)}, bf16[1040,128]{1,0:T(8,128)(2,1)S(1)}, u32[]{:S(2)}, u32[]{:S(2)}) collective-permute-start(bf16[1040,128]{1,0:T(8,128)(2,1)S(1)} %collective-permute-done.1.refs_1_), channel_id=1, source_target_pairs={{8,4},{5,9},{10,6},{7,11},{24,20},{21,25},{26,22},{23,27}} | collective-permute-start | bytes 798728 | tf_op jit(solution)/shard_map/ppermute | solution.py:248
  14.4 12.4 %collective-permute-start.7 = (bf16[1040,128]{1,0:T(8,128)(2,1)S(1)}, bf16[1040,128]{1,0:T(8,128)(2,1)S(1)}, u32[]{:S(2)}, u32[]{:S(2)}) collective-permute-start(bf16[1040,128]{1,0:T(8,128)(2,1)S(1)} %collective-permute-done.1.refs_1_), channel_id=1, source_target_pairs={{0,4},{13,9},{2,6},{15,11},{16,20},{29,25},{18,22},{31,27}} | collective-permute-start | bytes 798728 | tf_op jit(solution)/shard_map/ppermute | solution.py:248

commit v6 on v5

--- a/solution.py
+++ b/solution.py
@@ -74,7 +74,7 @@
 
 NEAR, ACROSS, FAR = 0, 2, 3
 BLOCKS = (
-    (0, None), (1, None), (0, FAR), (0, ACROSS), (1, FAR), (0, NEAR), (1, ACROSS), (1, NEAR),
+    (0, None), (1, None), (0, FAR), (0, ACROSS), (0, NEAR), (1, FAR), (1, ACROSS), (1, NEAR),
 )
 
 
@@ -138,13 +138,13 @@
     give_ref[tail : tail + 16, :] = moved[:, 2 * CAP :]
 
 
-def join_kernel(keep_ref, got_ref, near_ref, far_ref):
+def join_kernel(keep_ref, got_ref, *out_refs):
     u, _ = here()
     core = lax.rem(u, 2)
     tail = keep_ref.shape[0] - 16
     own_at = pl.multiple_of(core * CAP, CAP)
     other_at = pl.multiple_of((1 - core) * CAP, CAP)
-    for out_ref, start in ((far_ref, CAP), (near_ref, 0)):
+    for out_ref, start in zip(out_refs, (0, CAP) * 2):
         for t in range(tail // SLABS_ROWS):
             base = t * SLABS_ROWS
             out_ref[pl.ds(base + own_at, CAP), :] = keep_ref[base + start : base + start + CAP, :]
@@ -256,11 +256,11 @@
         name="sort_rows",
     )(embeddings, cluster.reshape(1, rows), row_ids.reshape(1, rows))
     got = lax.ppermute(give, "clus", [(c, c ^ 1) for c in range(4)])
-    near, far = pl.pallas_call(
+    near, direct, first, far = pl.pallas_call(
         join_kernel,
-        out_shape=[payload] * 2,
+        out_shape=[payload] * 4,
         in_specs=[VMEM] * 2,
-        out_specs=[VMEM] * 2,
+        out_specs=[VMEM] * 4,
         compiler_params=SMALL,
         name="join_cores",
     )(keep, got)
@@ -268,7 +268,9 @@
     arrived = []
     for other, place in BLOCKS:
         if other and place == FAR:
-            arrived.append(to_meeting(far, place, cross=1))
+            arrived.append(to_meeting(direct, place, cross=1))
+        elif not other and place == NEAR:
+            arrived.append(to_meeting(first, place))
         else:
             value = crossed if other else near
             arrived.append(value if place is None else to_meeting(value, place))

time: 39.1 us -> 38.5 us (0.985)
  starting transfers between devices: 18.7 us -> 14 us
  waiting for transfers between devices: 5.52 us -> 7.81 us
  blocking collectives: 11.2 us -> 13 us
    ppermute x6, starting transfers between devices: 15.3 us -> 10.6 us  [to_meeting(): return lax.ppermute(value, everyone, pairs)]
    all_to_all x1, blocking collectives: 11.2 us -> 13 us  [meet(): lax.all_to_all(best, everyone, split_axis=0, concat_axis=0, tiled=True)]
    ppermute x6, waiting for transfers between devices: 3.82 us -> 5.5 us  [to_meeting(): return lax.ppermute(value, everyone, pairs)]
    ppermute x1, waiting for transfers between devices: 0.53 us -> 1.14 us  [meet(): crossed = lax.ppermute(far, 'clus', [(c, c ^ 2) for c in range(4)])]
  transfers between devices with their start and end apart: 8 -> 8, of which waited for: 3 -> 4; matrix products, arithmetic and copies ran while one was open for 0% -> 0% of each run, Pallas kernels for 0% -> 0%
where the time goes in v6:
time: 38.5 us; the launch traced here: 38.2 us
  starting transfers between devices  14 us (36%)
  blocking collectives  13 us (34%)
  waiting for transfers between devices  7.81 us (20%)
  local copies, waits for them, and re-layouts  1.73 us (4%)
  Pallas kernels  1.59 us (4%)
    all_to_all x1, blocking collectives, meet(): lax.all_to_all(best, everyone, split_axis=0, concat_axis=0, tiled=True)  13 us
    ppermute x6, starting transfers between devices, to_meeting(): return lax.ppermute(value, everyone, pairs)  10.6 us
    ppermute x6, waiting for transfers between devices, to_meeting(): return lax.ppermute(value, everyone, pairs)  5.5 us
    ppermute x1, starting transfers between devices, meet(): crossed = lax.ppermute(far, 'clus', [(c, c ^ 2) for c in range(4)])  2.92 us
    unnamed x6, local copies, waits for them, and re-layouts  1.73 us
    ppermute x1, waiting for transfers between devices, meet(): got = lax.ppermute(give, 'clus', [(c, c ^ 1) for c in range(4)])  1.17 us
    ppermute x1, waiting for transfers between devices, meet(): crossed = lax.ppermute(far, 'clus', [(c, c ^ 2) for c in range(4)])  1.14 us
    pallas_call x1, Pallas kernels, meet(): pl.pallas_call(home_kernel, out_shape=jax.ShapeDtypeStruct((1, rows), jnp...  0.83 us
  transfers between devices with their start and end apart: 8, of which 4 were waited for; matrix products, arithmetic and copies ran while one was open for 0% of the time, Pallas kernels for 0%

profile of v6, /device:TPU:0, one launch (start us, length us, event | category | flops | bytes accessed | tf_op | source)
XLA Modules:
  0.0 38.2 jit_solution(6926393419022394842)
XLA Ops:
  0.0 0.0 copy-start.2
  0.0 0.0 copy-start.1
  0.0 0.7 %copy-done.2 = s32[256]{0:T(256)S(1)} copy-done((s32[256]{0:T(256)S(1)}, s32[256]{0:T(256)}, u32[]{:S(2)}) %copy-start.2) | copy-done | bytes 1048
  0.7 0.0 copy-done.1
  0.7 0.0 copy-start
  0.7 1.0 %copy-done = bf16[256,1024]{1,0:T(8,128)(2,1)S(1)} copy-done((bf16[256,1024]{1,0:T(8,128)(2,1)S(1)}, bf16[256,1024]{1,0:T(8,128)(2,1)}, u32[]{:S(2)}) %copy-start) | copy-done | bytes 524312
  1.7 0.6 %sort_rows.1 = (bf16[1040,128]{1,0:T(8,128)(2,1)S(1)}, bf16[1040,128]{1,0:T(8,128)(2,1)S(1)}, s32[1,256]{1,0:T(1,128)S(1)}) custom-call(bf16[256,1024]{1,0:T(8,128)(2,1)S(1)} %copy-done, s32[1,256]{1,0:T(1,128)S(1)} %bitcast.3, s32[1,256]{1,0:T(1,128)S(1)} %bitcast.4), custom_call_target="tpu_custom_call" | custom-call | tf_op jit(solution)/shard_map/sort_rows/pallas_call | solution.py:250
  2.3 0.5 %collective-permute-start = (bf16[1040,128]{1,0:T(8,128)(2,1)S(1)}, bf16[1040,128]{1,0:T(8,128)(2,1)S(1)}, u32[]{:S(2)}, u32[]{:S(2)}) collective-permute-start(bf16[1040,128]{1,0:T(8,128)(2,1)S(1)} %get-tuple-element.13), channel_id=1, source_target_pairs={{0,1},{1,0},{2,3},{3,2},{4,5},{5,4},{6,7},{7,6},{8,9},{9,8},{10,11... | collective-permute-start | bytes 798728 | tf_op jit(solution)/shard_map/ppermute | solution.py:258
  2.8 1.2 %collective-permute-done.got_ref = bf16[1040,128]{1,0:T(8,128)(2,1)S(1)} collective-permute-done((bf16[1040,128]{1,0:T(8,128)(2,1)S(1)}, bf16[1040,128]{1,0:T(8,128)(2,1)S(1)}, u32[]{:S(2)}, u32[]{:S(2)}) %collective-permute-start) | collective-permute-done | bytes 266272 | tf_op jit(solution)/shard_map/ppermute | solution.py:258
  4.0 0.2 join_cores.1
  4.2 2.9 %collective-permute-start.1 = (bf16[1040,128]{1,0:T(8,128)(2,1)S(1)}, bf16[1040,128]{1,0:T(8,128)(2,1)S(1)}, u32[]{:S(2)}, u32[]{:S(2)}) collective-permute-start(bf16[1040,128]{1,0:T(8,128)(2,1)S(1)} %get-tuple-element.15), channel_id=1, source_target_pairs={{0,2},{1,3},{2,0},{3,1},{4,6},{5,7},{6,4},{7,5},{8,10},{9,11},{10,... | collective-permute-start | bytes 798728 | tf_op jit(solution)/shard_map/ppermute | solution.py:267
  7.1 3.5 %collective-permute-start.4 = (bf16[1040,128]{1,0:T(8,128)(2,1)S(1)}, bf16[1040,128]{1,0:T(8,128)(2,1)S(1)}, u32[]{:S(2)}, u32[]{:S(2)}) collective-permute-start(bf16[1040,128]{1,0:T(8,128)(2,1)S(1)} %get-tuple-element.16), channel_id=1, source_target_pairs={{0,4},{13,9},{2,6},{15,11},{16,20},{29,25},{18,22},{31,27}} | collective-permute-start | bytes 798728 | tf_op jit(solution)/shard_map/ppermute | solution.py:248
  10.6 0.7 %collective-permute-start.5 = (bf16[1040,128]{1,0:T(8,128)(2,1)S(1)}, bf16[1040,128]{1,0:T(8,128)(2,1)S(1)}, u32[]{:S(2)}, u32[]{:S(2)}) collective-permute-start(bf16[1040,128]{1,0:T(8,128)(2,1)S(1)} %get-tuple-element.17), channel_id=1, source_target_pairs={{14,4},{3,9},{12,6},{1,11},{30,20},{19,25},{28,22},{17,27}} | collective-permute-start | bytes 798728 | tf_op jit(solution)/shard_map/ppermute | solution.py:248
  11.3 0.7 %collective-permute-start.3 = (bf16[1040,128]{1,0:T(8,128)(2,1)S(1)}, bf16[1040,128]{1,0:T(8,128)(2,1)S(1)}, u32[]{:S(2)}, u32[]{:S(2)}) collective-permute-start(bf16[1040,128]{1,0:T(8,128)(2,1)S(1)} %get-tuple-element.14.refs_0_), channel_id=1, source_target_pairs={{8,4},{5,9},{10,6},{7,11},{24,20},{21,25},{26,22},{23,27}} | collective-permute-start | bytes 798728 | tf_op jit(solution)/shard_map/ppermute | solution.py:248
  11.9 0.7 %collective-permute-start.2 = (bf16[1040,128]{1,0:T(8,128)(2,1)S(1)}, bf16[1040,128]{1,0:T(8,128)(2,1)S(1)}, u32[]{:S(2)}, u32[]{:S(2)}) collective-permute-start(bf16[1040,128]{1,0:T(8,128)(2,1)S(1)} %get-tuple-element.14.refs_0_), channel_id=1, source_target_pairs={{12,4},{1,9},{14,6},{3,11},{28,20},{17,25},{30,22},{19,27}} | collective-permute-start | bytes 798728 | tf_op jit(solution)/shard_map/ppermute | solution.py:248
  12.6 1.1 %collective-permute-done.1.refs_1_ = bf16[1040,128]{1,0:T(8,128)(2,1)S(1)} collective-permute-done((bf16[1040,128]{1,0:T(8,128)(2,1)S(1)}, bf16[1040,128]{1,0:T(8,128)(2,1)S(1)}, u32[]{:S(2)}, u32[]{:S(2)}) %collective-permute-start.1) | collective-permute-done | bytes 266272 | tf_op jit(solution)/shard_map/ppermute | solution.py:267
  13.8 0.7 %collective-permute-start.6 = (bf16[1040,128]{1,0:T(8,128)(2,1)S(1)}, bf16[1040,128]{1,0:T(8,128)(2,1)S(1)}, u32[]{:S(2)}, u32[]{:S(2)}) collective-permute-start(bf16[1040,128]{1,0:T(8,128)(2,1)S(1)} %collective-permute-done.1.refs_1_), channel_id=1, source_target_pairs={{8,4},{5,9},{10,6},{7,11},{24,20},{21,25},{26,22},{23,27}} | collective-permute-start | bytes 798728 | tf_op jit(solution)/shard_map/ppermute | solution.py:248
  14.4 1.7 %collective-permute-done.4.refs_4_ = bf16[1040,128]{1,0:T(8,128)(2,1)S(1)} collective-permute-done((bf16[1040,128]{1,0:T(8,128)(2,1)S(1)}, bf16[1040,128]{1,0:T(8,128)(2,1)S(1)}, u32[]{:S(2)}, u32[]{:S(2)}) %collective-permute-start.4) | collective-permute-done | bytes 266272 | tf_op jit(solution)/shard_map/ppermute | solution.py:248
  16.1 4.4 %collective-permute-start.7 = (bf16[1040,128]{1,0:T(8,128)(2,1)S(1)}, bf16[1040,128]{1,0:T(8,128)(2,1)S(1)}, u32[]{:S(2)}, u32[]{:S(2)}) collective-permute-start(bf16[1040,128]{1,0:T(8,128)(2,1)S(1)} %collective-permute-done.1.refs_1_), channel_id=1, source_target_pairs={{0,4},{13,9},{2,6},{15,11},{16,20},{29,25},{18,22},{31,27}} | collective-permute-start | bytes 798728 | tf_op jit(solution)/shard_map/ppermute | solution.py:248
  20.5 0.0 collective-permute-done.5.refs_5_
  20.5 0.0 collective-permute-done.3.refs_3_
  20.5 0.0 collective-permute-done.2.refs_2_
  20.6 0.0 collective-permute-done.6.refs_6_
  20.6 3.8 %collective-permute-done.7.refs_7_ = bf16[1040,128]{1,0:T(8,128)(2,1)S(1)} collective-permute-done((bf16[1040,128]{1,0:T(8,128)(2,1)S(1)}, bf16[1040,128]{1,0:T(8,128)(2,1)S(1)}, u32[]{:S(2)}, u32[]{:S(2)}) %collective-permute-start.7) | collective-permute-done | bytes 266272 | tf_op jit(solution)/shard_map/ppermute | solution.py:248
  24.4 13.0 %all_to_all.5.got_ref = f32[16,1,128]{2,1,0:T(1,128)S(1)} all-to-all(f32[16,1,128]{2,1,0:T(1,128)S(1)} %meet_7_8.1), channel_id=1, replica_groups=mesh['groups'=2,'blk'=4,'clus'=4] {'blk','clus'}, dimensions={0} | all-to-all | bytes 16384 | tf_op jit(solution)/shard_map/all_to_all | solution.py:291
  37.4 0.8 %home_scores.1 = f32[1,256]{1,0:T(1,128)} custom-call(f32[16,1,128]{2,1,0:T(1,128)S(1)} %all_to_all.5.got_ref, s32[1,256]{1,0:T(1,128)S(1)} %get-tuple-element.18.target_ref), custom_call_target="tpu_custom_call" | custom-call | tf_op jit(solution)/shard_map/home_scores/pallas_call | solution.py:292
  (3 shorter events, 0.0 us)
Async XLA Ops:
  0.0 0.7 %copy-start.2 = (s32[256]{0:T(256)S(1)}, s32[256]{0:T(256)}, u32[]{:S(2)}) copy-start(s32[256]{0:T(256)} %param.5) | copy-start | bytes 3076
  0.0 0.7 %copy-start.1 = (s32[256]{0:T(256)S(1)}, s32[256]{0:T(256)}, u32[]{:S(2)}) copy-start(s32[256]{0:T(256)} %param.4) | copy-start | bytes 3076
  0.7 1.0 %copy-start = (bf16[256,1024]{1,0:T(8,128)(2,1)S(1)}, bf16[256,1024]{1,0:T(8,128)(2,1)}, u32[]{:S(2)}) copy-start(bf16[256,1024]{1,0:T(8,128)(2,1)} %emb_ref.1) | copy-start | bytes 1572868
  2.3 1.7 %collective-permute-start = (bf16[1040,128]{1,0:T(8,128)(2,1)S(1)}, bf16[1040,128]{1,0:T(8,128)(2,1)S(1)}, u32[]{:S(2)}, u32[]{:S(2)}) collective-permute-start(bf16[1040,128]{1,0:T(8,128)(2,1)S(1)} %get-tuple-element.13), channel_id=1, source_target_pairs={{0,1},{1,0},{2,3},{3,2},{4,5},{5,4},{6,7},{7,6},{8,9},{9,8},{10,11... | collective-permute-start | bytes 798728 | tf_op jit(solution)/shard_map/ppermute | solution.py:258
  4.2 9.6 %collective-permute-start.1 = (bf16[1040,128]{1,0:T(8,128)(2,1)S(1)}, bf16[1040,128]{1,0:T(8,128)(2,1)S(1)}, u32[]{:S(2)}, u32[]{:S(2)}) collective-permute-start(bf16[1040,128]{1,0:T(8,128)(2,1)S(1)} %get-tuple-element.15), channel_id=1, source_target_pairs={{0,2},{1,3},{2,0},{3,1},{4,6},{5,7},{6,4},{7,5},{8,10},{9,11},{10,... | collective-permute-start | bytes 798728 | tf_op jit(solution)/shard_map/ppermute | solution.py:267
  7.1 9.1 %collective-permute-start.4 = (bf16[1040,128]{1,0:T(8,128)(2,1)S(1)}, bf16[1040,128]{1,0:T(8,128)(2,1)S(1)}, u32[]{:S(2)}, u32[]{:S(2)}) collective-permute-start(bf16[1040,128]{1,0:T(8,128)(2,1)S(1)} %get-tuple-element.16), channel_id=1, source_target_pairs={{0,4},{13,9},{2,6},{15,11},{16,20},{29,25},{18,22},{31,27}} | collective-permute-start | bytes 798728 | tf_op jit(solution)/shard_map/ppermute | solution.py:248
  10.6 10.0 %collective-permute-start.5 = (bf16[1040,128]{1,0:T(8,128)(2,1)S(1)}, bf16[1040,128]{1,0:T(8,128)(2,1)S(1)}, u32[]{:S(2)}, u32[]{:S(2)}) collective-permute-start(bf16[1040,128]{1,0:T(8,128)(2,1)S(1)} %get-tuple-element.17), channel_id=1, source_target_pairs={{14,4},{3,9},{12,6},{1,11},{30,20},{19,25},{28,22},{17,27}} | collective-permute-start | bytes 798728 | tf_op jit(solution)/shard_map/ppermute | solution.py:248
  11.3 9.3 %collective-permute-start.3 = (bf16[1040,128]{1,0:T(8,128)(2,1)S(1)}, bf16[1040,128]{1,0:T(8,128)(2,1)S(1)}, u32[]{:S(2)}, u32[]{:S(2)}) collective-permute-start(bf16[1040,128]{1,0:T(8,128)(2,1)S(1)} %get-tuple-element.14.refs_0_), channel_id=1, source_target_pairs={{8,4},{5,9},{10,6},{7,11},{24,20},{21,25},{26,22},{23,27}} | collective-permute-start | bytes 798728 | tf_op jit(solution)/shard_map/ppermute | solution.py:248
  11.9 8.6 %collective-permute-start.2 = (bf16[1040,128]{1,0:T(8,128)(2,1)S(1)}, bf16[1040,128]{1,0:T(8,128)(2,1)S(1)}, u32[]{:S(2)}, u32[]{:S(2)}) collective-permute-start(bf16[1040,128]{1,0:T(8,128)(2,1)S(1)} %get-tuple-element.14.refs_0_), channel_id=1, source_target_pairs={{12,4},{1,9},{14,6},{3,11},{28,20},{17,25},{30,22},{19,27}} | collective-permute-start | bytes 798728 | tf_op jit(solution)/shard_map/ppermute | solution.py:248
  13.8 6.8 %collective-permute-start.6 = (bf16[1040,128]{1,0:T(8,128)(2,1)S(1)}, bf16[1040,128]{1,0:T(8,128)(2,1)S(1)}, u32[]{:S(2)}, u32[]{:S(2)}) collective-permute-start(bf16[1040,128]{1,0:T(8,128)(2,1)S(1)} %collective-permute-done.1.refs_1_), channel_id=1, source_target_pairs={{8,4},{5,9},{10,6},{7,11},{24,20},{21,25},{26,22},{23,27}} | collective-permute-start | bytes 798728 | tf_op jit(solution)/shard_map/ppermute | solution.py:248
  16.1 8.3 %collective-permute-start.7 = (bf16[1040,128]{1,0:T(8,128)(2,1)S(1)}, bf16[1040,128]{1,0:T(8,128)(2,1)S(1)}, u32[]{:S(2)}, u32[]{:S(2)}) collective-permute-start(bf16[1040,128]{1,0:T(8,128)(2,1)S(1)} %collective-permute-done.1.refs_1_), channel_id=1, source_target_pairs={{0,4},{13,9},{2,6},{15,11},{16,20},{29,25},{18,22},{31,27}} | collective-permute-start | bytes 798728 | tf_op jit(solution)/shard_map/ppermute | solution.py:248

commit v7 on v6

--- a/solution.py
+++ b/solution.py
@@ -74,7 +74,7 @@
 
 NEAR, ACROSS, FAR = 0, 2, 3
 BLOCKS = (
-    (0, None), (1, None), (0, FAR), (0, ACROSS), (0, NEAR), (1, FAR), (1, ACROSS), (1, NEAR),
+    (0, None), (1, None), (0, NEAR), (0, ACROSS), (0, FAR), (1, FAR), (1, ACROSS), (1, NEAR),
 )
 
 
@@ -269,7 +269,7 @@
     for other, place in BLOCKS:
         if other and place == FAR:
             arrived.append(to_meeting(direct, place, cross=1))
-        elif not other and place == NEAR:
+        elif not other and place == FAR:
             arrived.append(to_meeting(first, place))
         else:
             value = crossed if other else near

time: 38.5 us -> 36.8 us (0.956)
  waiting for transfers between devices: 7.81 us -> 5.05 us
  starting transfers between devices: 14 us -> 16.2 us
  blocking collectives: 13 us -> 12 us
    ppermute x6, starting transfers between devices: 10.6 us -> 12.7 us  [to_meeting(): return lax.ppermute(value, everyone, pairs)]
    ppermute x6, waiting for transfers between devices: 5.5 us -> 3.88 us  [to_meeting(): return lax.ppermute(value, everyone, pairs)]
    ppermute x1, waiting for transfers between devices: 1.14 us -> 0.01 us  [meet(): crossed = lax.ppermute(far, 'clus', [(c, c ^ 2) for c in range(4)])]
    all_to_all x1, blocking collectives: 13 us -> 12 us  [meet(): lax.all_to_all(best, everyone, split_axis=0, concat_axis=0, tiled=True)]
  transfers between devices with their start and end apart: 8 -> 8, of which waited for: 4 -> 3; matrix products, arithmetic and copies ran while one was open for 0% -> 0% of each run, Pallas kernels for 0% -> 0%
where the time goes in v7:
time: 36.8 us; the launch traced here: 36.6 us
  starting transfers between devices  16.2 us (44%)
  blocking collectives  12 us (33%)
  waiting for transfers between devices  5.05 us (14%)
  local copies, waits for them, and re-layouts  1.73 us (5%)
  Pallas kernels  1.55 us (4%)
    ppermute x6, starting transfers between devices, to_meeting(): return lax.ppermute(value, everyone, pairs)  12.7 us
    all_to_all x1, blocking collectives, meet(): lax.all_to_all(best, everyone, split_axis=0, concat_axis=0, tiled=True)  12 us
    ppermute x6, waiting for transfers between devices, to_meeting(): return lax.ppermute(value, everyone, pairs)  3.88 us
    ppermute x1, starting transfers between devices, meet(): crossed = lax.ppermute(far, 'clus', [(c, c ^ 2) for c in range(4)])  2.92 us
    unnamed x6, local copies, waits for them, and re-layouts  1.73 us
    ppermute x1, waiting for transfers between devices, meet(): got = lax.ppermute(give, 'clus', [(c, c ^ 1) for c in range(4)])  1.17 us
    pallas_call x1, Pallas kernels, meet(): pl.pallas_call(home_kernel, out_shape=jax.ShapeDtypeStruct((1, rows), jnp...  0.83 us
  transfers between devices with their start and end apart: 8, of which 3 were waited for; matrix products, arithmetic and copies ran while one was open for 0% of the time, Pallas kernels for 0%

profile of v7, /device:TPU:0, one launch (start us, length us, event | category | flops | bytes accessed | tf_op | source)
XLA Modules:
  0.0 36.6 jit_solution(2046680915779294974)
XLA Ops:
  0.0 0.0 copy-start.2
  0.0 0.0 copy-start.1
  0.0 0.7 %copy-done.2 = s32[256]{0:T(256)S(1)} copy-done((s32[256]{0:T(256)S(1)}, s32[256]{0:T(256)}, u32[]{:S(2)}) %copy-start.2) | copy-done | bytes 1048
  0.7 0.0 copy-done.1
  0.7 0.0 copy-start
  0.7 1.0 %copy-done = bf16[256,1024]{1,0:T(8,128)(2,1)S(1)} copy-done((bf16[256,1024]{1,0:T(8,128)(2,1)S(1)}, bf16[256,1024]{1,0:T(8,128)(2,1)}, u32[]{:S(2)}) %copy-start) | copy-done | bytes 524312
  1.7 0.6 %sort_rows.1 = (bf16[1040,128]{1,0:T(8,128)(2,1)S(1)}, bf16[1040,128]{1,0:T(8,128)(2,1)S(1)}, s32[1,256]{1,0:T(1,128)S(1)}) custom-call(bf16[256,1024]{1,0:T(8,128)(2,1)S(1)} %copy-done, s32[1,256]{1,0:T(1,128)S(1)} %bitcast.3, s32[1,256]{1,0:T(1,128)S(1)} %bitcast.4), custom_call_target="tpu_custom_call" | custom-call | tf_op jit(solution)/shard_map/sort_rows/pallas_call | solution.py:250
  2.3 0.5 %collective-permute-start = (bf16[1040,128]{1,0:T(8,128)(2,1)S(1)}, bf16[1040,128]{1,0:T(8,128)(2,1)S(1)}, u32[]{:S(2)}, u32[]{:S(2)}) collective-permute-start(bf16[1040,128]{1,0:T(8,128)(2,1)S(1)} %get-tuple-element.13), channel_id=1, source_target_pairs={{0,1},{1,0},{2,3},{3,2},{4,5},{5,4},{6,7},{7,6},{8,9},{9,8},{10,11... | collective-permute-start | bytes 798728 | tf_op jit(solution)/shard_map/ppermute | solution.py:258
  2.8 1.2 %collective-permute-done.got_ref = bf16[1040,128]{1,0:T(8,128)(2,1)S(1)} collective-permute-done((bf16[1040,128]{1,0:T(8,128)(2,1)S(1)}, bf16[1040,128]{1,0:T(8,128)(2,1)S(1)}, u32[]{:S(2)}, u32[]{:S(2)}) %collective-permute-start) | collective-permute-done | bytes 266272 | tf_op jit(solution)/shard_map/ppermute | solution.py:258
  4.0 0.2 join_cores.1
  4.2 2.9 %collective-permute-start.1 = (bf16[1040,128]{1,0:T(8,128)(2,1)S(1)}, bf16[1040,128]{1,0:T(8,128)(2,1)S(1)}, u32[]{:S(2)}, u32[]{:S(2)}) collective-permute-start(bf16[1040,128]{1,0:T(8,128)(2,1)S(1)} %get-tuple-element.15), channel_id=1, source_target_pairs={{0,2},{1,3},{2,0},{3,1},{4,6},{5,7},{6,4},{7,5},{8,10},{9,11},{10,... | collective-permute-start | bytes 798728 | tf_op jit(solution)/shard_map/ppermute | solution.py:267
  7.1 0.7 %collective-permute-start.4 = (bf16[1040,128]{1,0:T(8,128)(2,1)S(1)}, bf16[1040,128]{1,0:T(8,128)(2,1)S(1)}, u32[]{:S(2)}, u32[]{:S(2)}) collective-permute-start(bf16[1040,128]{1,0:T(8,128)(2,1)S(1)} %get-tuple-element.16), channel_id=1, source_target_pairs={{12,4},{1,9},{14,6},{3,11},{28,20},{17,25},{30,22},{19,27}} | collective-permute-start | bytes 798728 | tf_op jit(solution)/shard_map/ppermute | solution.py:248
  7.8 0.7 %collective-permute-start.5 = (bf16[1040,128]{1,0:T(8,128)(2,1)S(1)}, bf16[1040,128]{1,0:T(8,128)(2,1)S(1)}, u32[]{:S(2)}, u32[]{:S(2)}) collective-permute-start(bf16[1040,128]{1,0:T(8,128)(2,1)S(1)} %get-tuple-element.17), channel_id=1, source_target_pairs={{14,4},{3,9},{12,6},{1,11},{30,20},{19,25},{28,22},{17,27}} | collective-permute-start | bytes 798728 | tf_op jit(solution)/shard_map/ppermute | solution.py:248
  8.4 0.7 %collective-permute-start.3 = (bf16[1040,128]{1,0:T(8,128)(2,1)S(1)}, bf16[1040,128]{1,0:T(8,128)(2,1)S(1)}, u32[]{:S(2)}, u32[]{:S(2)}) collective-permute-start(bf16[1040,128]{1,0:T(8,128)(2,1)S(1)} %get-tuple-element.14.refs_0_), channel_id=1, source_target_pairs={{8,4},{5,9},{10,6},{7,11},{24,20},{21,25},{26,22},{23,27}} | collective-permute-start | bytes 798728 | tf_op jit(solution)/shard_map/ppermute | solution.py:248
  9.1 5.3 %collective-permute-start.2 = (bf16[1040,128]{1,0:T(8,128)(2,1)S(1)}, bf16[1040,128]{1,0:T(8,128)(2,1)S(1)}, u32[]{:S(2)}, u32[]{:S(2)}) collective-permute-start(bf16[1040,128]{1,0:T(8,128)(2,1)S(1)} %get-tuple-element.14.refs_0_), channel_id=1, source_target_pairs={{0,4},{13,9},{2,6},{15,11},{16,20},{29,25},{18,22},{31,27}} | collective-permute-start | bytes 798728 | tf_op jit(solution)/shard_map/ppermute | solution.py:248
  14.5 0.0 collective-permute-done.1.refs_1_
  14.5 0.7 %collective-permute-start.6 = (bf16[1040,128]{1,0:T(8,128)(2,1)S(1)}, bf16[1040,128]{1,0:T(8,128)(2,1)S(1)}, u32[]{:S(2)}, u32[]{:S(2)}) collective-permute-start(bf16[1040,128]{1,0:T(8,128)(2,1)S(1)} %collective-permute-done.1.refs_1_), channel_id=1, source_target_pairs={{8,4},{5,9},{10,6},{7,11},{24,20},{21,25},{26,22},{23,27}} | collective-permute-start | bytes 798728 | tf_op jit(solution)/shard_map/ppermute | solution.py:248
  15.2 0.0 collective-permute-done.4.refs_4_
  15.2 4.7 %collective-permute-start.7 = (bf16[1040,128]{1,0:T(8,128)(2,1)S(1)}, bf16[1040,128]{1,0:T(8,128)(2,1)S(1)}, u32[]{:S(2)}, u32[]{:S(2)}) collective-permute-start(bf16[1040,128]{1,0:T(8,128)(2,1)S(1)} %collective-permute-done.1.refs_1_), channel_id=1, source_target_pairs={{0,4},{13,9},{2,6},{15,11},{16,20},{29,25},{18,22},{31,27}} | collective-permute-start | bytes 798728 | tf_op jit(solution)/shard_map/ppermute | solution.py:248
  19.9 0.0 collective-permute-done.5.refs_5_
  19.9 0.0 collective-permute-done.3.refs_3_
  19.9 0.2 collective-permute-done.2.refs_2_
  20.1 0.0 collective-permute-done.6.refs_6_
  20.1 3.6 %collective-permute-done.7.refs_7_ = bf16[1040,128]{1,0:T(8,128)(2,1)S(1)} collective-permute-done((bf16[1040,128]{1,0:T(8,128)(2,1)S(1)}, bf16[1040,128]{1,0:T(8,128)(2,1)S(1)}, u32[]{:S(2)}, u32[]{:S(2)}) %collective-permute-start.7) | collective-permute-done | bytes 266272 | tf_op jit(solution)/shard_map/ppermute | solution.py:248
  23.8 12.0 %all_to_all.5.got_ref = f32[16,1,128]{2,1,0:T(1,128)S(1)} all-to-all(f32[16,1,128]{2,1,0:T(1,128)S(1)} %meet_7_8.1), channel_id=1, replica_groups=mesh['groups'=2,'blk'=4,'clus'=4] {'blk','clus'}, dimensions={0} | all-to-all | bytes 16384 | tf_op jit(solution)/shard_map/all_to_all | solution.py:291
  35.7 0.8 %home_scores.1 = f32[1,256]{1,0:T(1,128)} custom-call(f32[16,1,128]{2,1,0:T(1,128)S(1)} %all_to_all.5.got_ref, s32[1,256]{1,0:T(1,128)S(1)} %get-tuple-element.18.target_ref), custom_call_target="tpu_custom_call" | custom-call | tf_op jit(solution)/shard_map/home_scores/pallas_call | solution.py:292
  (3 shorter events, 0.0 us)
Async XLA Ops:
  0.0 0.7 %copy-start.2 = (s32[256]{0:T(256)S(1)}, s32[256]{0:T(256)}, u32[]{:S(2)}) copy-start(s32[256]{0:T(256)} %param.5) | copy-start | bytes 3076
  0.0 0.7 %copy-start.1 = (s32[256]{0:T(256)S(1)}, s32[256]{0:T(256)}, u32[]{:S(2)}) copy-start(s32[256]{0:T(256)} %param.4) | copy-start | bytes 3076
  0.7 1.0 %copy-start = (bf16[256,1024]{1,0:T(8,128)(2,1)S(1)}, bf16[256,1024]{1,0:T(8,128)(2,1)}, u32[]{:S(2)}) copy-start(bf16[256,1024]{1,0:T(8,128)(2,1)} %emb_ref.1) | copy-start | bytes 1572868
  2.3 1.7 %collective-permute-start = (bf16[1040,128]{1,0:T(8,128)(2,1)S(1)}, bf16[1040,128]{1,0:T(8,128)(2,1)S(1)}, u32[]{:S(2)}, u32[]{:S(2)}) collective-permute-start(bf16[1040,128]{1,0:T(8,128)(2,1)S(1)} %get-tuple-element.13), channel_id=1, source_target_pairs={{0,1},{1,0},{2,3},{3,2},{4,5},{5,4},{6,7},{7,6},{8,9},{9,8},{10,11... | collective-permute-start | bytes 798728 | tf_op jit(solution)/shard_map/ppermute | solution.py:258
  4.2 10.3 %collective-permute-start.1 = (bf16[1040,128]{1,0:T(8,128)(2,1)S(1)}, bf16[1040,128]{1,0:T(8,128)(2,1)S(1)}, u32[]{:S(2)}, u32[]{:S(2)}) collective-permute-start(bf16[1040,128]{1,0:T(8,128)(2,1)S(1)} %get-tuple-element.15), channel_id=1, source_target_pairs={{0,2},{1,3},{2,0},{3,1},{4,6},{5,7},{6,4},{7,5},{8,10},{9,11},{10,... | collective-permute-start | bytes 798728 | tf_op jit(solution)/shard_map/ppermute | solution.py:267
  7.1 8.1 %collective-permute-start.4 = (bf16[1040,128]{1,0:T(8,128)(2,1)S(1)}, bf16[1040,128]{1,0:T(8,128)(2,1)S(1)}, u32[]{:S(2)}, u32[]{:S(2)}) collective-permute-start(bf16[1040,128]{1,0:T(8,128)(2,1)S(1)} %get-tuple-element.16), channel_id=1, source_target_pairs={{12,4},{1,9},{14,6},{3,11},{28,20},{17,25},{30,22},{19,27}} | collective-permute-start | bytes 798728 | tf_op jit(solution)/shard_map/ppermute | solution.py:248
  7.8 12.1 %collective-permute-start.5 = (bf16[1040,128]{1,0:T(8,128)(2,1)S(1)}, bf16[1040,128]{1,0:T(8,128)(2,1)S(1)}, u32[]{:S(2)}, u32[]{:S(2)}) collective-permute-start(bf16[1040,128]{1,0:T(8,128)(2,1)S(1)} %get-tuple-element.17), channel_id=1, source_target_pairs={{14,4},{3,9},{12,6},{1,11},{30,20},{19,25},{28,22},{17,27}} | collective-permute-start | bytes 798728 | tf_op jit(solution)/shard_map/ppermute | solution.py:248
  8.4 11.4 %collective-permute-start.3 = (bf16[1040,128]{1,0:T(8,128)(2,1)S(1)}, bf16[1040,128]{1,0:T(8,128)(2,1)S(1)}, u32[]{:S(2)}, u32[]{:S(2)}) collective-permute-start(bf16[1040,128]{1,0:T(8,128)(2,1)S(1)} %get-tuple-element.14.refs_0_), channel_id=1, source_target_pairs={{8,4},{5,9},{10,6},{7,11},{24,20},{21,25},{26,22},{23,27}} | collective-permute-start | bytes 798728 | tf_op jit(solution)/shard_map/ppermute | solution.py:248
  9.1 11.0 %collective-permute-start.2 = (bf16[1040,128]{1,0:T(8,128)(2,1)S(1)}, bf16[1040,128]{1,0:T(8,128)(2,1)S(1)}, u32[]{:S(2)}, u32[]{:S(2)}) collective-permute-start(bf16[1040,128]{1,0:T(8,128)(2,1)S(1)} %get-tuple-element.14.refs_0_), channel_id=1, source_target_pairs={{0,4},{13,9},{2,6},{15,11},{16,20},{29,25},{18,22},{31,27}} | collective-permute-start | bytes 798728 | tf_op jit(solution)/shard_map/ppermute | solution.py:248
  14.5 5.6 %collective-permute-start.6 = (bf16[1040,128]{1,0:T(8,128)(2,1)S(1)}, bf16[1040,128]{1,0:T(8,128)(2,1)S(1)}, u32[]{:S(2)}, u32[]{:S(2)}) collective-permute-start(bf16[1040,128]{1,0:T(8,128)(2,1)S(1)} %collective-permute-done.1.refs_1_), channel_id=1, source_target_pairs={{8,4},{5,9},{10,6},{7,11},{24,20},{21,25},{26,22},{23,27}} | collective-permute-start | bytes 798728 | tf_op jit(solution)/shard_map/ppermute | solution.py:248
  15.2 8.6 %collective-permute-start.7 = (bf16[1040,128]{1,0:T(8,128)(2,1)S(1)}, bf16[1040,128]{1,0:T(8,128)(2,1)S(1)}, u32[]{:S(2)}, u32[]{:S(2)}) collective-permute-start(bf16[1040,128]{1,0:T(8,128)(2,1)S(1)} %collective-permute-done.1.refs_1_), channel_id=1, source_target_pairs={{0,4},{13,9},{2,6},{15,11},{16,20},{29,25},{18,22},{31,27}} | collective-permute-start | bytes 798728 | tf_op jit(solution)/shard_map/ppermute | solution.py:248

commit v8 on v7

--- a/solution.py
+++ b/solution.py
@@ -74,7 +74,7 @@
 
 NEAR, ACROSS, FAR = 0, 2, 3
 BLOCKS = (
-    (0, None), (1, None), (0, NEAR), (0, ACROSS), (0, FAR), (1, FAR), (1, ACROSS), (1, NEAR),
+    (0, None), (1, None), (0, FAR), (1, FAR), (0, NEAR), (0, ACROSS), (1, NEAR), (1, ACROSS),
 )
 
 
@@ -88,40 +88,37 @@
     return u, b
 
 
-def put_slabs(ref, start, rows):
+def put_slabs(ref, rows):
     for t in range(rows.shape[1] // 128):
-        ref[pl.ds(start + t * SLABS_ROWS, rows.shape[0]), :] = rows[:, t * 128 : (t + 1) * 128]
-
-
-def get_slabs(ref, start, count, slabs):
+        ref[t * SLABS_ROWS : (t + 1) * SLABS_ROWS, :] = rows[:, t * 128 : (t + 1) * 128]
+
+
+def get_slabs(ref):
+    slabs = (ref.shape[0] - 16) // SLABS_ROWS
     return jnp.concatenate(
-        [ref[t * SLABS_ROWS + start : t * SLABS_ROWS + start + count, :] for t in range(slabs)], axis=1
-    )
-
-
-def sort_kernel(emb_ref, cluster_ref, ids_ref, keep_ref, give_ref, target_ref):
+        [ref[t * SLABS_ROWS : (t + 1) * SLABS_ROWS, :] for t in range(slabs)], axis=1
+    )
+
+
+def sorted_rows(emb_ref, cluster_ref, ids_ref):
     rows, width = emb_ref.shape
-    slots = 4 * CAP
+    slots = 2 * CAP
     u, _ = here()
     cluster = cluster_ref[...]
-    slot = cluster ^ u
-    onehot = lax.broadcasted_iota(jnp.int32, (8, rows), 0) == slot
+    onehot = lax.broadcasted_iota(jnp.int32, (8, rows), 0) == cluster
     earlier = (
         lax.broadcasted_iota(jnp.int32, (rows, rows), 0)
         < lax.broadcasted_iota(jnp.int32, (rows, rows), 1)
     ).astype(jnp.bfloat16)
     before = jnp.dot(onehot.astype(jnp.bfloat16), earlier, preferred_element_type=jnp.float32)
     position = jnp.sum(jnp.where(onehot, before, 0.0), axis=0, keepdims=True).astype(jnp.int32)
-    target_ref[...] = cluster * CAP + position
-    order = (slot & 1) * 2 + (slot >> 1)
+    start = jnp.where(cluster == u, 0, jnp.where(cluster == u ^ 2, CAP, -4 * CAP))
     place = (
-        lax.broadcasted_iota(jnp.int32, (slots, rows), 0) == order * CAP + position
+        lax.broadcasted_iota(jnp.int32, (slots, rows), 0) == start + position
     ).astype(jnp.bfloat16)
     values = jnp.dot(place, emb_ref[...], preferred_element_type=jnp.float32)
     mean = jnp.mean(values * values, axis=1, keepdims=True)
     unit = (values * lax.rsqrt(mean + EPS) * width ** (-0.5)).astype(jnp.bfloat16)
-    put_slabs(keep_ref, 0, unit[: 2 * CAP])
-    put_slabs(give_ref, 0, unit[2 * CAP :])
     ids = ids_ref[...]
     row = lax.broadcasted_iota(jnp.int32, (16, rows), 0)
     parts = jnp.where(row == 0, ids >> 8, jnp.where(row == 1, ids & 255, 1))
@@ -132,57 +129,69 @@
         preferred_element_type=jnp.float32,
     )
     row = lax.broadcasted_iota(jnp.int32, (16, slots), 0)
-    moved = jnp.where((moved[2:3] == 0.0) & (row == 0), 256.0, moved).astype(jnp.bfloat16)
-    tail = width // 128 * SLABS_ROWS
-    keep_ref[tail : tail + 16, :] = moved[:, : 2 * CAP]
-    give_ref[tail : tail + 16, :] = moved[:, 2 * CAP :]
-
-
-def join_kernel(keep_ref, got_ref, *out_refs):
+    moved = jnp.where((moved[2:3] == 0.0) & (row == 0), 256.0, moved)
+    return unit, moved, cluster * CAP + position
+
+
+def sort_kernel(emb_ref, cluster_ref, ids_ref, keep_ref, target_ref):
+    unit, moved, target = sorted_rows(emb_ref, cluster_ref, ids_ref)
+    put_slabs(keep_ref, unit)
+    keep_ref[keep_ref.shape[0] - 16 :, :] = moved.astype(jnp.bfloat16)
+    target_ref[...] = target
+
+
+def join_kernel(keep_ref, emb_ref, cluster_ref, ids_ref, *out_refs):
+    unit, moved, _ = sorted_rows(emb_ref, cluster_ref, ids_ref)
     u, _ = here()
     core = lax.rem(u, 2)
     tail = keep_ref.shape[0] - 16
     own_at = pl.multiple_of(core * CAP, CAP)
     other_at = pl.multiple_of((1 - core) * CAP, CAP)
+    kept = keep_ref[tail:, :].astype(jnp.float32)
     for out_ref, start in zip(out_refs, (0, CAP) * 2):
         for t in range(tail // SLABS_ROWS):
             base = t * SLABS_ROWS
             out_ref[pl.ds(base + own_at, CAP), :] = keep_ref[base + start : base + start + CAP, :]
-            out_ref[pl.ds(base + other_at, CAP), :] = got_ref[base + start : base + start + CAP, :]
-        own = keep_ref[tail:, :].astype(jnp.float32)[:, start : start + CAP]
-        other = got_ref[tail:, :].astype(jnp.float32)[:, start : start + CAP]
-        first = jnp.where(core == 0, own, other)
-        second = jnp.where(core == 0, other, own)
-        out_ref[tail:, :] = jnp.concatenate([first, second], axis=1).astype(jnp.bfloat16)
+            out_ref[pl.ds(base + other_at, CAP), :] = unit[
+                start : start + CAP, t * 128 : (t + 1) * 128
+            ]
+        own = kept[:, start : start + CAP]
+        other = moved[:, start : start + CAP]
+        pieces = [jnp.where(core == 0, own, other), jnp.where(core == 0, other, own)]
+        out_ref[tail:, :] = jnp.concatenate(pieces, axis=1).astype(jnp.bfloat16)
 
 
 def take_in(refs, best, first, last):
     tail = refs[0].shape[0] - 16
-    slabs = tail // SLABS_ROWS
     ids_of = []
     for r in refs[:last]:
         parts = r[tail:, :].astype(jnp.float32)
         ids_of.append(parts[0:1] * 256.0 + parts[1:2])
     best = list(best)
-    for new in range(first, last):
-        rows = get_slabs(refs[new], 0, SLABS_ROWS, slabs)
-        down = jnp.broadcast_to(ids_of[new], (SLABS_ROWS, 128)).T
-        own = jnp.full((SLABS_ROWS, 128), -1.0, jnp.float32)
+
+    def pair(q):
+        return jnp.concatenate([get_slabs(refs[q]), get_slabs(refs[q + 1])], axis=0)
+
+    for new in range(first, last, 2):
+        rows = pair(new)
+        down = jnp.concatenate(
+            [jnp.broadcast_to(ids_of[q], (SLABS_ROWS, 128)).T for q in (new, new + 1)], axis=0
+        )
+        own = jnp.full((2 * SLABS_ROWS, 128), -1.0, jnp.float32)
         for start in range(0, new + 1, 2):
-            group = range(start, min(start + 2, new + 1))
-            others = jnp.concatenate(
-                [get_slabs(refs[q], 0, SLABS_ROWS, slabs) for q in group], axis=0
+            scores = lax.dot_general(
+                rows, pair(start), (((1,), (1,)), ((), ())), preferred_element_type=jnp.float32
             )
-            scores = lax.dot_general(
-                rows, others, (((1,), (1,)), ((), ())), preferred_element_type=jnp.float32
-            )
-            for n, q in enumerate(group):
+            for n in range(2):
+                q = start + n
                 part = scores[:, n * 128 : (n + 1) * 128]
                 own = jnp.maximum(own, jnp.where(ids_of[q] < down, part, -1.0))
-                if q != new:
+                if start != new:
                     theirs = jnp.where(down < ids_of[q], part, -1.0)
                     best[q] = jnp.maximum(best[q], jnp.max(theirs, axis=0, keepdims=True))
-        best.append(jnp.max(own.T, axis=0, keepdims=True))
+        for n in range(2):
+            side = own[n * SLABS_ROWS : (n + 1) * SLABS_ROWS]
+            best.append(jnp.max(side.T, axis=0, keepdims=True))
     return best
 
 
@@ -247,23 +256,28 @@
         ]
         return lax.ppermute(value, everyone, pairs)
 
-    keep, give, target = pl.pallas_call(
+    raw = (embeddings, cluster, row_ids)
+    swapped = [lax.ppermute(value, "clus", [(c, c ^ 1) for c in range(4)]) for value in raw]
+
+    def flat(values):
+        return [values[0], values[1].reshape(1, rows), values[2].reshape(1, rows)]
+
+    keep, target = pl.pallas_call(
         sort_kernel,
-        out_shape=[payload, payload, jax.ShapeDtypeStruct((1, rows), jnp.int32)],
+        out_shape=[payload, jax.ShapeDtypeStruct((1, rows), jnp.int32)],
         in_specs=[VMEM] * 3,
-        out_specs=[VMEM] * 3,
+        out_specs=[VMEM] * 2,
         compiler_params=SMALL,
         name="sort_rows",
-    )(embeddings, cluster.reshape(1, rows), row_ids.reshape(1, rows))
-    got = lax.ppermute(give, "clus", [(c, c ^ 1) for c in range(4)])
+    )(*flat(raw))
     near, direct, first, far = pl.pallas_call(
         join_kernel,
         out_shape=[payload] * 4,
-        in_specs=[VMEM] * 2,
+        in_specs=[VMEM] * 4,
         out_specs=[VMEM] * 4,
         compiler_params=SMALL,
         name="join_cores",
-    )(keep, got)
+    )(keep, *flat(swapped))
     crossed = lax.ppermute(far, "clus", [(c, c ^ 2) for c in range(4)])
     arrived = []
     for other, place in BLOCKS:
@@ -285,9 +299,9 @@
             name=f"meet_{first}_{last}",
         )(*arrived[:last], *known)
 
-    best = meeting(meet_kernel, 0, 6, [], (8, 128))
-    best = meeting(meet_kernel, 6, 7, [best], (8, 128))
-    best = meeting(last_meet_kernel, 7, 8, [best], (16, 1, 128))
+    best = meeting(meet_kernel, 0, 4, [], (8, 128))
+    best = meeting(meet_kernel, 4, 6, [best], (8, 128))
+    best = meeting(last_meet_kernel, 6, 8, [best], (16, 1, 128))
     returned = lax.all_to_all(best, everyone, split_axis=0, concat_axis=0, tiled=True)
     out = pl.pallas_call(
         home_kernel,

time: 36.8 us -> 35.3 us (0.959)
  waiting for transfers between devices: 5.05 us -> 3.87 us
  blocking collectives: 12 us -> 11.2 us
    ppermute x1 -> x3, waiting for transfers between devices: 1.17 us -> 0.01 us  [meet(): lax.ppermute(value, 'clus', [(c, c ^ 1) for c in range(4)])]
    all_to_all x1, blocking collectives: 12 us -> 11.2 us  [meet(): lax.all_to_all(best, everyone, split_axis=0, concat_axis=0, tiled=True)]
    ppermute x1 -> x3, starting transfers between devices: 0.52 us -> 0.96 us  [meet(): lax.ppermute(value, 'clus', [(c, c ^ 1) for c in range(4)])]
    ppermute x1, starting transfers between devices: 2.92 us -> 2.56 us  [meet(): crossed = lax.ppermute(far, 'clus', [(c, c ^ 2) for c in range(4)])]
  transfers between devices with their start and end apart: 8 -> 10, of which waited for: 3 -> 2; matrix products, arithmetic and copies ran while one was open for 0% -> 0% of each run, Pallas kernels for 0% -> 1%
where the time goes in v8:
time: 35.3 us; the launch traced here: 35.1 us
  starting transfers between devices  16.2 us (46%)
  blocking collectives  11.2 us (32%)
  waiting for transfers between devices  3.87 us (11%)
  Pallas kernels  1.89 us (5%)
  local copies, waits for them, and re-layouts  1.73 us (5%)
    ppermute x6, starting transfers between devices, to_meeting(): return lax.ppermute(value, everyone, pairs)  12.7 us
    all_to_all x1, blocking collectives, meet(): lax.all_to_all(best, everyone, split_axis=0, concat_axis=0, tiled=True)  11.2 us
    ppermute x6, waiting for transfers between devices, to_meeting(): return lax.ppermute(value, everyone, pairs)  3.86 us
    ppermute x1, starting transfers between devices, meet(): crossed = lax.ppermute(far, 'clus', [(c, c ^ 2) for c in range(4)])  2.56 us
    unnamed x6, local copies, waits for them, and re-layouts  1.73 us
    ppermute x3, starting transfers between devices, meet(): lax.ppermute(value, 'clus', [(c, c ^ 1) for c in range(4)])  0.96 us
    pallas_call x1, Pallas kernels, meet(): pl.pallas_call(home_kernel, out_shape=jax.ShapeDtypeStruct((1, rows), jnp...  0.83 us
  transfers between devices with their start and end apart: 10, of which 2 were waited for; matrix products, arithmetic and copies ran while one was open for 0% of the time, Pallas kernels for 1%

profile of v8, /device:TPU:0, one launch (start us, length us, event | category | flops | bytes accessed | tf_op | source)
XLA Modules:
  0.0 35.1 jit_solution(7713703048314462527)
XLA Ops:
  0.0 0.5 %collective-permute-start = (bf16[256,1024]{1,0:T(8,128)(2,1)}, bf16[256,1024]{1,0:T(8,128)(2,1)S(1)}, u32[]{:S(2)}, u32[]{:S(2)}) collective-permute-start(bf16[256,1024]{1,0:T(8,128)(2,1)} %emb_ref.1), channel_id=1, source_target_pairs={{0,1},{1,0},{2,3},{3,2},{4,5},{5,4},{6,7},{7,6},{8,9},{9,8},{10,11... | collective-permute-start | bytes 1572872 | tf_op jit(solution)/shard_map/ppermute | solution.py:260
  0.5 0.1 collective-permute-start.1
  0.5 0.5 %collective-permute-start.2 = (s32[256]{0:T(256)}, s32[256]{0:T(256)S(1)}, u32[]{:S(2)}, u32[]{:S(2)}) collective-permute-start(s32[256]{0:T(256)} %param.5), channel_id=1, source_target_pairs={{0,1},{1,0},{2,3},{3,2},{4,5},{5,4},{6,7},{7,6},{8,9},{9,8},{10,11... | collective-permute-start | bytes 3080 | tf_op jit(solution)/shard_map/ppermute | solution.py:260
  1.0 0.0 copy-start.2
  1.0 0.0 copy-start.1
  1.0 0.7 %copy-done.2 = s32[256]{0:T(256)S(1)} copy-done((s32[256]{0:T(256)S(1)}, s32[256]{0:T(256)}, u32[]{:S(2)}) %copy-start.2) | copy-done | bytes 1048
  1.6 0.0 copy-done.1
  1.7 0.0 copy-start
  1.7 1.0 %copy-done = bf16[256,1024]{1,0:T(8,128)(2,1)S(1)} copy-done((bf16[256,1024]{1,0:T(8,128)(2,1)S(1)}, bf16[256,1024]{1,0:T(8,128)(2,1)}, u32[]{:S(2)}) %copy-start) | copy-done | bytes 524312
  2.7 0.5 %sort_rows.1 = (bf16[1040,128]{1,0:T(8,128)(2,1)S(1)}, s32[1,256]{1,0:T(1,128)S(1)}) custom-call(bf16[256,1024]{1,0:T(8,128)(2,1)S(1)} %copy-done, s32[1,256]{1,0:T(1,128)S(1)} %bitcast.5, s32[1,256]{1,0:T(1,128)S(1)} %bitcast.6), custom_call_target="tpu_custom_call" | custom-call | tf_op jit(solution)/shard_map/sort_rows/pallas_call | solution.py:265
  3.2 0.0 collective-permute-done.1
  3.2 0.0 collective-permute-done.2
  3.2 0.0 collective-permute-done.emb_ref
  3.2 0.6 %join_cores.1 = (bf16[1040,128]{1,0:T(8,128)(2,1)S(1)}, bf16[1040,128]{1,0:T(8,128)(2,1)S(1)}, bf16[1040,128]{1,0:T(8,128)(2,1)S(1)}, bf16[1040,128]{1,0:T(8,128)(2,1)S(1)}) custom-call(bf16[1040,128]{1,0:T(8,128)(2,1)S(1)} %get-tuple-element.11.keep_ref, bf16[256,1024]{1,0:T(8,128)(2,1)S(1)} %collective-permute-done.emb_ref, s32[1,256]{1,0:T(1,128)S(1)} %bitcast.7, ...), custom_call_target="tpu_custom_call" | custom-call | tf_op jit(solution)/shard_map/join_cores/pallas_call | solution.py:273
  3.8 2.6 %collective-permute-start.3 = (bf16[1040,128]{1,0:T(8,128)(2,1)S(1)}, bf16[1040,128]{1,0:T(8,128)(2,1)S(1)}, u32[]{:S(2)}, u32[]{:S(2)}) collective-permute-start(bf16[1040,128]{1,0:T(8,128)(2,1)S(1)} %get-tuple-element.13), channel_id=1, source_target_pairs={{0,2},{1,3},{2,0},{3,1},{4,6},{5,7},{6,4},{7,5},{8,10},{9,11},{10,... | collective-permute-start | bytes 798728 | tf_op jit(solution)/shard_map/ppermute | solution.py:281
  6.3 0.7 %collective-permute-start.4 = (bf16[1040,128]{1,0:T(8,128)(2,1)S(1)}, bf16[1040,128]{1,0:T(8,128)(2,1)S(1)}, u32[]{:S(2)}, u32[]{:S(2)}) collective-permute-start(bf16[1040,128]{1,0:T(8,128)(2,1)S(1)} %get-tuple-element.14), channel_id=1, source_target_pairs={{12,4},{1,9},{14,6},{3,11},{28,20},{17,25},{30,22},{19,27}} | collective-permute-start | bytes 798728 | tf_op jit(solution)/shard_map/ppermute | solution.py:257
  7.0 0.7 %collective-permute-start.5 = (bf16[1040,128]{1,0:T(8,128)(2,1)S(1)}, bf16[1040,128]{1,0:T(8,128)(2,1)S(1)}, u32[]{:S(2)}, u32[]{:S(2)}) collective-permute-start(bf16[1040,128]{1,0:T(8,128)(2,1)S(1)} %get-tuple-element.15), channel_id=1, source_target_pairs={{14,4},{3,9},{12,6},{1,11},{30,20},{19,25},{28,22},{17,27}} | collective-permute-start | bytes 798728 | tf_op jit(solution)/shard_map/ppermute | solution.py:257
  7.7 0.7 %collective-permute-start.7 = (bf16[1040,128]{1,0:T(8,128)(2,1)S(1)}, bf16[1040,128]{1,0:T(8,128)(2,1)S(1)}, u32[]{:S(2)}, u32[]{:S(2)}) collective-permute-start(bf16[1040,128]{1,0:T(8,128)(2,1)S(1)} %get-tuple-element.12.refs_0_), channel_id=1, source_target_pairs={{8,4},{5,9},{10,6},{7,11},{24,20},{21,25},{26,22},{23,27}} | collective-permute-start | bytes 798728 | tf_op jit(solution)/shard_map/ppermute | solution.py:257
  8.4 5.3 %collective-permute-start.6 = (bf16[1040,128]{1,0:T(8,128)(2,1)S(1)}, bf16[1040,128]{1,0:T(8,128)(2,1)S(1)}, u32[]{:S(2)}, u32[]{:S(2)}) collective-permute-start(bf16[1040,128]{1,0:T(8,128)(2,1)S(1)} %get-tuple-element.12.refs_0_), channel_id=1, source_target_pairs={{0,4},{13,9},{2,6},{15,11},{16,20},{29,25},{18,22},{31,27}} | collective-permute-start | bytes 798728 | tf_op jit(solution)/shard_map/ppermute | solution.py:257
  13.7 0.0 collective-permute-done.3.refs_1_
  13.7 0.7 %collective-permute-start.9 = (bf16[1040,128]{1,0:T(8,128)(2,1)S(1)}, bf16[1040,128]{1,0:T(8,128)(2,1)S(1)}, u32[]{:S(2)}, u32[]{:S(2)}) collective-permute-start(bf16[1040,128]{1,0:T(8,128)(2,1)S(1)} %collective-permute-done.3.refs_1_), channel_id=1, source_target_pairs={{8,4},{5,9},{10,6},{7,11},{24,20},{21,25},{26,22},{23,27}} | collective-permute-start | bytes 798728 | tf_op jit(solution)/shard_map/ppermute | solution.py:257
  14.4 0.0 collective-permute-done.4.refs_2_
  14.4 4.7 %collective-permute-start.8 = (bf16[1040,128]{1,0:T(8,128)(2,1)S(1)}, bf16[1040,128]{1,0:T(8,128)(2,1)S(1)}, u32[]{:S(2)}, u32[]{:S(2)}) collective-permute-start(bf16[1040,128]{1,0:T(8,128)(2,1)S(1)} %collective-permute-done.3.refs_1_), channel_id=1, source_target_pairs={{0,4},{13,9},{2,6},{15,11},{16,20},{29,25},{18,22},{31,27}} | collective-permute-start | bytes 798728 | tf_op jit(solution)/shard_map/ppermute | solution.py:257
  19.1 0.0 collective-permute-done.5.refs_3_
  19.2 0.0 collective-permute-done.7.refs_5_
  19.2 0.6 %collective-permute-done.6.refs_4_ = bf16[1040,128]{1,0:T(8,128)(2,1)S(1)} collective-permute-done((bf16[1040,128]{1,0:T(8,128)(2,1)S(1)}, bf16[1040,128]{1,0:T(8,128)(2,1)S(1)}, u32[]{:S(2)}, u32[]{:S(2)}) %collective-permute-start.6) | collective-permute-done | bytes 266272 | tf_op jit(solution)/shard_map/ppermute | solution.py:257
  19.8 0.0 collective-permute-done.9.refs_7_
  19.8 3.3 %collective-permute-done.8.refs_6_ = bf16[1040,128]{1,0:T(8,128)(2,1)S(1)} collective-permute-done((bf16[1040,128]{1,0:T(8,128)(2,1)S(1)}, bf16[1040,128]{1,0:T(8,128)(2,1)S(1)}, u32[]{:S(2)}, u32[]{:S(2)}) %collective-permute-start.8) | collective-permute-done | bytes 266272 | tf_op jit(solution)/shard_map/ppermute | solution.py:257
  23.0 11.2 %all_to_all.5.got_ref = f32[16,1,128]{2,1,0:T(1,128)S(1)} all-to-all(f32[16,1,128]{2,1,0:T(1,128)S(1)} %meet_6_8.1), channel_id=1, replica_groups=mesh['groups'=2,'blk'=4,'clus'=4] {'blk','clus'}, dimensions={0} | all-to-all | bytes 16384 | tf_op jit(solution)/shard_map/all_to_all | solution.py:305
  34.2 0.8 %home_scores.1 = f32[1,256]{1,0:T(1,128)} custom-call(f32[16,1,128]{2,1,0:T(1,128)S(1)} %all_to_all.5.got_ref, s32[1,256]{1,0:T(1,128)S(1)} %get-tuple-element.16.target_ref), custom_call_target="tpu_custom_call" | custom-call | tf_op jit(solution)/shard_map/home_scores/pallas_call | solution.py:306
  (3 shorter events, 0.0 us)
Async XLA Ops:
  0.0 3.2 %collective-permute-start = (bf16[256,1024]{1,0:T(8,128)(2,1)}, bf16[256,1024]{1,0:T(8,128)(2,1)S(1)}, u32[]{:S(2)}, u32[]{:S(2)}) collective-permute-start(bf16[256,1024]{1,0:T(8,128)(2,1)} %emb_ref.1), channel_id=1, source_target_pairs={{0,1},{1,0},{2,3},{3,2},{4,5},{5,4},{6,7},{7,6},{8,9},{9,8},{10,11... | collective-permute-start | bytes 1572872 | tf_op jit(solution)/shard_map/ppermute | solution.py:260
  0.5 2.7 %collective-permute-start.1 = (s32[256]{0:T(256)}, s32[256]{0:T(256)S(1)}, u32[]{:S(2)}, u32[]{:S(2)}) collective-permute-start(s32[256]{0:T(256)} %param.4), channel_id=1, source_target_pairs={{0,1},{1,0},{2,3},{3,2},{4,5},{5,4},{6,7},{7,6},{8,9},{9,8},{10,11... | collective-permute-start | bytes 3080 | tf_op jit(solution)/shard_map/ppermute | solution.py:260
  0.5 2.7 %collective-permute-start.2 = (s32[256]{0:T(256)}, s32[256]{0:T(256)S(1)}, u32[]{:S(2)}, u32[]{:S(2)}) collective-permute-start(s32[256]{0:T(256)} %param.5), channel_id=1, source_target_pairs={{0,1},{1,0},{2,3},{3,2},{4,5},{5,4},{6,7},{7,6},{8,9},{9,8},{10,11... | collective-permute-start | bytes 3080 | tf_op jit(solution)/shard_map/ppermute | solution.py:260
  1.0 0.7 %copy-start.2 = (s32[256]{0:T(256)S(1)}, s32[256]{0:T(256)}, u32[]{:S(2)}) copy-start(s32[256]{0:T(256)} %param.5) | copy-start | bytes 3076
  1.0 0.7 %copy-start.1 = (s32[256]{0:T(256)S(1)}, s32[256]{0:T(256)}, u32[]{:S(2)}) copy-start(s32[256]{0:T(256)} %param.4) | copy-start | bytes 3076
  1.7 1.0 %copy-start = (bf16[256,1024]{1,0:T(8,128)(2,1)S(1)}, bf16[256,1024]{1,0:T(8,128)(2,1)}, u32[]{:S(2)}) copy-start(bf16[256,1024]{1,0:T(8,128)(2,1)} %emb_ref.1) | copy-start | bytes 1572868
  3.8 9.9 %collective-permute-start.3 = (bf16[1040,128]{1,0:T(8,128)(2,1)S(1)}, bf16[1040,128]{1,0:T(8,128)(2,1)S(1)}, u32[]{:S(2)}, u32[]{:S(2)}) collective-permute-start(bf16[1040,128]{1,0:T(8,128)(2,1)S(1)} %get-tuple-element.13), channel_id=1, source_target_pairs={{0,2},{1,3},{2,0},{3,1},{4,6},{5,7},{6,4},{7,5},{8,10},{9,11},{10,... | collective-permute-start | bytes 798728 | tf_op jit(solution)/shard_map/ppermute | solution.py:281
  6.3 8.1 %collective-permute-start.4 = (bf16[1040,128]{1,0:T(8,128)(2,1)S(1)}, bf16[1040,128]{1,0:T(8,128)(2,1)S(1)}, u32[]{:S(2)}, u32[]{:S(2)}) collective-permute-start(bf16[1040,128]{1,0:T(8,128)(2,1)S(1)} %get-tuple-element.14), channel_id=1, source_target_pairs={{12,4},{1,9},{14,6},{3,11},{28,20},{17,25},{30,22},{19,27}} | collective-permute-start | bytes 798728 | tf_op jit(solution)/shard_map/ppermute | solution.py:257
  7.0 12.1 %collective-permute-start.5 = (bf16[1040,128]{1,0:T(8,128)(2,1)S(1)}, bf16[1040,128]{1,0:T(8,128)(2,1)S(1)}, u32[]{:S(2)}, u32[]{:S(2)}) collective-permute-start(bf16[1040,128]{1,0:T(8,128)(2,1)S(1)} %get-tuple-element.15), channel_id=1, source_target_pairs={{14,4},{3,9},{12,6},{1,11},{30,20},{19,25},{28,22},{17,27}} | collective-permute-start | bytes 798728 | tf_op jit(solution)/shard_map/ppermute | solution.py:257
  7.7 11.5 %collective-permute-start.7 = (bf16[1040,128]{1,0:T(8,128)(2,1)S(1)}, bf16[1040,128]{1,0:T(8,128)(2,1)S(1)}, u32[]{:S(2)}, u32[]{:S(2)}) collective-permute-start(bf16[1040,128]{1,0:T(8,128)(2,1)S(1)} %get-tuple-element.12.refs_0_), channel_id=1, source_target_pairs={{8,4},{5,9},{10,6},{7,11},{24,20},{21,25},{26,22},{23,27}} | collective-permute-start | bytes 798728 | tf_op jit(solution)/shard_map/ppermute | solution.py:257
  8.4 11.4 %collective-permute-start.6 = (bf16[1040,128]{1,0:T(8,128)(2,1)S(1)}, bf16[1040,128]{1,0:T(8,128)(2,1)S(1)}, u32[]{:S(2)}, u32[]{:S(2)}) collective-permute-start(bf16[1040,128]{1,0:T(8,128)(2,1)S(1)} %get-tuple-element.12.refs_0_), channel_id=1, source_target_pairs={{0,4},{13,9},{2,6},{15,11},{16,20},{29,25},{18,22},{31,27}} | collective-permute-start | bytes 798728 | tf_op jit(solution)/shard_map/ppermute | solution.py:257
  13.7 6.0 %collective-permute-start.9 = (bf16[1040,128]{1,0:T(8,128)(2,1)S(1)}, bf16[1040,128]{1,0:T(8,128)(2,1)S(1)}, u32[]{:S(2)}, u32[]{:S(2)}) collective-permute-start(bf16[1040,128]{1,0:T(8,128)(2,1)S(1)} %collective-permute-done.3.refs_1_), channel_id=1, source_target_pairs={{8,4},{5,9},{10,6},{7,11},{24,20},{21,25},{26,22},{23,27}} | collective-permute-start | bytes 798728 | tf_op jit(solution)/shard_map/ppermute | solution.py:257
  14.4 8.6 %collective-permute-start.8 = (bf16[1040,128]{1,0:T(8,128)(2,1)S(1)}, bf16[1040,128]{1,0:T(8,128)(2,1)S(1)}, u32[]{:S(2)}, u32[]{:S(2)}) collective-permute-start(bf16[1040,128]{1,0:T(8,128)(2,1)S(1)} %collective-permute-done.3.refs_1_), channel_id=1, source_target_pairs={{0,4},{13,9},{2,6},{15,11},{16,20},{29,25},{18,22},{31,27}} | collective-permute-start | bytes 798728 | tf_op jit(solution)/shard_map/ppermute | solution.py:257

commit v9 on v8

--- a/solution.py
+++ b/solution.py
@@ -74,7 +74,7 @@
 
 NEAR, ACROSS, FAR = 0, 2, 3
 BLOCKS = (
-    (0, None), (1, None), (0, FAR), (1, FAR), (0, NEAR), (0, ACROSS), (1, NEAR), (1, ACROSS),
+    (0, None), (0, FAR), (1, FAR), (1, None), (0, NEAR), (0, ACROSS), (1, NEAR), (1, ACROSS),
 )
 
 
@@ -222,6 +222,10 @@
                 best_ref[at_blk * 4 + chip * 2 + c] = row
 
 
+def after_kernel(_, value_ref, out_ref):
+    pass
+
+
 def home_kernel(got_ref, target_ref, out_ref):
     u, _ = here()
     core = lax.rem(u, 2)
@@ -279,16 +283,6 @@
         name="join_cores",
     )(keep, *flat(swapped))
     crossed = lax.ppermute(far, "clus", [(c, c ^ 2) for c in range(4)])
-    arrived = []
-    for other, place in BLOCKS:
-        if other and place == FAR:
-            arrived.append(to_meeting(direct, place, cross=1))
-        elif not other and place == FAR:
-            arrived.append(to_meeting(first, place))
-        else:
-            value = crossed if other else near
-            arrived.append(value if place is None else to_meeting(value, place))
-
     def meeting(kernel, first, last, known, shape):
         return pl.pallas_call(
             functools.partial(kernel, first, last),
@@ -299,7 +293,21 @@
             name=f"meet_{first}_{last}",
         )(*arrived[:last], *known)
 
-    best = meeting(meet_kernel, 0, 4, [], (8, 128))
+    arrived = [near, to_meeting(first, FAR)]
+    best = meeting(meet_kernel, 0, 2, [], (8, 128))
+    crossed = pl.pallas_call(
+        after_kernel,
+        out_shape=payload,
+        in_specs=[pl.BlockSpec(memory_space=pl.ANY)] * 2,
+        out_specs=pl.BlockSpec(memory_space=pl.ANY),
+        input_output_aliases={1: 0},
+        compiler_params=SMALL,
+        name="after_far",
+    )(best, crossed)
+    arrived += [to_meeting(direct, FAR, cross=1), crossed]
+    arrived += [to_meeting(near, NEAR), to_meeting(near, ACROSS)]
+    arrived += [to_meeting(crossed, NEAR), to_meeting(crossed, ACROSS)]
+    best = meeting(meet_kernel, 2, 4, [best], (8, 128))
     best = meeting(meet_kernel, 4, 6, [best], (8, 128))
     best = meeting(last_meet_kernel, 6, 8, [best], (16, 1, 128))
     returned = lax.all_to_all(best, everyone, split_axis=0, concat_axis=0, tiled=True)

time: 35.3 us -> 36.4 us (1.031)
  blocking collectives: 11.2 us -> 12 us
    all_to_all x1, blocking collectives: 11.2 us -> 12 us  [meet(): lax.all_to_all(best, everyone, split_axis=0, concat_axis=0, tiled=True)]
  transfers between devices with their start and end apart: 10 -> 10, of which waited for: 2 -> 1; matrix products, arithmetic and copies ran while one was open for 0% -> 0% of each run, Pallas kernels for 1% -> 1%
where the time goes in v9:
time: 36.4 us; the launch traced here: 36.1 us
  starting transfers between devices  16.4 us (45%)
  blocking collectives  12 us (33%)
  waiting for transfers between devices  3.83 us (11%)
  Pallas kernels  1.92 us (5%)
  local copies, waits for them, and re-layouts  1.73 us (5%)
    ppermute x6, starting transfers between devices, to_meeting(): return lax.ppermute(value, everyone, pairs)  12.9 us
    all_to_all x1, blocking collectives, meet(): lax.all_to_all(best, everyone, split_axis=0, concat_axis=0, tiled=True)  12 us
    ppermute x6, waiting for transfers between devices, to_meeting(): return lax.ppermute(value, everyone, pairs)  3.82 us
    ppermute x1, starting transfers between devices, meet(): crossed = lax.ppermute(far, 'clus', [(c, c ^ 2) for c in range(4)])  2.56 us
    unnamed x6, local copies, waits for them, and re-layouts  1.73 us
    ppermute x3, starting transfers between devices, meet(): lax.ppermute(value, 'clus', [(c, c ^ 1) for c in range(4)])  0.96 us
    pallas_call x1, Pallas kernels, meet(): pl.pallas_call(home_kernel, out_shape=jax.ShapeDtypeStruct((1, rows), jnp...  0.83 us
  transfers between devices with their start and end apart: 10, of which 1 were waited for; matrix products, arithmetic and copies ran while one was open for 0% of the time, Pallas kernels for 1%

profile of v9, /device:TPU:0, one launch (start us, length us, event | category | flops | bytes accessed | tf_op | source)
XLA Modules:
  0.0 36.1 jit_solution(16748386996192712009)
XLA Ops:
  0.0 0.5 %collective-permute-start = (bf16[256,1024]{1,0:T(8,128)(2,1)}, bf16[256,1024]{1,0:T(8,128)(2,1)S(1)}, u32[]{:S(2)}, u32[]{:S(2)}) collective-permute-start(bf16[256,1024]{1,0:T(8,128)(2,1)} %emb_ref.1), channel_id=1, source_target_pairs={{0,1},{1,0},{2,3},{3,2},{4,5},{5,4},{6,7},{7,6},{8,9},{9,8},{10,11... | collective-permute-start | bytes 1572872 | tf_op jit(solution)/shard_map/ppermute | solution.py:264
  0.5 0.1 collective-permute-start.1
  0.5 0.5 %collective-permute-start.2 = (s32[256]{0:T(256)}, s32[256]{0:T(256)S(1)}, u32[]{:S(2)}, u32[]{:S(2)}) collective-permute-start(s32[256]{0:T(256)} %param.5), channel_id=1, source_target_pairs={{0,1},{1,0},{2,3},{3,2},{4,5},{5,4},{6,7},{7,6},{8,9},{9,8},{10,11... | collective-permute-start | bytes 3080 | tf_op jit(solution)/shard_map/ppermute | solution.py:264
  1.0 0.0 copy-start.2
  1.0 0.0 copy-start.1
  1.0 0.7 %copy-done.2 = s32[256]{0:T(256)S(1)} copy-done((s32[256]{0:T(256)S(1)}, s32[256]{0:T(256)}, u32[]{:S(2)}) %copy-start.2) | copy-done | bytes 1048
  1.6 0.0 copy-done.1
  1.7 0.0 copy-start
  1.7 1.0 %copy-done = bf16[256,1024]{1,0:T(8,128)(2,1)S(1)} copy-done((bf16[256,1024]{1,0:T(8,128)(2,1)S(1)}, bf16[256,1024]{1,0:T(8,128)(2,1)}, u32[]{:S(2)}) %copy-start) | copy-done | bytes 524312
  2.7 0.5 %sort_rows.1 = (bf16[1040,128]{1,0:T(8,128)(2,1)S(1)}, s32[1,256]{1,0:T(1,128)S(1)}) custom-call(bf16[256,1024]{1,0:T(8,128)(2,1)S(1)} %copy-done, s32[1,256]{1,0:T(1,128)S(1)} %bitcast.5, s32[1,256]{1,0:T(1,128)S(1)} %bitcast.6), custom_call_target="tpu_custom_call" | custom-call | tf_op jit(solution)/shard_map/sort_rows/pallas_call | solution.py:269
  3.2 0.0 collective-permute-done.1
  3.2 0.0 collective-permute-done.2
  3.2 0.0 collective-permute-done.emb_ref
  3.2 0.6 %join_cores.1 = (bf16[1040,128]{1,0:T(8,128)(2,1)S(1)}, bf16[1040,128]{1,0:T(8,128)(2,1)S(1)}, bf16[1040,128]{1,0:T(8,128)(2,1)S(1)}, bf16[1040,128]{1,0:T(8,128)(2,1)S(1)}) custom-call(bf16[1040,128]{1,0:T(8,128)(2,1)S(1)} %get-tuple-element.11.keep_ref, bf16[256,1024]{1,0:T(8,128)(2,1)S(1)} %collective-permute-done.emb_ref, s32[1,256]{1,0:T(1,128)S(1)} %bitcast.7, ...), custom_call_target="tpu_custom_call" | custom-call | tf_op jit(solution)/shard_map/join_cores/pallas_call | solution.py:277
  3.8 0.7 %collective-permute-start.3 = (bf16[1040,128]{1,0:T(8,128)(2,1)S(1)}, bf16[1040,128]{1,0:T(8,128)(2,1)S(1)}, u32[]{:S(2)}, u32[]{:S(2)}) collective-permute-start(bf16[1040,128]{1,0:T(8,128)(2,1)S(1)} %get-tuple-element.13), channel_id=1, source_target_pairs={{12,4},{1,9},{14,6},{3,11},{28,20},{17,25},{30,22},{19,27}} | collective-permute-start | bytes 798728 | tf_op jit(solution)/shard_map/ppermute | solution.py:261
  4.5 2.6 %collective-permute-start.5 = (bf16[1040,128]{1,0:T(8,128)(2,1)S(1)}, bf16[1040,128]{1,0:T(8,128)(2,1)S(1)}, u32[]{:S(2)}, u32[]{:S(2)}) collective-permute-start(bf16[1040,128]{1,0:T(8,128)(2,1)S(1)} %get-tuple-element.15), channel_id=1, source_target_pairs={{0,2},{1,3},{2,0},{3,1},{4,6},{5,7},{6,4},{7,5},{8,10},{9,11},{10,... | collective-permute-start | bytes 798728 | tf_op jit(solution)/shard_map/ppermute | solution.py:285
  7.0 0.7 %collective-permute-start.7 = (bf16[1040,128]{1,0:T(8,128)(2,1)S(1)}, bf16[1040,128]{1,0:T(8,128)(2,1)S(1)}, u32[]{:S(2)}, u32[]{:S(2)}) collective-permute-start(bf16[1040,128]{1,0:T(8,128)(2,1)S(1)} %get-tuple-element.12.refs_0_), channel_id=1, source_target_pairs={{8,4},{5,9},{10,6},{7,11},{24,20},{21,25},{26,22},{23,27}} | collective-permute-start | bytes 798728 | tf_op jit(solution)/shard_map/ppermute | solution.py:261
  7.7 4.7 %collective-permute-start.6 = (bf16[1040,128]{1,0:T(8,128)(2,1)S(1)}, bf16[1040,128]{1,0:T(8,128)(2,1)S(1)}, u32[]{:S(2)}, u32[]{:S(2)}) collective-permute-start(bf16[1040,128]{1,0:T(8,128)(2,1)S(1)} %get-tuple-element.12.refs_0_), channel_id=1, source_target_pairs={{0,4},{13,9},{2,6},{15,11},{16,20},{29,25},{18,22},{31,27}} | collective-permute-start | bytes 798728 | tf_op jit(solution)/shard_map/ppermute | solution.py:261
  12.4 0.7 %collective-permute-start.4 = (bf16[1040,128]{1,0:T(8,128)(2,1)S(1)}, bf16[1040,128]{1,0:T(8,128)(2,1)S(1)}, u32[]{:S(2)}, u32[]{:S(2)}) collective-permute-start(bf16[1040,128]{1,0:T(8,128)(2,1)S(1)} %get-tuple-element.14), channel_id=1, source_target_pairs={{14,4},{3,9},{12,6},{1,11},{30,20},{19,25},{28,22},{17,27}} | collective-permute-start | bytes 798728 | tf_op jit(solution)/shard_map/ppermute | solution.py:261
  13.1 0.0 collective-permute-done.3.refs_1_
  13.2 0.0 collective-permute-done.5.value_ref
  13.2 0.7 %collective-permute-start.9 = (bf16[1040,128]{1,0:T(8,128)(2,1)S(1)}, bf16[1040,128]{1,0:T(8,128)(2,1)S(1)}, u32[]{:S(2)}, u32[]{:S(2)}) collective-permute-start(bf16[1040,128]{1,0:T(8,128)(2,1)S(1)} %after_far.1.refs_3_), channel_id=1, source_target_pairs={{8,4},{5,9},{10,6},{7,11},{24,20},{21,25},{26,22},{23,27}} | collective-permute-start | bytes 798728 | tf_op jit(solution)/shard_map/ppermute | solution.py:261
  13.9 5.5 %collective-permute-start.8 = (bf16[1040,128]{1,0:T(8,128)(2,1)S(1)}, bf16[1040,128]{1,0:T(8,128)(2,1)S(1)}, u32[]{:S(2)}, u32[]{:S(2)}) collective-permute-start(bf16[1040,128]{1,0:T(8,128)(2,1)S(1)} %after_far.1.refs_3_), channel_id=1, source_target_pairs={{0,4},{13,9},{2,6},{15,11},{16,20},{29,25},{18,22},{31,27}} | collective-permute-start | bytes 798728 | tf_op jit(solution)/shard_map/ppermute | solution.py:261
  19.3 0.0 collective-permute-done.4.refs_2_
  19.4 0.0 collective-permute-done.7.refs_5_
  19.4 0.0 collective-permute-done.6.refs_4_
  19.4 0.0 collective-permute-done.9.refs_7_
  19.4 3.8 %collective-permute-done.8.refs_6_ = bf16[1040,128]{1,0:T(8,128)(2,1)S(1)} collective-permute-done((bf16[1040,128]{1,0:T(8,128)(2,1)S(1)}, bf16[1040,128]{1,0:T(8,128)(2,1)S(1)}, u32[]{:S(2)}, u32[]{:S(2)}) %collective-permute-start.8) | collective-permute-done | bytes 266272 | tf_op jit(solution)/shard_map/ppermute | solution.py:261
  23.2 12.0 %all_to_all.5.got_ref = f32[16,1,128]{2,1,0:T(1,128)S(1)} all-to-all(f32[16,1,128]{2,1,0:T(1,128)S(1)} %meet_6_8.1), channel_id=1, replica_groups=mesh['groups'=2,'blk'=4,'clus'=4] {'blk','clus'}, dimensions={0} | all-to-all | bytes 16384 | tf_op jit(solution)/shard_map/all_to_all | solution.py:313
  35.3 0.8 %home_scores.1 = f32[1,256]{1,0:T(1,128)} custom-call(f32[16,1,128]{2,1,0:T(1,128)S(1)} %all_to_all.5.got_ref, s32[1,256]{1,0:T(1,128)S(1)} %get-tuple-element.16.target_ref), custom_call_target="tpu_custom_call" | custom-call | tf_op jit(solution)/shard_map/home_scores/pallas_call | solution.py:314
  (5 shorter events, 0.1 us)
Async XLA Ops:
  0.0 3.2 %collective-permute-start = (bf16[256,1024]{1,0:T(8,128)(2,1)}, bf16[256,1024]{1,0:T(8,128)(2,1)S(1)}, u32[]{:S(2)}, u32[]{:S(2)}) collective-permute-start(bf16[256,1024]{1,0:T(8,128)(2,1)} %emb_ref.1), channel_id=1, source_target_pairs={{0,1},{1,0},{2,3},{3,2},{4,5},{5,4},{6,7},{7,6},{8,9},{9,8},{10,11... | collective-permute-start | bytes 1572872 | tf_op jit(solution)/shard_map/ppermute | solution.py:264
  0.5 2.7 %collective-permute-start.1 = (s32[256]{0:T(256)}, s32[256]{0:T(256)S(1)}, u32[]{:S(2)}, u32[]{:S(2)}) collective-permute-start(s32[256]{0:T(256)} %param.4), channel_id=1, source_target_pairs={{0,1},{1,0},{2,3},{3,2},{4,5},{5,4},{6,7},{7,6},{8,9},{9,8},{10,11... | collective-permute-start | bytes 3080 | tf_op jit(solution)/shard_map/ppermute | solution.py:264
  0.5 2.7 %collective-permute-start.2 = (s32[256]{0:T(256)}, s32[256]{0:T(256)S(1)}, u32[]{:S(2)}, u32[]{:S(2)}) collective-permute-start(s32[256]{0:T(256)} %param.5), channel_id=1, source_target_pairs={{0,1},{1,0},{2,3},{3,2},{4,5},{5,4},{6,7},{7,6},{8,9},{9,8},{10,11... | collective-permute-start | bytes 3080 | tf_op jit(solution)/shard_map/ppermute | solution.py:264
  1.0 0.7 %copy-start.2 = (s32[256]{0:T(256)S(1)}, s32[256]{0:T(256)}, u32[]{:S(2)}) copy-start(s32[256]{0:T(256)} %param.5) | copy-start | bytes 3076
  1.0 0.7 %copy-start.1 = (s32[256]{0:T(256)S(1)}, s32[256]{0:T(256)}, u32[]{:S(2)}) copy-start(s32[256]{0:T(256)} %param.4) | copy-start | bytes 3076
  1.7 1.0 %copy-start = (bf16[256,1024]{1,0:T(8,128)(2,1)S(1)}, bf16[256,1024]{1,0:T(8,128)(2,1)}, u32[]{:S(2)}) copy-start(bf16[256,1024]{1,0:T(8,128)(2,1)} %emb_ref.1) | copy-start | bytes 1572868
  3.8 9.3 %collective-permute-start.3 = (bf16[1040,128]{1,0:T(8,128)(2,1)S(1)}, bf16[1040,128]{1,0:T(8,128)(2,1)S(1)}, u32[]{:S(2)}, u32[]{:S(2)}) collective-permute-start(bf16[1040,128]{1,0:T(8,128)(2,1)S(1)} %get-tuple-element.13), channel_id=1, source_target_pairs={{12,4},{1,9},{14,6},{3,11},{28,20},{17,25},{30,22},{19,27}} | collective-permute-start | bytes 798728 | tf_op jit(solution)/shard_map/ppermute | solution.py:261
  4.5 8.7 %collective-permute-start.5 = (bf16[1040,128]{1,0:T(8,128)(2,1)S(1)}, bf16[1040,128]{1,0:T(8,128)(2,1)S(1)}, u32[]{:S(2)}, u32[]{:S(2)}) collective-permute-start(bf16[1040,128]{1,0:T(8,128)(2,1)S(1)} %get-tuple-element.15), channel_id=1, source_target_pairs={{0,2},{1,3},{2,0},{3,1},{4,6},{5,7},{6,4},{7,5},{8,10},{9,11},{10,... | collective-permute-start | bytes 798728 | tf_op jit(solution)/shard_map/ppermute | solution.py:285
  7.0 12.3 %collective-permute-start.7 = (bf16[1040,128]{1,0:T(8,128)(2,1)S(1)}, bf16[1040,128]{1,0:T(8,128)(2,1)S(1)}, u32[]{:S(2)}, u32[]{:S(2)}) collective-permute-start(bf16[1040,128]{1,0:T(8,128)(2,1)S(1)} %get-tuple-element.12.refs_0_), channel_id=1, source_target_pairs={{8,4},{5,9},{10,6},{7,11},{24,20},{21,25},{26,22},{23,27}} | collective-permute-start | bytes 798728 | tf_op jit(solution)/shard_map/ppermute | solution.py:261
  7.7 11.7 %collective-permute-start.6 = (bf16[1040,128]{1,0:T(8,128)(2,1)S(1)}, bf16[1040,128]{1,0:T(8,128)(2,1)S(1)}, u32[]{:S(2)}, u32[]{:S(2)}) collective-permute-start(bf16[1040,128]{1,0:T(8,128)(2,1)S(1)} %get-tuple-element.12.refs_0_), channel_id=1, source_target_pairs={{0,4},{13,9},{2,6},{15,11},{16,20},{29,25},{18,22},{31,27}} | collective-permute-start | bytes 798728 | tf_op jit(solution)/shard_map/ppermute | solution.py:261
  12.4 6.9 %collective-permute-start.4 = (bf16[1040,128]{1,0:T(8,128)(2,1)S(1)}, bf16[1040,128]{1,0:T(8,128)(2,1)S(1)}, u32[]{:S(2)}, u32[]{:S(2)}) collective-permute-start(bf16[1040,128]{1,0:T(8,128)(2,1)S(1)} %get-tuple-element.14), channel_id=1, source_target_pairs={{14,4},{3,9},{12,6},{1,11},{30,20},{19,25},{28,22},{17,27}} | collective-permute-start | bytes 798728 | tf_op jit(solution)/shard_map/ppermute | solution.py:261
  13.2 6.2 %collective-permute-start.9 = (bf16[1040,128]{1,0:T(8,128)(2,1)S(1)}, bf16[1040,128]{1,0:T(8,128)(2,1)S(1)}, u32[]{:S(2)}, u32[]{:S(2)}) collective-permute-start(bf16[1040,128]{1,0:T(8,128)(2,1)S(1)} %after_far.1.refs_3_), channel_id=1, source_target_pairs={{8,4},{5,9},{10,6},{7,11},{24,20},{21,25},{26,22},{23,27}} | collective-permute-start | bytes 798728 | tf_op jit(solution)/shard_map/ppermute | solution.py:261
  13.9 9.4 %collective-permute-start.8 = (bf16[1040,128]{1,0:T(8,128)(2,1)S(1)}, bf16[1040,128]{1,0:T(8,128)(2,1)S(1)}, u32[]{:S(2)}, u32[]{:S(2)}) collective-permute-start(bf16[1040,128]{1,0:T(8,128)(2,1)S(1)} %after_far.1.refs_3_), channel_id=1, source_target_pairs={{0,4},{13,9},{2,6},{15,11},{16,20},{29,25},{18,22},{31,27}} | collective-permute-start | bytes 798728 | tf_op jit(solution)/shard_map/ppermute | solution.py:261

commit v10 on v8

--- a/solution.py
+++ b/solution.py
@@ -74,7 +74,7 @@
 
 NEAR, ACROSS, FAR = 0, 2, 3
 BLOCKS = (
-    (0, None), (1, None), (0, FAR), (1, FAR), (0, NEAR), (0, ACROSS), (1, NEAR), (1, ACROSS),
+    (0, None), (1, None), (0, FAR), (1, FAR), (0, NEAR), (1, ACROSS), (0, ACROSS), (1, NEAR),
 )
 
 
@@ -281,7 +281,7 @@
     crossed = lax.ppermute(far, "clus", [(c, c ^ 2) for c in range(4)])
     arrived = []
     for other, place in BLOCKS:
-        if other and place == FAR:
+        if other and place in (FAR, ACROSS):
             arrived.append(to_meeting(direct, place, cross=1))
         elif not other and place == FAR:
             arrived.append(to_meeting(first, place))

time: 35.3 us -> 35.4 us (level)
  no operation moved by 1% of the time
where the time goes in v10:
time: 35.4 us; the launch traced here: 35.1 us
  starting transfers between devices  16.2 us (46%)
  blocking collectives  11.3 us (32%)
  waiting for transfers between devices  3.87 us (11%)
  Pallas kernels  1.89 us (5%)
  local copies, waits for them, and re-layouts  1.73 us (5%)
    ppermute x6, starting transfers between devices, to_meeting(): return lax.ppermute(value, everyone, pairs)  12.7 us
    all_to_all x1, blocking collectives, meet(): lax.all_to_all(best, everyone, split_axis=0, concat_axis=0, tiled=True)  11.3 us
    ppermute x6, waiting for transfers between devices, to_meeting(): return lax.ppermute(value, everyone, pairs)  3.86 us
    ppermute x1, starting transfers between devices, meet(): crossed = lax.ppermute(far, 'clus', [(c, c ^ 2) for c in range(4)])  2.56 us
    unnamed x6, local copies, waits for them, and re-layouts  1.73 us
    ppermute x3, starting transfers between devices, meet(): lax.ppermute(value, 'clus', [(c, c ^ 1) for c in range(4)])  0.96 us
    pallas_call x1, Pallas kernels, meet(): pl.pallas_call(home_kernel, out_shape=jax.ShapeDtypeStruct((1, rows), jnp...  0.83 us
  transfers between devices with their start and end apart: 10, of which 2 were waited for; matrix products, arithmetic and copies ran while one was open for 0% of the time, Pallas kernels for 1%

profile of v10, /device:TPU:0, one launch (start us, length us, event | category | flops | bytes accessed | tf_op | source)
XLA Modules:
  0.0 35.1 jit_solution(11821818914062126002)
XLA Ops:
  0.0 0.5 %collective-permute-start = (bf16[256,1024]{1,0:T(8,128)(2,1)}, bf16[256,1024]{1,0:T(8,128)(2,1)S(1)}, u32[]{:S(2)}, u32[]{:S(2)}) collective-permute-start(bf16[256,1024]{1,0:T(8,128)(2,1)} %emb_ref.1), channel_id=1, source_target_pairs={{0,1},{1,0},{2,3},{3,2},{4,5},{5,4},{6,7},{7,6},{8,9},{9,8},{10,11... | collective-permute-start | bytes 1572872 | tf_op jit(solution)/shard_map/ppermute | solution.py:260
  0.5 0.1 collective-permute-start.1
  0.5 0.5 %collective-permute-start.2 = (s32[256]{0:T(256)}, s32[256]{0:T(256)S(1)}, u32[]{:S(2)}, u32[]{:S(2)}) collective-permute-start(s32[256]{0:T(256)} %param.5), channel_id=1, source_target_pairs={{0,1},{1,0},{2,3},{3,2},{4,5},{5,4},{6,7},{7,6},{8,9},{9,8},{10,11... | collective-permute-start | bytes 3080 | tf_op jit(solution)/shard_map/ppermute | solution.py:260
  1.0 0.0 copy-start.2
  1.0 0.0 copy-start.1
  1.0 0.7 %copy-done.2 = s32[256]{0:T(256)S(1)} copy-done((s32[256]{0:T(256)S(1)}, s32[256]{0:T(256)}, u32[]{:S(2)}) %copy-start.2) | copy-done | bytes 1048
  1.6 0.0 copy-done.1
  1.7 0.0 copy-start
  1.7 1.0 %copy-done = bf16[256,1024]{1,0:T(8,128)(2,1)S(1)} copy-done((bf16[256,1024]{1,0:T(8,128)(2,1)S(1)}, bf16[256,1024]{1,0:T(8,128)(2,1)}, u32[]{:S(2)}) %copy-start) | copy-done | bytes 524312
  2.7 0.5 %sort_rows.1 = (bf16[1040,128]{1,0:T(8,128)(2,1)S(1)}, s32[1,256]{1,0:T(1,128)S(1)}) custom-call(bf16[256,1024]{1,0:T(8,128)(2,1)S(1)} %copy-done, s32[1,256]{1,0:T(1,128)S(1)} %bitcast.5, s32[1,256]{1,0:T(1,128)S(1)} %bitcast.6), custom_call_target="tpu_custom_call" | custom-call | tf_op jit(solution)/shard_map/sort_rows/pallas_call | solution.py:265
  3.2 0.0 collective-permute-done.1
  3.2 0.0 collective-permute-done.2
  3.2 0.0 collective-permute-done.emb_ref
  3.2 0.6 %join_cores.1 = (bf16[1040,128]{1,0:T(8,128)(2,1)S(1)}, bf16[1040,128]{1,0:T(8,128)(2,1)S(1)}, bf16[1040,128]{1,0:T(8,128)(2,1)S(1)}, bf16[1040,128]{1,0:T(8,128)(2,1)S(1)}) custom-call(bf16[1040,128]{1,0:T(8,128)(2,1)S(1)} %get-tuple-element.11.keep_ref, bf16[256,1024]{1,0:T(8,128)(2,1)S(1)} %collective-permute-done.emb_ref, s32[1,256]{1,0:T(1,128)S(1)} %bitcast.7, ...), custom_call_target="tpu_custom_call" | custom-call | tf_op jit(solution)/shard_map/join_cores/pallas_call | solution.py:273
  3.8 2.6 %collective-permute-start.3 = (bf16[1040,128]{1,0:T(8,128)(2,1)S(1)}, bf16[1040,128]{1,0:T(8,128)(2,1)S(1)}, u32[]{:S(2)}, u32[]{:S(2)}) collective-permute-start(bf16[1040,128]{1,0:T(8,128)(2,1)S(1)} %get-tuple-element.13), channel_id=1, source_target_pairs={{0,2},{1,3},{2,0},{3,1},{4,6},{5,7},{6,4},{7,5},{8,10},{9,11},{10,... | collective-permute-start | bytes 798728 | tf_op jit(solution)/shard_map/ppermute | solution.py:281
  6.3 0.7 %collective-permute-start.4 = (bf16[1040,128]{1,0:T(8,128)(2,1)S(1)}, bf16[1040,128]{1,0:T(8,128)(2,1)S(1)}, u32[]{:S(2)}, u32[]{:S(2)}) collective-permute-start(bf16[1040,128]{1,0:T(8,128)(2,1)S(1)} %get-tuple-element.14), channel_id=1, source_target_pairs={{12,4},{1,9},{14,6},{3,11},{28,20},{17,25},{30,22},{19,27}} | collective-permute-start | bytes 798728 | tf_op jit(solution)/shard_map/ppermute | solution.py:257
  7.0 0.7 %collective-permute-start.7 = (bf16[1040,128]{1,0:T(8,128)(2,1)S(1)}, bf16[1040,128]{1,0:T(8,128)(2,1)S(1)}, u32[]{:S(2)}, u32[]{:S(2)}) collective-permute-start(bf16[1040,128]{1,0:T(8,128)(2,1)S(1)} %get-tuple-element.15), channel_id=1, source_target_pairs={{10,4},{7,9},{8,6},{5,11},{26,20},{23,25},{24,22},{21,27}} | collective-permute-start | bytes 798728 | tf_op jit(solution)/shard_map/ppermute | solution.py:257
  7.7 0.7 %collective-permute-start.5 = (bf16[1040,128]{1,0:T(8,128)(2,1)S(1)}, bf16[1040,128]{1,0:T(8,128)(2,1)S(1)}, u32[]{:S(2)}, u32[]{:S(2)}) collective-permute-start(bf16[1040,128]{1,0:T(8,128)(2,1)S(1)} %get-tuple-element.15), channel_id=1, source_target_pairs={{14,4},{3,9},{12,6},{1,11},{30,20},{19,25},{28,22},{17,27}} | collective-permute-start | bytes 798728 | tf_op jit(solution)/shard_map/ppermute | solution.py:257
  8.4 5.3 %collective-permute-start.6 = (bf16[1040,128]{1,0:T(8,128)(2,1)S(1)}, bf16[1040,128]{1,0:T(8,128)(2,1)S(1)}, u32[]{:S(2)}, u32[]{:S(2)}) collective-permute-start(bf16[1040,128]{1,0:T(8,128)(2,1)S(1)} %get-tuple-element.12.refs_0_), channel_id=1, source_target_pairs={{0,4},{13,9},{2,6},{15,11},{16,20},{29,25},{18,22},{31,27}} | collective-permute-start | bytes 798728 | tf_op jit(solution)/shard_map/ppermute | solution.py:257
  13.7 0.0 collective-permute-done.3.refs_1_
  13.7 0.7 %collective-permute-start.8 = (bf16[1040,128]{1,0:T(8,128)(2,1)S(1)}, bf16[1040,128]{1,0:T(8,128)(2,1)S(1)}, u32[]{:S(2)}, u32[]{:S(2)}) collective-permute-start(bf16[1040,128]{1,0:T(8,128)(2,1)S(1)} %get-tuple-element.12.refs_0_), channel_id=1, source_target_pairs={{8,4},{5,9},{10,6},{7,11},{24,20},{21,25},{26,22},{23,27}} | collective-permute-start | bytes 798728 | tf_op jit(solution)/shard_map/ppermute | solution.py:257
  14.4 0.0 collective-permute-done.4.refs_2_
  14.4 4.7 %collective-permute-start.9 = (bf16[1040,128]{1,0:T(8,128)(2,1)S(1)}, bf16[1040,128]{1,0:T(8,128)(2,1)S(1)}, u32[]{:S(2)}, u32[]{:S(2)}) collective-permute-start(bf16[1040,128]{1,0:T(8,128)(2,1)S(1)} %collective-permute-done.3.refs_1_), channel_id=1, source_target_pairs={{0,4},{13,9},{2,6},{15,11},{16,20},{29,25},{18,22},{31,27}} | collective-permute-start | bytes 798728 | tf_op jit(solution)/shard_map/ppermute | solution.py:257
  19.1 0.0 collective-permute-done.5.refs_3_
  19.2 0.0 collective-permute-done.7.refs_5_
  19.2 0.6 %collective-permute-done.6.refs_4_ = bf16[1040,128]{1,0:T(8,128)(2,1)S(1)} collective-permute-done((bf16[1040,128]{1,0:T(8,128)(2,1)S(1)}, bf16[1040,128]{1,0:T(8,128)(2,1)S(1)}, u32[]{:S(2)}, u32[]{:S(2)}) %collective-permute-start.6) | collective-permute-done | bytes 266272 | tf_op jit(solution)/shard_map/ppermute | solution.py:257
  19.8 0.0 collective-permute-done.8.refs_6_
  19.8 3.3 %collective-permute-done.9.refs_7_ = bf16[1040,128]{1,0:T(8,128)(2,1)S(1)} collective-permute-done((bf16[1040,128]{1,0:T(8,128)(2,1)S(1)}, bf16[1040,128]{1,0:T(8,128)(2,1)S(1)}, u32[]{:S(2)}, u32[]{:S(2)}) %collective-permute-start.9) | collective-permute-done | bytes 266272 | tf_op jit(solution)/shard_map/ppermute | solution.py:257
  23.0 11.3 %all_to_all.5.got_ref = f32[16,1,128]{2,1,0:T(1,128)S(1)} all-to-all(f32[16,1,128]{2,1,0:T(1,128)S(1)} %meet_6_8.1), channel_id=1, replica_groups=mesh['groups'=2,'blk'=4,'clus'=4] {'blk','clus'}, dimensions={0} | all-to-all | bytes 16384 | tf_op jit(solution)/shard_map/all_to_all | solution.py:305
  34.3 0.8 %home_scores.1 = f32[1,256]{1,0:T(1,128)} custom-call(f32[16,1,128]{2,1,0:T(1,128)S(1)} %all_to_all.5.got_ref, s32[1,256]{1,0:T(1,128)S(1)} %get-tuple-element.16.target_ref), custom_call_target="tpu_custom_call" | custom-call | tf_op jit(solution)/shard_map/home_scores/pallas_call | solution.py:306
  (3 shorter events, 0.0 us)
Async XLA Ops:
  0.0 3.2 %collective-permute-start = (bf16[256,1024]{1,0:T(8,128)(2,1)}, bf16[256,1024]{1,0:T(8,128)(2,1)S(1)}, u32[]{:S(2)}, u32[]{:S(2)}) collective-permute-start(bf16[256,1024]{1,0:T(8,128)(2,1)} %emb_ref.1), channel_id=1, source_target_pairs={{0,1},{1,0},{2,3},{3,2},{4,5},{5,4},{6,7},{7,6},{8,9},{9,8},{10,11... | collective-permute-start | bytes 1572872 | tf_op jit(solution)/shard_map/ppermute | solution.py:260
  0.5 2.7 %collective-permute-start.1 = (s32[256]{0:T(256)}, s32[256]{0:T(256)S(1)}, u32[]{:S(2)}, u32[]{:S(2)}) collective-permute-start(s32[256]{0:T(256)} %param.4), channel_id=1, source_target_pairs={{0,1},{1,0},{2,3},{3,2},{4,5},{5,4},{6,7},{7,6},{8,9},{9,8},{10,11... | collective-permute-start | bytes 3080 | tf_op jit(solution)/shard_map/ppermute | solution.py:260
  0.5 2.7 %collective-permute-start.2 = (s32[256]{0:T(256)}, s32[256]{0:T(256)S(1)}, u32[]{:S(2)}, u32[]{:S(2)}) collective-permute-start(s32[256]{0:T(256)} %param.5), channel_id=1, source_target_pairs={{0,1},{1,0},{2,3},{3,2},{4,5},{5,4},{6,7},{7,6},{8,9},{9,8},{10,11... | collective-permute-start | bytes 3080 | tf_op jit(solution)/shard_map/ppermute | solution.py:260
  1.0 0.7 %copy-start.2 = (s32[256]{0:T(256)S(1)}, s32[256]{0:T(256)}, u32[]{:S(2)}) copy-start(s32[256]{0:T(256)} %param.5) | copy-start | bytes 3076
  1.0 0.7 %copy-start.1 = (s32[256]{0:T(256)S(1)}, s32[256]{0:T(256)}, u32[]{:S(2)}) copy-start(s32[256]{0:T(256)} %param.4) | copy-start | bytes 3076
  1.7 1.0 %copy-start = (bf16[256,1024]{1,0:T(8,128)(2,1)S(1)}, bf16[256,1024]{1,0:T(8,128)(2,1)}, u32[]{:S(2)}) copy-start(bf16[256,1024]{1,0:T(8,128)(2,1)} %emb_ref.1) | copy-start | bytes 1572868
  3.8 9.9 %collective-permute-start.3 = (bf16[1040,128]{1,0:T(8,128)(2,1)S(1)}, bf16[1040,128]{1,0:T(8,128)(2,1)S(1)}, u32[]{:S(2)}, u32[]{:S(2)}) collective-permute-start(bf16[1040,128]{1,0:T(8,128)(2,1)S(1)} %get-tuple-element.13), channel_id=1, source_target_pairs={{0,2},{1,3},{2,0},{3,1},{4,6},{5,7},{6,4},{7,5},{8,10},{9,11},{10,... | collective-permute-start | bytes 798728 | tf_op jit(solution)/shard_map/ppermute | solution.py:281
  6.3 8.1 %collective-permute-start.4 = (bf16[1040,128]{1,0:T(8,128)(2,1)S(1)}, bf16[1040,128]{1,0:T(8,128)(2,1)S(1)}, u32[]{:S(2)}, u32[]{:S(2)}) collective-permute-start(bf16[1040,128]{1,0:T(8,128)(2,1)S(1)} %get-tuple-element.14), channel_id=1, source_target_pairs={{12,4},{1,9},{14,6},{3,11},{28,20},{17,25},{30,22},{19,27}} | collective-permute-start | bytes 798728 | tf_op jit(solution)/shard_map/ppermute | solution.py:257
  7.0 12.2 %collective-permute-start.7 = (bf16[1040,128]{1,0:T(8,128)(2,1)S(1)}, bf16[1040,128]{1,0:T(8,128)(2,1)S(1)}, u32[]{:S(2)}, u32[]{:S(2)}) collective-permute-start(bf16[1040,128]{1,0:T(8,128)(2,1)S(1)} %get-tuple-element.15), channel_id=1, source_target_pairs={{10,4},{7,9},{8,6},{5,11},{26,20},{23,25},{24,22},{21,27}} | collective-permute-start | bytes 798728 | tf_op jit(solution)/shard_map/ppermute | solution.py:257
  7.7 11.4 %collective-permute-start.5 = (bf16[1040,128]{1,0:T(8,128)(2,1)S(1)}, bf16[1040,128]{1,0:T(8,128)(2,1)S(1)}, u32[]{:S(2)}, u32[]{:S(2)}) collective-permute-start(bf16[1040,128]{1,0:T(8,128)(2,1)S(1)} %get-tuple-element.15), channel_id=1, source_target_pairs={{14,4},{3,9},{12,6},{1,11},{30,20},{19,25},{28,22},{17,27}} | collective-permute-start | bytes 798728 | tf_op jit(solution)/shard_map/ppermute | solution.py:257
  8.4 11.4 %collective-permute-start.6 = (bf16[1040,128]{1,0:T(8,128)(2,1)S(1)}, bf16[1040,128]{1,0:T(8,128)(2,1)S(1)}, u32[]{:S(2)}, u32[]{:S(2)}) collective-permute-start(bf16[1040,128]{1,0:T(8,128)(2,1)S(1)} %get-tuple-element.12.refs_0_), channel_id=1, source_target_pairs={{0,4},{13,9},{2,6},{15,11},{16,20},{29,25},{18,22},{31,27}} | collective-permute-start | bytes 798728 | tf_op jit(solution)/shard_map/ppermute | solution.py:257
  13.7 6.0 %collective-permute-start.8 = (bf16[1040,128]{1,0:T(8,128)(2,1)S(1)}, bf16[1040,128]{1,0:T(8,128)(2,1)S(1)}, u32[]{:S(2)}, u32[]{:S(2)}) collective-permute-start(bf16[1040,128]{1,0:T(8,128)(2,1)S(1)} %get-tuple-element.12.refs_0_), channel_id=1, source_target_pairs={{8,4},{5,9},{10,6},{7,11},{24,20},{21,25},{26,22},{23,27}} | collective-permute-start | bytes 798728 | tf_op jit(solution)/shard_map/ppermute | solution.py:257
  14.4 8.6 %collective-permute-start.9 = (bf16[1040,128]{1,0:T(8,128)(2,1)S(1)}, bf16[1040,128]{1,0:T(8,128)(2,1)S(1)}, u32[]{:S(2)}, u32[]{:S(2)}) collective-permute-start(bf16[1040,128]{1,0:T(8,128)(2,1)S(1)} %collective-permute-done.3.refs_1_), channel_id=1, source_target_pairs={{0,4},{13,9},{2,6},{15,11},{16,20},{29,25},{18,22},{31,27}} | collective-permute-start | bytes 798728 | tf_op jit(solution)/shard_map/ppermute | solution.py:257

commit v11 on v8

--- a/solution.py
+++ b/solution.py
@@ -211,6 +211,8 @@
     u, b = here()
     core = lax.rem(u, 2)
 
+    best_ref[...] = jnp.zeros_like(best_ref)
+
     @pl.when(b == middle_of(core))
     def _():
         known = [refs[last][q : q + 1, :] for q in range(first)]
@@ -218,18 +220,17 @@
             other, place = BLOCKS[q]
             at_blk = b if place is None else jnp.where(core == 0, place, 3 - place)
             chip = (u >> 1) ^ other
-            for c in range(2):
-                best_ref[at_blk * 4 + chip * 2 + c] = row
+            best_ref[u * 8 + at_blk * 2 + chip] = row
 
 
 def home_kernel(got_ref, target_ref, out_ref):
-    u, _ = here()
+    u, b = here()
     core = lax.rem(u, 2)
     slots = 4 * CAP
     rows = target_ref.shape[1]
     pieces = []
     for c in range(4):
-        row = got_ref[middle_of(c % 2) * 4 + c]
+        row = got_ref[c * 8 + b * 2 + (u >> 1)]
         pieces.append(jnp.where(core == 0, row[:, :CAP], row[:, CAP:]))
     best = jnp.concatenate(pieces, axis=1)
     high = best.astype(jnp.bfloat16).astype(jnp.float32)
@@ -301,8 +302,8 @@
 
     best = meeting(meet_kernel, 0, 4, [], (8, 128))
     best = meeting(meet_kernel, 4, 6, [best], (8, 128))
-    best = meeting(last_meet_kernel, 6, 8, [best], (16, 1, 128))
-    returned = lax.all_to_all(best, everyone, split_axis=0, concat_axis=0, tiled=True)
+    best = meeting(last_meet_kernel, 6, 8, [best], (32, 1, 128))
+    returned = lax.psum(best, everyone)
     out = pl.pallas_call(
         home_kernel,
         out_shape=jax.ShapeDtypeStruct((1, rows), jnp.float32),

time: 35.3 us -> 83 us (2.35)
  blocking collectives: 11.2 us -> 58.8 us
    psum x0 -> x1, blocking collectives: none -> 58.8 us  [meet(): returned = lax.psum(best, everyone)]
    all_to_all x1 -> x0, blocking collectives: 11.2 us -> none  [meet(): lax.all_to_all(best, everyone, split_axis=0, concat_axis=0, tiled=True)]
where the time goes in v11:
time: 83 us; the launch traced here: 82.7 us
  blocking collectives  58.8 us (71%)
  starting transfers between devices  16.2 us (20%)
  waiting for transfers between devices  3.87 us (5%)
  Pallas kernels  1.91 us (2%)
  local copies, waits for them, and re-layouts  1.73 us (2%)
    psum x1, blocking collectives, meet(): returned = lax.psum(best, everyone)  58.8 us
    ppermute x6, starting transfers between devices, to_meeting(): return lax.ppermute(value, everyone, pairs)  12.7 us
    ppermute x6, waiting for transfers between devices, to_meeting(): return lax.ppermute(value, everyone, pairs)  3.86 us
    ppermute x1, starting transfers between devices, meet(): crossed = lax.ppermute(far, 'clus', [(c, c ^ 2) for c in range(4)])  2.55 us
    unnamed x6, local copies, waits for them, and re-layouts  1.73 us
  transfers between devices with their start and end apart: 10, of which 2 were waited for; matrix products, arithmetic and copies ran while one was open for 0% of the time, Pallas kernels for 1%

profile of v11, /device:TPU:0, one launch (start us, length us, event | category | flops | bytes accessed | tf_op | source)
XLA Modules:
  0.0 82.7 jit_solution(3119315255482204582)
XLA Ops:
  0.0 0.5 collective-permute-start
  0.5 0.1 collective-permute-start.1
  0.5 0.5 collective-permute-start.2
  1.0 0.0 copy-start.2
  1.0 0.0 copy-start.1
  1.0 0.7 copy-done.2
  1.6 0.0 copy-done.1
  1.7 0.0 copy-start
  1.7 1.0 %copy-done = bf16[256,1024]{1,0:T(8,128)(2,1)S(1)} copy-done((bf16[256,1024]{1,0:T(8,128)(2,1)S(1)}, bf16[256,1024]{1,0:T(8,128)(2,1)}, u32[]{:S(2)}) %copy-start) | copy-done | bytes 524312
  2.7 0.5 sort_rows.1
  3.2 0.0 collective-permute-done.1
  3.2 0.0 collective-permute-done.2
  3.2 0.0 collective-permute-done.emb_ref
  3.2 0.6 join_cores.1
  3.8 2.6 %collective-permute-start.3 = (bf16[1040,128]{1,0:T(8,128)(2,1)S(1)}, bf16[1040,128]{1,0:T(8,128)(2,1)S(1)}, u32[]{:S(2)}, u32[]{:S(2)}) collective-permute-start(bf16[1040,128]{1,0:T(8,128)(2,1)S(1)} %get-tuple-element.13), channel_id=1, source_target_pairs={{0,2},{1,3},{2,0},{3,1},{4,6},{5,7},{6,4},{7,5},{8,10},{9,11},{10,... | collective-permute-start | bytes 798728 | tf_op jit(solution)/shard_map/ppermute | solution.py:282
  6.3 0.7 collective-permute-start.4
  7.0 0.7 collective-permute-start.5
  7.7 0.7 collective-permute-start.7
  8.4 5.3 %collective-permute-start.6 = (bf16[1040,128]{1,0:T(8,128)(2,1)S(1)}, bf16[1040,128]{1,0:T(8,128)(2,1)S(1)}, u32[]{:S(2)}, u32[]{:S(2)}) collective-permute-start(bf16[1040,128]{1,0:T(8,128)(2,1)S(1)} %get-tuple-element.12.refs_0_), channel_id=1, source_target_pairs={{0,4},{13,9},{2,6},{15,11},{16,20},{29,25},{18,22},{31,27}} | collective-permute-start | bytes 798728 | tf_op jit(solution)/shard_map/ppermute | solution.py:258
  13.7 0.0 collective-permute-done.3.refs_1_
  13.7 0.7 collective-permute-start.9
  14.4 0.0 collective-permute-done.4.refs_2_
  14.4 4.7 %collective-permute-start.8 = (bf16[1040,128]{1,0:T(8,128)(2,1)S(1)}, bf16[1040,128]{1,0:T(8,128)(2,1)S(1)}, u32[]{:S(2)}, u32[]{:S(2)}) collective-permute-start(bf16[1040,128]{1,0:T(8,128)(2,1)S(1)} %collective-permute-done.3.refs_1_), channel_id=1, source_target_pairs={{0,4},{13,9},{2,6},{15,11},{16,20},{29,25},{18,22},{31,27}} | collective-permute-start | bytes 798728 | tf_op jit(solution)/shard_map/ppermute | solution.py:258
  19.1 0.0 collective-permute-done.5.refs_3_
  19.2 0.0 collective-permute-done.7.refs_5_
  19.2 0.6 collective-permute-done.6.refs_4_
  19.8 0.0 collective-permute-done.9.refs_7_
  19.8 3.3 %collective-permute-done.8.refs_6_ = bf16[1040,128]{1,0:T(8,128)(2,1)S(1)} collective-permute-done((bf16[1040,128]{1,0:T(8,128)(2,1)S(1)}, bf16[1040,128]{1,0:T(8,128)(2,1)S(1)}, u32[]{:S(2)}, u32[]{:S(2)}) %collective-permute-start.8) | collective-permute-done | bytes 266272 | tf_op jit(solution)/shard_map/ppermute | solution.py:258
  23.1 58.8 %psum.7.got_ref = f32[32,1,128]{2,1,0:T(1,128)S(1)} all-reduce(f32[32,1,128]{2,1,0:T(1,128)S(1)} %meet_6_8.1), channel_id=1, replica_groups=mesh['groups'=2,'blk'=4,'clus'=4] {'blk','clus'}, use_global_device_ids=true, to_apply=%region_0.0 | all-reduce | flops 4096 | bytes 32768 | tf_op jit(solution)/shard_map/psum | solution.py:306
  81.9 0.8 %home_scores.1 = f32[1,256]{1,0:T(1,128)} custom-call(f32[32,1,128]{2,1,0:T(1,128)S(1)} %psum.7.got_ref, s32[1,256]{1,0:T(1,128)S(1)} %get-tuple-element.16.target_ref), custom_call_target="tpu_custom_call" | custom-call | tf_op jit(solution)/shard_map/home_scores/pallas_call | solution.py:307
  (3 shorter events, 0.0 us)
Async XLA Ops:
  0.0 3.2 %collective-permute-start = (bf16[256,1024]{1,0:T(8,128)(2,1)}, bf16[256,1024]{1,0:T(8,128)(2,1)S(1)}, u32[]{:S(2)}, u32[]{:S(2)}) collective-permute-start(bf16[256,1024]{1,0:T(8,128)(2,1)} %emb_ref.1), channel_id=1, source_target_pairs={{0,1},{1,0},{2,3},{3,2},{4,5},{5,4},{6,7},{7,6},{8,9},{9,8},{10,11... | collective-permute-start | bytes 1572872 | tf_op jit(solution)/shard_map/ppermute | solution.py:261
  0.5 2.7 %collective-permute-start.1 = (s32[256]{0:T(256)}, s32[256]{0:T(256)S(1)}, u32[]{:S(2)}, u32[]{:S(2)}) collective-permute-start(s32[256]{0:T(256)} %param.4), channel_id=1, source_target_pairs={{0,1},{1,0},{2,3},{3,2},{4,5},{5,4},{6,7},{7,6},{8,9},{9,8},{10,11... | collective-permute-start | bytes 3080 | tf_op jit(solution)/shard_map/ppermute | solution.py:261
  0.5 2.7 %collective-permute-start.2 = (s32[256]{0:T(256)}, s32[256]{0:T(256)S(1)}, u32[]{:S(2)}, u32[]{:S(2)}) collective-permute-start(s32[256]{0:T(256)} %param.5), channel_id=1, source_target_pairs={{0,1},{1,0},{2,3},{3,2},{4,5},{5,4},{6,7},{7,6},{8,9},{9,8},{10,11... | collective-permute-start | bytes 3080 | tf_op jit(solution)/shard_map/ppermute | solution.py:261
  1.0 0.7 copy-start.2
  1.0 0.7 copy-start.1
  1.7 1.0 %copy-start = (bf16[256,1024]{1,0:T(8,128)(2,1)S(1)}, bf16[256,1024]{1,0:T(8,128)(2,1)}, u32[]{:S(2)}) copy-start(bf16[256,1024]{1,0:T(8,128)(2,1)} %emb_ref.1) | copy-start | bytes 1572868
  3.8 10.0 %collective-permute-start.3 = (bf16[1040,128]{1,0:T(8,128)(2,1)S(1)}, bf16[1040,128]{1,0:T(8,128)(2,1)S(1)}, u32[]{:S(2)}, u32[]{:S(2)}) collective-permute-start(bf16[1040,128]{1,0:T(8,128)(2,1)S(1)} %get-tuple-element.13), channel_id=1, source_target_pairs={{0,2},{1,3},{2,0},{3,1},{4,6},{5,7},{6,4},{7,5},{8,10},{9,11},{10,... | collective-permute-start | bytes 798728 | tf_op jit(solution)/shard_map/ppermute | solution.py:282
  6.3 8.1 %collective-permute-start.4 = (bf16[1040,128]{1,0:T(8,128)(2,1)S(1)}, bf16[1040,128]{1,0:T(8,128)(2,1)S(1)}, u32[]{:S(2)}, u32[]{:S(2)}) collective-permute-start(bf16[1040,128]{1,0:T(8,128)(2,1)S(1)} %get-tuple-element.14), channel_id=1, source_target_pairs={{12,4},{1,9},{14,6},{3,11},{28,20},{17,25},{30,22},{19,27}} | collective-permute-start | bytes 798728 | tf_op jit(solution)/shard_map/ppermute | solution.py:258
  7.0 12.1 %collective-permute-start.5 = (bf16[1040,128]{1,0:T(8,128)(2,1)S(1)}, bf16[1040,128]{1,0:T(8,128)(2,1)S(1)}, u32[]{:S(2)}, u32[]{:S(2)}) collective-permute-start(bf16[1040,128]{1,0:T(8,128)(2,1)S(1)} %get-tuple-element.15), channel_id=1, source_target_pairs={{14,4},{3,9},{12,6},{1,11},{30,20},{19,25},{28,22},{17,27}} | collective-permute-start | bytes 798728 | tf_op jit(solution)/shard_map/ppermute | solution.py:258
  7.7 11.5 %collective-permute-start.7 = (bf16[1040,128]{1,0:T(8,128)(2,1)S(1)}, bf16[1040,128]{1,0:T(8,128)(2,1)S(1)}, u32[]{:S(2)}, u32[]{:S(2)}) collective-permute-start(bf16[1040,128]{1,0:T(8,128)(2,1)S(1)} %get-tuple-element.12.refs_0_), channel_id=1, source_target_pairs={{8,4},{5,9},{10,6},{7,11},{24,20},{21,25},{26,22},{23,27}} | collective-permute-start | bytes 798728 | tf_op jit(solution)/shard_map/ppermute | solution.py:258
  8.4 11.4 %collective-permute-start.6 = (bf16[1040,128]{1,0:T(8,128)(2,1)S(1)}, bf16[1040,128]{1,0:T(8,128)(2,1)S(1)}, u32[]{:S(2)}, u32[]{:S(2)}) collective-permute-start(bf16[1040,128]{1,0:T(8,128)(2,1)S(1)} %get-tuple-element.12.refs_0_), channel_id=1, source_target_pairs={{0,4},{13,9},{2,6},{15,11},{16,20},{29,25},{18,22},{31,27}} | collective-permute-start | bytes 798728 | tf_op jit(solution)/shard_map/ppermute | solution.py:258
  13.7 6.0 %collective-permute-start.9 = (bf16[1040,128]{1,0:T(8,128)(2,1)S(1)}, bf16[1040,128]{1,0:T(8,128)(2,1)S(1)}, u32[]{:S(2)}, u32[]{:S(2)}) collective-permute-start(bf16[1040,128]{1,0:T(8,128)(2,1)S(1)} %collective-permute-done.3.refs_1_), channel_id=1, source_target_pairs={{8,4},{5,9},{10,6},{7,11},{24,20},{21,25},{26,22},{23,27}} | collective-permute-start | bytes 798728 | tf_op jit(solution)/shard_map/ppermute | solution.py:258
  14.4 8.6 %collective-permute-start.8 = (bf16[1040,128]{1,0:T(8,128)(2,1)S(1)}, bf16[1040,128]{1,0:T(8,128)(2,1)S(1)}, u32[]{:S(2)}, u32[]{:S(2)}) collective-permute-start(bf16[1040,128]{1,0:T(8,128)(2,1)S(1)} %collective-permute-done.3.refs_1_), channel_id=1, source_target_pairs={{0,4},{13,9},{2,6},{15,11},{16,20},{29,25},{18,22},{31,27}} | collective-permute-start | bytes 798728 | tf_op jit(solution)/shard_map/ppermute | solution.py:258

commit v12 on v9

--- a/solution.py
+++ b/solution.py
@@ -74,7 +74,7 @@
 
 NEAR, ACROSS, FAR = 0, 2, 3
 BLOCKS = (
-    (0, None), (0, FAR), (1, FAR), (1, None), (0, NEAR), (0, ACROSS), (1, NEAR), (1, ACROSS),
+    (0, None), (0, FAR), (1, FAR), (1, None), (0, ACROSS), (1, ACROSS), (0, NEAR), (1, NEAR),
 )
 
 
@@ -305,8 +305,8 @@
         name="after_far",
     )(best, crossed)
     arrived += [to_meeting(direct, FAR, cross=1), crossed]
-    arrived += [to_meeting(near, NEAR), to_meeting(near, ACROSS)]
-    arrived += [to_meeting(crossed, NEAR), to_meeting(crossed, ACROSS)]
+    arrived += [to_meeting(near, ACROSS), to_meeting(direct, ACROSS, cross=1)]
+    arrived += [to_meeting(near, NEAR), to_meeting(crossed, NEAR)]
     best = meeting(meet_kernel, 2, 4, [best], (8, 128))
     best = meeting(meet_kernel, 4, 6, [best], (8, 128))
     best = meeting(last_meet_kernel, 6, 8, [best], (16, 1, 128))

time: 36.4 us -> 40.3 us (1.11)
  starting transfers between devices: 16.4 us -> 19.2 us
  blocking collectives: 12 us -> 13.1 us
    ppermute x6, starting transfers between devices: 12.9 us -> 15.7 us  [to_meeting(): return lax.ppermute(value, everyone, pairs)]
    all_to_all x1, blocking collectives: 12 us -> 13.1 us  [meet(): lax.all_to_all(best, everyone, split_axis=0, concat_axis=0, tiled=True)]
where the time goes in v12:
time: 40.3 us; the launch traced here: 40 us
  starting transfers between devices  19.2 us (48%)
  blocking collectives  13.1 us (33%)
  waiting for transfers between devices  3.83 us (10%)
  Pallas kernels  1.92 us (5%)
  local copies, waits for them, and re-layouts  1.73 us (4%)
    ppermute x6, starting transfers between devices, to_meeting(): return lax.ppermute(value, everyone, pairs)  15.7 us
    all_to_all x1, blocking collectives, meet(): lax.all_to_all(best, everyone, split_axis=0, concat_axis=0, tiled=True)  13.1 us
    ppermute x6, waiting for transfers between devices, to_meeting(): return lax.ppermute(value, everyone, pairs)  3.82 us
    ppermute x1, starting transfers between devices, meet(): crossed = lax.ppermute(far, 'clus', [(c, c ^ 2) for c in range(4)])  2.56 us
    unnamed x6, local copies, waits for them, and re-layouts  1.73 us
    ppermute x3, starting transfers between devices, meet(): lax.ppermute(value, 'clus', [(c, c ^ 1) for c in range(4)])  0.96 us
    pallas_call x1, Pallas kernels, meet(): pl.pallas_call(home_kernel, out_shape=jax.ShapeDtypeStruct((1, rows), jnp...  0.83 us
  transfers between devices with their start and end apart: 10, of which 1 were waited for; matrix products, arithmetic and copies ran while one was open for 0% of the time, Pallas kernels for 1%

profile of v12, /device:TPU:0, one launch (start us, length us, event | category | flops | bytes accessed | tf_op | source)
XLA Modules:
  0.0 40.0 jit_solution(4547325430976549364)
XLA Ops:
  0.0 0.5 %collective-permute-start = (bf16[256,1024]{1,0:T(8,128)(2,1)}, bf16[256,1024]{1,0:T(8,128)(2,1)S(1)}, u32[]{:S(2)}, u32[]{:S(2)}) collective-permute-start(bf16[256,1024]{1,0:T(8,128)(2,1)} %emb_ref.1), channel_id=1, source_target_pairs={{0,1},{1,0},{2,3},{3,2},{4,5},{5,4},{6,7},{7,6},{8,9},{9,8},{10,11... | collective-permute-start | bytes 1572872 | tf_op jit(solution)/shard_map/ppermute | solution.py:264
  0.5 0.1 collective-permute-start.1
  0.5 0.5 %collective-permute-start.2 = (s32[256]{0:T(256)}, s32[256]{0:T(256)S(1)}, u32[]{:S(2)}, u32[]{:S(2)}) collective-permute-start(s32[256]{0:T(256)} %param.5), channel_id=1, source_target_pairs={{0,1},{1,0},{2,3},{3,2},{4,5},{5,4},{6,7},{7,6},{8,9},{9,8},{10,11... | collective-permute-start | bytes 3080 | tf_op jit(solution)/shard_map/ppermute | solution.py:264
  1.0 0.0 copy-start.2
  1.0 0.0 copy-start.1
  1.0 0.7 %copy-done.2 = s32[256]{0:T(256)S(1)} copy-done((s32[256]{0:T(256)S(1)}, s32[256]{0:T(256)}, u32[]{:S(2)}) %copy-start.2) | copy-done | bytes 1048
  1.6 0.0 copy-done.1
  1.7 0.0 copy-start
  1.7 1.0 %copy-done = bf16[256,1024]{1,0:T(8,128)(2,1)S(1)} copy-done((bf16[256,1024]{1,0:T(8,128)(2,1)S(1)}, bf16[256,1024]{1,0:T(8,128)(2,1)}, u32[]{:S(2)}) %copy-start) | copy-done | bytes 524312
  2.7 0.5 %sort_rows.1 = (bf16[1040,128]{1,0:T(8,128)(2,1)S(1)}, s32[1,256]{1,0:T(1,128)S(1)}) custom-call(bf16[256,1024]{1,0:T(8,128)(2,1)S(1)} %copy-done, s32[1,256]{1,0:T(1,128)S(1)} %bitcast.5, s32[1,256]{1,0:T(1,128)S(1)} %bitcast.6), custom_call_target="tpu_custom_call" | custom-call | tf_op jit(solution)/shard_map/sort_rows/pallas_call | solution.py:269
  3.2 0.0 collective-permute-done.1
  3.2 0.0 collective-permute-done.2
  3.2 0.0 collective-permute-done.emb_ref
  3.2 0.6 %join_cores.1 = (bf16[1040,128]{1,0:T(8,128)(2,1)S(1)}, bf16[1040,128]{1,0:T(8,128)(2,1)S(1)}, bf16[1040,128]{1,0:T(8,128)(2,1)S(1)}, bf16[1040,128]{1,0:T(8,128)(2,1)S(1)}) custom-call(bf16[1040,128]{1,0:T(8,128)(2,1)S(1)} %get-tuple-element.11.keep_ref, bf16[256,1024]{1,0:T(8,128)(2,1)S(1)} %collective-permute-done.emb_ref, s32[1,256]{1,0:T(1,128)S(1)} %bitcast.7, ...), custom_call_target="tpu_custom_call" | custom-call | tf_op jit(solution)/shard_map/join_cores/pallas_call | solution.py:277
  3.8 0.7 %collective-permute-start.3 = (bf16[1040,128]{1,0:T(8,128)(2,1)S(1)}, bf16[1040,128]{1,0:T(8,128)(2,1)S(1)}, u32[]{:S(2)}, u32[]{:S(2)}) collective-permute-start(bf16[1040,128]{1,0:T(8,128)(2,1)S(1)} %get-tuple-element.13), channel_id=1, source_target_pairs={{12,4},{1,9},{14,6},{3,11},{28,20},{17,25},{30,22},{19,27}} | collective-permute-start | bytes 798728 | tf_op jit(solution)/shard_map/ppermute | solution.py:261
  4.5 2.6 %collective-permute-start.5 = (bf16[1040,128]{1,0:T(8,128)(2,1)S(1)}, bf16[1040,128]{1,0:T(8,128)(2,1)S(1)}, u32[]{:S(2)}, u32[]{:S(2)}) collective-permute-start(bf16[1040,128]{1,0:T(8,128)(2,1)S(1)} %get-tuple-element.15), channel_id=1, source_target_pairs={{0,2},{1,3},{2,0},{3,1},{4,6},{5,7},{6,4},{7,5},{8,10},{9,11},{10,... | collective-permute-start | bytes 798728 | tf_op jit(solution)/shard_map/ppermute | solution.py:285
  7.0 0.7 %collective-permute-start.7 = (bf16[1040,128]{1,0:T(8,128)(2,1)S(1)}, bf16[1040,128]{1,0:T(8,128)(2,1)S(1)}, u32[]{:S(2)}, u32[]{:S(2)}) collective-permute-start(bf16[1040,128]{1,0:T(8,128)(2,1)S(1)} %get-tuple-element.14), channel_id=1, source_target_pairs={{10,4},{7,9},{8,6},{5,11},{26,20},{23,25},{24,22},{21,27}} | collective-permute-start | bytes 798728 | tf_op jit(solution)/shard_map/ppermute | solution.py:261
  7.7 0.7 %collective-permute-start.4 = (bf16[1040,128]{1,0:T(8,128)(2,1)S(1)}, bf16[1040,128]{1,0:T(8,128)(2,1)S(1)}, u32[]{:S(2)}, u32[]{:S(2)}) collective-permute-start(bf16[1040,128]{1,0:T(8,128)(2,1)S(1)} %get-tuple-element.14), channel_id=1, source_target_pairs={{14,4},{3,9},{12,6},{1,11},{30,20},{19,25},{28,22},{17,27}} | collective-permute-start | bytes 798728 | tf_op jit(solution)/shard_map/ppermute | solution.py:261
  8.4 5.3 %collective-permute-start.8 = (bf16[1040,128]{1,0:T(8,128)(2,1)S(1)}, bf16[1040,128]{1,0:T(8,128)(2,1)S(1)}, u32[]{:S(2)}, u32[]{:S(2)}) collective-permute-start(bf16[1040,128]{1,0:T(8,128)(2,1)S(1)} %get-tuple-element.12.refs_0_), channel_id=1, source_target_pairs={{0,4},{13,9},{2,6},{15,11},{16,20},{29,25},{18,22},{31,27}} | collective-permute-start | bytes 798728 | tf_op jit(solution)/shard_map/ppermute | solution.py:261
  13.7 0.0 collective-permute-done.3.refs_1_
  13.7 0.7 %collective-permute-start.6 = (bf16[1040,128]{1,0:T(8,128)(2,1)S(1)}, bf16[1040,128]{1,0:T(8,128)(2,1)S(1)}, u32[]{:S(2)}, u32[]{:S(2)}) collective-permute-start(bf16[1040,128]{1,0:T(8,128)(2,1)S(1)} %get-tuple-element.12.refs_0_), channel_id=1, source_target_pairs={{8,4},{5,9},{10,6},{7,11},{24,20},{21,25},{26,22},{23,27}} | collective-permute-start | bytes 798728 | tf_op jit(solution)/shard_map/ppermute | solution.py:261
  14.5 0.0 collective-permute-done.5.value_ref
  14.5 7.7 %collective-permute-start.9 = (bf16[1040,128]{1,0:T(8,128)(2,1)S(1)}, bf16[1040,128]{1,0:T(8,128)(2,1)S(1)}, u32[]{:S(2)}, u32[]{:S(2)}) collective-permute-start(bf16[1040,128]{1,0:T(8,128)(2,1)S(1)} %after_far.1.refs_3_), channel_id=1, source_target_pairs={{0,4},{13,9},{2,6},{15,11},{16,20},{29,25},{18,22},{31,27}} | collective-permute-start | bytes 798728 | tf_op jit(solution)/shard_map/ppermute | solution.py:261
  22.2 0.0 collective-permute-done.4.refs_2_
  22.2 0.0 collective-permute-done.7.refs_5_
  22.2 0.0 collective-permute-done.6.refs_4_
  22.2 0.0 collective-permute-done.8.refs_6_
  22.3 3.8 %collective-permute-done.9.refs_7_ = bf16[1040,128]{1,0:T(8,128)(2,1)S(1)} collective-permute-done((bf16[1040,128]{1,0:T(8,128)(2,1)S(1)}, bf16[1040,128]{1,0:T(8,128)(2,1)S(1)}, u32[]{:S(2)}, u32[]{:S(2)}) %collective-permute-start.9) | collective-permute-done | bytes 266272 | tf_op jit(solution)/shard_map/ppermute | solution.py:261
  26.1 13.1 %all_to_all.5.got_ref = f32[16,1,128]{2,1,0:T(1,128)S(1)} all-to-all(f32[16,1,128]{2,1,0:T(1,128)S(1)} %meet_6_8.1), channel_id=1, replica_groups=mesh['groups'=2,'blk'=4,'clus'=4] {'blk','clus'}, dimensions={0} | all-to-all | bytes 16384 | tf_op jit(solution)/shard_map/all_to_all | solution.py:313
  39.2 0.8 %home_scores.1 = f32[1,256]{1,0:T(1,128)} custom-call(f32[16,1,128]{2,1,0:T(1,128)S(1)} %all_to_all.5.got_ref, s32[1,256]{1,0:T(1,128)S(1)} %get-tuple-element.16.target_ref), custom_call_target="tpu_custom_call" | custom-call | tf_op jit(solution)/shard_map/home_scores/pallas_call | solution.py:314
  (5 shorter events, 0.1 us)
Async XLA Ops:
  0.0 3.2 %collective-permute-start = (bf16[256,1024]{1,0:T(8,128)(2,1)}, bf16[256,1024]{1,0:T(8,128)(2,1)S(1)}, u32[]{:S(2)}, u32[]{:S(2)}) collective-permute-start(bf16[256,1024]{1,0:T(8,128)(2,1)} %emb_ref.1), channel_id=1, source_target_pairs={{0,1},{1,0},{2,3},{3,2},{4,5},{5,4},{6,7},{7,6},{8,9},{9,8},{10,11... | collective-permute-start | bytes 1572872 | tf_op jit(solution)/shard_map/ppermute | solution.py:264
  0.5 2.7 %collective-permute-start.1 = (s32[256]{0:T(256)}, s32[256]{0:T(256)S(1)}, u32[]{:S(2)}, u32[]{:S(2)}) collective-permute-start(s32[256]{0:T(256)} %param.4), channel_id=1, source_target_pairs={{0,1},{1,0},{2,3},{3,2},{4,5},{5,4},{6,7},{7,6},{8,9},{9,8},{10,11... | collective-permute-start | bytes 3080 | tf_op jit(solution)/shard_map/ppermute | solution.py:264
  0.5 2.7 %collective-permute-start.2 = (s32[256]{0:T(256)}, s32[256]{0:T(256)S(1)}, u32[]{:S(2)}, u32[]{:S(2)}) collective-permute-start(s32[256]{0:T(256)} %param.5), channel_id=1, source_target_pairs={{0,1},{1,0},{2,3},{3,2},{4,5},{5,4},{6,7},{7,6},{8,9},{9,8},{10,11... | collective-permute-start | bytes 3080 | tf_op jit(solution)/shard_map/ppermute | solution.py:264
  1.0 0.7 %copy-start.2 = (s32[256]{0:T(256)S(1)}, s32[256]{0:T(256)}, u32[]{:S(2)}) copy-start(s32[256]{0:T(256)} %param.5) | copy-start | bytes 3076
  1.0 0.7 %copy-start.1 = (s32[256]{0:T(256)S(1)}, s32[256]{0:T(256)}, u32[]{:S(2)}) copy-start(s32[256]{0:T(256)} %param.4) | copy-start | bytes 3076
  1.7 1.0 %copy-start = (bf16[256,1024]{1,0:T(8,128)(2,1)S(1)}, bf16[256,1024]{1,0:T(8,128)(2,1)}, u32[]{:S(2)}) copy-start(bf16[256,1024]{1,0:T(8,128)(2,1)} %emb_ref.1) | copy-start | bytes 1572868
  3.8 9.9 %collective-permute-start.3 = (bf16[1040,128]{1,0:T(8,128)(2,1)S(1)}, bf16[1040,128]{1,0:T(8,128)(2,1)S(1)}, u32[]{:S(2)}, u32[]{:S(2)}) collective-permute-start(bf16[1040,128]{1,0:T(8,128)(2,1)S(1)} %get-tuple-element.13), channel_id=1, source_target_pairs={{12,4},{1,9},{14,6},{3,11},{28,20},{17,25},{30,22},{19,27}} | collective-permute-start | bytes 798728 | tf_op jit(solution)/shard_map/ppermute | solution.py:261
  4.5 10.0 %collective-permute-start.5 = (bf16[1040,128]{1,0:T(8,128)(2,1)S(1)}, bf16[1040,128]{1,0:T(8,128)(2,1)S(1)}, u32[]{:S(2)}, u32[]{:S(2)}) collective-permute-start(bf16[1040,128]{1,0:T(8,128)(2,1)S(1)} %get-tuple-element.15), channel_id=1, source_target_pairs={{0,2},{1,3},{2,0},{3,1},{4,6},{5,7},{6,4},{7,5},{8,10},{9,11},{10,... | collective-permute-start | bytes 798728 | tf_op jit(solution)/shard_map/ppermute | solution.py:285
  7.0 15.2 %collective-permute-start.7 = (bf16[1040,128]{1,0:T(8,128)(2,1)S(1)}, bf16[1040,128]{1,0:T(8,128)(2,1)S(1)}, u32[]{:S(2)}, u32[]{:S(2)}) collective-permute-start(bf16[1040,128]{1,0:T(8,128)(2,1)S(1)} %get-tuple-element.14), channel_id=1, source_target_pairs={{10,4},{7,9},{8,6},{5,11},{26,20},{23,25},{24,22},{21,27}} | collective-permute-start | bytes 798728 | tf_op jit(solution)/shard_map/ppermute | solution.py:261
  7.7 14.5 %collective-permute-start.4 = (bf16[1040,128]{1,0:T(8,128)(2,1)S(1)}, bf16[1040,128]{1,0:T(8,128)(2,1)S(1)}, u32[]{:S(2)}, u32[]{:S(2)}) collective-permute-start(bf16[1040,128]{1,0:T(8,128)(2,1)S(1)} %get-tuple-element.14), channel_id=1, source_target_pairs={{14,4},{3,9},{12,6},{1,11},{30,20},{19,25},{28,22},{17,27}} | collective-permute-start | bytes 798728 | tf_op jit(solution)/shard_map/ppermute | solution.py:261
  8.4 13.9 %collective-permute-start.8 = (bf16[1040,128]{1,0:T(8,128)(2,1)S(1)}, bf16[1040,128]{1,0:T(8,128)(2,1)S(1)}, u32[]{:S(2)}, u32[]{:S(2)}) collective-permute-start(bf16[1040,128]{1,0:T(8,128)(2,1)S(1)} %get-tuple-element.12.refs_0_), channel_id=1, source_target_pairs={{0,4},{13,9},{2,6},{15,11},{16,20},{29,25},{18,22},{31,27}} | collective-permute-start | bytes 798728 | tf_op jit(solution)/shard_map/ppermute | solution.py:261
  13.7 8.5 %collective-permute-start.6 = (bf16[1040,128]{1,0:T(8,128)(2,1)S(1)}, bf16[1040,128]{1,0:T(8,128)(2,1)S(1)}, u32[]{:S(2)}, u32[]{:S(2)}) collective-permute-start(bf16[1040,128]{1,0:T(8,128)(2,1)S(1)} %get-tuple-element.12.refs_0_), channel_id=1, source_target_pairs={{8,4},{5,9},{10,6},{7,11},{24,20},{21,25},{26,22},{23,27}} | collective-permute-start | bytes 798728 | tf_op jit(solution)/shard_map/ppermute | solution.py:261
  14.5 11.6 %collective-permute-start.9 = (bf16[1040,128]{1,0:T(8,128)(2,1)S(1)}, bf16[1040,128]{1,0:T(8,128)(2,1)S(1)}, u32[]{:S(2)}, u32[]{:S(2)}) collective-permute-start(bf16[1040,128]{1,0:T(8,128)(2,1)S(1)} %after_far.1.refs_3_), channel_id=1, source_target_pairs={{0,4},{13,9},{2,6},{15,11},{16,20},{29,25},{18,22},{31,27}} | collective-permute-start | bytes 798728 | tf_op jit(solution)/shard_map/ppermute | solution.py:261

commit v13 on v8

--- a/solution.py
+++ b/solution.py
@@ -74,7 +74,7 @@
 
 NEAR, ACROSS, FAR = 0, 2, 3
 BLOCKS = (
-    (0, None), (1, None), (0, FAR), (1, FAR), (0, NEAR), (0, ACROSS), (1, NEAR), (1, ACROSS),
+    (0, None), (1, None), (0, FAR), (1, FAR), (0, NEAR), (0, ACROSS), (1, ACROSS), (1, NEAR),
 )
 
 
@@ -100,26 +100,23 @@
     )
 
 
-def sorted_rows(emb_ref, cluster_ref, ids_ref):
-    rows, width = emb_ref.shape
+def earlier_kernel(out_ref):
+    shape = out_ref.shape
+    row, column = (lax.broadcasted_iota(jnp.int32, shape, n) for n in range(2))
+    out_ref[...] = (row < column).astype(jnp.bfloat16)
+
+
+def ranked(cluster, ids, earlier):
+    rows = cluster.shape[1]
     slots = 2 * CAP
     u, _ = here()
-    cluster = cluster_ref[...]
     onehot = lax.broadcasted_iota(jnp.int32, (8, rows), 0) == cluster
-    earlier = (
-        lax.broadcasted_iota(jnp.int32, (rows, rows), 0)
-        < lax.broadcasted_iota(jnp.int32, (rows, rows), 1)
-    ).astype(jnp.bfloat16)
     before = jnp.dot(onehot.astype(jnp.bfloat16), earlier, preferred_element_type=jnp.float32)
     position = jnp.sum(jnp.where(onehot, before, 0.0), axis=0, keepdims=True).astype(jnp.int32)
     start = jnp.where(cluster == u, 0, jnp.where(cluster == u ^ 2, CAP, -4 * CAP))
     place = (
         lax.broadcasted_iota(jnp.int32, (slots, rows), 0) == start + position
     ).astype(jnp.bfloat16)
-    values = jnp.dot(place, emb_ref[...], preferred_element_type=jnp.float32)
-    mean = jnp.mean(values * values, axis=1, keepdims=True)
-    unit = (values * lax.rsqrt(mean + EPS) * width ** (-0.5)).astype(jnp.bfloat16)
-    ids = ids_ref[...]
     row = lax.broadcasted_iota(jnp.int32, (16, rows), 0)
     parts = jnp.where(row == 0, ids >> 8, jnp.where(row == 1, ids & 255, 1))
     moved = lax.dot_general(
@@ -130,24 +127,33 @@
     )
     row = lax.broadcasted_iota(jnp.int32, (16, slots), 0)
     moved = jnp.where((moved[2:3] == 0.0) & (row == 0), 256.0, moved)
-    return unit, moved, cluster * CAP + position
-
-
-def sort_kernel(emb_ref, cluster_ref, ids_ref, keep_ref, target_ref):
-    unit, moved, target = sorted_rows(emb_ref, cluster_ref, ids_ref)
-    put_slabs(keep_ref, unit)
-    keep_ref[keep_ref.shape[0] - 16 :, :] = moved.astype(jnp.bfloat16)
-    target_ref[...] = target
-
-
-def join_kernel(keep_ref, emb_ref, cluster_ref, ids_ref, *out_refs):
-    unit, moved, _ = sorted_rows(emb_ref, cluster_ref, ids_ref)
+    return cluster * CAP + position, place, moved
+
+
+def unit_slots(place, emb):
+    values = jnp.dot(place, emb, preferred_element_type=jnp.float32)
+    mean = jnp.mean(values * values, axis=1, keepdims=True)
+    return (values * lax.rsqrt(mean + EPS) * emb.shape[1] ** (-0.5)).astype(jnp.bfloat16)
+
+
+def rank_kernel(cluster_ref, ids_ref, earlier_ref, target_ref, place_ref, kept_ids_ref):
+    found = ranked(cluster_ref[...], ids_ref[...], earlier_ref[...])
+    target_ref[...], place_ref[...], kept_ids_ref[...] = found
+
+
+def sort_kernel(emb_ref, place_ref, keep_ref):
+    put_slabs(keep_ref, unit_slots(place_ref[...], emb_ref[...]))
+
+
+def join_kernel(keep_ref, kept_ids_ref, earlier_ref, emb_ref, cluster_ref, ids_ref, *out_refs):
+    _, place, moved = ranked(cluster_ref[...], ids_ref[...], earlier_ref[...])
+    unit = unit_slots(place, emb_ref[...])
     u, _ = here()
     core = lax.rem(u, 2)
-    tail = keep_ref.shape[0] - 16
+    tail = keep_ref.shape[0]
     own_at = pl.multiple_of(core * CAP, CAP)
     other_at = pl.multiple_of((1 - core) * CAP, CAP)
-    kept = keep_ref[tail:, :].astype(jnp.float32)
+    kept = kept_ids_ref[...]
     for out_ref, start in zip(out_refs, (0, CAP) * 2):
         for t in range(tail // SLABS_ROWS):
             base = t * SLABS_ROWS
@@ -259,25 +265,46 @@
     raw = (embeddings, cluster, row_ids)
     swapped = [lax.ppermute(value, "clus", [(c, c ^ 1) for c in range(4)]) for value in raw]
 
-    def flat(values):
-        return [values[0], values[1].reshape(1, rows), values[2].reshape(1, rows)]
-
-    keep, target = pl.pallas_call(
+    def row(value):
+        return value.reshape(1, rows)
+
+    ahead = pl.CostEstimate(flops=10**10, bytes_accessed=10**7, transcendentals=0)
+    earlier = pl.pallas_call(
+        earlier_kernel,
+        out_shape=jax.ShapeDtypeStruct((rows, rows), jnp.bfloat16),
+        out_specs=VMEM,
+        compiler_params=SMALL,
+        cost_estimate=ahead,
+        name="earlier_rows",
+    )()
+    target, place, kept_ids = pl.pallas_call(
+        rank_kernel,
+        out_shape=[
+            jax.ShapeDtypeStruct((1, rows), jnp.int32),
+            jax.ShapeDtypeStruct((2 * CAP, rows), jnp.bfloat16),
+            jax.ShapeDtypeStruct((16, 2 * CAP), jnp.float32),
+        ],
+        in_specs=[VMEM] * 3,
+        out_specs=[VMEM] * 3,
+        compiler_params=SMALL,
+        name="rank_rows",
+    )(row(cluster), row(row_ids), earlier)
+    keep = pl.pallas_call(
         sort_kernel,
-        out_shape=[payload, jax.ShapeDtypeStruct((1, rows), jnp.int32)],
-        in_specs=[VMEM] * 3,
-        out_specs=[VMEM] * 2,
+        out_shape=jax.ShapeDtypeStruct((payload.shape[0] - 16, 128), jnp.bfloat16),
+        in_specs=[VMEM] * 2,
+        out_specs=VMEM,
         compiler_params=SMALL,
         name="sort_rows",
-    )(*flat(raw))
+    )(embeddings, place)
     near, direct, first, far = pl.pallas_call(
         join_kernel,
         out_shape=[payload] * 4,
-        in_specs=[VMEM] * 4,
+        in_specs=[VMEM] * 6,
         out_specs=[VMEM] * 4,
         compiler_params=SMALL,
         name="join_cores",
-    )(keep, *flat(swapped))
+    )(keep, kept_ids, earlier, swapped[0], row(swapped[1]), row(swapped[2]))
     crossed = lax.ppermute(far, "clus", [(c, c ^ 2) for c in range(4)])
     arrived = []
     for other, place in BLOCKS:

time: 35.3 us -> 35.1 us (level)
  waiting for transfers between devices: 3.87 us -> 5.07 us
  starting transfers between devices: 16.2 us -> 15 us
  local copies, waits for them, and re-layouts: 1.73 us -> 0.68 us
  blocking collectives: 11.2 us -> 11.9 us
    ppermute x6, starting transfers between devices: 12.7 us -> 11.1 us  [to_meeting(): return lax.ppermute(value, everyone, pairs)]
    unnamed x6, local copies, waits for them, and re-layouts: 1.73 us -> 0.68 us
    ppermute x6, waiting for transfers between devices: 3.86 us -> 4.72 us  [to_meeting(): return lax.ppermute(value, everyone, pairs)]
    all_to_all x1, blocking collectives: 11.2 us -> 11.9 us  [meet(): lax.all_to_all(best, everyone, split_axis=0, concat_axis=0, tiled=True)]
    ppermute x1, starting transfers between devices: 2.56 us -> 2.92 us  [meet(): crossed = lax.ppermute(far, 'clus', [(c, c ^ 2) for c in range(4)])]
    pallas_call x2 -> x4, Pallas kernels: 1.04 us -> 1.28 us  [the longest x1 0.59 us: meet(): pl.pallas_call(join_kernel, out_shape=[payload] * 4, in_specs=[VMEM] * 6,...]
  transfers between devices with their start and end apart: 10 -> 10, of which waited for: 2 -> 3; matrix products, arithmetic and copies ran while one was open for 0% -> 0% of each run, Pallas kernels for 1% -> 2%
where the time goes in v13:
time: 35.1 us; the launch traced here: 34.9 us
  starting transfers between devices  15 us (43%)
  blocking collectives  11.9 us (34%)
  waiting for transfers between devices  5.07 us (14%)
  Pallas kernels  2.13 us (6%)
  local copies, waits for them, and re-layouts  0.68 us (2%)
    all_to_all x1, blocking collectives, meet(): lax.all_to_all(best, everyone, split_axis=0, concat_axis=0, tiled=True)  11.9 us
    ppermute x6, starting transfers between devices, to_meeting(): return lax.ppermute(value, everyone, pairs)  11.1 us
    ppermute x6, waiting for transfers between devices, to_meeting(): return lax.ppermute(value, everyone, pairs)  4.72 us
    ppermute x1, starting transfers between devices, meet(): crossed = lax.ppermute(far, 'clus', [(c, c ^ 2) for c in range(4)])  2.92 us
    ppermute x3, starting transfers between devices, meet(): lax.ppermute(value, 'clus', [(c, c ^ 1) for c in range(4)])  0.96 us
    pallas_call x1, Pallas kernels, meet(): pl.pallas_call(home_kernel, out_shape=jax.ShapeDtypeStruct((1, rows), jnp...  0.83 us
  transfers between devices with their start and end apart: 10, of which 3 were waited for; matrix products, arithmetic and copies ran while one was open for 0% of the time, Pallas kernels for 2%

profile of v13, /device:TPU:0, one launch (start us, length us, event | category | flops | bytes accessed | tf_op | source)
XLA Modules:
  0.0 34.9 jit_solution(1046780257582392982)
XLA Ops:
  0.0 0.0 copy-start
  0.0 0.5 %collective-permute-start.1 = (s32[256]{0:T(256)}, s32[256]{0:T(256)S(1)}, u32[]{:S(2)}, u32[]{:S(2)}) collective-permute-start(s32[256]{0:T(256)} %param.4), channel_id=1, source_target_pairs={{0,1},{1,0},{2,3},{3,2},{4,5},{5,4},{6,7},{7,6},{8,9},{9,8},{10,11... | collective-permute-start | bytes 3080 | tf_op jit(solution)/shard_map/ppermute | solution.py:266
  0.5 0.1 collective-permute-start.2
  0.5 0.4 %collective-permute-start = (bf16[256,1024]{1,0:T(8,128)(2,1)}, bf16[256,1024]{1,0:T(8,128)(2,1)S(1)}, u32[]{:S(2)}, u32[]{:S(2)}) collective-permute-start(bf16[256,1024]{1,0:T(8,128)(2,1)} %emb_ref.1), channel_id=1, source_target_pairs={{0,1},{1,0},{2,3},{3,2},{4,5},{5,4},{6,7},{7,6},{8,9},{9,8},{10,11... | collective-permute-start | bytes 1572872 | tf_op jit(solution)/shard_map/ppermute | solution.py:266
  1.0 0.0 copy-start.2
  1.0 0.0 copy-start.1
  1.0 0.6 %copy-done.2 = s32[256]{0:T(256)S(1)} copy-done((s32[256]{0:T(256)S(1)}, s32[256]{0:T(256)}, u32[]{:S(2)}) %copy-start.2) | copy-done | bytes 1048
  1.6 0.0 copy-done.1
  1.7 0.3 rank_rows.1
  2.0 0.0 copy-done
  2.0 0.4 %sort_rows.1.keep_ref = bf16[1024,128]{1,0:T(8,128)(2,1)S(1)} custom-call(bf16[256,1024]{1,0:T(8,128)(2,1)S(1)} %copy-done, bf16[128,256]{1,0:T(8,128)(2,1)S(1)} %get-tuple-element.12.place_ref), custom_call_target="tpu_custom_call" | custom-call | tf_op jit(solution)/shard_map/sort_rows/pallas_call | solution.py:292
  2.3 0.0 collective-permute-done.1
  2.4 0.0 collective-permute-done.2
  2.4 0.3 collective-permute-done.emb_ref
  2.7 0.6 %join_cores.1 = (bf16[1040,128]{1,0:T(8,128)(2,1)S(1)}, bf16[1040,128]{1,0:T(8,128)(2,1)S(1)}, bf16[1040,128]{1,0:T(8,128)(2,1)S(1)}, bf16[1040,128]{1,0:T(8,128)(2,1)S(1)}) custom-call(bf16[1024,128]{1,0:T(8,128)(2,1)S(1)} %sort_rows.1.keep_ref, f32[16,128]{1,0:T(8,128)S(1)} %get-tuple-element.13.kept_ids_ref, ...), custom_call_target="tpu_custom_call" | custom-call | tf_op jit(solution)/shard_map/join_cores/pallas_call | solution.py:300
  3.3 2.9 %collective-permute-start.3 = (bf16[1040,128]{1,0:T(8,128)(2,1)S(1)}, bf16[1040,128]{1,0:T(8,128)(2,1)S(1)}, u32[]{:S(2)}, u32[]{:S(2)}) collective-permute-start(bf16[1040,128]{1,0:T(8,128)(2,1)S(1)} %get-tuple-element.15), channel_id=1, source_target_pairs={{0,2},{1,3},{2,0},{3,1},{4,6},{5,7},{6,4},{7,5},{8,10},{9,11},{10,... | collective-permute-start | bytes 798728 | tf_op jit(solution)/shard_map/ppermute | solution.py:308
  6.2 0.7 %collective-permute-start.4 = (bf16[1040,128]{1,0:T(8,128)(2,1)S(1)}, bf16[1040,128]{1,0:T(8,128)(2,1)S(1)}, u32[]{:S(2)}, u32[]{:S(2)}) collective-permute-start(bf16[1040,128]{1,0:T(8,128)(2,1)S(1)} %get-tuple-element.16), channel_id=1, source_target_pairs={{12,4},{1,9},{14,6},{3,11},{28,20},{17,25},{30,22},{19,27}} | collective-permute-start | bytes 798728 | tf_op jit(solution)/shard_map/ppermute | solution.py:263
  6.9 0.7 %collective-permute-start.5 = (bf16[1040,128]{1,0:T(8,128)(2,1)S(1)}, bf16[1040,128]{1,0:T(8,128)(2,1)S(1)}, u32[]{:S(2)}, u32[]{:S(2)}) collective-permute-start(bf16[1040,128]{1,0:T(8,128)(2,1)S(1)} %get-tuple-element.17), channel_id=1, source_target_pairs={{14,4},{3,9},{12,6},{1,11},{30,20},{19,25},{28,22},{17,27}} | collective-permute-start | bytes 798728 | tf_op jit(solution)/shard_map/ppermute | solution.py:263
  7.6 0.7 %collective-permute-start.7 = (bf16[1040,128]{1,0:T(8,128)(2,1)S(1)}, bf16[1040,128]{1,0:T(8,128)(2,1)S(1)}, u32[]{:S(2)}, u32[]{:S(2)}) collective-permute-start(bf16[1040,128]{1,0:T(8,128)(2,1)S(1)} %get-tuple-element.14.refs_0_), channel_id=1, source_target_pairs={{8,4},{5,9},{10,6},{7,11},{24,20},{21,25},{26,22},{23,27}} | collective-permute-start | bytes 798728 | tf_op jit(solution)/shard_map/ppermute | solution.py:263
  8.3 5.3 %collective-permute-start.6 = (bf16[1040,128]{1,0:T(8,128)(2,1)S(1)}, bf16[1040,128]{1,0:T(8,128)(2,1)S(1)}, u32[]{:S(2)}, u32[]{:S(2)}) collective-permute-start(bf16[1040,128]{1,0:T(8,128)(2,1)S(1)} %get-tuple-element.14.refs_0_), channel_id=1, source_target_pairs={{0,4},{13,9},{2,6},{15,11},{16,20},{29,25},{18,22},{31,27}} | collective-permute-start | bytes 798728 | tf_op jit(solution)/shard_map/ppermute | solution.py:263
  13.6 0.0 collective-permute-done.3.refs_1_
  13.6 3.0 %collective-permute-start.9 = (bf16[1040,128]{1,0:T(8,128)(2,1)S(1)}, bf16[1040,128]{1,0:T(8,128)(2,1)S(1)}, u32[]{:S(2)}, u32[]{:S(2)}) collective-permute-start(bf16[1040,128]{1,0:T(8,128)(2,1)S(1)} %collective-permute-done.3.refs_1_), channel_id=1, source_target_pairs={{0,4},{13,9},{2,6},{15,11},{16,20},{29,25},{18,22},{31,27}} | collective-permute-start | bytes 798728 | tf_op jit(solution)/shard_map/ppermute | solution.py:263
  16.7 0.0 collective-permute-done.4.refs_2_
  16.7 0.7 %collective-permute-start.8 = (bf16[1040,128]{1,0:T(8,128)(2,1)S(1)}, bf16[1040,128]{1,0:T(8,128)(2,1)S(1)}, u32[]{:S(2)}, u32[]{:S(2)}) collective-permute-start(bf16[1040,128]{1,0:T(8,128)(2,1)S(1)} %collective-permute-done.3.refs_1_), channel_id=1, source_target_pairs={{8,4},{5,9},{10,6},{7,11},{24,20},{21,25},{26,22},{23,27}} | collective-permute-start | bytes 798728 | tf_op jit(solution)/shard_map/ppermute | solution.py:263
  17.4 0.0 collective-permute-done.5.refs_3_
  17.4 0.0 collective-permute-done.7.refs_5_
  17.4 1.9 %collective-permute-done.6.refs_4_ = bf16[1040,128]{1,0:T(8,128)(2,1)S(1)} collective-permute-done((bf16[1040,128]{1,0:T(8,128)(2,1)S(1)}, bf16[1040,128]{1,0:T(8,128)(2,1)S(1)}, u32[]{:S(2)}, u32[]{:S(2)}) %collective-permute-start.6) | collective-permute-done | bytes 266272 | tf_op jit(solution)/shard_map/ppermute | solution.py:263
  19.3 2.9 %collective-permute-done.9.refs_7_ = bf16[1040,128]{1,0:T(8,128)(2,1)S(1)} collective-permute-done((bf16[1040,128]{1,0:T(8,128)(2,1)S(1)}, bf16[1040,128]{1,0:T(8,128)(2,1)S(1)}, u32[]{:S(2)}, u32[]{:S(2)}) %collective-permute-start.9) | collective-permute-done | bytes 266272 | tf_op jit(solution)/shard_map/ppermute | solution.py:263
  22.1 0.0 collective-permute-done.8.refs_6_
  22.1 11.9 %all_to_all.5.got_ref = f32[16,1,128]{2,1,0:T(1,128)S(1)} all-to-all(f32[16,1,128]{2,1,0:T(1,128)S(1)} %meet_6_8.1), channel_id=1, replica_groups=mesh['groups'=2,'blk'=4,'clus'=4] {'blk','clus'}, dimensions={0} | all-to-all | bytes 16384 | tf_op jit(solution)/shard_map/all_to_all | solution.py:332
  34.0 0.8 %home_scores.1 = f32[1,256]{1,0:T(1,128)} custom-call(f32[16,1,128]{2,1,0:T(1,128)S(1)} %all_to_all.5.got_ref, s32[1,256]{1,0:T(1,128)S(1)} %get-tuple-element.18.target_ref), custom_call_target="tpu_custom_call" | custom-call | tf_op jit(solution)/shard_map/home_scores/pallas_call | solution.py:333
  (4 shorter events, 0.0 us)
Async XLA Ops:
  0.0 2.0 %copy-start = (bf16[256,1024]{1,0:T(8,128)(2,1)S(1)}, bf16[256,1024]{1,0:T(8,128)(2,1)}, u32[]{:S(2)}) copy-start(bf16[256,1024]{1,0:T(8,128)(2,1)} %emb_ref.1) | copy-start | bytes 1572868
  0.0 2.3 %collective-permute-start.1 = (s32[256]{0:T(256)}, s32[256]{0:T(256)S(1)}, u32[]{:S(2)}, u32[]{:S(2)}) collective-permute-start(s32[256]{0:T(256)} %param.4), channel_id=1, source_target_pairs={{0,1},{1,0},{2,3},{3,2},{4,5},{5,4},{6,7},{7,6},{8,9},{9,8},{10,11... | collective-permute-start | bytes 3080 | tf_op jit(solution)/shard_map/ppermute | solution.py:266
  0.5 1.9 %collective-permute-start.2 = (s32[256]{0:T(256)}, s32[256]{0:T(256)S(1)}, u32[]{:S(2)}, u32[]{:S(2)}) collective-permute-start(s32[256]{0:T(256)} %param.5), channel_id=1, source_target_pairs={{0,1},{1,0},{2,3},{3,2},{4,5},{5,4},{6,7},{7,6},{8,9},{9,8},{10,11... | collective-permute-start | bytes 3080 | tf_op jit(solution)/shard_map/ppermute | solution.py:266
  0.5 2.2 %collective-permute-start = (bf16[256,1024]{1,0:T(8,128)(2,1)}, bf16[256,1024]{1,0:T(8,128)(2,1)S(1)}, u32[]{:S(2)}, u32[]{:S(2)}) collective-permute-start(bf16[256,1024]{1,0:T(8,128)(2,1)} %emb_ref.1), channel_id=1, source_target_pairs={{0,1},{1,0},{2,3},{3,2},{4,5},{5,4},{6,7},{7,6},{8,9},{9,8},{10,11... | collective-permute-start | bytes 1572872 | tf_op jit(solution)/shard_map/ppermute | solution.py:266
  1.0 0.7 %copy-start.2 = (s32[256]{0:T(256)S(1)}, s32[256]{0:T(256)}, u32[]{:S(2)}) copy-start(s32[256]{0:T(256)} %param.5) | copy-start | bytes 3076
  1.0 0.7 %copy-start.1 = (s32[256]{0:T(256)S(1)}, s32[256]{0:T(256)}, u32[]{:S(2)}) copy-start(s32[256]{0:T(256)} %param.4) | copy-start | bytes 3076
  3.3 10.3 %collective-permute-start.3 = (bf16[1040,128]{1,0:T(8,128)(2,1)S(1)}, bf16[1040,128]{1,0:T(8,128)(2,1)S(1)}, u32[]{:S(2)}, u32[]{:S(2)}) collective-permute-start(bf16[1040,128]{1,0:T(8,128)(2,1)S(1)} %get-tuple-element.15), channel_id=1, source_target_pairs={{0,2},{1,3},{2,0},{3,1},{4,6},{5,7},{6,4},{7,5},{8,10},{9,11},{10,... | collective-permute-start | bytes 798728 | tf_op jit(solution)/shard_map/ppermute | solution.py:308
  6.2 10.4 %collective-permute-start.4 = (bf16[1040,128]{1,0:T(8,128)(2,1)S(1)}, bf16[1040,128]{1,0:T(8,128)(2,1)S(1)}, u32[]{:S(2)}, u32[]{:S(2)}) collective-permute-start(bf16[1040,128]{1,0:T(8,128)(2,1)S(1)} %get-tuple-element.16), channel_id=1, source_target_pairs={{12,4},{1,9},{14,6},{3,11},{28,20},{17,25},{30,22},{19,27}} | collective-permute-start | bytes 798728 | tf_op jit(solution)/shard_map/ppermute | solution.py:263
  6.9 10.5 %collective-permute-start.5 = (bf16[1040,128]{1,0:T(8,128)(2,1)S(1)}, bf16[1040,128]{1,0:T(8,128)(2,1)S(1)}, u32[]{:S(2)}, u32[]{:S(2)}) collective-permute-start(bf16[1040,128]{1,0:T(8,128)(2,1)S(1)} %get-tuple-element.17), channel_id=1, source_target_pairs={{14,4},{3,9},{12,6},{1,11},{30,20},{19,25},{28,22},{17,27}} | collective-permute-start | bytes 798728 | tf_op jit(solution)/shard_map/ppermute | solution.py:263
  7.6 9.8 %collective-permute-start.7 = (bf16[1040,128]{1,0:T(8,128)(2,1)S(1)}, bf16[1040,128]{1,0:T(8,128)(2,1)S(1)}, u32[]{:S(2)}, u32[]{:S(2)}) collective-permute-start(bf16[1040,128]{1,0:T(8,128)(2,1)S(1)} %get-tuple-element.14.refs_0_), channel_id=1, source_target_pairs={{8,4},{5,9},{10,6},{7,11},{24,20},{21,25},{26,22},{23,27}} | collective-permute-start | bytes 798728 | tf_op jit(solution)/shard_map/ppermute | solution.py:263
  8.3 11.0 %collective-permute-start.6 = (bf16[1040,128]{1,0:T(8,128)(2,1)S(1)}, bf16[1040,128]{1,0:T(8,128)(2,1)S(1)}, u32[]{:S(2)}, u32[]{:S(2)}) collective-permute-start(bf16[1040,128]{1,0:T(8,128)(2,1)S(1)} %get-tuple-element.14.refs_0_), channel_id=1, source_target_pairs={{0,4},{13,9},{2,6},{15,11},{16,20},{29,25},{18,22},{31,27}} | collective-permute-start | bytes 798728 | tf_op jit(solution)/shard_map/ppermute | solution.py:263
  13.6 8.5 %collective-permute-start.9 = (bf16[1040,128]{1,0:T(8,128)(2,1)S(1)}, bf16[1040,128]{1,0:T(8,128)(2,1)S(1)}, u32[]{:S(2)}, u32[]{:S(2)}) collective-permute-start(bf16[1040,128]{1,0:T(8,128)(2,1)S(1)} %collective-permute-done.3.refs_1_), channel_id=1, source_target_pairs={{0,4},{13,9},{2,6},{15,11},{16,20},{29,25},{18,22},{31,27}} | collective-permute-start | bytes 798728 | tf_op jit(solution)/shard_map/ppermute | solution.py:263
  16.7 5.4 %collective-permute-start.8 = (bf16[1040,128]{1,0:T(8,128)(2,1)S(1)}, bf16[1040,128]{1,0:T(8,128)(2,1)S(1)}, u32[]{:S(2)}, u32[]{:S(2)}) collective-permute-start(bf16[1040,128]{1,0:T(8,128)(2,1)S(1)} %collective-permute-done.3.refs_1_), channel_id=1, source_target_pairs={{8,4},{5,9},{10,6},{7,11},{24,20},{21,25},{26,22},{23,27}} | collective-permute-start | bytes 798728 | tf_op jit(solution)/shard_map/ppermute | solution.py:263

commit v14 on v13

--- a/solution.py
+++ b/solution.py
@@ -74,7 +74,7 @@
 
 NEAR, ACROSS, FAR = 0, 2, 3
 BLOCKS = (
-    (0, None), (1, None), (0, FAR), (1, FAR), (0, NEAR), (0, ACROSS), (1, ACROSS), (1, NEAR),
+    (0, None), (1, None), (0, ACROSS), (1, FAR), (0, NEAR), (0, FAR), (1, NEAR), (1, ACROSS),
 )
 
 
@@ -145,9 +145,9 @@
     put_slabs(keep_ref, unit_slots(place_ref[...], emb_ref[...]))
 
 
-def join_kernel(keep_ref, kept_ids_ref, earlier_ref, emb_ref, cluster_ref, ids_ref, *out_refs):
-    _, place, moved = ranked(cluster_ref[...], ids_ref[...], earlier_ref[...])
-    unit = unit_slots(place, emb_ref[...])
+def join_kernel(keep_ref, kept_ids_ref, emb_ref, place_ref, ids_ref, *out_refs):
+    unit = unit_slots(place_ref[...], emb_ref[...])
+    moved = ids_ref[...]
     u, _ = here()
     core = lax.rem(u, 2)
     tail = keep_ref.shape[0]
@@ -277,18 +277,23 @@
         cost_estimate=ahead,
         name="earlier_rows",
     )()
-    target, place, kept_ids = pl.pallas_call(
-        rank_kernel,
-        out_shape=[
-            jax.ShapeDtypeStruct((1, rows), jnp.int32),
-            jax.ShapeDtypeStruct((2 * CAP, rows), jnp.bfloat16),
-            jax.ShapeDtypeStruct((16, 2 * CAP), jnp.float32),
-        ],
-        in_specs=[VMEM] * 3,
-        out_specs=[VMEM] * 3,
-        compiler_params=SMALL,
-        name="rank_rows",
-    )(row(cluster), row(row_ids), earlier)
+
+    def rank(clusters, ids, name):
+        return pl.pallas_call(
+            rank_kernel,
+            out_shape=[
+                jax.ShapeDtypeStruct((1, rows), jnp.int32),
+                jax.ShapeDtypeStruct((2 * CAP, rows), jnp.bfloat16),
+                jax.ShapeDtypeStruct((16, 2 * CAP), jnp.float32),
+            ],
+            in_specs=[VMEM] * 3,
+            out_specs=[VMEM] * 3,
+            compiler_params=SMALL,
+            name=name,
+        )(row(clusters), row(ids), earlier)
+
+    target, place, kept_ids = rank(cluster, row_ids, "rank_rows")
+    _, place2, ids2 = rank(swapped[1], swapped[2], "rank_others")
     keep = pl.pallas_call(
         sort_kernel,
         out_shape=jax.ShapeDtypeStruct((payload.shape[0] - 16, 128), jnp.bfloat16),
@@ -300,17 +305,17 @@
     near, direct, first, far = pl.pallas_call(
         join_kernel,
         out_shape=[payload] * 4,
-        in_specs=[VMEM] * 6,
+        in_specs=[VMEM] * 5,
         out_specs=[VMEM] * 4,
         compiler_params=SMALL,
         name="join_cores",
-    )(keep, kept_ids, earlier, swapped[0], row(swapped[1]), row(swapped[2]))
+    )(keep, kept_ids, swapped[0], place2, ids2)
     crossed = lax.ppermute(far, "clus", [(c, c ^ 2) for c in range(4)])
     arrived = []
     for other, place in BLOCKS:
         if other and place == FAR:
             arrived.append(to_meeting(direct, place, cross=1))
-        elif not other and place == FAR:
+        elif not other and place == ACROSS:
             arrived.append(to_meeting(first, place))
         else:
             value = crossed if other else near

time: 35.1 us -> 37.3 us (1.063)
  starting transfers between devices: 15 us -> 17.9 us
  waiting for transfers between devices: 5.07 us -> 3.83 us
  Pallas kernels: 2.13 us -> 2.72 us
    ppermute x6, starting transfers between devices: 11.1 us -> 14.3 us  [to_meeting(): return lax.ppermute(value, everyone, pairs)]
    ppermute x6, waiting for transfers between devices: 4.72 us -> 3.82 us  [to_meeting(): return lax.ppermute(value, everyone, pairs)]
    pallas_call x2 -> x3, Pallas kernels: 0.89 us -> 1.45 us  [the longest x2 1.04 us: rank(): pl.pallas_call(rank_kernel, out_shape=[jax.ShapeDtypeStruct((1, rows), jn...]
  transfers between devices with their start and end apart: 10 -> 10, of which waited for: 3 -> 1; matrix products, arithmetic and copies ran while one was open for 0% -> 0% of each run, Pallas kernels for 2% -> 4%
where the time goes in v14:
time: 37.3 us; the launch traced here: 37.1 us
  starting transfers between devices  17.9 us (48%)
  blocking collectives  11.8 us (32%)
  waiting for transfers between devices  3.83 us (10%)
  Pallas kernels  2.72 us (7%)
  local copies, waits for them, and re-layouts  0.68 us (2%)
    ppermute x6, starting transfers between devices, to_meeting(): return lax.ppermute(value, everyone, pairs)  14.3 us
    all_to_all x1, blocking collectives, meet(): lax.all_to_all(best, everyone, split_axis=0, concat_axis=0, tiled=True)  11.8 us
    ppermute x6, waiting for transfers between devices, to_meeting(): return lax.ppermute(value, everyone, pairs)  3.82 us
    ppermute x1, starting transfers between devices, meet(): crossed = lax.ppermute(far, 'clus', [(c, c ^ 2) for c in range(4)])  2.61 us
    pallas_call x2, Pallas kernels, rank(): pl.pallas_call(rank_kernel, out_shape=[jax.ShapeDtypeStruct((1, rows), jn...  1.04 us
    ppermute x3, starting transfers between devices, meet(): lax.ppermute(value, 'clus', [(c, c ^ 1) for c in range(4)])  0.96 us
    pallas_call x1, Pallas kernels, meet(): pl.pallas_call(home_kernel, out_shape=jax.ShapeDtypeStruct((1, rows), jnp...  0.83 us
  transfers between devices with their start and end apart: 10, of which 1 were waited for; matrix products, arithmetic and copies ran while one was open for 0% of the time, Pallas kernels for 4%

profile of v14, /device:TPU:0, one launch (start us, length us, event | category | flops | bytes accessed | tf_op | source)
XLA Modules:
  0.0 37.1 jit_solution(6701243363120550273)
XLA Ops:
  0.0 0.0 copy-start
  0.0 0.5 %collective-permute-start.1 = (s32[256]{0:T(256)}, s32[256]{0:T(256)S(1)}, u32[]{:S(2)}, u32[]{:S(2)}) collective-permute-start(s32[256]{0:T(256)} %param.4), channel_id=1, source_target_pairs={{0,1},{1,0},{2,3},{3,2},{4,5},{5,4},{6,7},{7,6},{8,9},{9,8},{10,11... | collective-permute-start | bytes 3080 | tf_op jit(solution)/shard_map/ppermute | solution.py:266
  0.5 0.1 collective-permute-start.2
  0.5 0.4 %collective-permute-start = (bf16[256,1024]{1,0:T(8,128)(2,1)}, bf16[256,1024]{1,0:T(8,128)(2,1)S(1)}, u32[]{:S(2)}, u32[]{:S(2)}) collective-permute-start(bf16[256,1024]{1,0:T(8,128)(2,1)} %emb_ref.1), channel_id=1, source_target_pairs={{0,1},{1,0},{2,3},{3,2},{4,5},{5,4},{6,7},{7,6},{8,9},{9,8},{10,11... | collective-permute-start | bytes 1572872 | tf_op jit(solution)/shard_map/ppermute | solution.py:266
  1.0 0.0 copy-start.2
  1.0 0.0 copy-start.1
  1.0 0.6 %copy-done.2 = s32[256]{0:T(256)S(1)} copy-done((s32[256]{0:T(256)S(1)}, s32[256]{0:T(256)}, u32[]{:S(2)}) %copy-start.2) | copy-done | bytes 1048
  1.6 0.0 copy-done.1
  1.7 0.3 rank_rows.1
  2.0 0.0 copy-done
  2.0 0.4 sort_rows.1.keep_ref
  2.4 0.0 collective-permute-done.1
  2.4 0.0 collective-permute-done.2
  2.4 0.7 %rank_others.1 = (s32[1,256]{1,0:T(1,128)}, bf16[128,256]{1,0:T(8,128)(2,1)S(1)}, f32[16,128]{1,0:T(8,128)S(1)}) custom-call(s32[1,256]{1,0:T(1,128)S(1)} %bitcast.7, s32[1,256]{1,0:T(1,128)S(1)} %bitcast.8, bf16[256,256]{1,0:T(8,128)(2,1)S(1)} %earlier_rows.1.earlier_ref), custom_call_target="tpu_custom_call" | custom-call | tf_op jit(solution)/shard_map/rank_others/pallas_call | solution.py:282
  3.1 0.0 collective-permute-done.emb_ref
  3.1 0.4 %join_cores.1 = (bf16[1040,128]{1,0:T(8,128)(2,1)S(1)}, bf16[1040,128]{1,0:T(8,128)(2,1)S(1)}, bf16[1040,128]{1,0:T(8,128)(2,1)S(1)}, bf16[1040,128]{1,0:T(8,128)(2,1)S(1)}) custom-call(bf16[1024,128]{1,0:T(8,128)(2,1)S(1)} %sort_rows.1.keep_ref, f32[16,128]{1,0:T(8,128)S(1)} %get-tuple-element.15.kept_ids_ref, ...), custom_call_target="tpu_custom_call" | custom-call | tf_op jit(solution)/shard_map/join_cores/pallas_call | solution.py:305
  3.5 2.6 %collective-permute-start.3 = (bf16[1040,128]{1,0:T(8,128)(2,1)S(1)}, bf16[1040,128]{1,0:T(8,128)(2,1)S(1)}, u32[]{:S(2)}, u32[]{:S(2)}) collective-permute-start(bf16[1040,128]{1,0:T(8,128)(2,1)S(1)} %get-tuple-element.19), channel_id=1, source_target_pairs={{0,2},{1,3},{2,0},{3,1},{4,6},{5,7},{6,4},{7,5},{8,10},{9,11},{10,... | collective-permute-start | bytes 798728 | tf_op jit(solution)/shard_map/ppermute | solution.py:313
  6.2 0.7 %collective-permute-start.4 = (bf16[1040,128]{1,0:T(8,128)(2,1)S(1)}, bf16[1040,128]{1,0:T(8,128)(2,1)S(1)}, u32[]{:S(2)}, u32[]{:S(2)}) collective-permute-start(bf16[1040,128]{1,0:T(8,128)(2,1)S(1)} %get-tuple-element.20), channel_id=1, source_target_pairs={{8,4},{5,9},{10,6},{7,11},{24,20},{21,25},{26,22},{23,27}} | collective-permute-start | bytes 798728 | tf_op jit(solution)/shard_map/ppermute | solution.py:263
  6.8 0.7 %collective-permute-start.5 = (bf16[1040,128]{1,0:T(8,128)(2,1)S(1)}, bf16[1040,128]{1,0:T(8,128)(2,1)S(1)}, u32[]{:S(2)}, u32[]{:S(2)}) collective-permute-start(bf16[1040,128]{1,0:T(8,128)(2,1)S(1)} %get-tuple-element.21), channel_id=1, source_target_pairs={{14,4},{3,9},{12,6},{1,11},{30,20},{19,25},{28,22},{17,27}} | collective-permute-start | bytes 798728 | tf_op jit(solution)/shard_map/ppermute | solution.py:263
  7.5 0.7 %collective-permute-start.7 = (bf16[1040,128]{1,0:T(8,128)(2,1)S(1)}, bf16[1040,128]{1,0:T(8,128)(2,1)S(1)}, u32[]{:S(2)}, u32[]{:S(2)}) collective-permute-start(bf16[1040,128]{1,0:T(8,128)(2,1)S(1)} %get-tuple-element.18.refs_0_), channel_id=1, source_target_pairs={{12,4},{1,9},{14,6},{3,11},{28,20},{17,25},{30,22},{19,27}} | collective-permute-start | bytes 798728 | tf_op jit(solution)/shard_map/ppermute | solution.py:263
  8.2 5.3 %collective-permute-start.6 = (bf16[1040,128]{1,0:T(8,128)(2,1)S(1)}, bf16[1040,128]{1,0:T(8,128)(2,1)S(1)}, u32[]{:S(2)}, u32[]{:S(2)}) collective-permute-start(bf16[1040,128]{1,0:T(8,128)(2,1)S(1)} %get-tuple-element.18.refs_0_), channel_id=1, source_target_pairs={{0,4},{13,9},{2,6},{15,11},{16,20},{29,25},{18,22},{31,27}} | collective-permute-start | bytes 798728 | tf_op jit(solution)/shard_map/ppermute | solution.py:263
  13.6 0.0 collective-permute-done.3.refs_1_
  13.6 0.7 %collective-permute-start.9 = (bf16[1040,128]{1,0:T(8,128)(2,1)S(1)}, bf16[1040,128]{1,0:T(8,128)(2,1)S(1)}, u32[]{:S(2)}, u32[]{:S(2)}) collective-permute-start(bf16[1040,128]{1,0:T(8,128)(2,1)S(1)} %collective-permute-done.3.refs_1_), channel_id=1, source_target_pairs={{8,4},{5,9},{10,6},{7,11},{24,20},{21,25},{26,22},{23,27}} | collective-permute-start | bytes 798728 | tf_op jit(solution)/shard_map/ppermute | solution.py:263
  14.2 0.0 collective-permute-done.4.refs_2_
  14.3 6.3 %collective-permute-start.8 = (bf16[1040,128]{1,0:T(8,128)(2,1)S(1)}, bf16[1040,128]{1,0:T(8,128)(2,1)S(1)}, u32[]{:S(2)}, u32[]{:S(2)}) collective-permute-start(bf16[1040,128]{1,0:T(8,128)(2,1)S(1)} %collective-permute-done.3.refs_1_), channel_id=1, source_target_pairs={{0,4},{13,9},{2,6},{15,11},{16,20},{29,25},{18,22},{31,27}} | collective-permute-start | bytes 798728 | tf_op jit(solution)/shard_map/ppermute | solution.py:263
  20.5 0.0 collective-permute-done.5.refs_3_
  20.6 0.0 collective-permute-done.7.refs_5_
  20.6 0.0 collective-permute-done.6.refs_4_
  20.6 0.0 collective-permute-done.9.refs_7_
  20.6 3.8 %collective-permute-done.8.refs_6_ = bf16[1040,128]{1,0:T(8,128)(2,1)S(1)} collective-permute-done((bf16[1040,128]{1,0:T(8,128)(2,1)S(1)}, bf16[1040,128]{1,0:T(8,128)(2,1)S(1)}, u32[]{:S(2)}, u32[]{:S(2)}) %collective-permute-start.8) | collective-permute-done | bytes 266272 | tf_op jit(solution)/shard_map/ppermute | solution.py:263
  24.4 11.8 %all_to_all.5.got_ref = f32[16,1,128]{2,1,0:T(1,128)S(1)} all-to-all(f32[16,1,128]{2,1,0:T(1,128)S(1)} %meet_6_8.1), channel_id=1, replica_groups=mesh['groups'=2,'blk'=4,'clus'=4] {'blk','clus'}, dimensions={0} | all-to-all | bytes 16384 | tf_op jit(solution)/shard_map/all_to_all | solution.py:337
  36.3 0.8 %home_scores.1 = f32[1,256]{1,0:T(1,128)} custom-call(f32[16,1,128]{2,1,0:T(1,128)S(1)} %all_to_all.5.got_ref, s32[1,256]{1,0:T(1,128)S(1)} %get-tuple-element.22.target_ref), custom_call_target="tpu_custom_call" | custom-call | tf_op jit(solution)/shard_map/home_scores/pallas_call | solution.py:338
  (4 shorter events, 0.1 us)
Async XLA Ops:
  0.0 2.0 %copy-start = (bf16[256,1024]{1,0:T(8,128)(2,1)S(1)}, bf16[256,1024]{1,0:T(8,128)(2,1)}, u32[]{:S(2)}) copy-start(bf16[256,1024]{1,0:T(8,128)(2,1)} %emb_ref.1) | copy-start | bytes 1572868
  0.0 2.4 %collective-permute-start.1 = (s32[256]{0:T(256)}, s32[256]{0:T(256)S(1)}, u32[]{:S(2)}, u32[]{:S(2)}) collective-permute-start(s32[256]{0:T(256)} %param.4), channel_id=1, source_target_pairs={{0,1},{1,0},{2,3},{3,2},{4,5},{5,4},{6,7},{7,6},{8,9},{9,8},{10,11... | collective-permute-start | bytes 3080 | tf_op jit(solution)/shard_map/ppermute | solution.py:266
  0.5 1.9 %collective-permute-start.2 = (s32[256]{0:T(256)}, s32[256]{0:T(256)S(1)}, u32[]{:S(2)}, u32[]{:S(2)}) collective-permute-start(s32[256]{0:T(256)} %param.5), channel_id=1, source_target_pairs={{0,1},{1,0},{2,3},{3,2},{4,5},{5,4},{6,7},{7,6},{8,9},{9,8},{10,11... | collective-permute-start | bytes 3080 | tf_op jit(solution)/shard_map/ppermute | solution.py:266
  0.5 2.6 %collective-permute-start = (bf16[256,1024]{1,0:T(8,128)(2,1)}, bf16[256,1024]{1,0:T(8,128)(2,1)S(1)}, u32[]{:S(2)}, u32[]{:S(2)}) collective-permute-start(bf16[256,1024]{1,0:T(8,128)(2,1)} %emb_ref.1), channel_id=1, source_target_pairs={{0,1},{1,0},{2,3},{3,2},{4,5},{5,4},{6,7},{7,6},{8,9},{9,8},{10,11... | collective-permute-start | bytes 1572872 | tf_op jit(solution)/shard_map/ppermute | solution.py:266
  1.0 0.7 %copy-start.2 = (s32[256]{0:T(256)S(1)}, s32[256]{0:T(256)}, u32[]{:S(2)}) copy-start(s32[256]{0:T(256)} %param.5) | copy-start | bytes 3076
  1.0 0.7 %copy-start.1 = (s32[256]{0:T(256)S(1)}, s32[256]{0:T(256)}, u32[]{:S(2)}) copy-start(s32[256]{0:T(256)} %param.4) | copy-start | bytes 3076
  3.5 10.0 %collective-permute-start.3 = (bf16[1040,128]{1,0:T(8,128)(2,1)S(1)}, bf16[1040,128]{1,0:T(8,128)(2,1)S(1)}, u32[]{:S(2)}, u32[]{:S(2)}) collective-permute-start(bf16[1040,128]{1,0:T(8,128)(2,1)S(1)} %get-tuple-element.19), channel_id=1, source_target_pairs={{0,2},{1,3},{2,0},{3,1},{4,6},{5,7},{6,4},{7,5},{8,10},{9,11},{10,... | collective-permute-start | bytes 798728 | tf_op jit(solution)/shard_map/ppermute | solution.py:313
  6.2 8.1 %collective-permute-start.4 = (bf16[1040,128]{1,0:T(8,128)(2,1)S(1)}, bf16[1040,128]{1,0:T(8,128)(2,1)S(1)}, u32[]{:S(2)}, u32[]{:S(2)}) collective-permute-start(bf16[1040,128]{1,0:T(8,128)(2,1)S(1)} %get-tuple-element.20), channel_id=1, source_target_pairs={{8,4},{5,9},{10,6},{7,11},{24,20},{21,25},{26,22},{23,27}} | collective-permute-start | bytes 798728 | tf_op jit(solution)/shard_map/ppermute | solution.py:263
  6.8 13.7 %collective-permute-start.5 = (bf16[1040,128]{1,0:T(8,128)(2,1)S(1)}, bf16[1040,128]{1,0:T(8,128)(2,1)S(1)}, u32[]{:S(2)}, u32[]{:S(2)}) collective-permute-start(bf16[1040,128]{1,0:T(8,128)(2,1)S(1)} %get-tuple-element.21), channel_id=1, source_target_pairs={{14,4},{3,9},{12,6},{1,11},{30,20},{19,25},{28,22},{17,27}} | collective-permute-start | bytes 798728 | tf_op jit(solution)/shard_map/ppermute | solution.py:263
  7.5 13.1 %collective-permute-start.7 = (bf16[1040,128]{1,0:T(8,128)(2,1)S(1)}, bf16[1040,128]{1,0:T(8,128)(2,1)S(1)}, u32[]{:S(2)}, u32[]{:S(2)}) collective-permute-start(bf16[1040,128]{1,0:T(8,128)(2,1)S(1)} %get-tuple-element.18.refs_0_), channel_id=1, source_target_pairs={{12,4},{1,9},{14,6},{3,11},{28,20},{17,25},{30,22},{19,27}} | collective-permute-start | bytes 798728 | tf_op jit(solution)/shard_map/ppermute | solution.py:263
  8.2 12.4 %collective-permute-start.6 = (bf16[1040,128]{1,0:T(8,128)(2,1)S(1)}, bf16[1040,128]{1,0:T(8,128)(2,1)S(1)}, u32[]{:S(2)}, u32[]{:S(2)}) collective-permute-start(bf16[1040,128]{1,0:T(8,128)(2,1)S(1)} %get-tuple-element.18.refs_0_), channel_id=1, source_target_pairs={{0,4},{13,9},{2,6},{15,11},{16,20},{29,25},{18,22},{31,27}} | collective-permute-start | bytes 798728 | tf_op jit(solution)/shard_map/ppermute | solution.py:263
  13.6 7.1 %collective-permute-start.9 = (bf16[1040,128]{1,0:T(8,128)(2,1)S(1)}, bf16[1040,128]{1,0:T(8,128)(2,1)S(1)}, u32[]{:S(2)}, u32[]{:S(2)}) collective-permute-start(bf16[1040,128]{1,0:T(8,128)(2,1)S(1)} %collective-permute-done.3.refs_1_), channel_id=1, source_target_pairs={{8,4},{5,9},{10,6},{7,11},{24,20},{21,25},{26,22},{23,27}} | collective-permute-start | bytes 798728 | tf_op jit(solution)/shard_map/ppermute | solution.py:263
  14.3 10.2 %collective-permute-start.8 = (bf16[1040,128]{1,0:T(8,128)(2,1)S(1)}, bf16[1040,128]{1,0:T(8,128)(2,1)S(1)}, u32[]{:S(2)}, u32[]{:S(2)}) collective-permute-start(bf16[1040,128]{1,0:T(8,128)(2,1)S(1)} %collective-permute-done.3.refs_1_), channel_id=1, source_target_pairs={{0,4},{13,9},{2,6},{15,11},{16,20},{29,25},{18,22},{31,27}} | collective-permute-start | bytes 798728 | tf_op jit(solution)/shard_map/ppermute | solution.py:263

commit v15 on v13

--- a/solution.py
+++ b/solution.py
@@ -74,7 +74,7 @@
 
 NEAR, ACROSS, FAR = 0, 2, 3
 BLOCKS = (
-    (0, None), (1, None), (0, FAR), (1, FAR), (0, NEAR), (0, ACROSS), (1, ACROSS), (1, NEAR),
+    (0, None), (1, FAR), (1, ACROSS), (1, NEAR), (0, FAR), (1, None), (0, ACROSS), (0, NEAR),
 )
 
 
@@ -148,21 +148,27 @@
 def join_kernel(keep_ref, kept_ids_ref, earlier_ref, emb_ref, cluster_ref, ids_ref, *out_refs):
     _, place, moved = ranked(cluster_ref[...], ids_ref[...], earlier_ref[...])
     unit = unit_slots(place, emb_ref[...])
-    u, _ = here()
+    u, b = here()
     core = lax.rem(u, 2)
+    meeting = b == middle_of(core)
     tail = keep_ref.shape[0]
     own_at = pl.multiple_of(core * CAP, CAP)
     other_at = pl.multiple_of((1 - core) * CAP, CAP)
     kept = kept_ids_ref[...]
-    for out_ref, start in zip(out_refs, (0, CAP) * 2):
+    mixed_at = pl.multiple_of(jnp.where(meeting, CAP, 0), CAP)
+
+    def side(value, which):
+        axis = 1 if value.shape[0] == 16 else 0
+        near, far = (lax.slice_in_dim(value, n * CAP, (n + 1) * CAP, axis=axis) for n in range(2))
+        return (near, far, jnp.where(meeting, far, near))[which]
+
+    for which, out_ref in enumerate(out_refs):
+        start = (0, CAP, mixed_at)[which]
         for t in range(tail // SLABS_ROWS):
             base = t * SLABS_ROWS
-            out_ref[pl.ds(base + own_at, CAP), :] = keep_ref[base + start : base + start + CAP, :]
-            out_ref[pl.ds(base + other_at, CAP), :] = unit[
-                start : start + CAP, t * 128 : (t + 1) * 128
-            ]
-        own = kept[:, start : start + CAP]
-        other = moved[:, start : start + CAP]
+            out_ref[pl.ds(base + own_at, CAP), :] = keep_ref[pl.ds(base + start, CAP), :]
+            out_ref[pl.ds(base + other_at, CAP), :] = side(unit[:, t * 128 : (t + 1) * 128], which)
+        own, other = side(kept, which), side(moved, which)
         pieces = [jnp.where(core == 0, own, other), jnp.where(core == 0, other, own)]
         out_ref[tail:, :] = jnp.concatenate(pieces, axis=1).astype(jnp.bfloat16)
 
@@ -256,14 +262,20 @@
     everyone = ("blk", "clus")
     payload = jax.ShapeDtypeStruct((width // 128 * SLABS_ROWS + 16, 128), jnp.bfloat16)
 
-    def to_meeting(value, place, cross=0):
-        pairs = [
-            (blk_of(place, c % 2) * 4 + (c ^ 2 * cross), middle_of(c % 2) * 4 + c) for c in range(4)
-        ]
+    def to_meeting(value, *moves):
+        pairs = []
+        for c in range(4):
+            for other, place, aside in moves:
+                middle = middle_of(c % 2)
+                at_blk = middle if place is None else blk_of(place, c % 2)
+                pairs.append((at_blk * 4 + (c ^ 2 * other), middle * 4 + (c ^ aside)))
         return lax.ppermute(value, everyone, pairs)
 
+    def to_other_core(value):
+        return lax.ppermute(value, "clus", [(c, c ^ 1) for c in range(4)])
+
     raw = (embeddings, cluster, row_ids)
-    swapped = [lax.ppermute(value, "clus", [(c, c ^ 1) for c in range(4)]) for value in raw]
+    swapped = [to_other_core(value) for value in raw]
 
     def row(value):
         return value.reshape(1, rows)
@@ -297,24 +309,21 @@
         compiler_params=SMALL,
         name="sort_rows",
     )(embeddings, place)
-    near, direct, first, far = pl.pallas_call(
+    near, far, mixed = pl.pallas_call(
         join_kernel,
-        out_shape=[payload] * 4,
+        out_shape=[payload] * 3,
         in_specs=[VMEM] * 6,
-        out_specs=[VMEM] * 4,
+        out_specs=[VMEM] * 3,
         compiler_params=SMALL,
         name="join_cores",
     )(keep, kept_ids, earlier, swapped[0], row(swapped[1]), row(swapped[2]))
-    crossed = lax.ppermute(far, "clus", [(c, c ^ 2) for c in range(4)])
-    arrived = []
-    for other, place in BLOCKS:
-        if other and place == FAR:
-            arrived.append(to_meeting(direct, place, cross=1))
-        elif not other and place == FAR:
-            arrived.append(to_meeting(first, place))
-        else:
-            value = crossed if other else near
-            arrived.append(value if place is None else to_meeting(value, place))
+    far_on = to_meeting(far, (1, FAR, 0))
+    second = to_meeting(far, (1, ACROSS, 0), (1, NEAR, 1))
+    third = to_meeting(mixed, (0, FAR, 0), (1, None, 1))
+    fourth = to_meeting(near, (0, ACROSS, 0), (0, NEAR, 1))
+    arrived = [near, far_on]
+    for value in (second, third, fourth):
+        arrived += [value, to_other_core(value)]
 
     def meeting(kernel, first, last, known, shape):
         return pl.pallas_call(
@@ -326,7 +335,8 @@
             name=f"meet_{first}_{last}",
         )(*arrived[:last], *known)
 
-    best = meeting(meet_kernel, 0, 4, [], (8, 128))
+    best = meeting(meet_kernel, 0, 2, [], (8, 128))
+    best = meeting(meet_kernel, 2, 4, [best], (8, 128))
     best = meeting(meet_kernel, 4, 6, [best], (8, 128))
     best = meeting(last_meet_kernel, 6, 8, [best], (16, 1, 128))
     returned = lax.all_to_all(best, everyone, split_axis=0, concat_axis=0, tiled=True)

time: 35.1 us -> 36.8 us (1.048)
  blocking collectives: 11.9 us -> 14.8 us
  starting transfers between devices: 15 us -> 14 us
    all_to_all x1, blocking collectives: 11.9 us -> 14.8 us  [meet(): lax.all_to_all(best, everyone, split_axis=0, concat_axis=0, tiled=True)]
    ppermute x6 -> x4, waiting for transfers between devices: 4.72 us -> 3.09 us  [to_meeting(): return lax.ppermute(value, everyone, pairs)]
    ppermute x4 -> x6, waiting for transfers between devices: 0.35 us -> 1.82 us  [to_other_core(): return lax.ppermute(value, 'clus', [(c, c ^ 1) for c in range(4)])]
    ppermute x4 -> x6, starting transfers between devices: 3.89 us -> 3.31 us  [to_other_core(): return lax.ppermute(value, 'clus', [(c, c ^ 1) for c in range(4)])]
    ppermute x6 -> x4, starting transfers between devices: 11.1 us -> 10.7 us  [to_meeting(): return lax.ppermute(value, everyone, pairs)]
  transfers between devices with their start and end apart: 10 -> 10, of which waited for: 3 -> 4; matrix products, arithmetic and copies ran while one was open for 0% -> 0% of each run, Pallas kernels for 2% -> 2%
where the time goes in v15:
time: 36.8 us; the launch traced here: 36.6 us
  blocking collectives  14.8 us (40%)
  starting transfers between devices  14 us (38%)
  waiting for transfers between devices  4.91 us (13%)
  Pallas kernels  2.13 us (6%)
  local copies, waits for them, and re-layouts  0.68 us (2%)
    all_to_all x1, blocking collectives, meet(): lax.all_to_all(best, everyone, split_axis=0, concat_axis=0, tiled=True)  14.8 us
    ppermute x4, starting transfers between devices, to_meeting(): return lax.ppermute(value, everyone, pairs)  10.7 us
    ppermute x6, starting transfers between devices, to_other_core(): return lax.ppermute(value, 'clus', [(c, c ^ 1) for c in range(4)])  3.31 us
    ppermute x4, waiting for transfers between devices, to_meeting(): return lax.ppermute(value, everyone, pairs)  3.09 us
    ppermute x6, waiting for transfers between devices, to_other_core(): return lax.ppermute(value, 'clus', [(c, c ^ 1) for c in range(4)])  1.82 us
    pallas_call x1, Pallas kernels, meet(): pl.pallas_call(home_kernel, out_shape=jax.ShapeDtypeStruct((1, rows), jnp...  0.83 us
  transfers between devices with their start and end apart: 10, of which 4 were waited for; matrix products, arithmetic and copies ran while one was open for 0% of the time, Pallas kernels for 2%

profile of v15, /device:TPU:0, one launch (start us, length us, event | category | flops | bytes accessed | tf_op | source)
XLA Modules:
  0.0 36.6 jit_solution(5027445214542775328)
XLA Ops:
  0.0 0.0 copy-start
  0.0 0.5 %collective-permute-start.1 = (s32[256]{0:T(256)}, s32[256]{0:T(256)S(1)}, u32[]{:S(2)}, u32[]{:S(2)}) collective-permute-start(s32[256]{0:T(256)} %param.4), channel_id=1, source_target_pairs={{0,1},{1,0},{2,3},{3,2},{4,5},{5,4},{6,7},{7,6},{8,9},{9,8},{10,11... | collective-permute-start | bytes 3080 | tf_op jit(solution)/shard_map/ppermute | solution.py:275
  0.5 0.1 collective-permute-start.2
  0.5 0.4 %collective-permute-start = (bf16[256,1024]{1,0:T(8,128)(2,1)}, bf16[256,1024]{1,0:T(8,128)(2,1)S(1)}, u32[]{:S(2)}, u32[]{:S(2)}) collective-permute-start(bf16[256,1024]{1,0:T(8,128)(2,1)} %emb_ref.1), channel_id=1, source_target_pairs={{0,1},{1,0},{2,3},{3,2},{4,5},{5,4},{6,7},{7,6},{8,9},{9,8},{10,11... | collective-permute-start | bytes 1572872 | tf_op jit(solution)/shard_map/ppermute | solution.py:275
  1.0 0.0 copy-start.2
  1.0 0.0 copy-start.1
  1.0 0.6 %copy-done.2 = s32[256]{0:T(256)S(1)} copy-done((s32[256]{0:T(256)S(1)}, s32[256]{0:T(256)}, u32[]{:S(2)}) %copy-start.2) | copy-done | bytes 1048
  1.6 0.0 copy-done.1
  1.7 0.3 rank_rows.1
  2.0 0.0 copy-done
  2.0 0.4 %sort_rows.1.keep_ref = bf16[1024,128]{1,0:T(8,128)(2,1)S(1)} custom-call(bf16[256,1024]{1,0:T(8,128)(2,1)S(1)} %copy-done, bf16[128,256]{1,0:T(8,128)(2,1)S(1)} %get-tuple-element.11.place_ref), custom_call_target="tpu_custom_call" | custom-call | tf_op jit(solution)/shard_map/sort_rows/pallas_call | solution.py:304
  2.4 0.0 collective-permute-done.1
  2.4 0.0 collective-permute-done.2
  2.4 0.3 collective-permute-done.emb_ref
  2.7 0.6 %join_cores.1 = (bf16[1040,128]{1,0:T(8,128)(2,1)S(1)}, bf16[1040,128]{1,0:T(8,128)(2,1)S(1)}, bf16[1040,128]{1,0:T(8,128)(2,1)S(1)}) custom-call(bf16[1024,128]{1,0:T(8,128)(2,1)S(1)} %sort_rows.1.keep_ref, f32[16,128]{1,0:T(8,128)S(1)} %get-tuple-element.12.kept_ids_ref, bf16[256,256]{1,0:T(8,128)(2,1)S(1)} %earlier_rows.1.earlier_ref, ...), custom_call_target="tpu_custom_call" | custom-call | tf_op jit(solution)/shard_map/join_cores/pallas_call | solution.py:312
  3.3 5.5 %collective-permute-start.4 = (bf16[1040,128]{1,0:T(8,128)(2,1)S(1)}, bf16[1040,128]{1,0:T(8,128)(2,1)S(1)}, u32[]{:S(2)}, u32[]{:S(2)}) collective-permute-start(bf16[1040,128]{1,0:T(8,128)(2,1)S(1)} %get-tuple-element.14), channel_id=1, source_target_pairs={{10,4},{2,5},{7,9},{15,8},{8,6},{0,7},{5,11},{13,10},{26,20},{18,2... | collective-permute-start | bytes 798728 | tf_op jit(solution)/shard_map/ppermute | solution.py:272
  8.8 0.7 %collective-permute-start.6 = (bf16[1040,128]{1,0:T(8,128)(2,1)S(1)}, bf16[1040,128]{1,0:T(8,128)(2,1)S(1)}, u32[]{:S(2)}, u32[]{:S(2)}) collective-permute-start(bf16[1040,128]{1,0:T(8,128)(2,1)S(1)} %get-tuple-element.15), channel_id=1, source_target_pairs={{12,4},{6,5},{1,9},{11,8},{14,6},{4,7},{3,11},{9,10},{28,20},{22,2... | collective-permute-start | bytes 798728 | tf_op jit(solution)/shard_map/ppermute | solution.py:272
  9.5 3.8 %collective-permute-start.8 = (bf16[1040,128]{1,0:T(8,128)(2,1)S(1)}, bf16[1040,128]{1,0:T(8,128)(2,1)S(1)}, u32[]{:S(2)}, u32[]{:S(2)}) collective-permute-start(bf16[1040,128]{1,0:T(8,128)(2,1)S(1)} %get-tuple-element.13.refs_0_), channel_id=1, source_target_pairs={{8,4},{0,5},{5,9},{13,8},{10,6},{2,7},{7,11},{15,10},{24,20},{16,2... | collective-permute-start | bytes 798728 | tf_op jit(solution)/shard_map/ppermute | solution.py:272
  13.3 0.7 %collective-permute-start.3 = (bf16[1040,128]{1,0:T(8,128)(2,1)S(1)}, bf16[1040,128]{1,0:T(8,128)(2,1)S(1)}, u32[]{:S(2)}, u32[]{:S(2)}) collective-permute-start(bf16[1040,128]{1,0:T(8,128)(2,1)S(1)} %get-tuple-element.14), channel_id=1, source_target_pairs={{14,4},{3,9},{12,6},{1,11},{30,20},{19,25},{28,22},{17,27}} | collective-permute-start | bytes 798728 | tf_op jit(solution)/shard_map/ppermute | solution.py:272
  14.0 0.8 %collective-permute-done.4.refs_2_ = bf16[1040,128]{1,0:T(8,128)(2,1)S(1)} collective-permute-done((bf16[1040,128]{1,0:T(8,128)(2,1)S(1)}, bf16[1040,128]{1,0:T(8,128)(2,1)S(1)}, u32[]{:S(2)}, u32[]{:S(2)}) %collective-permute-start.4) | collective-permute-done | bytes 266272 | tf_op jit(solution)/shard_map/ppermute | solution.py:272
  14.8 2.3 %collective-permute-start.5 = (bf16[1040,128]{1,0:T(8,128)(2,1)S(1)}, bf16[1040,128]{1,0:T(8,128)(2,1)S(1)}, u32[]{:S(2)}, u32[]{:S(2)}) collective-permute-start(bf16[1040,128]{1,0:T(8,128)(2,1)S(1)} %collective-permute-done.4.refs_2_), channel_id=1, source_target_pairs={{0,1},{1,0},{2,3},{3,2},{4,5},{5,4},{6,7},{7,6},{8,9},{9,8},{10,11... | collective-permute-start | bytes 798728 | tf_op jit(solution)/shard_map/ppermute | solution.py:275
  17.1 0.0 collective-permute-done.6.refs_4_
  17.1 0.1 collective-permute-start.7
  17.2 2.3 %collective-permute-done.8.refs_6_ = bf16[1040,128]{1,0:T(8,128)(2,1)S(1)} collective-permute-done((bf16[1040,128]{1,0:T(8,128)(2,1)S(1)}, bf16[1040,128]{1,0:T(8,128)(2,1)S(1)}, u32[]{:S(2)}, u32[]{:S(2)}) %collective-permute-start.8) | collective-permute-done | bytes 266272 | tf_op jit(solution)/shard_map/ppermute | solution.py:272
  19.5 0.0 collective-permute-start.9
  19.5 0.0 collective-permute-done.3.refs_1_
  19.5 0.0 collective-permute-done.5.refs_3_
  19.5 0.0 collective-permute-done.7.refs_5_
  19.5 1.5 %collective-permute-done.9.refs_7_ = bf16[1040,128]{1,0:T(8,128)(2,1)S(1)} collective-permute-done((bf16[1040,128]{1,0:T(8,128)(2,1)S(1)}, bf16[1040,128]{1,0:T(8,128)(2,1)S(1)}, u32[]{:S(2)}, u32[]{:S(2)}) %collective-permute-start.9) | collective-permute-done | bytes 266272 | tf_op jit(solution)/shard_map/ppermute | solution.py:275
  21.0 14.8 %all_to_all.5.got_ref = f32[16,1,128]{2,1,0:T(1,128)S(1)} all-to-all(f32[16,1,128]{2,1,0:T(1,128)S(1)} %meet_6_8.1), channel_id=1, replica_groups=mesh['groups'=2,'blk'=4,'clus'=4] {'blk','clus'}, dimensions={0} | all-to-all | bytes 16384 | tf_op jit(solution)/shard_map/all_to_all | solution.py:342
  35.8 0.8 %home_scores.1 = f32[1,256]{1,0:T(1,128)} custom-call(f32[16,1,128]{2,1,0:T(1,128)S(1)} %all_to_all.5.got_ref, s32[1,256]{1,0:T(1,128)S(1)} %get-tuple-element.16.target_ref), custom_call_target="tpu_custom_call" | custom-call | tf_op jit(solution)/shard_map/home_scores/pallas_call | solution.py:343
  (5 shorter events, 0.1 us)
Async XLA Ops:
  0.0 2.0 %copy-start = (bf16[256,1024]{1,0:T(8,128)(2,1)S(1)}, bf16[256,1024]{1,0:T(8,128)(2,1)}, u32[]{:S(2)}) copy-start(bf16[256,1024]{1,0:T(8,128)(2,1)} %emb_ref.1) | copy-start | bytes 1572868
  0.0 2.4 %collective-permute-start.1 = (s32[256]{0:T(256)}, s32[256]{0:T(256)S(1)}, u32[]{:S(2)}, u32[]{:S(2)}) collective-permute-start(s32[256]{0:T(256)} %param.4), channel_id=1, source_target_pairs={{0,1},{1,0},{2,3},{3,2},{4,5},{5,4},{6,7},{7,6},{8,9},{9,8},{10,11... | collective-permute-start | bytes 3080 | tf_op jit(solution)/shard_map/ppermute | solution.py:275
  0.5 1.9 %collective-permute-start.2 = (s32[256]{0:T(256)}, s32[256]{0:T(256)S(1)}, u32[]{:S(2)}, u32[]{:S(2)}) collective-permute-start(s32[256]{0:T(256)} %param.5), channel_id=1, source_target_pairs={{0,1},{1,0},{2,3},{3,2},{4,5},{5,4},{6,7},{7,6},{8,9},{9,8},{10,11... | collective-permute-start | bytes 3080 | tf_op jit(solution)/shard_map/ppermute | solution.py:275
  0.5 2.2 %collective-permute-start = (bf16[256,1024]{1,0:T(8,128)(2,1)}, bf16[256,1024]{1,0:T(8,128)(2,1)S(1)}, u32[]{:S(2)}, u32[]{:S(2)}) collective-permute-start(bf16[256,1024]{1,0:T(8,128)(2,1)} %emb_ref.1), channel_id=1, source_target_pairs={{0,1},{1,0},{2,3},{3,2},{4,5},{5,4},{6,7},{7,6},{8,9},{9,8},{10,11... | collective-permute-start | bytes 1572872 | tf_op jit(solution)/shard_map/ppermute | solution.py:275
  1.0 0.7 %copy-start.2 = (s32[256]{0:T(256)S(1)}, s32[256]{0:T(256)}, u32[]{:S(2)}) copy-start(s32[256]{0:T(256)} %param.5) | copy-start | bytes 3076
  1.0 0.7 %copy-start.1 = (s32[256]{0:T(256)S(1)}, s32[256]{0:T(256)}, u32[]{:S(2)}) copy-start(s32[256]{0:T(256)} %param.4) | copy-start | bytes 3076
  3.3 11.5 %collective-permute-start.4 = (bf16[1040,128]{1,0:T(8,128)(2,1)S(1)}, bf16[1040,128]{1,0:T(8,128)(2,1)S(1)}, u32[]{:S(2)}, u32[]{:S(2)}) collective-permute-start(bf16[1040,128]{1,0:T(8,128)(2,1)S(1)} %get-tuple-element.14), channel_id=1, source_target_pairs={{10,4},{2,5},{7,9},{15,8},{8,6},{0,7},{5,11},{13,10},{26,20},{18,2... | collective-permute-start | bytes 798728 | tf_op jit(solution)/shard_map/ppermute | solution.py:272
  8.8 8.2 %collective-permute-start.6 = (bf16[1040,128]{1,0:T(8,128)(2,1)S(1)}, bf16[1040,128]{1,0:T(8,128)(2,1)S(1)}, u32[]{:S(2)}, u32[]{:S(2)}) collective-permute-start(bf16[1040,128]{1,0:T(8,128)(2,1)S(1)} %get-tuple-element.15), channel_id=1, source_target_pairs={{12,4},{6,5},{1,9},{11,8},{14,6},{4,7},{3,11},{9,10},{28,20},{22,2... | collective-permute-start | bytes 798728 | tf_op jit(solution)/shard_map/ppermute | solution.py:272
  9.5 9.9 %collective-permute-start.8 = (bf16[1040,128]{1,0:T(8,128)(2,1)S(1)}, bf16[1040,128]{1,0:T(8,128)(2,1)S(1)}, u32[]{:S(2)}, u32[]{:S(2)}) collective-permute-start(bf16[1040,128]{1,0:T(8,128)(2,1)S(1)} %get-tuple-element.13.refs_0_), channel_id=1, source_target_pairs={{8,4},{0,5},{5,9},{13,8},{10,6},{2,7},{7,11},{15,10},{24,20},{16,2... | collective-permute-start | bytes 798728 | tf_op jit(solution)/shard_map/ppermute | solution.py:272
  13.3 6.1 %collective-permute-start.3 = (bf16[1040,128]{1,0:T(8,128)(2,1)S(1)}, bf16[1040,128]{1,0:T(8,128)(2,1)S(1)}, u32[]{:S(2)}, u32[]{:S(2)}) collective-permute-start(bf16[1040,128]{1,0:T(8,128)(2,1)S(1)} %get-tuple-element.14), channel_id=1, source_target_pairs={{14,4},{3,9},{12,6},{1,11},{30,20},{19,25},{28,22},{17,27}} | collective-permute-start | bytes 798728 | tf_op jit(solution)/shard_map/ppermute | solution.py:272
  14.8 4.7 %collective-permute-start.5 = (bf16[1040,128]{1,0:T(8,128)(2,1)S(1)}, bf16[1040,128]{1,0:T(8,128)(2,1)S(1)}, u32[]{:S(2)}, u32[]{:S(2)}) collective-permute-start(bf16[1040,128]{1,0:T(8,128)(2,1)S(1)} %collective-permute-done.4.refs_2_), channel_id=1, source_target_pairs={{0,1},{1,0},{2,3},{3,2},{4,5},{5,4},{6,7},{7,6},{8,9},{9,8},{10,11... | collective-permute-start | bytes 798728 | tf_op jit(solution)/shard_map/ppermute | solution.py:275
  17.1 2.4 %collective-permute-start.7 = (bf16[1040,128]{1,0:T(8,128)(2,1)S(1)}, bf16[1040,128]{1,0:T(8,128)(2,1)S(1)}, u32[]{:S(2)}, u32[]{:S(2)}) collective-permute-start(bf16[1040,128]{1,0:T(8,128)(2,1)S(1)} %collective-permute-done.6.refs_4_), channel_id=1, source_target_pairs={{0,1},{1,0},{2,3},{3,2},{4,5},{5,4},{6,7},{7,6},{8,9},{9,8},{10,11... | collective-permute-start | bytes 798728 | tf_op jit(solution)/shard_map/ppermute | solution.py:275
  19.5 1.5 %collective-permute-start.9 = (bf16[1040,128]{1,0:T(8,128)(2,1)S(1)}, bf16[1040,128]{1,0:T(8,128)(2,1)S(1)}, u32[]{:S(2)}, u32[]{:S(2)}) collective-permute-start(bf16[1040,128]{1,0:T(8,128)(2,1)S(1)} %collective-permute-done.8.refs_6_), channel_id=1, source_target_pairs={{0,1},{1,0},{2,3},{3,2},{4,5},{5,4},{6,7},{7,6},{8,9},{9,8},{10,11... | collective-permute-start | bytes 798728 | tf_op jit(solution)/shard_map/ppermute | solution.py:275

commit v16 on v15

--- a/solution.py
+++ b/solution.py
@@ -74,7 +74,7 @@
 
 NEAR, ACROSS, FAR = 0, 2, 3
 BLOCKS = (
-    (0, None), (1, FAR), (1, ACROSS), (1, NEAR), (0, FAR), (1, None), (0, ACROSS), (0, NEAR),
+    (0, None), (1, FAR), (1, ACROSS), (1, NEAR), (0, ACROSS), (0, NEAR), (0, FAR), (1, None),
 )
 
 
@@ -317,12 +317,13 @@
         compiler_params=SMALL,
         name="join_cores",
     )(keep, kept_ids, earlier, swapped[0], row(swapped[1]), row(swapped[2]))
-    far_on = to_meeting(far, (1, FAR, 0))
-    second = to_meeting(far, (1, ACROSS, 0), (1, NEAR, 1))
-    third = to_meeting(mixed, (0, FAR, 0), (1, None, 1))
-    fourth = to_meeting(near, (0, ACROSS, 0), (0, NEAR, 1))
-    arrived = [near, far_on]
-    for value in (second, third, fourth):
+    rounds = (
+        to_meeting(far, (1, ACROSS, 0), (1, NEAR, 1)),
+        to_meeting(near, (0, ACROSS, 0), (0, NEAR, 1)),
+        to_meeting(mixed, (0, FAR, 0), (1, None, 1)),
+    )
+    arrived = [near, to_other_core(to_meeting(far, (1, FAR, 1)))]
+    for value in rounds:
         arrived += [value, to_other_core(value)]
 
     def meeting(kernel, first, last, known, shape):

time: 36.8 us -> 37.7 us (1.024)
  waiting for transfers between devices: 4.91 us -> 7.88 us
  blocking collectives: 14.8 us -> 12.7 us
    ppermute x4, waiting for transfers between devices: 3.09 us -> 6.13 us  [to_meeting(): return lax.ppermute(value, everyone, pairs)]
    all_to_all x1, blocking collectives: 14.8 us -> 12.7 us  [meet(): lax.all_to_all(best, everyone, split_axis=0, concat_axis=0, tiled=True)]
    ppermute x4, starting transfers between devices: 10.7 us -> 10.1 us  [to_meeting(): return lax.ppermute(value, everyone, pairs)]
    ppermute x6 -> x7, starting transfers between devices: 3.31 us -> 3.9 us  [to_other_core(): return lax.ppermute(value, 'clus', [(c, c ^ 1) for c in range(4)])]
    ppermute x6 -> x7, waiting for transfers between devices: 1.82 us -> 1.75 us  [to_other_core(): return lax.ppermute(value, 'clus', [(c, c ^ 1) for c in range(4)])]
  transfers between devices with their start and end apart: 10 -> 11, of which waited for: 4 -> 5; matrix products, arithmetic and copies ran while one was open for 0% -> 0% of each run, Pallas kernels for 2% -> 2%
where the time goes in v16:
time: 37.7 us; the launch traced here: 37.5 us
  starting transfers between devices  14 us (37%)
  blocking collectives  12.7 us (34%)
  waiting for transfers between devices  7.88 us (21%)
  Pallas kernels  2.09 us (6%)
  local copies, waits for them, and re-layouts  0.68 us (2%)
    all_to_all x1, blocking collectives, meet(): lax.all_to_all(best, everyone, split_axis=0, concat_axis=0, tiled=True)  12.7 us
    ppermute x4, starting transfers between devices, to_meeting(): return lax.ppermute(value, everyone, pairs)  10.1 us
    ppermute x4, waiting for transfers between devices, to_meeting(): return lax.ppermute(value, everyone, pairs)  6.13 us
    ppermute x7, starting transfers between devices, to_other_core(): return lax.ppermute(value, 'clus', [(c, c ^ 1) for c in range(4)])  3.9 us
    ppermute x7, waiting for transfers between devices, to_other_core(): return lax.ppermute(value, 'clus', [(c, c ^ 1) for c in range(4)])  1.75 us
    pallas_call x1, Pallas kernels, meet(): pl.pallas_call(home_kernel, out_shape=jax.ShapeDtypeStruct((1, rows), jnp...  0.83 us
  transfers between devices with their start and end apart: 11, of which 5 were waited for; matrix products, arithmetic and copies ran while one was open for 0% of the time, Pallas kernels for 2%

profile of v16, /device:TPU:0, one launch (start us, length us, event | category | flops | bytes accessed | tf_op | source)
XLA Modules:
  0.0 37.5 jit_solution(9089807895404266992)
XLA Ops:
  0.0 0.0 copy-start
  0.0 0.5 %collective-permute-start.1 = (s32[256]{0:T(256)}, s32[256]{0:T(256)S(1)}, u32[]{:S(2)}, u32[]{:S(2)}) collective-permute-start(s32[256]{0:T(256)} %param.4), channel_id=1, source_target_pairs={{0,1},{1,0},{2,3},{3,2},{4,5},{5,4},{6,7},{7,6},{8,9},{9,8},{10,11... | collective-permute-start | bytes 3080 | tf_op jit(solution)/shard_map/ppermute | solution.py:275
  0.5 0.1 collective-permute-start.2
  0.5 0.4 %collective-permute-start = (bf16[256,1024]{1,0:T(8,128)(2,1)}, bf16[256,1024]{1,0:T(8,128)(2,1)S(1)}, u32[]{:S(2)}, u32[]{:S(2)}) collective-permute-start(bf16[256,1024]{1,0:T(8,128)(2,1)} %emb_ref.1), channel_id=1, source_target_pairs={{0,1},{1,0},{2,3},{3,2},{4,5},{5,4},{6,7},{7,6},{8,9},{9,8},{10,11... | collective-permute-start | bytes 1572872 | tf_op jit(solution)/shard_map/ppermute | solution.py:275
  1.0 0.0 copy-start.2
  1.0 0.0 copy-start.1
  1.0 0.6 %copy-done.2 = s32[256]{0:T(256)S(1)} copy-done((s32[256]{0:T(256)S(1)}, s32[256]{0:T(256)}, u32[]{:S(2)}) %copy-start.2) | copy-done | bytes 1048
  1.6 0.0 copy-done.1
  1.7 0.3 rank_rows.1
  2.0 0.0 copy-done
  2.0 0.4 sort_rows.1.keep_ref
  2.4 0.0 collective-permute-done.1
  2.4 0.0 collective-permute-done.2
  2.4 0.3 collective-permute-done.emb_ref
  2.7 0.6 %join_cores.1 = (bf16[1040,128]{1,0:T(8,128)(2,1)S(1)}, bf16[1040,128]{1,0:T(8,128)(2,1)S(1)}, bf16[1040,128]{1,0:T(8,128)(2,1)S(1)}) custom-call(bf16[1024,128]{1,0:T(8,128)(2,1)S(1)} %sort_rows.1.keep_ref, f32[16,128]{1,0:T(8,128)S(1)} %get-tuple-element.12.kept_ids_ref, bf16[256,256]{1,0:T(8,128)(2,1)S(1)} %earlier_rows.1.earlier_ref, ...), custom_call_target="tpu_custom_call" | custom-call | tf_op jit(solution)/shard_map/join_cores/pallas_call | solution.py:312
  3.3 0.7 %collective-permute-start.3 = (bf16[1040,128]{1,0:T(8,128)(2,1)S(1)}, bf16[1040,128]{1,0:T(8,128)(2,1)S(1)}, u32[]{:S(2)}, u32[]{:S(2)}) collective-permute-start(bf16[1040,128]{1,0:T(8,128)(2,1)S(1)} %get-tuple-element.14), channel_id=1, source_target_pairs={{14,5},{3,8},{12,7},{1,10},{30,21},{19,24},{28,23},{17,26}} | collective-permute-start | bytes 798728 | tf_op jit(solution)/shard_map/ppermute | solution.py:272
  4.0 6.1 %collective-permute-start.5 = (bf16[1040,128]{1,0:T(8,128)(2,1)S(1)}, bf16[1040,128]{1,0:T(8,128)(2,1)S(1)}, u32[]{:S(2)}, u32[]{:S(2)}) collective-permute-start(bf16[1040,128]{1,0:T(8,128)(2,1)S(1)} %get-tuple-element.14), channel_id=1, source_target_pairs={{10,4},{2,5},{7,9},{15,8},{8,6},{0,7},{5,11},{13,10},{26,20},{18,2... | collective-permute-start | bytes 798728 | tf_op jit(solution)/shard_map/ppermute | solution.py:272
  10.1 2.6 %collective-permute-start.7 = (bf16[1040,128]{1,0:T(8,128)(2,1)S(1)}, bf16[1040,128]{1,0:T(8,128)(2,1)S(1)}, u32[]{:S(2)}, u32[]{:S(2)}) collective-permute-start(bf16[1040,128]{1,0:T(8,128)(2,1)S(1)} %get-tuple-element.13.refs_0_), channel_id=1, source_target_pairs={{8,4},{0,5},{5,9},{13,8},{10,6},{2,7},{7,11},{15,10},{24,20},{16,2... | collective-permute-start | bytes 798728 | tf_op jit(solution)/shard_map/ppermute | solution.py:272
  12.7 0.7 %collective-permute-start.9 = (bf16[1040,128]{1,0:T(8,128)(2,1)S(1)}, bf16[1040,128]{1,0:T(8,128)(2,1)S(1)}, u32[]{:S(2)}, u32[]{:S(2)}) collective-permute-start(bf16[1040,128]{1,0:T(8,128)(2,1)S(1)} %get-tuple-element.15), channel_id=1, source_target_pairs={{12,4},{6,5},{1,9},{11,8},{14,6},{4,7},{3,11},{9,10},{28,20},{22,2... | collective-permute-start | bytes 798728 | tf_op jit(solution)/shard_map/ppermute | solution.py:272
  13.4 0.0 collective-permute-done.3
  13.4 2.4 %collective-permute-start.4 = (bf16[1040,128]{1,0:T(8,128)(2,1)S(1)}, bf16[1040,128]{1,0:T(8,128)(2,1)S(1)}, u32[]{:S(2)}, u32[]{:S(2)}) collective-permute-start(bf16[1040,128]{1,0:T(8,128)(2,1)S(1)} %collective-permute-done.3), channel_id=1, source_target_pairs={{0,1},{1,0},{2,3},{3,2},{4,5},{5,4},{6,7},{7,6},{8,9},{9,8},{10,11... | collective-permute-start | bytes 798728 | tf_op jit(solution)/shard_map/ppermute | solution.py:275
  15.9 1.0 %collective-permute-done.5.refs_2_ = bf16[1040,128]{1,0:T(8,128)(2,1)S(1)} collective-permute-done((bf16[1040,128]{1,0:T(8,128)(2,1)S(1)}, bf16[1040,128]{1,0:T(8,128)(2,1)S(1)}, u32[]{:S(2)}, u32[]{:S(2)}) %collective-permute-start.5) | collective-permute-done | bytes 266272 | tf_op jit(solution)/shard_map/ppermute | solution.py:272
  16.8 0.0 collective-permute-start.6
  16.8 5.2 %collective-permute-done.7.refs_4_ = bf16[1040,128]{1,0:T(8,128)(2,1)S(1)} collective-permute-done((bf16[1040,128]{1,0:T(8,128)(2,1)S(1)}, bf16[1040,128]{1,0:T(8,128)(2,1)S(1)}, u32[]{:S(2)}, u32[]{:S(2)}) %collective-permute-start.7) | collective-permute-done | bytes 266272 | tf_op jit(solution)/shard_map/ppermute | solution.py:272
  22.0 0.0 collective-permute-start.8
  22.0 0.0 collective-permute-done.9.refs_6_
  22.0 0.5 %collective-permute-start.10 = (bf16[1040,128]{1,0:T(8,128)(2,1)S(1)}, bf16[1040,128]{1,0:T(8,128)(2,1)S(1)}, u32[]{:S(2)}, u32[]{:S(2)}) collective-permute-start(bf16[1040,128]{1,0:T(8,128)(2,1)S(1)} %collective-permute-done.9.refs_6_), channel_id=1, source_target_pairs={{0,1},{1,0},{2,3},{3,2},{4,5},{5,4},{6,7},{7,6},{8,9},{9,8},{10,11... | collective-permute-start | bytes 798728 | tf_op jit(solution)/shard_map/ppermute | solution.py:275
  22.5 0.0 collective-permute-done.4.refs_1_
  22.5 0.0 collective-permute-done.6.refs_3_
  22.5 1.0 %collective-permute-done.8.refs_5_ = bf16[1040,128]{1,0:T(8,128)(2,1)S(1)} collective-permute-done((bf16[1040,128]{1,0:T(8,128)(2,1)S(1)}, bf16[1040,128]{1,0:T(8,128)(2,1)S(1)}, u32[]{:S(2)}, u32[]{:S(2)}) %collective-permute-start.8) | collective-permute-done | bytes 266272 | tf_op jit(solution)/shard_map/ppermute | solution.py:275
  23.5 0.4 %collective-permute-done.10.refs_7_ = bf16[1040,128]{1,0:T(8,128)(2,1)S(1)} collective-permute-done((bf16[1040,128]{1,0:T(8,128)(2,1)S(1)}, bf16[1040,128]{1,0:T(8,128)(2,1)S(1)}, u32[]{:S(2)}, u32[]{:S(2)}) %collective-permute-start.10) | collective-permute-done | bytes 266272 | tf_op jit(solution)/shard_map/ppermute | solution.py:275
  23.9 12.7 %all_to_all.5.got_ref = f32[16,1,128]{2,1,0:T(1,128)S(1)} all-to-all(f32[16,1,128]{2,1,0:T(1,128)S(1)} %meet_6_8.1), channel_id=1, replica_groups=mesh['groups'=2,'blk'=4,'clus'=4] {'blk','clus'}, dimensions={0} | all-to-all | bytes 16384 | tf_op jit(solution)/shard_map/all_to_all | solution.py:343
  36.6 0.8 %home_scores.1 = f32[1,256]{1,0:T(1,128)} custom-call(f32[16,1,128]{2,1,0:T(1,128)S(1)} %all_to_all.5.got_ref, s32[1,256]{1,0:T(1,128)S(1)} %get-tuple-element.16.target_ref), custom_call_target="tpu_custom_call" | custom-call | tf_op jit(solution)/shard_map/home_scores/pallas_call | solution.py:344
  (5 shorter events, 0.0 us)
Async XLA Ops:
  0.0 2.0 %copy-start = (bf16[256,1024]{1,0:T(8,128)(2,1)S(1)}, bf16[256,1024]{1,0:T(8,128)(2,1)}, u32[]{:S(2)}) copy-start(bf16[256,1024]{1,0:T(8,128)(2,1)} %emb_ref.1) | copy-start | bytes 1572868
  0.0 2.4 %collective-permute-start.1 = (s32[256]{0:T(256)}, s32[256]{0:T(256)S(1)}, u32[]{:S(2)}, u32[]{:S(2)}) collective-permute-start(s32[256]{0:T(256)} %param.4), channel_id=1, source_target_pairs={{0,1},{1,0},{2,3},{3,2},{4,5},{5,4},{6,7},{7,6},{8,9},{9,8},{10,11... | collective-permute-start | bytes 3080 | tf_op jit(solution)/shard_map/ppermute | solution.py:275
  0.5 1.9 %collective-permute-start.2 = (s32[256]{0:T(256)}, s32[256]{0:T(256)S(1)}, u32[]{:S(2)}, u32[]{:S(2)}) collective-permute-start(s32[256]{0:T(256)} %param.5), channel_id=1, source_target_pairs={{0,1},{1,0},{2,3},{3,2},{4,5},{5,4},{6,7},{7,6},{8,9},{9,8},{10,11... | collective-permute-start | bytes 3080 | tf_op jit(solution)/shard_map/ppermute | solution.py:275
  0.5 2.2 %collective-permute-start = (bf16[256,1024]{1,0:T(8,128)(2,1)}, bf16[256,1024]{1,0:T(8,128)(2,1)S(1)}, u32[]{:S(2)}, u32[]{:S(2)}) collective-permute-start(bf16[256,1024]{1,0:T(8,128)(2,1)} %emb_ref.1), channel_id=1, source_target_pairs={{0,1},{1,0},{2,3},{3,2},{4,5},{5,4},{6,7},{7,6},{8,9},{9,8},{10,11... | collective-permute-start | bytes 1572872 | tf_op jit(solution)/shard_map/ppermute | solution.py:275
  1.0 0.7 %copy-start.2 = (s32[256]{0:T(256)S(1)}, s32[256]{0:T(256)}, u32[]{:S(2)}) copy-start(s32[256]{0:T(256)} %param.5) | copy-start | bytes 3076
  1.0 0.7 %copy-start.1 = (s32[256]{0:T(256)S(1)}, s32[256]{0:T(256)}, u32[]{:S(2)}) copy-start(s32[256]{0:T(256)} %param.4) | copy-start | bytes 3076
  3.3 10.1 %collective-permute-start.3 = (bf16[1040,128]{1,0:T(8,128)(2,1)S(1)}, bf16[1040,128]{1,0:T(8,128)(2,1)S(1)}, u32[]{:S(2)}, u32[]{:S(2)}) collective-permute-start(bf16[1040,128]{1,0:T(8,128)(2,1)S(1)} %get-tuple-element.14), channel_id=1, source_target_pairs={{14,5},{3,8},{12,7},{1,10},{30,21},{19,24},{28,23},{17,26}} | collective-permute-start | bytes 798728 | tf_op jit(solution)/shard_map/ppermute | solution.py:272
  4.0 12.8 %collective-permute-start.5 = (bf16[1040,128]{1,0:T(8,128)(2,1)S(1)}, bf16[1040,128]{1,0:T(8,128)(2,1)S(1)}, u32[]{:S(2)}, u32[]{:S(2)}) collective-permute-start(bf16[1040,128]{1,0:T(8,128)(2,1)S(1)} %get-tuple-element.14), channel_id=1, source_target_pairs={{10,4},{2,5},{7,9},{15,8},{8,6},{0,7},{5,11},{13,10},{26,20},{18,2... | collective-permute-start | bytes 798728 | tf_op jit(solution)/shard_map/ppermute | solution.py:272
  10.1 11.9 %collective-permute-start.7 = (bf16[1040,128]{1,0:T(8,128)(2,1)S(1)}, bf16[1040,128]{1,0:T(8,128)(2,1)S(1)}, u32[]{:S(2)}, u32[]{:S(2)}) collective-permute-start(bf16[1040,128]{1,0:T(8,128)(2,1)S(1)} %get-tuple-element.13.refs_0_), channel_id=1, source_target_pairs={{8,4},{0,5},{5,9},{13,8},{10,6},{2,7},{7,11},{15,10},{24,20},{16,2... | collective-permute-start | bytes 798728 | tf_op jit(solution)/shard_map/ppermute | solution.py:272
  12.7 9.3 %collective-permute-start.9 = (bf16[1040,128]{1,0:T(8,128)(2,1)S(1)}, bf16[1040,128]{1,0:T(8,128)(2,1)S(1)}, u32[]{:S(2)}, u32[]{:S(2)}) collective-permute-start(bf16[1040,128]{1,0:T(8,128)(2,1)S(1)} %get-tuple-element.15), channel_id=1, source_target_pairs={{12,4},{6,5},{1,9},{11,8},{14,6},{4,7},{3,11},{9,10},{28,20},{22,2... | collective-permute-start | bytes 798728 | tf_op jit(solution)/shard_map/ppermute | solution.py:272
  13.4 9.1 %collective-permute-start.4 = (bf16[1040,128]{1,0:T(8,128)(2,1)S(1)}, bf16[1040,128]{1,0:T(8,128)(2,1)S(1)}, u32[]{:S(2)}, u32[]{:S(2)}) collective-permute-start(bf16[1040,128]{1,0:T(8,128)(2,1)S(1)} %collective-permute-done.3), channel_id=1, source_target_pairs={{0,1},{1,0},{2,3},{3,2},{4,5},{5,4},{6,7},{7,6},{8,9},{9,8},{10,11... | collective-permute-start | bytes 798728 | tf_op jit(solution)/shard_map/ppermute | solution.py:275
  16.8 5.7 %collective-permute-start.6 = (bf16[1040,128]{1,0:T(8,128)(2,1)S(1)}, bf16[1040,128]{1,0:T(8,128)(2,1)S(1)}, u32[]{:S(2)}, u32[]{:S(2)}) collective-permute-start(bf16[1040,128]{1,0:T(8,128)(2,1)S(1)} %collective-permute-done.5.refs_2_), channel_id=1, source_target_pairs={{0,1},{1,0},{2,3},{3,2},{4,5},{5,4},{6,7},{7,6},{8,9},{9,8},{10,11... | collective-permute-start | bytes 798728 | tf_op jit(solution)/shard_map/ppermute | solution.py:275
  22.0 1.5 %collective-permute-start.8 = (bf16[1040,128]{1,0:T(8,128)(2,1)S(1)}, bf16[1040,128]{1,0:T(8,128)(2,1)S(1)}, u32[]{:S(2)}, u32[]{:S(2)}) collective-permute-start(bf16[1040,128]{1,0:T(8,128)(2,1)S(1)} %collective-permute-done.7.refs_4_), channel_id=1, source_target_pairs={{0,1},{1,0},{2,3},{3,2},{4,5},{5,4},{6,7},{7,6},{8,9},{9,8},{10,11... | collective-permute-start | bytes 798728 | tf_op jit(solution)/shard_map/ppermute | solution.py:275
  22.0 1.9 %collective-permute-start.10 = (bf16[1040,128]{1,0:T(8,128)(2,1)S(1)}, bf16[1040,128]{1,0:T(8,128)(2,1)S(1)}, u32[]{:S(2)}, u32[]{:S(2)}) collective-permute-start(bf16[1040,128]{1,0:T(8,128)(2,1)S(1)} %collective-permute-done.9.refs_6_), channel_id=1, source_target_pairs={{0,1},{1,0},{2,3},{3,2},{4,5},{5,4},{6,7},{7,6},{8,9},{9,8},{10,11... | collective-permute-start | bytes 798728 | tf_op jit(solution)/shard_map/ppermute | solution.py:275

commit v17 on v13

--- a/solution.py
+++ b/solution.py
@@ -74,7 +74,7 @@
 
 NEAR, ACROSS, FAR = 0, 2, 3
 BLOCKS = (
-    (0, None), (1, None), (0, FAR), (1, FAR), (0, NEAR), (0, ACROSS), (1, ACROSS), (1, NEAR),
+    (0, None), (1, None), (0, FAR), (1, FAR), (0, NEAR), (1, ACROSS), (0, ACROSS), (1, NEAR),
 )
 
 
@@ -305,10 +305,11 @@
         compiler_params=SMALL,
         name="join_cores",
     )(keep, kept_ids, earlier, swapped[0], row(swapped[1]), row(swapped[2]))
-    crossed = lax.ppermute(far, "clus", [(c, c ^ 2) for c in range(4)])
+    used = [(b, c) for c in range(4) for b in (middle_of(c % 2), blk_of(NEAR, c % 2))]
+    crossed = lax.ppermute(far, everyone, [(b * 4 + c, b * 4 + (c ^ 2)) for b, c in used])
     arrived = []
     for other, place in BLOCKS:
-        if other and place == FAR:
+        if other and place in (FAR, ACROSS):
             arrived.append(to_meeting(direct, place, cross=1))
         elif not other and place == FAR:
             arrived.append(to_meeting(first, place))

time: 35.1 us -> 37 us (1.054)
  starting transfers between devices: 15 us -> 18.5 us
  waiting for transfers between devices: 5.07 us -> 4.21 us
  blocking collectives: 11.9 us -> 11.1 us
    ppermute x1, starting transfers between devices: 2.92 us -> 4.77 us  [meet(): lax.ppermute(far, everyone, [(b * 4 + c, b * 4 + (c ^ 2)) for b, c in used])]
    ppermute x6, starting transfers between devices: 11.1 us -> 12.7 us  [to_meeting(): return lax.ppermute(value, everyone, pairs)]
    ppermute x6, waiting for transfers between devices: 4.72 us -> 3.86 us  [to_meeting(): return lax.ppermute(value, everyone, pairs)]
    all_to_all x1, blocking collectives: 11.9 us -> 11.1 us  [meet(): lax.all_to_all(best, everyone, split_axis=0, concat_axis=0, tiled=True)]
where the time goes in v17:
time: 37 us; the launch traced here: 36.7 us
  starting transfers between devices  18.5 us (50%)
  blocking collectives  11.1 us (30%)
  waiting for transfers between devices  4.21 us (11%)
  Pallas kernels  2.13 us (6%)
  local copies, waits for them, and re-layouts  0.68 us (2%)
    ppermute x6, starting transfers between devices, to_meeting(): return lax.ppermute(value, everyone, pairs)  12.7 us
    all_to_all x1, blocking collectives, meet(): lax.all_to_all(best, everyone, split_axis=0, concat_axis=0, tiled=True)  11.1 us
    ppermute x1, starting transfers between devices, meet(): lax.ppermute(far, everyone, [(b * 4 + c, b * 4 + (c ^ 2)) for b, c in used])  4.77 us
    ppermute x6, waiting for transfers between devices, to_meeting(): return lax.ppermute(value, everyone, pairs)  3.86 us
    ppermute x3, starting transfers between devices, meet(): lax.ppermute(value, 'clus', [(c, c ^ 1) for c in range(4)])  0.96 us
    pallas_call x1, Pallas kernels, meet(): pl.pallas_call(home_kernel, out_shape=jax.ShapeDtypeStruct((1, rows), jnp...  0.83 us
  transfers between devices with their start and end apart: 10, of which 3 were waited for; matrix products, arithmetic and copies ran while one was open for 0% of the time, Pallas kernels for 2%

profile of v17, /device:TPU:0, one launch (start us, length us, event | category | flops | bytes accessed | tf_op | source)
XLA Modules:
  0.0 36.7 jit_solution(2772372278325385198)
XLA Ops:
  0.0 0.0 copy-start
  0.0 0.5 %collective-permute-start.1 = (s32[256]{0:T(256)}, s32[256]{0:T(256)S(1)}, u32[]{:S(2)}, u32[]{:S(2)}) collective-permute-start(s32[256]{0:T(256)} %param.4), channel_id=1, source_target_pairs={{0,1},{1,0},{2,3},{3,2},{4,5},{5,4},{6,7},{7,6},{8,9},{9,8},{10,11... | collective-permute-start | bytes 3080 | tf_op jit(solution)/shard_map/ppermute | solution.py:266
  0.5 0.1 collective-permute-start.2
  0.5 0.4 %collective-permute-start = (bf16[256,1024]{1,0:T(8,128)(2,1)}, bf16[256,1024]{1,0:T(8,128)(2,1)S(1)}, u32[]{:S(2)}, u32[]{:S(2)}) collective-permute-start(bf16[256,1024]{1,0:T(8,128)(2,1)} %emb_ref.1), channel_id=1, source_target_pairs={{0,1},{1,0},{2,3},{3,2},{4,5},{5,4},{6,7},{7,6},{8,9},{9,8},{10,11... | collective-permute-start | bytes 1572872 | tf_op jit(solution)/shard_map/ppermute | solution.py:266
  1.0 0.0 copy-start.2
  1.0 0.0 copy-start.1
  1.0 0.6 %copy-done.2 = s32[256]{0:T(256)S(1)} copy-done((s32[256]{0:T(256)S(1)}, s32[256]{0:T(256)}, u32[]{:S(2)}) %copy-start.2) | copy-done | bytes 1048
  1.6 0.0 copy-done.1
  1.7 0.3 rank_rows.1
  2.0 0.0 copy-done
  2.0 0.4 sort_rows.1.keep_ref
  2.3 0.0 collective-permute-done.1
  2.4 0.0 collective-permute-done.2
  2.4 0.3 collective-permute-done.emb_ref
  2.7 0.6 %join_cores.1 = (bf16[1040,128]{1,0:T(8,128)(2,1)S(1)}, bf16[1040,128]{1,0:T(8,128)(2,1)S(1)}, bf16[1040,128]{1,0:T(8,128)(2,1)S(1)}, bf16[1040,128]{1,0:T(8,128)(2,1)S(1)}) custom-call(bf16[1024,128]{1,0:T(8,128)(2,1)S(1)} %sort_rows.1.keep_ref, f32[16,128]{1,0:T(8,128)S(1)} %get-tuple-element.13.kept_ids_ref, ...), custom_call_target="tpu_custom_call" | custom-call | tf_op jit(solution)/shard_map/join_cores/pallas_call | solution.py:300
  3.3 4.8 %collective-permute-start.3 = (bf16[1040,128]{1,0:T(8,128)(2,1)S(1)}, bf16[1040,128]{1,0:T(8,128)(2,1)S(1)}, u32[]{:S(2)}, u32[]{:S(2)}) collective-permute-start(bf16[1040,128]{1,0:T(8,128)(2,1)S(1)} %get-tuple-element.15), channel_id=1, source_target_pairs={{4,6},{0,2},{9,11},{13,15},{6,4},{2,0},{11,9},{15,13},{20,22},{16,... | collective-permute-start | bytes 798728 | tf_op jit(solution)/shard_map/ppermute | solution.py:309
  8.1 0.7 %collective-permute-start.4 = (bf16[1040,128]{1,0:T(8,128)(2,1)S(1)}, bf16[1040,128]{1,0:T(8,128)(2,1)S(1)}, u32[]{:S(2)}, u32[]{:S(2)}) collective-permute-start(bf16[1040,128]{1,0:T(8,128)(2,1)S(1)} %get-tuple-element.16), channel_id=1, source_target_pairs={{12,4},{1,9},{14,6},{3,11},{28,20},{17,25},{30,22},{19,27}} | collective-permute-start | bytes 798728 | tf_op jit(solution)/shard_map/ppermute | solution.py:263
  8.8 0.7 %collective-permute-start.7 = (bf16[1040,128]{1,0:T(8,128)(2,1)S(1)}, bf16[1040,128]{1,0:T(8,128)(2,1)S(1)}, u32[]{:S(2)}, u32[]{:S(2)}) collective-permute-start(bf16[1040,128]{1,0:T(8,128)(2,1)S(1)} %get-tuple-element.17), channel_id=1, source_target_pairs={{10,4},{7,9},{8,6},{5,11},{26,20},{23,25},{24,22},{21,27}} | collective-permute-start | bytes 798728 | tf_op jit(solution)/shard_map/ppermute | solution.py:263
  9.5 0.7 %collective-permute-start.5 = (bf16[1040,128]{1,0:T(8,128)(2,1)S(1)}, bf16[1040,128]{1,0:T(8,128)(2,1)S(1)}, u32[]{:S(2)}, u32[]{:S(2)}) collective-permute-start(bf16[1040,128]{1,0:T(8,128)(2,1)S(1)} %get-tuple-element.17), channel_id=1, source_target_pairs={{14,4},{3,9},{12,6},{1,11},{30,20},{19,25},{28,22},{17,27}} | collective-permute-start | bytes 798728 | tf_op jit(solution)/shard_map/ppermute | solution.py:263
  10.2 5.3 %collective-permute-start.6 = (bf16[1040,128]{1,0:T(8,128)(2,1)S(1)}, bf16[1040,128]{1,0:T(8,128)(2,1)S(1)}, u32[]{:S(2)}, u32[]{:S(2)}) collective-permute-start(bf16[1040,128]{1,0:T(8,128)(2,1)S(1)} %get-tuple-element.14.refs_0_), channel_id=1, source_target_pairs={{0,4},{13,9},{2,6},{15,11},{16,20},{29,25},{18,22},{31,27}} | collective-permute-start | bytes 798728 | tf_op jit(solution)/shard_map/ppermute | solution.py:263
  15.5 0.0 collective-permute-done.3.refs_1_
  15.5 0.7 %collective-permute-start.8 = (bf16[1040,128]{1,0:T(8,128)(2,1)S(1)}, bf16[1040,128]{1,0:T(8,128)(2,1)S(1)}, u32[]{:S(2)}, u32[]{:S(2)}) collective-permute-start(bf16[1040,128]{1,0:T(8,128)(2,1)S(1)} %get-tuple-element.14.refs_0_), channel_id=1, source_target_pairs={{8,4},{5,9},{10,6},{7,11},{24,20},{21,25},{26,22},{23,27}} | collective-permute-start | bytes 798728 | tf_op jit(solution)/shard_map/ppermute | solution.py:263
  16.2 0.0 collective-permute-done.4.refs_2_
  16.2 4.7 %collective-permute-start.9 = (bf16[1040,128]{1,0:T(8,128)(2,1)S(1)}, bf16[1040,128]{1,0:T(8,128)(2,1)S(1)}, u32[]{:S(2)}, u32[]{:S(2)}) collective-permute-start(bf16[1040,128]{1,0:T(8,128)(2,1)S(1)} %collective-permute-done.3.refs_1_), channel_id=1, source_target_pairs={{0,4},{13,9},{2,6},{15,11},{16,20},{29,25},{18,22},{31,27}} | collective-permute-start | bytes 798728 | tf_op jit(solution)/shard_map/ppermute | solution.py:263
  20.9 0.0 collective-permute-done.5.refs_3_
  20.9 0.0 collective-permute-done.7.refs_5_
  20.9 0.2 collective-permute-done.6.refs_4_
  21.1 0.0 collective-permute-done.8.refs_6_
  21.2 3.6 %collective-permute-done.9.refs_7_ = bf16[1040,128]{1,0:T(8,128)(2,1)S(1)} collective-permute-done((bf16[1040,128]{1,0:T(8,128)(2,1)S(1)}, bf16[1040,128]{1,0:T(8,128)(2,1)S(1)}, u32[]{:S(2)}, u32[]{:S(2)}) %collective-permute-start.9) | collective-permute-done | bytes 266272 | tf_op jit(solution)/shard_map/ppermute | solution.py:263
  24.8 11.1 %all_to_all.5.got_ref = f32[16,1,128]{2,1,0:T(1,128)S(1)} all-to-all(f32[16,1,128]{2,1,0:T(1,128)S(1)} %meet_6_8.1), channel_id=1, replica_groups=mesh['groups'=2,'blk'=4,'clus'=4] {'blk','clus'}, dimensions={0} | all-to-all | bytes 16384 | tf_op jit(solution)/shard_map/all_to_all | solution.py:333
  35.9 0.8 %home_scores.1 = f32[1,256]{1,0:T(1,128)} custom-call(f32[16,1,128]{2,1,0:T(1,128)S(1)} %all_to_all.5.got_ref, s32[1,256]{1,0:T(1,128)S(1)} %get-tuple-element.18.target_ref), custom_call_target="tpu_custom_call" | custom-call | tf_op jit(solution)/shard_map/home_scores/pallas_call | solution.py:334
  (4 shorter events, 0.0 us)
Async XLA Ops:
  0.0 2.0 %copy-start = (bf16[256,1024]{1,0:T(8,128)(2,1)S(1)}, bf16[256,1024]{1,0:T(8,128)(2,1)}, u32[]{:S(2)}) copy-start(bf16[256,1024]{1,0:T(8,128)(2,1)} %emb_ref.1) | copy-start | bytes 1572868
  0.0 2.3 %collective-permute-start.1 = (s32[256]{0:T(256)}, s32[256]{0:T(256)S(1)}, u32[]{:S(2)}, u32[]{:S(2)}) collective-permute-start(s32[256]{0:T(256)} %param.4), channel_id=1, source_target_pairs={{0,1},{1,0},{2,3},{3,2},{4,5},{5,4},{6,7},{7,6},{8,9},{9,8},{10,11... | collective-permute-start | bytes 3080 | tf_op jit(solution)/shard_map/ppermute | solution.py:266
  0.5 1.9 %collective-permute-start.2 = (s32[256]{0:T(256)}, s32[256]{0:T(256)S(1)}, u32[]{:S(2)}, u32[]{:S(2)}) collective-permute-start(s32[256]{0:T(256)} %param.5), channel_id=1, source_target_pairs={{0,1},{1,0},{2,3},{3,2},{4,5},{5,4},{6,7},{7,6},{8,9},{9,8},{10,11... | collective-permute-start | bytes 3080 | tf_op jit(solution)/shard_map/ppermute | solution.py:266
  0.5 2.2 %collective-permute-start = (bf16[256,1024]{1,0:T(8,128)(2,1)}, bf16[256,1024]{1,0:T(8,128)(2,1)S(1)}, u32[]{:S(2)}, u32[]{:S(2)}) collective-permute-start(bf16[256,1024]{1,0:T(8,128)(2,1)} %emb_ref.1), channel_id=1, source_target_pairs={{0,1},{1,0},{2,3},{3,2},{4,5},{5,4},{6,7},{7,6},{8,9},{9,8},{10,11... | collective-permute-start | bytes 1572872 | tf_op jit(solution)/shard_map/ppermute | solution.py:266
  1.0 0.7 %copy-start.2 = (s32[256]{0:T(256)S(1)}, s32[256]{0:T(256)}, u32[]{:S(2)}) copy-start(s32[256]{0:T(256)} %param.5) | copy-start | bytes 3076
  1.0 0.7 %copy-start.1 = (s32[256]{0:T(256)S(1)}, s32[256]{0:T(256)}, u32[]{:S(2)}) copy-start(s32[256]{0:T(256)} %param.4) | copy-start | bytes 3076
  3.3 12.2 %collective-permute-start.3 = (bf16[1040,128]{1,0:T(8,128)(2,1)S(1)}, bf16[1040,128]{1,0:T(8,128)(2,1)S(1)}, u32[]{:S(2)}, u32[]{:S(2)}) collective-permute-start(bf16[1040,128]{1,0:T(8,128)(2,1)S(1)} %get-tuple-element.15), channel_id=1, source_target_pairs={{4,6},{0,2},{9,11},{13,15},{6,4},{2,0},{11,9},{15,13},{20,22},{16,... | collective-permute-start | bytes 798728 | tf_op jit(solution)/shard_map/ppermute | solution.py:309
  8.1 8.1 %collective-permute-start.4 = (bf16[1040,128]{1,0:T(8,128)(2,1)S(1)}, bf16[1040,128]{1,0:T(8,128)(2,1)S(1)}, u32[]{:S(2)}, u32[]{:S(2)}) collective-permute-start(bf16[1040,128]{1,0:T(8,128)(2,1)S(1)} %get-tuple-element.16), channel_id=1, source_target_pairs={{12,4},{1,9},{14,6},{3,11},{28,20},{17,25},{30,22},{19,27}} | collective-permute-start | bytes 798728 | tf_op jit(solution)/shard_map/ppermute | solution.py:263
  8.8 12.2 %collective-permute-start.7 = (bf16[1040,128]{1,0:T(8,128)(2,1)S(1)}, bf16[1040,128]{1,0:T(8,128)(2,1)S(1)}, u32[]{:S(2)}, u32[]{:S(2)}) collective-permute-start(bf16[1040,128]{1,0:T(8,128)(2,1)S(1)} %get-tuple-element.17), channel_id=1, source_target_pairs={{10,4},{7,9},{8,6},{5,11},{26,20},{23,25},{24,22},{21,27}} | collective-permute-start | bytes 798728 | tf_op jit(solution)/shard_map/ppermute | solution.py:263
  9.5 11.4 %collective-permute-start.5 = (bf16[1040,128]{1,0:T(8,128)(2,1)S(1)}, bf16[1040,128]{1,0:T(8,128)(2,1)S(1)}, u32[]{:S(2)}, u32[]{:S(2)}) collective-permute-start(bf16[1040,128]{1,0:T(8,128)(2,1)S(1)} %get-tuple-element.17), channel_id=1, source_target_pairs={{14,4},{3,9},{12,6},{1,11},{30,20},{19,25},{28,22},{17,27}} | collective-permute-start | bytes 798728 | tf_op jit(solution)/shard_map/ppermute | solution.py:263
  10.2 11.0 %collective-permute-start.6 = (bf16[1040,128]{1,0:T(8,128)(2,1)S(1)}, bf16[1040,128]{1,0:T(8,128)(2,1)S(1)}, u32[]{:S(2)}, u32[]{:S(2)}) collective-permute-start(bf16[1040,128]{1,0:T(8,128)(2,1)S(1)} %get-tuple-element.14.refs_0_), channel_id=1, source_target_pairs={{0,4},{13,9},{2,6},{15,11},{16,20},{29,25},{18,22},{31,27}} | collective-permute-start | bytes 798728 | tf_op jit(solution)/shard_map/ppermute | solution.py:263
  15.5 5.6 %collective-permute-start.8 = (bf16[1040,128]{1,0:T(8,128)(2,1)S(1)}, bf16[1040,128]{1,0:T(8,128)(2,1)S(1)}, u32[]{:S(2)}, u32[]{:S(2)}) collective-permute-start(bf16[1040,128]{1,0:T(8,128)(2,1)S(1)} %get-tuple-element.14.refs_0_), channel_id=1, source_target_pairs={{8,4},{5,9},{10,6},{7,11},{24,20},{21,25},{26,22},{23,27}} | collective-permute-start | bytes 798728 | tf_op jit(solution)/shard_map/ppermute | solution.py:263
  16.2 8.6 %collective-permute-start.9 = (bf16[1040,128]{1,0:T(8,128)(2,1)S(1)}, bf16[1040,128]{1,0:T(8,128)(2,1)S(1)}, u32[]{:S(2)}, u32[]{:S(2)}) collective-permute-start(bf16[1040,128]{1,0:T(8,128)(2,1)S(1)} %collective-permute-done.3.refs_1_), channel_id=1, source_target_pairs={{0,4},{13,9},{2,6},{15,11},{16,20},{29,25},{18,22},{31,27}} | collective-permute-start | bytes 798728 | tf_op jit(solution)/shard_map/ppermute | solution.py:263

commit v18 on v13

--- a/solution.py
+++ b/solution.py
@@ -74,7 +74,7 @@
 
 NEAR, ACROSS, FAR = 0, 2, 3
 BLOCKS = (
-    (0, None), (1, None), (0, FAR), (1, FAR), (0, NEAR), (0, ACROSS), (1, ACROSS), (1, NEAR),
+    (0, None), (1, None), (0, FAR), (1, FAR), (0, NEAR), (0, ACROSS), (1, NEAR), (1, ACROSS),
 )
 
 

time: 35.1 us -> 35.1 us (level)
  starting transfers between devices: 15 us -> 16.6 us
  waiting for transfers between devices: 5.07 us -> 4.21 us
  blocking collectives: 11.9 us -> 11.1 us
    ppermute x6, starting transfers between devices: 11.1 us -> 12.7 us  [to_meeting(): return lax.ppermute(value, everyone, pairs)]
    ppermute x6, waiting for transfers between devices: 4.72 us -> 3.86 us  [to_meeting(): return lax.ppermute(value, everyone, pairs)]
    all_to_all x1, blocking collectives: 11.9 us -> 11.1 us  [meet(): lax.all_to_all(best, everyone, split_axis=0, concat_axis=0, tiled=True)]
where the time goes in v18:
time: 35.1 us; the launch traced here: 34.9 us
  starting transfers between devices  16.6 us (47%)
  blocking collectives  11.1 us (32%)
  waiting for transfers between devices  4.21 us (12%)
  Pallas kernels  2.13 us (6%)
  local copies, waits for them, and re-layouts  0.68 us (2%)
    ppermute x6, starting transfers between devices, to_meeting(): return lax.ppermute(value, everyone, pairs)  12.7 us
    all_to_all x1, blocking collectives, meet(): lax.all_to_all(best, everyone, split_axis=0, concat_axis=0, tiled=True)  11.1 us
    ppermute x6, waiting for transfers between devices, to_meeting(): return lax.ppermute(value, everyone, pairs)  3.86 us
    ppermute x1, starting transfers between devices, meet(): crossed = lax.ppermute(far, 'clus', [(c, c ^ 2) for c in range(4)])  2.92 us
    ppermute x3, starting transfers between devices, meet(): lax.ppermute(value, 'clus', [(c, c ^ 1) for c in range(4)])  0.96 us
    pallas_call x1, Pallas kernels, meet(): pl.pallas_call(home_kernel, out_shape=jax.ShapeDtypeStruct((1, rows), jnp...  0.83 us
  transfers between devices with their start and end apart: 10, of which 3 were waited for; matrix products, arithmetic and copies ran while one was open for 0% of the time, Pallas kernels for 2%

profile of v18, /device:TPU:0, one launch (start us, length us, event | category | flops | bytes accessed | tf_op | source)
XLA Modules:
  0.0 34.9 jit_solution(10891958755890996478)
XLA Ops:
  0.0 0.0 copy-start
  0.0 0.5 %collective-permute-start.1 = (s32[256]{0:T(256)}, s32[256]{0:T(256)S(1)}, u32[]{:S(2)}, u32[]{:S(2)}) collective-permute-start(s32[256]{0:T(256)} %param.4), channel_id=1, source_target_pairs={{0,1},{1,0},{2,3},{3,2},{4,5},{5,4},{6,7},{7,6},{8,9},{9,8},{10,11... | collective-permute-start | bytes 3080 | tf_op jit(solution)/shard_map/ppermute | solution.py:266
  0.5 0.1 collective-permute-start.2
  0.5 0.4 %collective-permute-start = (bf16[256,1024]{1,0:T(8,128)(2,1)}, bf16[256,1024]{1,0:T(8,128)(2,1)S(1)}, u32[]{:S(2)}, u32[]{:S(2)}) collective-permute-start(bf16[256,1024]{1,0:T(8,128)(2,1)} %emb_ref.1), channel_id=1, source_target_pairs={{0,1},{1,0},{2,3},{3,2},{4,5},{5,4},{6,7},{7,6},{8,9},{9,8},{10,11... | collective-permute-start | bytes 1572872 | tf_op jit(solution)/shard_map/ppermute | solution.py:266
  1.0 0.0 copy-start.2
  1.0 0.0 copy-start.1
  1.0 0.6 %copy-done.2 = s32[256]{0:T(256)S(1)} copy-done((s32[256]{0:T(256)S(1)}, s32[256]{0:T(256)}, u32[]{:S(2)}) %copy-start.2) | copy-done | bytes 1048
  1.6 0.0 copy-done.1
  1.7 0.3 rank_rows.1
  2.0 0.0 copy-done
  2.0 0.4 %sort_rows.1.keep_ref = bf16[1024,128]{1,0:T(8,128)(2,1)S(1)} custom-call(bf16[256,1024]{1,0:T(8,128)(2,1)S(1)} %copy-done, bf16[128,256]{1,0:T(8,128)(2,1)S(1)} %get-tuple-element.12.place_ref), custom_call_target="tpu_custom_call" | custom-call | tf_op jit(solution)/shard_map/sort_rows/pallas_call | solution.py:292
  2.3 0.0 collective-permute-done.1
  2.4 0.0 collective-permute-done.2
  2.4 0.3 collective-permute-done.emb_ref
  2.7 0.6 %join_cores.1 = (bf16[1040,128]{1,0:T(8,128)(2,1)S(1)}, bf16[1040,128]{1,0:T(8,128)(2,1)S(1)}, bf16[1040,128]{1,0:T(8,128)(2,1)S(1)}, bf16[1040,128]{1,0:T(8,128)(2,1)S(1)}) custom-call(bf16[1024,128]{1,0:T(8,128)(2,1)S(1)} %sort_rows.1.keep_ref, f32[16,128]{1,0:T(8,128)S(1)} %get-tuple-element.13.kept_ids_ref, ...), custom_call_target="tpu_custom_call" | custom-call | tf_op jit(solution)/shard_map/join_cores/pallas_call | solution.py:300
  3.3 2.9 %collective-permute-start.3 = (bf16[1040,128]{1,0:T(8,128)(2,1)S(1)}, bf16[1040,128]{1,0:T(8,128)(2,1)S(1)}, u32[]{:S(2)}, u32[]{:S(2)}) collective-permute-start(bf16[1040,128]{1,0:T(8,128)(2,1)S(1)} %get-tuple-element.15), channel_id=1, source_target_pairs={{0,2},{1,3},{2,0},{3,1},{4,6},{5,7},{6,4},{7,5},{8,10},{9,11},{10,... | collective-permute-start | bytes 798728 | tf_op jit(solution)/shard_map/ppermute | solution.py:308
  6.2 0.7 %collective-permute-start.4 = (bf16[1040,128]{1,0:T(8,128)(2,1)S(1)}, bf16[1040,128]{1,0:T(8,128)(2,1)S(1)}, u32[]{:S(2)}, u32[]{:S(2)}) collective-permute-start(bf16[1040,128]{1,0:T(8,128)(2,1)S(1)} %get-tuple-element.16), channel_id=1, source_target_pairs={{12,4},{1,9},{14,6},{3,11},{28,20},{17,25},{30,22},{19,27}} | collective-permute-start | bytes 798728 | tf_op jit(solution)/shard_map/ppermute | solution.py:263
  6.9 0.7 %collective-permute-start.5 = (bf16[1040,128]{1,0:T(8,128)(2,1)S(1)}, bf16[1040,128]{1,0:T(8,128)(2,1)S(1)}, u32[]{:S(2)}, u32[]{:S(2)}) collective-permute-start(bf16[1040,128]{1,0:T(8,128)(2,1)S(1)} %get-tuple-element.17), channel_id=1, source_target_pairs={{14,4},{3,9},{12,6},{1,11},{30,20},{19,25},{28,22},{17,27}} | collective-permute-start | bytes 798728 | tf_op jit(solution)/shard_map/ppermute | solution.py:263
  7.6 0.7 %collective-permute-start.7 = (bf16[1040,128]{1,0:T(8,128)(2,1)S(1)}, bf16[1040,128]{1,0:T(8,128)(2,1)S(1)}, u32[]{:S(2)}, u32[]{:S(2)}) collective-permute-start(bf16[1040,128]{1,0:T(8,128)(2,1)S(1)} %get-tuple-element.14.refs_0_), channel_id=1, source_target_pairs={{8,4},{5,9},{10,6},{7,11},{24,20},{21,25},{26,22},{23,27}} | collective-permute-start | bytes 798728 | tf_op jit(solution)/shard_map/ppermute | solution.py:263
  8.3 5.3 %collective-permute-start.6 = (bf16[1040,128]{1,0:T(8,128)(2,1)S(1)}, bf16[1040,128]{1,0:T(8,128)(2,1)S(1)}, u32[]{:S(2)}, u32[]{:S(2)}) collective-permute-start(bf16[1040,128]{1,0:T(8,128)(2,1)S(1)} %get-tuple-element.14.refs_0_), channel_id=1, source_target_pairs={{0,4},{13,9},{2,6},{15,11},{16,20},{29,25},{18,22},{31,27}} | collective-permute-start | bytes 798728 | tf_op jit(solution)/shard_map/ppermute | solution.py:263
  13.6 0.0 collective-permute-done.3.refs_1_
  13.6 0.7 %collective-permute-start.9 = (bf16[1040,128]{1,0:T(8,128)(2,1)S(1)}, bf16[1040,128]{1,0:T(8,128)(2,1)S(1)}, u32[]{:S(2)}, u32[]{:S(2)}) collective-permute-start(bf16[1040,128]{1,0:T(8,128)(2,1)S(1)} %collective-permute-done.3.refs_1_), channel_id=1, source_target_pairs={{8,4},{5,9},{10,6},{7,11},{24,20},{21,25},{26,22},{23,27}} | collective-permute-start | bytes 798728 | tf_op jit(solution)/shard_map/ppermute | solution.py:263
  14.3 0.0 collective-permute-done.4.refs_2_
  14.3 4.7 %collective-permute-start.8 = (bf16[1040,128]{1,0:T(8,128)(2,1)S(1)}, bf16[1040,128]{1,0:T(8,128)(2,1)S(1)}, u32[]{:S(2)}, u32[]{:S(2)}) collective-permute-start(bf16[1040,128]{1,0:T(8,128)(2,1)S(1)} %collective-permute-done.3.refs_1_), channel_id=1, source_target_pairs={{0,4},{13,9},{2,6},{15,11},{16,20},{29,25},{18,22},{31,27}} | collective-permute-start | bytes 798728 | tf_op jit(solution)/shard_map/ppermute | solution.py:263
  19.0 0.0 collective-permute-done.5.refs_3_
  19.1 0.0 collective-permute-done.7.refs_5_
  19.1 0.2 collective-permute-done.6.refs_4_
  19.3 0.0 collective-permute-done.9.refs_7_
  19.3 3.6 %collective-permute-done.8.refs_6_ = bf16[1040,128]{1,0:T(8,128)(2,1)S(1)} collective-permute-done((bf16[1040,128]{1,0:T(8,128)(2,1)S(1)}, bf16[1040,128]{1,0:T(8,128)(2,1)S(1)}, u32[]{:S(2)}, u32[]{:S(2)}) %collective-permute-start.8) | collective-permute-done | bytes 266272 | tf_op jit(solution)/shard_map/ppermute | solution.py:263
  22.9 11.1 %all_to_all.5.got_ref = f32[16,1,128]{2,1,0:T(1,128)S(1)} all-to-all(f32[16,1,128]{2,1,0:T(1,128)S(1)} %meet_6_8.1), channel_id=1, replica_groups=mesh['groups'=2,'blk'=4,'clus'=4] {'blk','clus'}, dimensions={0} | all-to-all | bytes 16384 | tf_op jit(solution)/shard_map/all_to_all | solution.py:332
  34.0 0.8 %home_scores.1 = f32[1,256]{1,0:T(1,128)} custom-call(f32[16,1,128]{2,1,0:T(1,128)S(1)} %all_to_all.5.got_ref, s32[1,256]{1,0:T(1,128)S(1)} %get-tuple-element.18.target_ref), custom_call_target="tpu_custom_call" | custom-call | tf_op jit(solution)/shard_map/home_scores/pallas_call | solution.py:333
  (4 shorter events, 0.0 us)
Async XLA Ops:
  0.0 2.0 %copy-start = (bf16[256,1024]{1,0:T(8,128)(2,1)S(1)}, bf16[256,1024]{1,0:T(8,128)(2,1)}, u32[]{:S(2)}) copy-start(bf16[256,1024]{1,0:T(8,128)(2,1)} %emb_ref.1) | copy-start | bytes 1572868
  0.0 2.3 %collective-permute-start.1 = (s32[256]{0:T(256)}, s32[256]{0:T(256)S(1)}, u32[]{:S(2)}, u32[]{:S(2)}) collective-permute-start(s32[256]{0:T(256)} %param.4), channel_id=1, source_target_pairs={{0,1},{1,0},{2,3},{3,2},{4,5},{5,4},{6,7},{7,6},{8,9},{9,8},{10,11... | collective-permute-start | bytes 3080 | tf_op jit(solution)/shard_map/ppermute | solution.py:266
  0.5 1.9 %collective-permute-start.2 = (s32[256]{0:T(256)}, s32[256]{0:T(256)S(1)}, u32[]{:S(2)}, u32[]{:S(2)}) collective-permute-start(s32[256]{0:T(256)} %param.5), channel_id=1, source_target_pairs={{0,1},{1,0},{2,3},{3,2},{4,5},{5,4},{6,7},{7,6},{8,9},{9,8},{10,11... | collective-permute-start | bytes 3080 | tf_op jit(solution)/shard_map/ppermute | solution.py:266
  0.5 2.2 %collective-permute-start = (bf16[256,1024]{1,0:T(8,128)(2,1)}, bf16[256,1024]{1,0:T(8,128)(2,1)S(1)}, u32[]{:S(2)}, u32[]{:S(2)}) collective-permute-start(bf16[256,1024]{1,0:T(8,128)(2,1)} %emb_ref.1), channel_id=1, source_target_pairs={{0,1},{1,0},{2,3},{3,2},{4,5},{5,4},{6,7},{7,6},{8,9},{9,8},{10,11... | collective-permute-start | bytes 1572872 | tf_op jit(solution)/shard_map/ppermute | solution.py:266
  1.0 0.7 %copy-start.2 = (s32[256]{0:T(256)S(1)}, s32[256]{0:T(256)}, u32[]{:S(2)}) copy-start(s32[256]{0:T(256)} %param.5) | copy-start | bytes 3076
  1.0 0.7 %copy-start.1 = (s32[256]{0:T(256)S(1)}, s32[256]{0:T(256)}, u32[]{:S(2)}) copy-start(s32[256]{0:T(256)} %param.4) | copy-start | bytes 3076
  3.3 10.3 %collective-permute-start.3 = (bf16[1040,128]{1,0:T(8,128)(2,1)S(1)}, bf16[1040,128]{1,0:T(8,128)(2,1)S(1)}, u32[]{:S(2)}, u32[]{:S(2)}) collective-permute-start(bf16[1040,128]{1,0:T(8,128)(2,1)S(1)} %get-tuple-element.15), channel_id=1, source_target_pairs={{0,2},{1,3},{2,0},{3,1},{4,6},{5,7},{6,4},{7,5},{8,10},{9,11},{10,... | collective-permute-start | bytes 798728 | tf_op jit(solution)/shard_map/ppermute | solution.py:308
  6.2 8.1 %collective-permute-start.4 = (bf16[1040,128]{1,0:T(8,128)(2,1)S(1)}, bf16[1040,128]{1,0:T(8,128)(2,1)S(1)}, u32[]{:S(2)}, u32[]{:S(2)}) collective-permute-start(bf16[1040,128]{1,0:T(8,128)(2,1)S(1)} %get-tuple-element.16), channel_id=1, source_target_pairs={{12,4},{1,9},{14,6},{3,11},{28,20},{17,25},{30,22},{19,27}} | collective-permute-start | bytes 798728 | tf_op jit(solution)/shard_map/ppermute | solution.py:263
  6.9 12.1 %collective-permute-start.5 = (bf16[1040,128]{1,0:T(8,128)(2,1)S(1)}, bf16[1040,128]{1,0:T(8,128)(2,1)S(1)}, u32[]{:S(2)}, u32[]{:S(2)}) collective-permute-start(bf16[1040,128]{1,0:T(8,128)(2,1)S(1)} %get-tuple-element.17), channel_id=1, source_target_pairs={{14,4},{3,9},{12,6},{1,11},{30,20},{19,25},{28,22},{17,27}} | collective-permute-start | bytes 798728 | tf_op jit(solution)/shard_map/ppermute | solution.py:263
  7.6 11.5 %collective-permute-start.7 = (bf16[1040,128]{1,0:T(8,128)(2,1)S(1)}, bf16[1040,128]{1,0:T(8,128)(2,1)S(1)}, u32[]{:S(2)}, u32[]{:S(2)}) collective-permute-start(bf16[1040,128]{1,0:T(8,128)(2,1)S(1)} %get-tuple-element.14.refs_0_), channel_id=1, source_target_pairs={{8,4},{5,9},{10,6},{7,11},{24,20},{21,25},{26,22},{23,27}} | collective-permute-start | bytes 798728 | tf_op jit(solution)/shard_map/ppermute | solution.py:263
  8.3 11.0 %collective-permute-start.6 = (bf16[1040,128]{1,0:T(8,128)(2,1)S(1)}, bf16[1040,128]{1,0:T(8,128)(2,1)S(1)}, u32[]{:S(2)}, u32[]{:S(2)}) collective-permute-start(bf16[1040,128]{1,0:T(8,128)(2,1)S(1)} %get-tuple-element.14.refs_0_), channel_id=1, source_target_pairs={{0,4},{13,9},{2,6},{15,11},{16,20},{29,25},{18,22},{31,27}} | collective-permute-start | bytes 798728 | tf_op jit(solution)/shard_map/ppermute | solution.py:263
  13.6 5.6 %collective-permute-start.9 = (bf16[1040,128]{1,0:T(8,128)(2,1)S(1)}, bf16[1040,128]{1,0:T(8,128)(2,1)S(1)}, u32[]{:S(2)}, u32[]{:S(2)}) collective-permute-start(bf16[1040,128]{1,0:T(8,128)(2,1)S(1)} %collective-permute-done.3.refs_1_), channel_id=1, source_target_pairs={{8,4},{5,9},{10,6},{7,11},{24,20},{21,25},{26,22},{23,27}} | collective-permute-start | bytes 798728 | tf_op jit(solution)/shard_map/ppermute | solution.py:263
  14.3 8.6 %collective-permute-start.8 = (bf16[1040,128]{1,0:T(8,128)(2,1)S(1)}, bf16[1040,128]{1,0:T(8,128)(2,1)S(1)}, u32[]{:S(2)}, u32[]{:S(2)}) collective-permute-start(bf16[1040,128]{1,0:T(8,128)(2,1)S(1)} %collective-permute-done.3.refs_1_), channel_id=1, source_target_pairs={{0,4},{13,9},{2,6},{15,11},{16,20},{29,25},{18,22},{31,27}} | collective-permute-start | bytes 798728 | tf_op jit(solution)/shard_map/ppermute | solution.py:263

commit v19 on v18

--- a/solution.py
+++ b/solution.py
@@ -74,7 +74,7 @@
 
 NEAR, ACROSS, FAR = 0, 2, 3
 BLOCKS = (
-    (0, None), (1, None), (0, FAR), (1, FAR), (0, NEAR), (0, ACROSS), (1, NEAR), (1, ACROSS),
+    (0, None), (1, None), (0, FAR), (1, FAR), (0, ACROSS), (0, NEAR), (1, NEAR), (1, ACROSS),
 )
 
 

time: 35.1 us -> 36 us (1.026)
  starting transfers between devices: 16.6 us -> 17.7 us
    ppermute x6, starting transfers between devices: 12.7 us -> 13.8 us  [to_meeting(): return lax.ppermute(value, everyone, pairs)]
  transfers between devices with their start and end apart: 10 -> 10, of which waited for: 3 -> 2; matrix products, arithmetic and copies ran while one was open for 0% -> 0% of each run, Pallas kernels for 2% -> 2%
where the time goes in v19:
time: 36 us; the launch traced here: 35.8 us
  starting transfers between devices  17.7 us (49%)
  blocking collectives  10.9 us (30%)
  waiting for transfers between devices  4.17 us (12%)
  Pallas kernels  2.15 us (6%)
  local copies, waits for them, and re-layouts  0.68 us (2%)
    ppermute x6, starting transfers between devices, to_meeting(): return lax.ppermute(value, everyone, pairs)  13.8 us
    all_to_all x1, blocking collectives, meet(): lax.all_to_all(best, everyone, split_axis=0, concat_axis=0, tiled=True)  10.9 us
    ppermute x6, waiting for transfers between devices, to_meeting(): return lax.ppermute(value, everyone, pairs)  3.82 us
    ppermute x1, starting transfers between devices, meet(): crossed = lax.ppermute(far, 'clus', [(c, c ^ 2) for c in range(4)])  2.92 us
    ppermute x3, starting transfers between devices, meet(): lax.ppermute(value, 'clus', [(c, c ^ 1) for c in range(4)])  0.96 us
    pallas_call x1, Pallas kernels, meet(): pl.pallas_call(home_kernel, out_shape=jax.ShapeDtypeStruct((1, rows), jnp...  0.83 us
  transfers between devices with their start and end apart: 10, of which 2 were waited for; matrix products, arithmetic and copies ran while one was open for 0% of the time, Pallas kernels for 2%

profile of v19, /device:TPU:0, one launch (start us, length us, event | category | flops | bytes accessed | tf_op | source)
XLA Modules:
  0.0 35.8 jit_solution(4452128323770005783)
XLA Ops:
  0.0 0.0 copy-start
  0.0 0.5 %collective-permute-start.1 = (s32[256]{0:T(256)}, s32[256]{0:T(256)S(1)}, u32[]{:S(2)}, u32[]{:S(2)}) collective-permute-start(s32[256]{0:T(256)} %param.4), channel_id=1, source_target_pairs={{0,1},{1,0},{2,3},{3,2},{4,5},{5,4},{6,7},{7,6},{8,9},{9,8},{10,11... | collective-permute-start | bytes 3080 | tf_op jit(solution)/shard_map/ppermute | solution.py:266
  0.5 0.1 collective-permute-start.2
  0.5 0.4 %collective-permute-start = (bf16[256,1024]{1,0:T(8,128)(2,1)}, bf16[256,1024]{1,0:T(8,128)(2,1)S(1)}, u32[]{:S(2)}, u32[]{:S(2)}) collective-permute-start(bf16[256,1024]{1,0:T(8,128)(2,1)} %emb_ref.1), channel_id=1, source_target_pairs={{0,1},{1,0},{2,3},{3,2},{4,5},{5,4},{6,7},{7,6},{8,9},{9,8},{10,11... | collective-permute-start | bytes 1572872 | tf_op jit(solution)/shard_map/ppermute | solution.py:266
  1.0 0.0 copy-start.2
  1.0 0.0 copy-start.1
  1.0 0.6 %copy-done.2 = s32[256]{0:T(256)S(1)} copy-done((s32[256]{0:T(256)S(1)}, s32[256]{0:T(256)}, u32[]{:S(2)}) %copy-start.2) | copy-done | bytes 1048
  1.6 0.0 copy-done.1
  1.7 0.3 rank_rows.1
  2.0 0.0 copy-done
  2.0 0.4 %sort_rows.1.keep_ref = bf16[1024,128]{1,0:T(8,128)(2,1)S(1)} custom-call(bf16[256,1024]{1,0:T(8,128)(2,1)S(1)} %copy-done, bf16[128,256]{1,0:T(8,128)(2,1)S(1)} %get-tuple-element.12.place_ref), custom_call_target="tpu_custom_call" | custom-call | tf_op jit(solution)/shard_map/sort_rows/pallas_call | solution.py:292
  2.3 0.0 collective-permute-done.1
  2.4 0.0 collective-permute-done.2
  2.4 0.3 collective-permute-done.emb_ref
  2.7 0.6 %join_cores.1 = (bf16[1040,128]{1,0:T(8,128)(2,1)S(1)}, bf16[1040,128]{1,0:T(8,128)(2,1)S(1)}, bf16[1040,128]{1,0:T(8,128)(2,1)S(1)}, bf16[1040,128]{1,0:T(8,128)(2,1)S(1)}) custom-call(bf16[1024,128]{1,0:T(8,128)(2,1)S(1)} %sort_rows.1.keep_ref, f32[16,128]{1,0:T(8,128)S(1)} %get-tuple-element.13.kept_ids_ref, ...), custom_call_target="tpu_custom_call" | custom-call | tf_op jit(solution)/shard_map/join_cores/pallas_call | solution.py:300
  3.3 2.9 %collective-permute-start.3 = (bf16[1040,128]{1,0:T(8,128)(2,1)S(1)}, bf16[1040,128]{1,0:T(8,128)(2,1)S(1)}, u32[]{:S(2)}, u32[]{:S(2)}) collective-permute-start(bf16[1040,128]{1,0:T(8,128)(2,1)S(1)} %get-tuple-element.15), channel_id=1, source_target_pairs={{0,2},{1,3},{2,0},{3,1},{4,6},{5,7},{6,4},{7,5},{8,10},{9,11},{10,... | collective-permute-start | bytes 798728 | tf_op jit(solution)/shard_map/ppermute | solution.py:308
  6.2 0.7 %collective-permute-start.4 = (bf16[1040,128]{1,0:T(8,128)(2,1)S(1)}, bf16[1040,128]{1,0:T(8,128)(2,1)S(1)}, u32[]{:S(2)}, u32[]{:S(2)}) collective-permute-start(bf16[1040,128]{1,0:T(8,128)(2,1)S(1)} %get-tuple-element.16), channel_id=1, source_target_pairs={{12,4},{1,9},{14,6},{3,11},{28,20},{17,25},{30,22},{19,27}} | collective-permute-start | bytes 798728 | tf_op jit(solution)/shard_map/ppermute | solution.py:263
  6.9 0.7 %collective-permute-start.5 = (bf16[1040,128]{1,0:T(8,128)(2,1)S(1)}, bf16[1040,128]{1,0:T(8,128)(2,1)S(1)}, u32[]{:S(2)}, u32[]{:S(2)}) collective-permute-start(bf16[1040,128]{1,0:T(8,128)(2,1)S(1)} %get-tuple-element.17), channel_id=1, source_target_pairs={{14,4},{3,9},{12,6},{1,11},{30,20},{19,25},{28,22},{17,27}} | collective-permute-start | bytes 798728 | tf_op jit(solution)/shard_map/ppermute | solution.py:263
  7.6 4.7 %collective-permute-start.7 = (bf16[1040,128]{1,0:T(8,128)(2,1)S(1)}, bf16[1040,128]{1,0:T(8,128)(2,1)S(1)}, u32[]{:S(2)}, u32[]{:S(2)}) collective-permute-start(bf16[1040,128]{1,0:T(8,128)(2,1)S(1)} %get-tuple-element.14.refs_0_), channel_id=1, source_target_pairs={{0,4},{13,9},{2,6},{15,11},{16,20},{29,25},{18,22},{31,27}} | collective-permute-start | bytes 798728 | tf_op jit(solution)/shard_map/ppermute | solution.py:263
  12.3 0.7 %collective-permute-start.6 = (bf16[1040,128]{1,0:T(8,128)(2,1)S(1)}, bf16[1040,128]{1,0:T(8,128)(2,1)S(1)}, u32[]{:S(2)}, u32[]{:S(2)}) collective-permute-start(bf16[1040,128]{1,0:T(8,128)(2,1)S(1)} %get-tuple-element.14.refs_0_), channel_id=1, source_target_pairs={{8,4},{5,9},{10,6},{7,11},{24,20},{21,25},{26,22},{23,27}} | collective-permute-start | bytes 798728 | tf_op jit(solution)/shard_map/ppermute | solution.py:263
  13.0 0.0 collective-permute-done.3.refs_1_
  13.0 0.7 %collective-permute-start.9 = (bf16[1040,128]{1,0:T(8,128)(2,1)S(1)}, bf16[1040,128]{1,0:T(8,128)(2,1)S(1)}, u32[]{:S(2)}, u32[]{:S(2)}) collective-permute-start(bf16[1040,128]{1,0:T(8,128)(2,1)S(1)} %collective-permute-done.3.refs_1_), channel_id=1, source_target_pairs={{8,4},{5,9},{10,6},{7,11},{24,20},{21,25},{26,22},{23,27}} | collective-permute-start | bytes 798728 | tf_op jit(solution)/shard_map/ppermute | solution.py:263
  13.7 0.0 collective-permute-done.4.refs_2_
  13.7 6.4 %collective-permute-start.8 = (bf16[1040,128]{1,0:T(8,128)(2,1)S(1)}, bf16[1040,128]{1,0:T(8,128)(2,1)S(1)}, u32[]{:S(2)}, u32[]{:S(2)}) collective-permute-start(bf16[1040,128]{1,0:T(8,128)(2,1)S(1)} %collective-permute-done.3.refs_1_), channel_id=1, source_target_pairs={{0,4},{13,9},{2,6},{15,11},{16,20},{29,25},{18,22},{31,27}} | collective-permute-start | bytes 798728 | tf_op jit(solution)/shard_map/ppermute | solution.py:263
  20.1 0.0 collective-permute-done.5.refs_3_
  20.2 0.0 collective-permute-done.7.refs_5_
  20.2 0.0 collective-permute-done.6.refs_4_
  20.2 0.0 collective-permute-done.9.refs_7_
  20.2 3.8 %collective-permute-done.8.refs_6_ = bf16[1040,128]{1,0:T(8,128)(2,1)S(1)} collective-permute-done((bf16[1040,128]{1,0:T(8,128)(2,1)S(1)}, bf16[1040,128]{1,0:T(8,128)(2,1)S(1)}, u32[]{:S(2)}, u32[]{:S(2)}) %collective-permute-start.8) | collective-permute-done | bytes 266272 | tf_op jit(solution)/shard_map/ppermute | solution.py:263
  24.0 10.9 %all_to_all.5.got_ref = f32[16,1,128]{2,1,0:T(1,128)S(1)} all-to-all(f32[16,1,128]{2,1,0:T(1,128)S(1)} %meet_6_8.1), channel_id=1, replica_groups=mesh['groups'=2,'blk'=4,'clus'=4] {'blk','clus'}, dimensions={0} | all-to-all | bytes 16384 | tf_op jit(solution)/shard_map/all_to_all | solution.py:332
  35.0 0.8 %home_scores.1 = f32[1,256]{1,0:T(1,128)} custom-call(f32[16,1,128]{2,1,0:T(1,128)S(1)} %all_to_all.5.got_ref, s32[1,256]{1,0:T(1,128)S(1)} %get-tuple-element.18.target_ref), custom_call_target="tpu_custom_call" | custom-call | tf_op jit(solution)/shard_map/home_scores/pallas_call | solution.py:333
  (4 shorter events, 0.1 us)
Async XLA Ops:
  0.0 2.0 %copy-start = (bf16[256,1024]{1,0:T(8,128)(2,1)S(1)}, bf16[256,1024]{1,0:T(8,128)(2,1)}, u32[]{:S(2)}) copy-start(bf16[256,1024]{1,0:T(8,128)(2,1)} %emb_ref.1) | copy-start | bytes 1572868
  0.0 2.3 %collective-permute-start.1 = (s32[256]{0:T(256)}, s32[256]{0:T(256)S(1)}, u32[]{:S(2)}, u32[]{:S(2)}) collective-permute-start(s32[256]{0:T(256)} %param.4), channel_id=1, source_target_pairs={{0,1},{1,0},{2,3},{3,2},{4,5},{5,4},{6,7},{7,6},{8,9},{9,8},{10,11... | collective-permute-start | bytes 3080 | tf_op jit(solution)/shard_map/ppermute | solution.py:266
  0.5 1.9 %collective-permute-start.2 = (s32[256]{0:T(256)}, s32[256]{0:T(256)S(1)}, u32[]{:S(2)}, u32[]{:S(2)}) collective-permute-start(s32[256]{0:T(256)} %param.5), channel_id=1, source_target_pairs={{0,1},{1,0},{2,3},{3,2},{4,5},{5,4},{6,7},{7,6},{8,9},{9,8},{10,11... | collective-permute-start | bytes 3080 | tf_op jit(solution)/shard_map/ppermute | solution.py:266
  0.5 2.2 %collective-permute-start = (bf16[256,1024]{1,0:T(8,128)(2,1)}, bf16[256,1024]{1,0:T(8,128)(2,1)S(1)}, u32[]{:S(2)}, u32[]{:S(2)}) collective-permute-start(bf16[256,1024]{1,0:T(8,128)(2,1)} %emb_ref.1), channel_id=1, source_target_pairs={{0,1},{1,0},{2,3},{3,2},{4,5},{5,4},{6,7},{7,6},{8,9},{9,8},{10,11... | collective-permute-start | bytes 1572872 | tf_op jit(solution)/shard_map/ppermute | solution.py:266
  1.0 0.7 %copy-start.2 = (s32[256]{0:T(256)S(1)}, s32[256]{0:T(256)}, u32[]{:S(2)}) copy-start(s32[256]{0:T(256)} %param.5) | copy-start | bytes 3076
  1.0 0.7 %copy-start.1 = (s32[256]{0:T(256)S(1)}, s32[256]{0:T(256)}, u32[]{:S(2)}) copy-start(s32[256]{0:T(256)} %param.4) | copy-start | bytes 3076
  3.3 9.7 %collective-permute-start.3 = (bf16[1040,128]{1,0:T(8,128)(2,1)S(1)}, bf16[1040,128]{1,0:T(8,128)(2,1)S(1)}, u32[]{:S(2)}, u32[]{:S(2)}) collective-permute-start(bf16[1040,128]{1,0:T(8,128)(2,1)S(1)} %get-tuple-element.15), channel_id=1, source_target_pairs={{0,2},{1,3},{2,0},{3,1},{4,6},{5,7},{6,4},{7,5},{8,10},{9,11},{10,... | collective-permute-start | bytes 798728 | tf_op jit(solution)/shard_map/ppermute | solution.py:308
  6.2 7.5 %collective-permute-start.4 = (bf16[1040,128]{1,0:T(8,128)(2,1)S(1)}, bf16[1040,128]{1,0:T(8,128)(2,1)S(1)}, u32[]{:S(2)}, u32[]{:S(2)}) collective-permute-start(bf16[1040,128]{1,0:T(8,128)(2,1)S(1)} %get-tuple-element.16), channel_id=1, source_target_pairs={{12,4},{1,9},{14,6},{3,11},{28,20},{17,25},{30,22},{19,27}} | collective-permute-start | bytes 798728 | tf_op jit(solution)/shard_map/ppermute | solution.py:263
  6.9 13.2 %collective-permute-start.5 = (bf16[1040,128]{1,0:T(8,128)(2,1)S(1)}, bf16[1040,128]{1,0:T(8,128)(2,1)S(1)}, u32[]{:S(2)}, u32[]{:S(2)}) collective-permute-start(bf16[1040,128]{1,0:T(8,128)(2,1)S(1)} %get-tuple-element.17), channel_id=1, source_target_pairs={{14,4},{3,9},{12,6},{1,11},{30,20},{19,25},{28,22},{17,27}} | collective-permute-start | bytes 798728 | tf_op jit(solution)/shard_map/ppermute | solution.py:263
  7.6 12.6 %collective-permute-start.7 = (bf16[1040,128]{1,0:T(8,128)(2,1)S(1)}, bf16[1040,128]{1,0:T(8,128)(2,1)S(1)}, u32[]{:S(2)}, u32[]{:S(2)}) collective-permute-start(bf16[1040,128]{1,0:T(8,128)(2,1)S(1)} %get-tuple-element.14.refs_0_), channel_id=1, source_target_pairs={{0,4},{13,9},{2,6},{15,11},{16,20},{29,25},{18,22},{31,27}} | collective-permute-start | bytes 798728 | tf_op jit(solution)/shard_map/ppermute | solution.py:263
  12.3 7.8 %collective-permute-start.6 = (bf16[1040,128]{1,0:T(8,128)(2,1)S(1)}, bf16[1040,128]{1,0:T(8,128)(2,1)S(1)}, u32[]{:S(2)}, u32[]{:S(2)}) collective-permute-start(bf16[1040,128]{1,0:T(8,128)(2,1)S(1)} %get-tuple-element.14.refs_0_), channel_id=1, source_target_pairs={{8,4},{5,9},{10,6},{7,11},{24,20},{21,25},{26,22},{23,27}} | collective-permute-start | bytes 798728 | tf_op jit(solution)/shard_map/ppermute | solution.py:263
  13.0 7.2 %collective-permute-start.9 = (bf16[1040,128]{1,0:T(8,128)(2,1)S(1)}, bf16[1040,128]{1,0:T(8,128)(2,1)S(1)}, u32[]{:S(2)}, u32[]{:S(2)}) collective-permute-start(bf16[1040,128]{1,0:T(8,128)(2,1)S(1)} %collective-permute-done.3.refs_1_), channel_id=1, source_target_pairs={{8,4},{5,9},{10,6},{7,11},{24,20},{21,25},{26,22},{23,27}} | collective-permute-start | bytes 798728 | tf_op jit(solution)/shard_map/ppermute | solution.py:263
  13.7 10.3 %collective-permute-start.8 = (bf16[1040,128]{1,0:T(8,128)(2,1)S(1)}, bf16[1040,128]{1,0:T(8,128)(2,1)S(1)}, u32[]{:S(2)}, u32[]{:S(2)}) collective-permute-start(bf16[1040,128]{1,0:T(8,128)(2,1)S(1)} %collective-permute-done.3.refs_1_), channel_id=1, source_target_pairs={{0,4},{13,9},{2,6},{15,11},{16,20},{29,25},{18,22},{31,27}} | collective-permute-start | bytes 798728 | tf_op jit(solution)/shard_map/ppermute | solution.py:263

commit v20 on v19

--- a/solution.py
+++ b/solution.py
@@ -74,7 +74,7 @@
 
 NEAR, ACROSS, FAR = 0, 2, 3
 BLOCKS = (
-    (0, None), (1, None), (0, FAR), (1, FAR), (0, ACROSS), (0, NEAR), (1, NEAR), (1, ACROSS),
+    (0, None), (1, None), (0, ACROSS), (0, FAR), (0, NEAR), (1, FAR), (1, NEAR), (1, ACROSS),
 )
 
 
@@ -310,7 +310,7 @@
     for other, place in BLOCKS:
         if other and place == FAR:
             arrived.append(to_meeting(direct, place, cross=1))
-        elif not other and place == FAR:
+        elif not other and place in (FAR, ACROSS):
             arrived.append(to_meeting(first, place))
         else:
             value = crossed if other else near

time: 36 us -> 35.1 us (0.975)
  starting transfers between devices: 17.7 us -> 16.6 us
    ppermute x6, starting transfers between devices: 13.8 us -> 12.7 us  [to_meeting(): return lax.ppermute(value, everyone, pairs)]
  transfers between devices with their start and end apart: 10 -> 10, of which waited for: 2 -> 3; matrix products, arithmetic and copies ran while one was open for 0% -> 0% of each run, Pallas kernels for 2% -> 2%
where the time goes in v20:
time: 35.1 us; the launch traced here: 34.9 us
  starting transfers between devices  16.6 us (47%)
  blocking collectives  11.1 us (32%)
  waiting for transfers between devices  4.21 us (12%)
  Pallas kernels  2.13 us (6%)
  local copies, waits for them, and re-layouts  0.68 us (2%)
    ppermute x6, starting transfers between devices, to_meeting(): return lax.ppermute(value, everyone, pairs)  12.7 us
    all_to_all x1, blocking collectives, meet(): lax.all_to_all(best, everyone, split_axis=0, concat_axis=0, tiled=True)  11.1 us
    ppermute x6, waiting for transfers between devices, to_meeting(): return lax.ppermute(value, everyone, pairs)  3.86 us
    ppermute x1, starting transfers between devices, meet(): crossed = lax.ppermute(far, 'clus', [(c, c ^ 2) for c in range(4)])  2.92 us
    ppermute x3, starting transfers between devices, meet(): lax.ppermute(value, 'clus', [(c, c ^ 1) for c in range(4)])  0.96 us
    pallas_call x1, Pallas kernels, meet(): pl.pallas_call(home_kernel, out_shape=jax.ShapeDtypeStruct((1, rows), jnp...  0.83 us
  transfers between devices with their start and end apart: 10, of which 3 were waited for; matrix products, arithmetic and copies ran while one was open for 0% of the time, Pallas kernels for 2%

profile of v20, /device:TPU:0, one launch (start us, length us, event | category | flops | bytes accessed | tf_op | source)
XLA Modules:
  0.0 34.9 jit_solution(2648047285984456235)
XLA Ops:
  0.0 0.0 copy-start
  0.0 0.5 %collective-permute-start.1 = (s32[256]{0:T(256)}, s32[256]{0:T(256)S(1)}, u32[]{:S(2)}, u32[]{:S(2)}) collective-permute-start(s32[256]{0:T(256)} %param.4), channel_id=1, source_target_pairs={{0,1},{1,0},{2,3},{3,2},{4,5},{5,4},{6,7},{7,6},{8,9},{9,8},{10,11... | collective-permute-start | bytes 3080 | tf_op jit(solution)/shard_map/ppermute | solution.py:266
  0.5 0.1 collective-permute-start.2
  0.5 0.4 %collective-permute-start = (bf16[256,1024]{1,0:T(8,128)(2,1)}, bf16[256,1024]{1,0:T(8,128)(2,1)S(1)}, u32[]{:S(2)}, u32[]{:S(2)}) collective-permute-start(bf16[256,1024]{1,0:T(8,128)(2,1)} %emb_ref.1), channel_id=1, source_target_pairs={{0,1},{1,0},{2,3},{3,2},{4,5},{5,4},{6,7},{7,6},{8,9},{9,8},{10,11... | collective-permute-start | bytes 1572872 | tf_op jit(solution)/shard_map/ppermute | solution.py:266
  1.0 0.0 copy-start.2
  1.0 0.0 copy-start.1
  1.0 0.6 %copy-done.2 = s32[256]{0:T(256)S(1)} copy-done((s32[256]{0:T(256)S(1)}, s32[256]{0:T(256)}, u32[]{:S(2)}) %copy-start.2) | copy-done | bytes 1048
  1.6 0.0 copy-done.1
  1.7 0.3 rank_rows.1
  2.0 0.0 copy-done
  2.0 0.4 %sort_rows.1.keep_ref = bf16[1024,128]{1,0:T(8,128)(2,1)S(1)} custom-call(bf16[256,1024]{1,0:T(8,128)(2,1)S(1)} %copy-done, bf16[128,256]{1,0:T(8,128)(2,1)S(1)} %get-tuple-element.12.place_ref), custom_call_target="tpu_custom_call" | custom-call | tf_op jit(solution)/shard_map/sort_rows/pallas_call | solution.py:292
  2.3 0.0 collective-permute-done.1
  2.4 0.0 collective-permute-done.2
  2.4 0.3 collective-permute-done.emb_ref
  2.7 0.6 %join_cores.1 = (bf16[1040,128]{1,0:T(8,128)(2,1)S(1)}, bf16[1040,128]{1,0:T(8,128)(2,1)S(1)}, bf16[1040,128]{1,0:T(8,128)(2,1)S(1)}, bf16[1040,128]{1,0:T(8,128)(2,1)S(1)}) custom-call(bf16[1024,128]{1,0:T(8,128)(2,1)S(1)} %sort_rows.1.keep_ref, f32[16,128]{1,0:T(8,128)S(1)} %get-tuple-element.13.kept_ids_ref, ...), custom_call_target="tpu_custom_call" | custom-call | tf_op jit(solution)/shard_map/join_cores/pallas_call | solution.py:300
  3.3 2.9 %collective-permute-start.3 = (bf16[1040,128]{1,0:T(8,128)(2,1)S(1)}, bf16[1040,128]{1,0:T(8,128)(2,1)S(1)}, u32[]{:S(2)}, u32[]{:S(2)}) collective-permute-start(bf16[1040,128]{1,0:T(8,128)(2,1)S(1)} %get-tuple-element.15), channel_id=1, source_target_pairs={{0,2},{1,3},{2,0},{3,1},{4,6},{5,7},{6,4},{7,5},{8,10},{9,11},{10,... | collective-permute-start | bytes 798728 | tf_op jit(solution)/shard_map/ppermute | solution.py:308
  6.2 0.7 %collective-permute-start.5 = (bf16[1040,128]{1,0:T(8,128)(2,1)S(1)}, bf16[1040,128]{1,0:T(8,128)(2,1)S(1)}, u32[]{:S(2)}, u32[]{:S(2)}) collective-permute-start(bf16[1040,128]{1,0:T(8,128)(2,1)S(1)} %get-tuple-element.16), channel_id=1, source_target_pairs={{12,4},{1,9},{14,6},{3,11},{28,20},{17,25},{30,22},{19,27}} | collective-permute-start | bytes 798728 | tf_op jit(solution)/shard_map/ppermute | solution.py:263
  6.9 0.7 %collective-permute-start.4 = (bf16[1040,128]{1,0:T(8,128)(2,1)S(1)}, bf16[1040,128]{1,0:T(8,128)(2,1)S(1)}, u32[]{:S(2)}, u32[]{:S(2)}) collective-permute-start(bf16[1040,128]{1,0:T(8,128)(2,1)S(1)} %get-tuple-element.16), channel_id=1, source_target_pairs={{8,4},{5,9},{10,6},{7,11},{24,20},{21,25},{26,22},{23,27}} | collective-permute-start | bytes 798728 | tf_op jit(solution)/shard_map/ppermute | solution.py:263
  7.6 0.7 %collective-permute-start.7 = (bf16[1040,128]{1,0:T(8,128)(2,1)S(1)}, bf16[1040,128]{1,0:T(8,128)(2,1)S(1)}, u32[]{:S(2)}, u32[]{:S(2)}) collective-permute-start(bf16[1040,128]{1,0:T(8,128)(2,1)S(1)} %get-tuple-element.17), channel_id=1, source_target_pairs={{14,4},{3,9},{12,6},{1,11},{30,20},{19,25},{28,22},{17,27}} | collective-permute-start | bytes 798728 | tf_op jit(solution)/shard_map/ppermute | solution.py:263
  8.3 5.3 %collective-permute-start.6 = (bf16[1040,128]{1,0:T(8,128)(2,1)S(1)}, bf16[1040,128]{1,0:T(8,128)(2,1)S(1)}, u32[]{:S(2)}, u32[]{:S(2)}) collective-permute-start(bf16[1040,128]{1,0:T(8,128)(2,1)S(1)} %get-tuple-element.14.refs_0_), channel_id=1, source_target_pairs={{0,4},{13,9},{2,6},{15,11},{16,20},{29,25},{18,22},{31,27}} | collective-permute-start | bytes 798728 | tf_op jit(solution)/shard_map/ppermute | solution.py:263
  13.6 0.0 collective-permute-done.3.refs_1_
  13.6 0.7 %collective-permute-start.9 = (bf16[1040,128]{1,0:T(8,128)(2,1)S(1)}, bf16[1040,128]{1,0:T(8,128)(2,1)S(1)}, u32[]{:S(2)}, u32[]{:S(2)}) collective-permute-start(bf16[1040,128]{1,0:T(8,128)(2,1)S(1)} %collective-permute-done.3.refs_1_), channel_id=1, source_target_pairs={{8,4},{5,9},{10,6},{7,11},{24,20},{21,25},{26,22},{23,27}} | collective-permute-start | bytes 798728 | tf_op jit(solution)/shard_map/ppermute | solution.py:263
  14.3 0.0 collective-permute-done.5.refs_3_
  14.3 4.7 %collective-permute-start.8 = (bf16[1040,128]{1,0:T(8,128)(2,1)S(1)}, bf16[1040,128]{1,0:T(8,128)(2,1)S(1)}, u32[]{:S(2)}, u32[]{:S(2)}) collective-permute-start(bf16[1040,128]{1,0:T(8,128)(2,1)S(1)} %collective-permute-done.3.refs_1_), channel_id=1, source_target_pairs={{0,4},{13,9},{2,6},{15,11},{16,20},{29,25},{18,22},{31,27}} | collective-permute-start | bytes 798728 | tf_op jit(solution)/shard_map/ppermute | solution.py:263
  19.0 0.0 collective-permute-done.4.refs_2_
  19.1 0.0 collective-permute-done.7.refs_5_
  19.1 0.2 collective-permute-done.6.refs_4_
  19.3 0.0 collective-permute-done.9.refs_7_
  19.3 3.6 %collective-permute-done.8.refs_6_ = bf16[1040,128]{1,0:T(8,128)(2,1)S(1)} collective-permute-done((bf16[1040,128]{1,0:T(8,128)(2,1)S(1)}, bf16[1040,128]{1,0:T(8,128)(2,1)S(1)}, u32[]{:S(2)}, u32[]{:S(2)}) %collective-permute-start.8) | collective-permute-done | bytes 266272 | tf_op jit(solution)/shard_map/ppermute | solution.py:263
  22.9 11.1 %all_to_all.5.got_ref = f32[16,1,128]{2,1,0:T(1,128)S(1)} all-to-all(f32[16,1,128]{2,1,0:T(1,128)S(1)} %meet_6_8.1), channel_id=1, replica_groups=mesh['groups'=2,'blk'=4,'clus'=4] {'blk','clus'}, dimensions={0} | all-to-all | bytes 16384 | tf_op jit(solution)/shard_map/all_to_all | solution.py:332
  34.0 0.8 %home_scores.1 = f32[1,256]{1,0:T(1,128)} custom-call(f32[16,1,128]{2,1,0:T(1,128)S(1)} %all_to_all.5.got_ref, s32[1,256]{1,0:T(1,128)S(1)} %get-tuple-element.18.target_ref), custom_call_target="tpu_custom_call" | custom-call | tf_op jit(solution)/shard_map/home_scores/pallas_call | solution.py:333
  (4 shorter events, 0.0 us)
Async XLA Ops:
  0.0 2.0 %copy-start = (bf16[256,1024]{1,0:T(8,128)(2,1)S(1)}, bf16[256,1024]{1,0:T(8,128)(2,1)}, u32[]{:S(2)}) copy-start(bf16[256,1024]{1,0:T(8,128)(2,1)} %emb_ref.1) | copy-start | bytes 1572868
  0.0 2.3 %collective-permute-start.1 = (s32[256]{0:T(256)}, s32[256]{0:T(256)S(1)}, u32[]{:S(2)}, u32[]{:S(2)}) collective-permute-start(s32[256]{0:T(256)} %param.4), channel_id=1, source_target_pairs={{0,1},{1,0},{2,3},{3,2},{4,5},{5,4},{6,7},{7,6},{8,9},{9,8},{10,11... | collective-permute-start | bytes 3080 | tf_op jit(solution)/shard_map/ppermute | solution.py:266
  0.5 1.9 %collective-permute-start.2 = (s32[256]{0:T(256)}, s32[256]{0:T(256)S(1)}, u32[]{:S(2)}, u32[]{:S(2)}) collective-permute-start(s32[256]{0:T(256)} %param.5), channel_id=1, source_target_pairs={{0,1},{1,0},{2,3},{3,2},{4,5},{5,4},{6,7},{7,6},{8,9},{9,8},{10,11... | collective-permute-start | bytes 3080 | tf_op jit(solution)/shard_map/ppermute | solution.py:266
  0.5 2.2 %collective-permute-start = (bf16[256,1024]{1,0:T(8,128)(2,1)}, bf16[256,1024]{1,0:T(8,128)(2,1)S(1)}, u32[]{:S(2)}, u32[]{:S(2)}) collective-permute-start(bf16[256,1024]{1,0:T(8,128)(2,1)} %emb_ref.1), channel_id=1, source_target_pairs={{0,1},{1,0},{2,3},{3,2},{4,5},{5,4},{6,7},{7,6},{8,9},{9,8},{10,11... | collective-permute-start | bytes 1572872 | tf_op jit(solution)/shard_map/ppermute | solution.py:266
  1.0 0.7 %copy-start.2 = (s32[256]{0:T(256)S(1)}, s32[256]{0:T(256)}, u32[]{:S(2)}) copy-start(s32[256]{0:T(256)} %param.5) | copy-start | bytes 3076
  1.0 0.7 %copy-start.1 = (s32[256]{0:T(256)S(1)}, s32[256]{0:T(256)}, u32[]{:S(2)}) copy-start(s32[256]{0:T(256)} %param.4) | copy-start | bytes 3076
  3.3 10.3 %collective-permute-start.3 = (bf16[1040,128]{1,0:T(8,128)(2,1)S(1)}, bf16[1040,128]{1,0:T(8,128)(2,1)S(1)}, u32[]{:S(2)}, u32[]{:S(2)}) collective-permute-start(bf16[1040,128]{1,0:T(8,128)(2,1)S(1)} %get-tuple-element.15), channel_id=1, source_target_pairs={{0,2},{1,3},{2,0},{3,1},{4,6},{5,7},{6,4},{7,5},{8,10},{9,11},{10,... | collective-permute-start | bytes 798728 | tf_op jit(solution)/shard_map/ppermute | solution.py:308
  6.2 8.1 %collective-permute-start.5 = (bf16[1040,128]{1,0:T(8,128)(2,1)S(1)}, bf16[1040,128]{1,0:T(8,128)(2,1)S(1)}, u32[]{:S(2)}, u32[]{:S(2)}) collective-permute-start(bf16[1040,128]{1,0:T(8,128)(2,1)S(1)} %get-tuple-element.16), channel_id=1, source_target_pairs={{12,4},{1,9},{14,6},{3,11},{28,20},{17,25},{30,22},{19,27}} | collective-permute-start | bytes 798728 | tf_op jit(solution)/shard_map/ppermute | solution.py:263
  6.9 12.1 %collective-permute-start.4 = (bf16[1040,128]{1,0:T(8,128)(2,1)S(1)}, bf16[1040,128]{1,0:T(8,128)(2,1)S(1)}, u32[]{:S(2)}, u32[]{:S(2)}) collective-permute-start(bf16[1040,128]{1,0:T(8,128)(2,1)S(1)} %get-tuple-element.16), channel_id=1, source_target_pairs={{8,4},{5,9},{10,6},{7,11},{24,20},{21,25},{26,22},{23,27}} | collective-permute-start | bytes 798728 | tf_op jit(solution)/shard_map/ppermute | solution.py:263
  7.6 11.5 %collective-permute-start.7 = (bf16[1040,128]{1,0:T(8,128)(2,1)S(1)}, bf16[1040,128]{1,0:T(8,128)(2,1)S(1)}, u32[]{:S(2)}, u32[]{:S(2)}) collective-permute-start(bf16[1040,128]{1,0:T(8,128)(2,1)S(1)} %get-tuple-element.17), channel_id=1, source_target_pairs={{14,4},{3,9},{12,6},{1,11},{30,20},{19,25},{28,22},{17,27}} | collective-permute-start | bytes 798728 | tf_op jit(solution)/shard_map/ppermute | solution.py:263
  8.3 11.0 %collective-permute-start.6 = (bf16[1040,128]{1,0:T(8,128)(2,1)S(1)}, bf16[1040,128]{1,0:T(8,128)(2,1)S(1)}, u32[]{:S(2)}, u32[]{:S(2)}) collective-permute-start(bf16[1040,128]{1,0:T(8,128)(2,1)S(1)} %get-tuple-element.14.refs_0_), channel_id=1, source_target_pairs={{0,4},{13,9},{2,6},{15,11},{16,20},{29,25},{18,22},{31,27}} | collective-permute-start | bytes 798728 | tf_op jit(solution)/shard_map/ppermute | solution.py:263
  13.6 5.6 %collective-permute-start.9 = (bf16[1040,128]{1,0:T(8,128)(2,1)S(1)}, bf16[1040,128]{1,0:T(8,128)(2,1)S(1)}, u32[]{:S(2)}, u32[]{:S(2)}) collective-permute-start(bf16[1040,128]{1,0:T(8,128)(2,1)S(1)} %collective-permute-done.3.refs_1_), channel_id=1, source_target_pairs={{8,4},{5,9},{10,6},{7,11},{24,20},{21,25},{26,22},{23,27}} | collective-permute-start | bytes 798728 | tf_op jit(solution)/shard_map/ppermute | solution.py:263
  14.3 8.6 %collective-permute-start.8 = (bf16[1040,128]{1,0:T(8,128)(2,1)S(1)}, bf16[1040,128]{1,0:T(8,128)(2,1)S(1)}, u32[]{:S(2)}, u32[]{:S(2)}) collective-permute-start(bf16[1040,128]{1,0:T(8,128)(2,1)S(1)} %collective-permute-done.3.refs_1_), channel_id=1, source_target_pairs={{0,4},{13,9},{2,6},{15,11},{16,20},{29,25},{18,22},{31,27}} | collective-permute-start | bytes 798728 | tf_op jit(solution)/shard_map/ppermute | solution.py:263
